TPU v7x, 32 devices: a whole 2x2x4 slice. The times are simulated.
32 devices in a mesh: grp: 4 (over y, x), seq: 8 (over z, core).
Axes of the slice: x: 2, y: 2, z: 4, core: 2. Of those that a mesh axis runs over, the one named last changes fastest.
Arguments:
- tokens: bfloat16 [4, 4, 1024, 384], P('grp', None, 'seq'), may hold values from -6 to 6
- cotangent: bfloat16 [4, 4, 1024, 384], P('grp', None, 'seq'), may hold values from -6 to 6
- lengths: int32 [4, 4, 8], P('grp'), may hold values from 1 to 1017, as said below
- valid_mask: int32 [4, 4, 1024], P('grp'), may hold values 0 or 1
- lead_index: int32 [4], P('grp'), may hold values from 0 to 7
- sample_counts: int32 [4], replicated, may hold values from 1 to 16
- lead_table: bfloat16 [8, 384], replicated, may hold values from -6 to 6
- modulation_weight: bfloat16 [384, 2304], replicated, may hold values from -0.3125 to 0.3125
- modulation_bias: bfloat16 [2304], replicated, may hold values from -4 to 4
- attend_weight: bfloat16 [384, 1152], replicated, may hold values from -0.3125 to 0.3125
- output_weight: bfloat16 [384, 384], replicated, may hold values from -1.25 to 1.25
- output_bias: bfloat16 [384], replicated, may hold values from -4 to 4
- expand_weight: bfloat16 [384, 1536], replicated, may hold values from -0.3125 to 0.3125
- expand_bias: bfloat16 [1536], replicated, may hold values from -4 to 4
- shrink_weight: bfloat16 [1536, 384], replicated, may hold values from -0.15625 to 0.15625
- shrink_bias: bfloat16 [384], replicated, may hold values from -4 to 4
Outputs:
- output: bfloat16 [4, 4, 1024, 384], P('grp', None, 'seq')
- grad_tokens: float32 [4, 4, 1024, 384], P('grp', None, 'seq')
- grad_lead_table: float32 [8, 384], replicated
- grad_modulation_weight: float32 [384, 2304], replicated
- grad_modulation_bias: float32 [2304], replicated
- grad_attend_weight: float32 [384, 1152], replicated
- grad_output_weight: float32 [384, 384], replicated
- grad_output_bias: float32 [384], replicated
- grad_expand_weight: float32 [384, 1536], replicated
- grad_expand_bias: float32 [1536], replicated
- grad_shrink_weight: float32 [1536, 384], replicated
- grad_shrink_bias: float32 [384], replicated
Inputs may be any that keep to these rules, and one draw needn't show every extreme that they name: Each sequence's 8 lengths are positive and sum to 1024. In every group one sequence holds a document of 1017 positions.
All inputs are finite; a program needn't handle non-finite values. No bound on the sum of `valid_mask` on one device may be relied on, other than what follows from the above.
Results may differ from a plain program's by a relative error of at most 0.02.
Values may be sent and summed in bfloat16 or wider, within the bound.
No kernel may reach another device: no remote copies, remote signals or barrier semaphores. Data moves between devices by JAX's collectives and lax.ppermute only.
A program may use at most 320 MiB of HBM per device.

v0:
```python
from functools import partial
import math

import jax
import jax.numpy as jnp
from jax import lax
from jax.experimental import pallas as pl
from jax.experimental.pallas import tpu as pltpu
from jax.sharding import PartitionSpec as P

HEADS = 6
LEADS = 8

EPSILON = 1e-06
MASKED = -1e30

bf16 = jnp.bfloat16
f32 = jnp.float32


def normalize(values):
    centred = values - jnp.mean(values, axis=-1, keepdims=True)
    inverse = lax.rsqrt(jnp.mean(centred * centred, axis=-1, keepdims=True) + EPSILON)
    return (centred * inverse, inverse)


def normalize_back(grad, normed, inverse):
    return inverse * (
        grad
        - jnp.mean(grad, axis=-1, keepdims=True)
        - normed * jnp.mean(grad * normed, axis=-1, keepdims=True)
    )


def row_product(left, right):
    return lax.dot_general(left, right, (((0,), (0,)), ((), ())), preferred_element_type=f32)


def back_product(grad, weight):
    return lax.dot_general(grad, weight, (((1,), (1,)), ((), ())), preferred_element_type=f32)


def product(left, right):
    return jnp.dot(left, right, preferred_element_type=f32)


def total(parts):
    result = parts[0].astype(f32)
    for part in parts[1:]:
        result = result + part.astype(f32)
    return result


def owner_shift(seq_size, owners, share, step):
    return [(d, ((d // share + step) % owners) * share + d % share) for d in range(seq_size)]


def rows_to_owner(blocks, owner, share):
    owners = blocks.shape[0]
    seq_size = lax.axis_size("seq")
    pieces = []
    for step in range(owners):
        block = lax.dynamic_index_in_dim(blocks, (owner + step) % owners, 0, False)
        if step:
            block = lax.ppermute(block, "seq", owner_shift(seq_size, owners, share, step))
        pieces.append(block)
    return pieces


def rows_from_owner(pieces, share):
    owners = len(pieces)
    seq_size = lax.axis_size("seq")
    return [pieces[0]] + [
        lax.ppermute(pieces[step], "seq", owner_shift(seq_size, owners, share, owners - step))
        for step in range(1, owners)
    ]


def share_rows(rows, rank, share):
    seq_size = lax.axis_size("seq")
    if share == 2:
        return lax.ppermute(rows, "seq", [(d, d ^ 1) for d in range(seq_size)])
    groups = [list(range(first, first + share)) for first in range(0, seq_size, share)]
    gathered = lax.all_gather(rows, "seq", axis_index_groups=groups)
    gathered = jnp.roll(gathered, -rank, axis=0)[1:]
    return gathered.reshape((share - 1) * rows.shape[0], rows.shape[1])


def return_rows(rest, rank, share):
    seq_size = lax.axis_size("seq")
    if share == 2:
        return lax.ppermute(rest, "seq", [(d, d ^ 1) for d in range(seq_size)])
    groups = [list(range(first, first + share)) for first in range(0, seq_size, share)]
    parts = rest.reshape(share - 1, rest.shape[0] // (share - 1), rest.shape[1])
    parts = jnp.concatenate([jnp.zeros_like(parts[:1]), parts], axis=0)
    parts = jnp.roll(parts, rank, axis=0)
    return lax.psum_scatter(parts, "seq", scatter_dimension=0, axis_index_groups=groups)


def swap_cores(values):
    seq_size = lax.axis_size("seq")
    return lax.ppermute(values, "seq", [(d, d ^ 1) for d in range(seq_size)])


def line_size():
    return lax.axis_size("seq") // 2


def line_send(values, step):
    seq_size = lax.axis_size("seq")
    return lax.ppermute(values, "seq", [(d, (d + 2 * step) % seq_size) for d in range(seq_size)])


def plane_send(values, step):
    grp_size = lax.axis_size("grp")
    return lax.ppermute(values, "grp", [(d, plane_at(d, step)) for d in range(grp_size)])


def plane_at(group, step):
    grp_size = lax.axis_size("grp")
    if grp_size & (grp_size - 1) == 0:
        return group ^ step
    return (group + step) % grp_size


def plane_back(group, other):
    grp_size = lax.axis_size("grp")
    if grp_size & (grp_size - 1) == 0:
        return group ^ other
    return (group - other) % grp_size


def rows_at(values, at, count):
    return lax.dynamic_slice_in_dim(values, at * count, count, 0)


def plane_steps():
    return range(1, lax.axis_size("grp"))


def plane_parts(values):
    grp_size = lax.axis_size("grp")
    group = lax.axis_index("grp")
    count = values.shape[0] // grp_size
    return [rows_at(values, plane_at(group, step), count) for step in range(grp_size)]


def send_plane(parts):
    return [parts[0]] + [plane_send(parts[step], step) for step in plane_steps()]


def gather_plane(values):
    return [values] + [plane_send(values, step) for step in plane_steps()]


def line_parts(values):
    length = line_size()
    place = lax.axis_index("seq") // 2
    count = values.shape[0] // length
    return [rows_at(values, (place + step) % length, count) for step in range(length)]


def send_line(parts):
    return [parts[0]] + [line_send(parts[step], step) for step in range(1, len(parts))]


def sum_line(values):
    length = line_size()
    groups = [list(range(core, 2 * length, 2)) for core in range(2)]
    return lax.psum(values, "seq", axis_index_groups=groups)


def low_total(parts):
    return total(parts).astype(bf16)


def after(values, *others):
    return lax.optimization_barrier((values,) + others)[0]


def columns(values, width):
    return [values[:, at : at + width] for at in range(0, values.shape[1], width)]


def sum_share(values, share):
    seq_size = lax.axis_size("seq")
    groups = [list(range(first, first + share)) for first in range(0, seq_size, share)]
    return lax.psum(values, "seq", axis_index_groups=groups)


def after_all(values, *others):
    return lax.optimization_barrier(tuple(values) + others)[: len(values)]


def attention_kernel(
    score_scale, query, key, value, query_seg, query_pos, open_seg, key_pos, probs, attended, bias
):
    @pl.when(pl.program_id(1) == 0)
    def _():
        allow = (query_seg[...] == open_seg[...]) | (query_pos[...] == key_pos[...])
        bias[...] = jnp.where(allow, 0.0, MASKED)

    scaled = (query[0].astype(f32) * score_scale).astype(bf16)
    scores = back_product(scaled, key[0]) + bias[...]
    expo = jnp.exp(scores - jnp.max(scores, axis=1, keepdims=True))
    low = (expo * (1.0 / jnp.sum(expo, axis=1, keepdims=True))).astype(bf16)
    probs[0] = low
    attended[0] = product(low, value[0])


def attention(queries, keys, values, query_seg, query_pos, open_seg, key_pos, score_scale):
    head_count, rows, head_width = queries.shape
    key_count = keys.shape[1]
    step = max(32, min(rows, 2**18 // key_count))
    row_block = lambda i, h: (h, i, 0)
    key_block = lambda i, h: (h, 0, 0)
    size = head_count * rows * key_count
    return pl.pallas_call(
        partial(attention_kernel, score_scale),
        grid=(rows // step, head_count),
        in_specs=[
            pl.BlockSpec((1, step, head_width), row_block),
            pl.BlockSpec((1, key_count, head_width), key_block),
            pl.BlockSpec((1, key_count, head_width), key_block),
            pl.BlockSpec((step, 1), lambda i, h: (i, 0)),
            pl.BlockSpec((step, 1), lambda i, h: (i, 0)),
            pl.BlockSpec((1, key_count), lambda i, h: (0, 0)),
            pl.BlockSpec((1, key_count), lambda i, h: (0, 0)),
        ],
        out_specs=[
            pl.BlockSpec((1, step, key_count), row_block),
            pl.BlockSpec((1, step, head_width), row_block),
        ],
        out_shape=[
            jax.ShapeDtypeStruct((head_count, rows, key_count), bf16),
            jax.ShapeDtypeStruct((head_count, rows, head_width), f32),
        ],
        scratch_shapes=[pltpu.VMEM((step, key_count), f32)],
        compiler_params=pltpu.CompilerParams(vmem_limit_bytes=40 * 2**20),
        cost_estimate=pl.CostEstimate(
            flops=4 * size * head_width, bytes_accessed=2 * size, transcendentals=size
        ),
        name="attention",
    )(queries, keys, values, query_seg, query_pos, open_seg, key_pos)


GELU_RATE = math.sqrt(2.0 / math.pi)
GELU_CUBE = 0.044715
SHIFT_ONE, SCALE_ONE, GATE_ONE, SHIFT_TWO, SCALE_TWO, GATE_TWO, SHARE, EMBEDDING = range(8)


def inner(left, right):
    return row_product(left, right)


def column_sum(values):
    return jnp.sum(values, axis=0, keepdims=True)


def whole(*shape):
    return pl.BlockSpec(shape, lambda *_: (0,) * len(shape))


def kernel_params(mebibytes):
    return pltpu.CompilerParams(vmem_limit_bytes=mebibytes * 2**20)


def prepare_kernel(factor, place, lead, counts, table, weight, bias, attend_weight, mod, turned):
    width = table.shape[1]
    here = lax.broadcasted_iota(jnp.int32, table.shape, 0) == lead[0]
    embedding = column_sum(jnp.where(here, table[...].astype(f32), 0.0))
    lifted = (embedding / (1.0 + jnp.exp(-embedding))).astype(bf16)
    modulation = product(lifted, weight[...]) + bias[:, : weight.shape[1]]
    for part in range(6):
        mod[part : part + 1, :] = modulation[:, part * width : (part + 1) * width]
    every, mine = 0, 0
    for group in range(counts.shape[0]):
        every = every + counts[group]
        mine = mine + jnp.where(place[3] == group, counts[group], 0)
    row = jnp.zeros((1, width), jnp.int32)
    mod[SHARE : SHARE + 1, :] = (row + mine).astype(f32) / (row + every).astype(f32) * factor
    mod[EMBEDDING : EMBEDDING + 1, :] = embedding
    turned[...] = attend_weight[...].T


def prepare(place, lead, counts, table, weight, bias, attend_weight, positions):
    width = table.shape[1]
    operands = (table, weight, bias, attend_weight)
    shapes = [
        jax.ShapeDtypeStruct((8, width), f32),
        jax.ShapeDtypeStruct(attend_weight.shape[::-1], bf16),
    ]
    return pl.pallas_call(
        partial(prepare_kernel, counts.shape[0] / math.sqrt(positions)),
        grid=(1,),
        in_specs=[pl.BlockSpec(memory_space=pltpu.SMEM)] * 3 + [whole(*item.shape) for item in operands],
        out_specs=[whole(*item.shape) for item in shapes],
        out_shape=shapes,
        compiler_params=kernel_params(12),
        name="prepare",
    )(place, lead, counts, *operands)


def forward_kernel(
    head_width, score_scale, owners, place, lengths, own, rest, valid, mod, weight,
    expo, query, key_value, attended_wide, inverse_total, attended, bias,
):
    pair = pl.program_id(0)
    rows, width = own.shape
    key_count = rows + rest.shape[0]

    @pl.when(pair == 0)
    def _():
        shift, scale = mod[SHIFT_ONE : SHIFT_ONE + 1, :], 1.0 + mod[SCALE_ONE : SCALE_ONE + 1, :]
        first = (normalize(own[...].astype(f32))[0] * scale + shift).astype(bf16)
        query[...] = back_product(weight[:width, :], first).astype(bf16)
        key_value[:, :rows] = back_product(weight[width:, :], first).astype(bf16)
        for at in range(0, rest.shape[0], rows):
            part = normalize(rest[at : at + rows, :].astype(f32))[0]
            part = (part * scale + shift).astype(bf16)
            key_value[:, rows + at : 2 * rows + at] = back_product(weight[width:, :], part).astype(bf16)

        owner, rank = place[0], place[1]
        share = key_count // rows
        count = rows // owners
        ends = []
        for doc in range(lengths.shape[1]):
            ends.append(lengths[owner, doc] + (ends[-1] if doc else 0))

        def segment(positions):
            return sum((positions >= end).astype(jnp.int32) for end in ends)

        def block_at(r, step):
            return lax.rem(owner - step + owners, owners) * share + lax.rem(rank + r, share)

        lane = lax.broadcasted_iota(jnp.int32, (1, count), 1)
        query_pos = jnp.concatenate(
            [block_at(0, step) * count + lane for step in range(owners)], axis=1
        )
        query_seg = segment(query_pos)
        down = lax.broadcasted_iota(jnp.int32, (count, 1), 0)
        mine = lax.broadcasted_iota(jnp.int32, (owners, count), 0) == owner
        for r in range(share):
            for step in range(owners):
                block = block_at(r, step)
                key_pos = block * count + down
                open_rows = valid[:, pl.ds(pl.multiple_of(block * count, count), count)]
                open_rows = jnp.where((open_rows > 0) & mine, 1.0, 0.0)
                open_row = jnp.broadcast_to(column_sum(open_rows), (count, count))
                open_key = open_row.T[:, :1] > 0.5
                open_seg = jnp.where(open_key, segment(key_pos), -1)
                allow = (query_seg == open_seg) | (query_pos == key_pos)
                at = (r * owners + step) * count
                bias[at : at + count, :] = jnp.where(allow, 0.0, MASKED)

    for i in range(2):
        first = pl.multiple_of((2 * pair + i) * head_width, head_width)
        here = pl.ds(first, head_width)
        scaled = (query[here, :].astype(f32) * score_scale).astype(bf16)
        scores = inner(key_value[here, :], scaled) + bias[...]
        wide = jnp.exp(scores - jnp.max(scores, axis=0, keepdims=True))
        inverse = 1.0 / column_sum(wide)
        low = wide.astype(bf16)
        expo[i] = low
        inverse_total[i] = inverse
        values = key_value[pl.ds(pl.multiple_of(width + first, head_width), head_width), :]
        attended_wide[here, :] = product(values, low) * inverse

    @pl.when(pair == pl.num_programs(0) - 1)
    def _():
        attended[...] = attended_wide[...].T.astype(bf16)


def forward_attention(place, lengths, valid, own, rest, mod, weight):
    rows, width = own.shape
    key_count = rows + rest.shape[0]
    head_width = width // HEADS
    size = HEADS * rows * key_count
    scalars = pl.BlockSpec(memory_space=pltpu.SMEM)
    return pl.pallas_call(
        partial(forward_kernel, head_width, 1.0 / math.sqrt(head_width), lengths.shape[0]),
        grid=(HEADS // 2,),
        in_specs=[scalars, scalars] + [whole(*item.shape) for item in (own, rest, valid, mod, weight)],
        out_specs=[
            pl.BlockSpec((2, key_count, rows), lambda p: (p, 0, 0)),
            whole(width, rows),
            whole(2 * width, key_count),
            whole(width, rows),
            pl.BlockSpec((2, 1, rows), lambda p: (p, 0, 0)),
            whole(rows, width),
        ],
        out_shape=[
            pltpu.HBM((HEADS, key_count, rows), bf16),
            jax.ShapeDtypeStruct((width, rows), bf16),
            jax.ShapeDtypeStruct((2 * width, key_count), bf16),
            jax.ShapeDtypeStruct((width, rows), f32),
            jax.ShapeDtypeStruct((HEADS, 1, rows), f32),
            jax.ShapeDtypeStruct((rows, width), bf16),
        ],
        scratch_shapes=[pltpu.VMEM((key_count, rows), f32)],
        compiler_params=kernel_params(20),
        cost_estimate=pl.CostEstimate(
            flops=16 * size * head_width, bytes_accessed=2 * size, transcendentals=size
        ),
        name="forward_attention",
    )(place, lengths, own, rest, valid, mod, weight)


def middle_kernel(
    place, own, attended, cotangent, mod, bias, output_weight, expand_weight, shrink_weight,
    keep, send, packed_output, grad_attended, grad_residual, sums, *output,
):
    first_core = place[2] == 0
    rows, width = own.shape
    blocks = expand_weight.shape[1] // width
    row = lambda at: mod[at : at + 1, :]
    bias_row = lambda at: bias[:, at * width : (at + 1) * width]
    share = row(SHARE)
    scale_two = 1.0 + row(SCALE_TWO)
    branch_one = product(attended[...], output_weight[...]) + bias_row(6)
    residual = own[...].astype(f32) + row(GATE_ONE) * branch_one
    normed, inverse = normalize(residual)
    mixed = (normed * scale_two + row(SHIFT_TWO)).astype(bf16)
    wide = cotangent[...].astype(f32)
    grad_two = (wide * row(GATE_TWO)).astype(bf16)
    sums[...] = jnp.zeros_like(sums)
    branch_two = jnp.zeros((rows, width), f32) + bias_row(7 + blocks)
    grad_mixed = jnp.zeros((rows, width), f32)
    for block in range(blocks):
        part = slice(block * width, (block + 1) * width)
        hidden = product(mixed, expand_weight[:, part]) + bias_row(7 + block)
        square = hidden * hidden
        bent = jnp.tanh(GELU_RATE * hidden * (1.0 + GELU_CUBE * square))
        half = 0.5 + 0.5 * bent
        slope = half + 0.5 * hidden * (1.0 - bent * bent) * (
            GELU_RATE + (3.0 * GELU_CUBE * GELU_RATE) * square
        )
        active = (hidden * half).astype(bf16)
        branch_two = branch_two + product(active, shrink_weight[part, :])
        grad_hidden = (back_product(grad_two, shrink_weight[part, :]) * slope).astype(bf16)
        grad_shrink = inner(active, grad_two) * share
        grad_expand = inner(mixed, grad_hidden) * share
        keep[part, :] = jnp.where(first_core, grad_shrink, grad_expand).astype(bf16)
        send[part, :] = jnp.where(first_core, grad_expand, grad_shrink).astype(bf16)
        sums[7 + block : 8 + block, :] = column_sum(grad_hidden.astype(f32)) * share
        grad_mixed = grad_mixed + back_product(grad_hidden, expand_weight[:, part])
    result = (residual + row(GATE_TWO) * branch_two).astype(bf16)
    count = rows // len(output)
    for step in range(len(output)):
        output[step][...] = result[step * count : (step + 1) * count, :]
    sums[5:6, :] = column_sum(wide * branch_two) * share
    sums[7 + blocks : 8 + blocks, :] = column_sum(grad_two.astype(f32)) * share
    sums[4:5, :] = column_sum(grad_mixed * normed) * share
    sums[3:4, :] = column_sum(grad_mixed) * share
    grad_wide = wide + normalize_back(grad_mixed * scale_two, normed, inverse)
    grad_residual[...] = grad_wide
    sums[2:3, :] = column_sum(grad_wide * branch_one) * share
    grad_one = (grad_wide * row(GATE_ONE)).astype(bf16)
    sums[6:7, :] = column_sum(grad_one.astype(f32)) * share
    packed_output[...] = (inner(attended[...], grad_one) * share).astype(bf16)
    grad_attended[...] = back_product(output_weight[...], grad_one).astype(bf16)


def middle(
    owners, place, own, attended, cotangent, mod, bias, output_weight, expand_weight, shrink_weight
):
    rows, width = own.shape
    hidden = expand_weight.shape[1]
    operands = (
        own, attended, cotangent, mod, bias, output_weight, expand_weight, shrink_weight
    )
    shapes = [
        jax.ShapeDtypeStruct((hidden, width), bf16),
        jax.ShapeDtypeStruct((hidden, width), bf16),
        pltpu.HBM((width, width), bf16),
        pltpu.HBM((width, rows), bf16),
        pltpu.HBM((rows, width), f32),
        jax.ShapeDtypeStruct((16, width), f32),
    ] + [jax.ShapeDtypeStruct((rows // owners, width), bf16)] * owners
    return pl.pallas_call(
        middle_kernel,
        grid=(1,),
        in_specs=[pl.BlockSpec(memory_space=pltpu.SMEM)] + [whole(*item.shape) for item in operands],
        out_specs=[whole(*item.shape) for item in shapes],
        out_shape=shapes,
        compiler_params=kernel_params(16),
        cost_estimate=pl.CostEstimate(
            flops=16 * rows * width * hidden, bytes_accessed=2**24, transcendentals=rows * hidden
        ),
        name="middle",
    )(place, *operands)


def backward_kernel(
    head_width, score_scale, place, expo, query, key_value, attended_wide, inverse_total,
    grad_attended, own, rest, mod, weight, packed_output, sums_in, keep, send, own_part, sums,
    grad_query, grad_key, grad_value,
):
    pair = pl.program_id(0)
    rows, width = own.shape
    grad_keys, grad_values = [], []
    for i in range(2):
        first = pl.multiple_of((2 * pair + i) * head_width, head_width)
        here = pl.ds(first, head_width)
        scaled = (query[here, :].astype(f32) * score_scale).astype(bf16)
        keys = key_value[here, :]
        values = key_value[pl.ds(pl.multiple_of(width + first, head_width), head_width), :]
        grads = (grad_attended[here, :].astype(f32) * inverse_total[i]).astype(bf16)
        delta = column_sum(grads.astype(f32) * attended_wide[here, :])
        low = expo[i]
        grad_scores = (low.astype(f32) * (inner(values, grads) - delta)).astype(bf16)
        grad_values.append(back_product(low, grads))
        grad_keys.append(back_product(grad_scores, scaled))
        grad_query[here, :] = (product(keys, grad_scores) * score_scale).astype(bf16)
    grad_key[pair] = jnp.concatenate(grad_keys, axis=1).astype(bf16)
    grad_value[pair] = jnp.concatenate(grad_values, axis=1).astype(bf16)

    @pl.when(pair == pl.num_programs(0) - 1)
    def _():
        row = lambda at: mod[at : at + 1, :]
        share = row(SHARE)
        shift, scale = row(SHIFT_ONE), 1.0 + row(SCALE_ONE)
        pairs = range(HEADS // 2)
        packed_key = jnp.zeros((width, width), f32)
        packed_value = jnp.zeros((width, width), f32)
        total_shift = jnp.zeros((1, width), f32)
        total_scale = jnp.zeros((1, width), f32)
        for at in range(0, rows + rest.shape[0], rows):
            here = slice(at, at + rows)
            source = own[...] if at == 0 else rest[at - rows : at, :]
            normed = normalize(source.astype(f32))[0]
            mixed = (normed * scale + shift).astype(bf16)
            keys = jnp.concatenate([grad_key[pair, here, :] for pair in pairs], axis=1)
            values = jnp.concatenate([grad_value[pair, here, :] for pair in pairs], axis=1)
            part = product(keys, weight[width : 2 * width, :]) + product(
                values, weight[2 * width :, :]
            )
            if at == 0:
                part = part + inner(grad_query[...], weight[:width, :])
                own_part[...] = part
                packed_query = product(grad_query[...], mixed).T
            else:
                send[2 * width + at - rows : 2 * width + at, :] = part.astype(bf16)
            packed_key = packed_key + inner(mixed, keys)
            packed_value = packed_value + inner(mixed, values)
            total_shift = total_shift + column_sum(part)
            total_scale = total_scale + column_sum(part * normed)
        first_core = place[2] == 0
        packed = [packed_query * share, packed_key * share, packed_value * share, packed_output[...].astype(f32)]
        for half in range(2):
            here = slice(half * width, (half + 1) * width)
            keep[here, :] = jnp.where(first_core, packed[half], packed[2 + half]).astype(bf16)
            send[here, :] = jnp.where(first_core, packed[2 + half], packed[half]).astype(bf16)
        sums[...] = sums_in[...]
        sums[0:1, :] = total_shift * share
        sums[1:2, :] = total_scale * share
        send[2 * width + rest.shape[0] :, :] = sums[...].astype(bf16)


def backward_attention(place, saved, grad_attended, own, rest, mod, weight, packed_output, sums):
    expo, query, key_value, attended_wide, inverse_total = saved
    rows, width = own.shape
    key_count = rows + rest.shape[0]
    head_width = width // HEADS
    size = HEADS * rows * key_count
    operands = (
        query, key_value, attended_wide, inverse_total, grad_attended, own, rest, mod, weight,
        packed_output, sums,
    )
    specs = [whole(*item.shape) for item in operands]
    specs[3] = pl.BlockSpec((2, 1, rows), lambda p: (p, 0, 0))
    shapes = [
        jax.ShapeDtypeStruct((2 * width, width), bf16),
        jax.ShapeDtypeStruct((2 * width + rest.shape[0] + sums.shape[0], width), bf16),
        jax.ShapeDtypeStruct((rows, width), f32),
        jax.ShapeDtypeStruct(sums.shape, f32),
    ]
    return pl.pallas_call(
        partial(backward_kernel, head_width, 1.0 / math.sqrt(head_width)),
        grid=(HEADS // 2,),
        in_specs=[
            pl.BlockSpec(memory_space=pltpu.SMEM),
            pl.BlockSpec((2, key_count, rows), lambda p: (p, 0, 0)),
        ]
        + specs,
        out_specs=[whole(*item.shape) for item in shapes],
        out_shape=shapes,
        scratch_shapes=[
            pltpu.VMEM((width, rows), bf16),
            pltpu.VMEM((HEADS // 2, key_count, 2 * head_width), bf16),
            pltpu.VMEM((HEADS // 2, key_count, 2 * head_width), bf16),
        ],
        compiler_params=kernel_params(16),
        cost_estimate=pl.CostEstimate(
            flops=32 * size * head_width, bytes_accessed=2 * size, transcendentals=0
        ),
        name="backward_attention",
    )(place, pltpu.with_memory_space_constraint(expo, pltpu.HBM), *operands)


def finish_kernel(own, part, received, grad_residual, mod, sums, *results):
    rows, width = own.shape
    count = rows // len(results)
    normed, inverse = normalize(own[...].astype(f32))
    first = received.shape[0] - rows - sums.shape[0]
    grad = (part[...] + received[first : first + rows, :].astype(f32)) * (1.0 + mod[SCALE_ONE : SCALE_ONE + 1, :])
    grad = (grad_residual[...] + normalize_back(grad, normed, inverse)).astype(bf16)
    both = (sums[...] + received[first + rows :, :].astype(f32)).astype(bf16)
    for step, result in enumerate(results):
        result[:count, :] = grad[step * count : (step + 1) * count, :]
        result[count:, :] = both


def finish_rows(owners, own, part, received, grad_residual, mod, sums):
    operands = (own, part, received, grad_residual, mod, sums)
    shape = (own.shape[0] // owners + sums.shape[0], own.shape[1])
    return pl.pallas_call(
        finish_kernel,
        grid=(1,),
        in_specs=[whole(*item.shape) for item in operands],
        out_specs=[whole(*shape)] * owners,
        out_shape=[jax.ShapeDtypeStruct(shape, bf16)] * owners,
        compiler_params=kernel_params(12),
        name="finish_rows",
    )(*operands)


def placed_kernel(owners, place, *refs):
    pieces, result = refs[:owners], refs[owners]
    for step in range(owners):
        result[lax.rem(place[0] + step, owners)] = pieces[step][...]


def placed(place, pieces):
    owners = len(pieces)
    shape = (owners,) + pieces[0].shape
    return pl.pallas_call(
        partial(placed_kernel, owners),
        grid=(1,),
        in_specs=[pl.BlockSpec(memory_space=pltpu.SMEM)] + [whole(*item.shape) for item in pieces],
        out_specs=whole(*shape),
        out_shape=jax.ShapeDtypeStruct(shape, pieces[0].dtype),
        compiler_params=kernel_params(8),
        name="placed",
    )(place, *pieces)


def placed_sums_kernel(owners, place, lead, mod, *refs):
    pieces, (result, vector) = refs[:owners], refs[owners:]
    count = result.shape[1]
    for step in range(owners):
        result[lax.rem(place[0] + step, owners)] = pieces[step][:count, :].astype(f32)
    below = total([piece[count:, :] for piece in pieces])
    row = lax.broadcasted_iota(jnp.int32, below.shape, 0)
    below = jnp.where(row == 12, mod[EMBEDDING : EMBEDDING + 1, :], below)
    below = jnp.where(row == 13, jnp.full(below.shape, lead[0]).astype(f32), below)
    vector[...] = below.astype(bf16)


def placed_sums(place, lead, mod, pieces):
    owners = len(pieces)
    below, width = 16, mod.shape[1]
    shapes = [
        jax.ShapeDtypeStruct((owners, pieces[0].shape[0] - below, width), f32),
        jax.ShapeDtypeStruct((below, width), bf16),
    ]
    return pl.pallas_call(
        partial(placed_sums_kernel, owners),
        grid=(1,),
        in_specs=[pl.BlockSpec(memory_space=pltpu.SMEM)] * 2
        + [whole(*mod.shape)]
        + [whole(*item.shape) for item in pieces],
        out_specs=[whole(*item.shape) for item in shapes],
        out_shape=shapes,
        compiler_params=kernel_params(8),
        name="placed_sums",
    )(place, lead, mod, *pieces)


def ordered_kernel(grp_size, line, count, targets, place, *refs):
    own, received, outputs = refs[:grp_size], refs[grp_size : 2 * grp_size], refs[2 * grp_size :]
    width = own[0].shape[1]
    core, group, at_line = place[2], place[3], place[4]

    def write(side, ref, b):
        for c in range(line):
            from_c = lax.rem(at_line - c + line, line)
            here = pl.ds(pl.multiple_of(from_c * count, count), count)
            first = ((side * grp_size + b) * line + c) * count
            output, row, column = targets[first // width]
            row = row + first % width
            outputs[output][row : row + count, column : column + width] = ref[here, :].astype(f32)

    def choose(side, refs_here):
        for step in range(grp_size):
            for g in range(grp_size):
                b = g ^ step if grp_size & (grp_size - 1) == 0 else (g - step) % grp_size

                @pl.when(group == g)
                def _():
                    write(side, refs_here[step], b)

    for side in range(2):

        @pl.when(core == side)
        def _():
            choose(side, own)
            choose(1 - side, received)


def ordered(place, own, rows, targets, shapes):
    line = 1 if line_size() > 4 else line_size()
    received = [swap_cores(part) for part in own]
    shapes = [jax.ShapeDtypeStruct(shape, f32) for shape in shapes]
    return pl.pallas_call(
        partial(ordered_kernel, len(own), line, rows // line, targets),
        grid=(1,),
        in_specs=[pl.BlockSpec(memory_space=pltpu.SMEM)]
        + [whole(rows, part.shape[1]) for part in own + received],
        out_specs=[whole(*item.shape) for item in shapes],
        out_shape=shapes,
        compiler_params=kernel_params(16),
        name="ordered",
    )(place, *own, *received)


def vectors_kernel(parts_count, *refs):
    parts = [ref[...].astype(f32) for ref in refs[:parts_count]]
    weight = refs[parts_count]
    grad_weight, grad_bias, table, biases = refs[parts_count + 1 :]
    width = parts[0].shape[1]
    biases[...] = total([part[6:12] for part in parts])
    stacked = jnp.concatenate([part[12:13] for part in parts] + [jnp.zeros((8 - parts_count, width), f32)])
    gate = 1.0 / (1.0 + jnp.exp(-stacked))
    lifted = (stacked * gate).astype(bf16).astype(f32).T
    grad_lifted = jnp.zeros((8, width), f32)
    for block in range(6):
        rows = [part[block : block + 1] for part in parts]
        here = slice(block * width, (block + 1) * width)
        grad_weight[:, here] = total([lifted[:, p : p + 1] * row for p, row in enumerate(rows)])
        grad_bias[:, here] = total(rows)
        rows = jnp.concatenate(rows + [jnp.zeros((8 - parts_count, width), f32)])
        high = rows.astype(bf16)
        low = (rows - high.astype(f32)).astype(bf16)
        grad_lifted = grad_lifted + back_product(high, weight[:, here]) + back_product(low, weight[:, here])
    grad_embedding = grad_lifted * gate * (1.0 + stacked * (1.0 - gate))
    lead = lax.broadcasted_iota(jnp.int32, (LEADS, width), 0).astype(f32)
    table[...] = total(
        [
            jnp.where(lead == parts[p][13:14], grad_embedding[p : p + 1], 0.0)
            for p in range(parts_count)
        ]
    )


def vectors(parts, first, weight):
    width = weight.shape[0]
    shapes = [weight.shape, (1, weight.shape[1]), (LEADS, width), (6, width)]
    shapes = [jax.ShapeDtypeStruct(shape, f32) for shape in shapes]
    return pl.pallas_call(
        partial(vectors_kernel, len(parts)),
        grid=(1,),
        in_specs=[pl.BlockSpec((16, width), lambda i: (first // 16, 0)) for _ in parts]
        + [whole(*weight.shape)],
        out_specs=[whole(*item.shape) for item in shapes],
        out_shape=shapes,
        compiler_params=kernel_params(16),
        name="vectors",
    )(*parts, weight)


def long_forward(owner, rank, share, lengths, valid, own, rest, mod, weight):
    rows, width = own.shape
    owners = lengths.shape[0]
    count = rows // owners
    steps = jnp.arange(owners, dtype=jnp.int32)
    ranks = (rank + jnp.arange(share, dtype=jnp.int32)) % share
    blocks = (((owner - steps) % owners)[None, :] * share + ranks[:, None]).reshape(-1, 1)
    key_pos = blocks * count + jnp.arange(count, dtype=jnp.int32)[None, :]
    doc_ends = jnp.cumsum(lax.dynamic_index_in_dim(lengths, owner, 0, False))
    key_seg = sum((key_pos >= doc_ends[doc]).astype(jnp.int32) for doc in range(doc_ends.shape[0]))
    own_valid = lax.dynamic_index_in_dim(valid, owner, 0, False).reshape(-1, count)
    key_valid = own_valid[blocks[:, 0]] > 0
    open_seg = jnp.where(key_valid, key_seg, -1).reshape(1, -1)
    key_pos = key_pos.reshape(1, -1)
    query_seg = key_seg.reshape(-1, 1)[:rows]
    query_pos = key_pos.reshape(-1, 1)[:rows]
    head_width = width // HEADS
    normed = normalize(jnp.concatenate([own, rest], axis=0).astype(f32))[0]
    mixed = (normed * (1.0 + mod[SCALE_ONE]) + mod[SHIFT_ONE]).astype(bf16)
    heads = lambda v: v.reshape(v.shape[0], HEADS, head_width).transpose(1, 0, 2)
    queries = heads(back_product(mixed[:rows], weight[:width]).astype(bf16))
    key_value = back_product(mixed, weight[width:]).astype(bf16)
    keys = heads(key_value[:, :width])
    values = heads(key_value[:, width:])
    probs, attended = attention(
        queries, keys, values, query_seg, query_pos, open_seg, key_pos, 1.0 / math.sqrt(head_width)
    )
    flat = attended.transpose(1, 0, 2).reshape(rows, width).astype(bf16)
    return ((probs, queries, keys, values, attended, normed, mixed), flat)


def long_backward(place, saved, grad_attended, own, rest, mod, weight, packed_output, sums):
    probs, queries, keys, values, attended, normed, mixed = saved
    rows, width = own.shape
    head_width = width // HEADS
    score_scale = 1.0 / math.sqrt(head_width)
    grad_heads = grad_attended.reshape(HEADS, head_width, rows).transpose(0, 2, 1)
    deltas = jnp.sum(grad_heads.astype(f32) * attended, axis=-1, keepdims=True)
    grad_probs = jnp.einsum("hqd,hkd->hqk", grad_heads, values, preferred_element_type=f32)
    grad_scores = (probs.astype(f32) * (grad_probs - deltas)).astype(bf16)
    grad_query = jnp.einsum("hqk,hkd->hqd", grad_scores, keys, preferred_element_type=f32)
    grad_key = jnp.einsum("hqk,hqd->hkd", grad_scores, queries, preferred_element_type=f32)
    grad_value = jnp.einsum("hqk,hqd->hkd", probs, grad_heads, preferred_element_type=f32)
    flat = lambda v: v.transpose(1, 0, 2).reshape(v.shape[1], width)
    grad_query = (flat(grad_query) * score_scale).astype(bf16)
    grad_key = (flat(grad_key) * score_scale).astype(bf16)
    grad_value = flat(grad_value).astype(bf16)
    part = product(grad_key, weight[width : 2 * width]) + product(grad_value, weight[2 * width :])
    part = jnp.concatenate([part[:rows] + product(grad_query, weight[:width]), part[rows:]], axis=0)
    share = mod[SHARE]
    first = jnp.concatenate([row_product(mixed[:rows], grad_query), row_product(mixed, grad_key)])
    first = (first * share).astype(bf16)
    second = jnp.concatenate(
        [(row_product(mixed, grad_value) * share).astype(bf16), packed_output]
    )
    first_core = place[2] == 0
    keep = jnp.where(first_core, first, second)
    send = jnp.where(first_core, second, first)
    total_rows = jnp.stack([jnp.sum(part, axis=0), jnp.sum(part * normed, axis=0)]) * share
    sums = jnp.concatenate([total_rows, sums[2:]], axis=0)
    send = jnp.concatenate([send, part[rows:].astype(bf16), sums.astype(bf16)])
    return (keep, send, part[:rows], sums)


def on_device(
    tokens,
    cotangent,
    lengths,
    valid_mask,
    lead_index,
    sample_counts,
    lead_table,
    modulation_weight,
    modulation_bias,
    attend_weight,
    output_weight,
    output_bias,
    expand_weight,
    expand_bias,
    shrink_weight,
    shrink_bias,
):
    owners = tokens.shape[1]
    block_rows = tokens.shape[2]
    width = tokens.shape[3]
    hidden_width = expand_bias.shape[0]
    seq_size = lax.axis_size("seq")
    share = seq_size // owners
    seq_length = block_rows * seq_size
    rows = owners * block_rows
    place = lax.axis_index("seq")
    owner = place // share
    rank = place % share

    where = jnp.stack([owner, rank, place % 2, lax.axis_index("grp"), place // 2]).astype(jnp.int32)

    token_pieces = rows_to_owner(tokens[0], owner, share)

    bias = [modulation_bias, output_bias, expand_bias, shrink_bias]
    bias = jnp.concatenate(bias).astype(f32)[None]
    mod, weight = prepare(
        where, lead_index, sample_counts, lead_table, modulation_weight, bias, attend_weight,
        owners * seq_length,
    )
    grad_pieces = rows_to_owner(after(cotangent[0], mod), owner, share)
    token_pieces = after_all(token_pieces, mod)
    own_tokens = jnp.concatenate(token_pieces, axis=0)
    rest_tokens = share_rows(own_tokens, rank, share)
    short = seq_length <= 2048
    if short:
        *saved, attended = forward_attention(
            where, lengths[0], valid_mask[0], own_tokens, rest_tokens, mod, weight
        )
    else:
        saved, attended = long_forward(
            owner, rank, share, lengths[0], valid_mask[0], own_tokens, rest_tokens, mod, weight
        )
    grad_out = jnp.concatenate(after_all(grad_pieces, attended), axis=0)
    ff_keep, ff_send, packed_output, grad_attended, grad_residual, sums, *output_pieces = middle(
        owners, where, own_tokens, attended, grad_out, mod, bias, output_weight, expand_weight,
        shrink_weight,
    )
    output_pieces = rows_from_owner(output_pieces, share)
    ff_core = low_total([ff_keep, swap_cores(ff_send)])
    ff_parts = send_plane(plane_parts(ff_core))
    grad_attended = after(grad_attended, ff_core)
    backward = backward_attention if short else long_backward
    held = backward(
        where, saved, grad_attended, own_tokens, rest_tokens, mod, weight, packed_output, sums
    )
    at_keep, send, own_part, sums = after_all(held, *ff_parts[1:], *output_pieces)
    ff_plane = low_total(ff_parts)
    line = line_size() <= 4
    if line:
        ff_parts = send_line(line_parts(ff_plane))
    if share == 2:
        received = swap_cores(send)
    else:
        received = swap_cores(send[: 2 * width])
        vector = sum_share(sums, share)
        rest_part = return_rows(send[2 * width : -sums.shape[0]], rank, share)
        received = jnp.concatenate([received, rest_part, (vector - sums).astype(bf16)])
    at_core = low_total([at_keep, received[: 2 * width]])
    at_slices = plane_parts(at_core)
    if line:
        ff_parts = after_all(ff_parts, *at_slices)
    at_parts = send_plane(at_slices)
    at_plane = low_total(at_parts)
    if line:
        ff_line = low_total(ff_parts)
        ff_pieces = send_line([ff_line] * line_size())
        at_line = low_total(send_line(line_parts(at_plane)))
        at_pieces = send_line([at_line] * line_size())
    else:
        ff_pieces = [sum_line(ff_plane)]
        at_pieces = [sum_line(at_plane)]
    finished = finish_rows(
        owners, own_tokens, own_part, after(received, *ff_pieces), grad_residual, mod, sums
    )
    grad_pieces = rows_from_owner(finished, share)
    ff_parts = gather_plane(jnp.concatenate(ff_pieces))
    grad_tokens, vector = placed_sums(where, lead_index, mod, grad_pieces)
    at_parts = gather_plane(jnp.concatenate(at_pieces + [vector]))
    ff_parts = list(after_all(ff_parts, vector, *at_pieces))
    ff_blocks = hidden_width // width
    targets = [(0, i * width, 0) for i in range(ff_blocks)] + [(1, 0, i * width) for i in range(ff_blocks)]
    grad_shrink, grad_expand = ordered(
        where, ff_parts, ff_parts[0].shape[0], targets, [shrink_weight.shape, expand_weight.shape]
    )
    output = placed(where, after_all(output_pieces, vector))
    at_parts = list(after_all(at_parts, grad_shrink, output))
    targets = [(0, 0, i * width) for i in range(3)] + [(1, 0, 0)]
    count = at_parts[0].shape[0] - vector.shape[0]
    grad_attend, grad_output = ordered(
        where, at_parts, count, targets, [attend_weight.shape, output_weight.shape]
    )
    grad_mod_weight, grad_mod_bias, grad_table, biases = vectors(at_parts, count, modulation_weight)
    return (
        output[None],
        grad_tokens[None],
        grad_table,
        grad_mod_weight,
        grad_mod_bias.reshape(-1),
        grad_attend,
        grad_output,
        biases[0],
        grad_expand,
        biases[1 : 1 + ff_blocks].reshape(-1),
        grad_shrink,
        biases[1 + ff_blocks],
    )


def solution(mesh):
    rows = P("grp", None, "seq", None)
    placed = (rows, rows, P("grp", None, None), P("grp", None, None), P("grp")) + (P(),) * 11
    return jax.shard_map(
        on_device,
        mesh=mesh,
        in_specs=placed,
        out_specs=(rows, rows) + (P(),) * 10,
        check_vma=False,
    )
```

profile of v0, /device:TPU:0, one launch (start us, length us, event | category | flops | bytes accessed | tf_op | source)
XLA Modules:
  0.0 138.8 jit_solution(17187318161473950676)
XLA Ops:
  0.8 1.1 dynamic-slice_bitcast_fusion.4
  1.9 3.1 %collective-permute-start = (bf16[128,384]{1,0:T(8,128)(2,1)S(1)}, bf16[128,384]{1,0:T(8,128)(2,1)S(1)}, u32[]{:S(2)}, u32[]{:S(2)}) collective-permute-start(bf16[128,384]{1,0:T(8,128)(2,1)S(1)} %get-tuple-element.163), channel_id=1, source_target_pairs={{0,2},{1,3},{2,4},{3,5},{4,6},{5,7},{6,0},{7,1},{8,10},{9,11},{10,... | collective-permute-start | bytes 294920 | tf_op jit(solution)/shard_map/ppermute | solution.py:65
  5.0 2.6 %collective-permute-start.1 = (bf16[128,384]{1,0:T(8,128)(2,1)S(1)}, bf16[128,384]{1,0:T(8,128)(2,1)S(1)}, u32[]{:S(2)}, u32[]{:S(2)}) collective-permute-start(bf16[128,384]{1,0:T(8,128)(2,1)S(1)} %get-tuple-element.165), channel_id=1, source_target_pairs={{0,4},{1,5},{2,6},{3,7},{4,0},{5,1},{6,2},{7,3},{8,12},{9,13},{10,... | collective-permute-start | bytes 294920 | tf_op jit(solution)/shard_map/ppermute | solution.py:65
  7.6 1.3 collective-permute-start.2
  8.9 0.7 concatenate.30
  9.6 0.7 concatenate.32
  10.3 0.7 concatenate.31
  11.0 0.7 concatenate.33
  12.5 1.5 %copy-done = bf16[384,2304]{1,0:T(8,128)(2,1)S(1)} copy-done((bf16[384,2304]{1,0:T(8,128)(2,1)S(1)}, bf16[384,2304]{1,0:T(8,128)(2,1)}, u32[]{:S(2)}) %copy-start) | copy-done | bytes 1769496
  13.9 0.7 copy-done.4
  14.6 0.7 copy-done.5
  15.3 0.9 prepare.1
  16.5 0.7 collective-permute-start.4
  17.2 1.4 %collective-permute-start.5 = (bf16[128,384]{1,0:T(8,128)(2,1)S(1)}, bf16[128,384]{1,0:T(8,128)(2,1)S(1)}, u32[]{:S(2)}, u32[]{:S(2)}) collective-permute-start(bf16[128,384]{1,0:T(8,128)(2,1)S(1)} %get-tuple-element.159), channel_id=1, source_target_pairs={{0,4},{1,5},{2,6},{3,7},{4,0},{5,1},{6,2},{7,3},{8,12},{9,13},{10,... | collective-permute-start | bytes 294920 | tf_op jit(solution)/shard_map/ppermute | solution.py:65
  18.6 1.7 %collective-permute-start.6 = (bf16[128,384]{1,0:T(8,128)(2,1)S(1)}, bf16[128,384]{1,0:T(8,128)(2,1)S(1)}, u32[]{:S(2)}, u32[]{:S(2)}) collective-permute-start(bf16[128,384]{1,0:T(8,128)(2,1)S(1)} %get-tuple-element.158), channel_id=1, source_target_pairs={{0,6},{1,7},{2,0},{3,1},{4,2},{5,3},{6,4},{7,5},{8,14},{9,15},{10,... | collective-permute-start | bytes 294920 | tf_op jit(solution)/shard_map/ppermute | solution.py:65
  20.4 10.3 %forward_attention.1 = (bf16[6,1024,512]{2,1,0:T(8,128)(2,1)}, bf16[384,512]{1,0:T(8,128)(2,1)S(1)}, bf16[768,1024]{1,0:T(8,128)(2,1)S(1)}, f32[384,512]{1,0:T(8...) custom-call(s32[5]{0:T(128)S(1)} %stack.17.place, s32[4,8]{1,0:T(4,128)S(1)} %bitcast.25, ...), custom_call_target="tpu_custom_call" | custom-call | flops 3221225472 | bytes 6291456 | tf_op jit(solution)/shard_map/forward_attention/pallas_call | solution.py:380
  30.8 0.7 copy-done.19
  31.6 9.7 %middle.1 = (bf16[1536,384]{1,0:T(8,128)(2,1)S(1)}, bf16[1536,384]{1,0:T(8,128)(2,1)}, bf16[384,384]{1,0:T(8,128)(2,1)}, bf16[384,512]{1,0:T(8,128)(2,1)}, f32[5...) custom-call(s32[5]{0:T(128)S(1)} %stack.17.place, ...), custom_call_target="tpu_custom_call" | custom-call | flops 4831838208 | bytes 16777216 | tf_op jit(solution)/shard_map/middle/pallas_call | solution.py:480
  41.4 1.3 collective-permute-start.7
  42.7 0.9 collective-permute-start.8
  43.6 1.9 %collective-permute-start.9 = (bf16[128,384]{1,0:T(8,128)(2,1)S(1)}, bf16[128,384]{1,0:T(8,128)(2,1)S(1)}, u32[]{:S(2)}, u32[]{:S(2)}) collective-permute-start(bf16[128,384]{1,0:T(8,128)(2,1)S(1)} %get-tuple-element.94), channel_id=1, source_target_pairs={{0,2},{1,3},{2,4},{3,5},{4,6},{5,7},{6,0},{7,1},{8,10},{9,11},{10,... | collective-permute-start | bytes 294920 | tf_op jit(solution)/shard_map/ppermute | solution.py:74
  45.5 1.7 %add_convert_fusion = bf16[1536,384]{1,0:T(8,128)(2,1)S(1)} fusion(bf16[1536,384]{1,0:T(8,128)(2,1)} %collective-permute-done.10, bf16[1536,384]{1,0:T(8,128)(2,1)S(1)} %get-tuple-element.101), kind=kLoop, calls=%fused_computation | loop fusion | flops 2359296 | bytes 3538944 | tf_op jit(solution)/shard_map/convert_element_type | solution.py:174
  47.4 1.6 %collective-permute-start.11 = (bf16[384,384]{1,0:T(8,128)(2,1)S(1)}, bf16[384,384]{1,0:T(8,128)(2,1)S(1)}, u32[]{:S(2)}, u32[]{:S(2)}) collective-permute-start(bf16[384,384]{1,0:T(8,128)(2,1)S(1)} %get-tuple-element.154), channel_id=1, source_target_pairs={{0,8},{8,0},{16,24},{24,16},{1,9},{9,1},{17,25},{25,17},{2,10},{10... | collective-permute-start | bytes 884744 | tf_op jit(solution)/shard_map/ppermute | solution.py:116
  49.0 1.5 %collective-permute-start.12 = (bf16[384,384]{1,0:T(8,128)(2,1)S(1)}, bf16[384,384]{1,0:T(8,128)(2,1)S(1)}, u32[]{:S(2)}, u32[]{:S(2)}) collective-permute-start(bf16[384,384]{1,0:T(8,128)(2,1)S(1)} %get-tuple-element.153), channel_id=1, source_target_pairs={{0,16},{8,24},{16,0},{24,8},{1,17},{9,25},{17,1},{25,9},{2,18},{10... | collective-permute-start | bytes 884744 | tf_op jit(solution)/shard_map/ppermute | solution.py:116
  51.0 11.6 %backward_attention.1 = (bf16[768,384]{1,0:T(8,128)(2,1)S(1)}, bf16[1296,384]{1,0:T(8,128)(2,1)}, f32[512,384]{1,0:T(8,128)S(1)}, f32[16,384]{1,0:T(8,128)S(1)}) custom-call(s32[5]{0:T(128)S(1)} %stack.17.place, bf16[6,1024,512]{2,1,0:T(8,128)(2,1)} %get-tuple-element.95.expo, bf16[384,512]{1,0:T(8,128)(2,1)S(1)} %copy-done.20, ...), custom_call_target="tpu_custom_call" | custom-call | flops 6442450944 | bytes 6291456 | tf_op jit(solution)/shard_map/backward_attention/pallas_call | solution.py:578
  62.6 0.9 collective-permute-done.12
  63.5 0.7 copy-done.27
  64.4 2.8 %collective-permute-done.14.received = bf16[1296,384]{1,0:T(8,128)(2,1)S(1)} collective-permute-done((bf16[1296,384]{1,0:T(8,128)(2,1)}, bf16[1296,384]{1,0:T(8,128)(2,1)S(1)}, u32[]{:S(2)}, u32[]{:S(2)}) %collective-permute-start.14) | collective-permute-done | bytes 995360 | tf_op jit(solution)/shard_map/ppermute | solution.py:102
  67.4 1.2 collective-permute-start.24
  68.6 1.1 collective-permute-start.25
  69.6 1.3 collective-permute-start.26
  70.9 1.1 add_convert_fusion.2
  72.1 0.7 collective-permute-start.15
  72.8 2.0 %collective-permute-start.16 = (bf16[96,384]{1,0:T(8,128)(2,1)S(1)}, bf16[96,384]{1,0:T(8,128)(2,1)S(1)}, u32[]{:S(2)}, u32[]{:S(2)}) collective-permute-start(bf16[96,384]{1,0:T(8,128)(2,1)S(1)} %get-tuple-element.167), channel_id=1, source_target_pairs={{0,4},{1,5},{2,6},{3,7},{4,0},{5,1},{6,2},{7,3},{8,12},{9,13},{10,... | collective-permute-start | bytes 221192 | tf_op jit(solution)/shard_map/ppermute | solution.py:111
  74.8 1.9 %collective-permute-start.17 = (bf16[96,384]{1,0:T(8,128)(2,1)S(1)}, bf16[96,384]{1,0:T(8,128)(2,1)S(1)}, u32[]{:S(2)}, u32[]{:S(2)}) collective-permute-start(bf16[96,384]{1,0:T(8,128)(2,1)S(1)} %get-tuple-element.166), channel_id=1, source_target_pairs={{0,6},{1,7},{2,0},{3,1},{4,2},{5,3},{6,4},{7,5},{8,14},{9,15},{10,... | collective-permute-start | bytes 221192 | tf_op jit(solution)/shard_map/ppermute | solution.py:111
  76.7 0.7 collective-permute-done.26
  77.5 1.6 %collective-permute-done.15 = bf16[96,384]{1,0:T(8,128)(2,1)S(1)} collective-permute-done((bf16[96,384]{1,0:T(8,128)(2,1)S(1)}, bf16[96,384]{1,0:T(8,128)(2,1)S(1)}, u32[]{:S(2)}, u32[]{:S(2)}) %collective-permute-start.15) | collective-permute-done | bytes 73760 | tf_op jit(solution)/shard_map/ppermute | solution.py:111
  79.1 1.7 %collective-permute-done.16 = bf16[96,384]{1,0:T(8,128)(2,1)S(1)} collective-permute-done((bf16[96,384]{1,0:T(8,128)(2,1)S(1)}, bf16[96,384]{1,0:T(8,128)(2,1)S(1)}, u32[]{:S(2)}, u32[]{:S(2)}) %collective-permute-start.16) | collective-permute-done | bytes 73760 | tf_op jit(solution)/shard_map/ppermute | solution.py:111
  80.8 1.5 %collective-permute-start.18 = (bf16[96,384]{1,0:T(8,128)(2,1)S(1)}, bf16[96,384]{1,0:T(8,128)(2,1)S(1)}, u32[]{:S(2)}, u32[]{:S(2)}) collective-permute-start(bf16[96,384]{1,0:T(8,128)(2,1)S(1)} %add_convert_fusion.4), channel_id=1, source_target_pairs={{0,2},{1,3},{2,4},{3,5},{4,6},{5,7},{6,0},{7,1},{8,10},{9,11},{10,... | collective-permute-start | bytes 221192 | tf_op jit(solution)/shard_map/ppermute | solution.py:111
  82.3 2.1 %collective-permute-start.19 = (bf16[96,384]{1,0:T(8,128)(2,1)S(1)}, bf16[96,384]{1,0:T(8,128)(2,1)S(1)}, u32[]{:S(2)}, u32[]{:S(2)}) collective-permute-start(bf16[96,384]{1,0:T(8,128)(2,1)S(1)} %add_convert_fusion.4), channel_id=1, source_target_pairs={{0,4},{1,5},{2,6},{3,7},{4,0},{5,1},{6,2},{7,3},{8,12},{9,13},{10,... | collective-permute-start | bytes 221192 | tf_op jit(solution)/shard_map/ppermute | solution.py:111
  84.8 1.7 %collective-permute-start.27 = (bf16[48,384]{1,0:T(8,128)(2,1)S(1)}, bf16[48,384]{1,0:T(8,128)(2,1)S(1)}, u32[]{:S(2)}, u32[]{:S(2)}) collective-permute-start(bf16[48,384]{1,0:T(8,128)(2,1)S(1)} %get-tuple-element.170), channel_id=1, source_target_pairs={{0,2},{1,3},{2,4},{3,5},{4,6},{5,7},{6,0},{7,1},{8,10},{9,11},{10,... | collective-permute-start | bytes 110600 | tf_op jit(solution)/shard_map/ppermute | solution.py:111
  86.5 0.8 collective-permute-start.28
  87.7 2.0 %collective-permute-start.29 = (bf16[48,384]{1,0:T(8,128)(2,1)S(1)}, bf16[48,384]{1,0:T(8,128)(2,1)S(1)}, u32[]{:S(2)}, u32[]{:S(2)}) collective-permute-start(bf16[48,384]{1,0:T(8,128)(2,1)S(1)} %get-tuple-element.171), channel_id=1, source_target_pairs={{0,6},{1,7},{2,0},{3,1},{4,2},{5,3},{6,4},{7,5},{8,14},{9,15},{10,... | collective-permute-start | bytes 110600 | tf_op jit(solution)/shard_map/ppermute | solution.py:111
  89.7 0.9 collective-permute-done.19
  90.6 1.2 collective-permute-start.36
  91.8 1.0 collective-permute-start.37
  92.8 0.6 finish_rows.1
  93.4 1.4 %collective-permute-start.38 = (bf16[384,384]{1,0:T(8,128)(2,1)S(1)}, bf16[384,384]{1,0:T(8,128)(2,1)S(1)}, u32[]{:S(2)}, u32[]{:S(2)}) collective-permute-start(bf16[384,384]{1,0:T(8,128)(2,1)S(1)} %pad_maximum_fusion.1.refs_0_), channel_id=1, source_target_pairs={{0,24},{8,16},{16,8},{24,0},{1,25},{9,17},{17,9},{25,1},{2,26},{10... | collective-permute-start | bytes 884744 | tf_op jit(solution)/shard_map/ppermute | solution.py:116
  94.9 3.6 %collective-permute-start.21 = (bf16[144,384]{1,0:T(8,128)(2,1)S(1)}, bf16[144,384]{1,0:T(8,128)(2,1)S(1)}, u32[]{:S(2)}, u32[]{:S(2)}) collective-permute-start(bf16[144,384]{1,0:T(8,128)(2,1)S(1)} %get-tuple-element.121), channel_id=1, source_target_pairs={{0,6},{1,7},{2,0},{3,1},{4,2},{5,3},{6,4},{7,5},{8,14},{9,15},{10,... | collective-permute-start | bytes 331784 | tf_op jit(solution)/shard_map/ppermute | solution.py:74
  98.5 6.2 %collective-permute-done.30 = bf16[48,384]{1,0:T(8,128)(2,1)S(1)} collective-permute-done((bf16[48,384]{1,0:T(8,128)(2,1)S(1)}, bf16[48,384]{1,0:T(8,128)(2,1)S(1)}, u32[]{:S(2)}, u32[]{:S(2)}) %collective-permute-start.30) | collective-permute-done | bytes 36896 | tf_op jit(solution)/shard_map/ppermute | solution.py:111
  104.7 1.0 collective-permute-start.22
  105.8 7.6 %collective-permute-done.22.refs_2_ = bf16[144,384]{1,0:T(8,128)(2,1)S(1)} collective-permute-done((bf16[144,384]{1,0:T(8,128)(2,1)S(1)}, bf16[144,384]{1,0:T(8,128)(2,1)S(1)}, u32[]{:S(2)}, u32[]{:S(2)}) %collective-permute-start.22) | collective-permute-done | bytes 110624 | tf_op jit(solution)/shard_map/ppermute | solution.py:74
  113.5 1.5 %placed_sums.1 = (f32[4,128,384]{2,1,0:T(8,128)}, bf16[16,384]{1,0:T(8,128)(2,1)S(1)}) custom-call(s32[5]{0:T(128)S(1)} %stack.17.place, s32[1]{0:T(128)S(6)} %copy.35.lead, f32[8,384]{1,0:T(8,128)S(1)} %get-tuple-element.79.mod, bf16[144,384]{1,0:T(8,128)(2,1)S(1)} %get-tuple-element.120.refs_0_, bf16[144,384]{1,0:T(8,128)(2,1)S(1)} %collective-permute-done.21.refs_1_, ...), custom_call_target="tpu_custom_call" | custom-call | tf_op jit(solution)/shard_map/placed_sums/pallas_call | solution.py:667
  114.9 3.3 %collective-permute-done.31 = bf16[48,384]{1,0:T(8,128)(2,1)S(1)} collective-permute-done((bf16[48,384]{1,0:T(8,128)(2,1)S(1)}, bf16[48,384]{1,0:T(8,128)(2,1)S(1)}, u32[]{:S(2)}, u32[]{:S(2)}) %collective-permute-start.31) | collective-permute-done | bytes 36896 | tf_op jit(solution)/shard_map/ppermute | solution.py:111
  119.5 1.2 collective-permute-start.33
  120.7 0.9 collective-permute-start.34
  121.6 1.4 %collective-permute-start.35 = (bf16[208,384]{1,0:T(8,128)(2,1)S(1)}, bf16[208,384]{1,0:T(8,128)(2,1)S(1)}, u32[]{:S(2)}, u32[]{:S(2)}) collective-permute-start(bf16[208,384]{1,0:T(8,128)(2,1)S(1)} %constant_dynamic-update-slice_fusion.4.refs_0_), channel_id=1, source_target_pairs={{0,24},{8,16},{16,8},{24,0},{1,25},{9,17},{17,9},{25,1},{2,26},{10... | collective-permute-start | bytes 479240 | tf_op jit(solution)/shard_map/ppermute | solution.py:116
  123.0 1.3 placed.1
  124.4 3.4 %ordered.2 = (f32[1536,384]{1,0:T(8,128)}, f32[384,1536]{1,0:T(8,128)}) custom-call(s32[5]{0:T(128)S(1)} %stack.17.place, bf16[384,384]{1,0:T(8,128)(2,1)S(1)} %pad_maximum_fusion.1.refs_0_, bf16[384,384]{1,0:T(8,128)(2,1)S(1)} %collective-permute-done.36.refs_1_, bf16[384,384]{1,0:T(8,128)(2,1)S(1)} %collective-permute-done.37.refs_2_, ...), custom_call_target="tpu_custom_call" | custom-call | tf_op jit(solution)/shard_map/ordered/pallas_call | solution.py:715
  127.8 0.8 collective-permute-done.34.refs_2_
  128.6 1.4 %collective-permute-done.35.refs_3_ = bf16[208,384]{1,0:T(8,128)(2,1)S(1)} collective-permute-done((bf16[208,384]{1,0:T(8,128)(2,1)S(1)}, bf16[208,384]{1,0:T(8,128)(2,1)S(1)}, u32[]{:S(2)}, u32[]{:S(2)}) %collective-permute-start.35) | collective-permute-done | bytes 159776 | tf_op jit(solution)/shard_map/ppermute | solution.py:116
  131.0 3.7 %vectors.1 = (f32[384,2304]{1,0:T(8,128)}, f32[1,2304]{1,0:T(1,128)S(1)}, f32[8,384]{1,0:T(8,128)}, f32[6,384]{1,0:T(8,128)S(1)}) custom-call(bf16[208,384]{1,0:T(8,128)(2,1)S(1)} %constant_dynamic-update-slice_fusion.4.refs_0_, bf16[208,384]{1,0:T(8,128)(2,1)S(1)} %collective-permute-done.33.refs_1_, bf16[208,384]{1,0:T(8,128)(2,1)S(1)} %collective-permute-done.34.refs_2_, ...), custom_call_target="tpu_custom_call" | custom-call | tf_op jit(solution)/shard_map/vectors/pallas_call | solution.py:760
  135.3 0.6 reduce
  136.6 2.3 %ordered.3 = (f32[384,1152]{1,0:T(8,128)}, f32[384,384]{1,0:T(8,128)}) custom-call(s32[5]{0:T(128)S(1)} %stack.17.place, bf16[208,384]{1,0:T(8,128)(2,1)S(1)} %constant_dynamic-update-slice_fusion.4.refs_0_, bf16[208,384]{1,0:T(8,128)(2,1)S(1)} %collective-permute-done.33.refs_1_, bf16[208,384]{1,0:T(8,128)(2,1)S(1)} %collective-permute-done.34.refs_2_, ...), custom_call_target="tpu_custom_call" | custom-call | tf_op jit(solution)/shard_map/ordered/pallas_call | solution.py:715
  (134 shorter events, 6.0 us)
Async XLA Ops:
  0.6 11.8 %copy-start.2 = (bf16[384,1152]{1,0:T(8,128)(2,1)S(1)}, bf16[384,1152]{1,0:T(8,128)(2,1)}, u32[]{:S(2)}) copy-start(bf16[384,1152]{1,0:T(8,128)(2,1)} %attend_weight.1) | copy-start | bytes 2654212
  1.9 14.3 %collective-permute-start = (bf16[128,384]{1,0:T(8,128)(2,1)S(1)}, bf16[128,384]{1,0:T(8,128)(2,1)S(1)}, u32[]{:S(2)}, u32[]{:S(2)}) collective-permute-start(bf16[128,384]{1,0:T(8,128)(2,1)S(1)} %get-tuple-element.163), channel_id=1, source_target_pairs={{0,2},{1,3},{2,4},{3,5},{4,6},{5,7},{6,0},{7,1},{8,10},{9,11},{10,... | collective-permute-start | bytes 294920 | tf_op jit(solution)/shard_map/ppermute | solution.py:65
  5.0 11.3 %collective-permute-start.1 = (bf16[128,384]{1,0:T(8,128)(2,1)S(1)}, bf16[128,384]{1,0:T(8,128)(2,1)S(1)}, u32[]{:S(2)}, u32[]{:S(2)}) collective-permute-start(bf16[128,384]{1,0:T(8,128)(2,1)S(1)} %get-tuple-element.165), channel_id=1, source_target_pairs={{0,4},{1,5},{2,6},{3,7},{4,0},{5,1},{6,2},{7,3},{8,12},{9,13},{10,... | collective-permute-start | bytes 294920 | tf_op jit(solution)/shard_map/ppermute | solution.py:65
  7.6 8.7 %collective-permute-start.2 = (bf16[128,384]{1,0:T(8,128)(2,1)S(1)}, bf16[128,384]{1,0:T(8,128)(2,1)S(1)}, u32[]{:S(2)}, u32[]{:S(2)}) collective-permute-start(bf16[128,384]{1,0:T(8,128)(2,1)S(1)} %get-tuple-element.162), channel_id=1, source_target_pairs={{0,6},{1,7},{2,0},{3,1},{4,2},{5,3},{6,4},{7,5},{8,14},{9,15},{10,... | collective-permute-start | bytes 294920 | tf_op jit(solution)/shard_map/ppermute | solution.py:65
  16.2 14.6 %copy-start.8 = (bf16[1152,384]{1,0:T(8,128)(2,1)}, bf16[1152,384]{1,0:T(8,128)(2,1)S(1)}, u32[]{:S(2)}) copy-start(bf16[1152,384]{1,0:T(8,128)(2,1)S(1)} %get-tuple-element.84.weight) | copy-start | bytes 2654212
  16.4 4.0 %collective-permute-start.3 = (bf16[512,384]{1,0:T(8,128)(2,1)S(1)}, bf16[512,384]{1,0:T(8,128)(2,1)S(1)}, u32[]{:S(2)}, u32[]{:S(2)}) collective-permute-start(bf16[512,384]{1,0:T(8,128)(2,1)S(1)} %constant_dynamic-update-slice_fusion.own), channel_id=1, source_target_pairs={{0,1},{1,0},{2,3},{3,2},{4,5},{5,4},{6,7},{7,6},{8,9},{9,8},{10,11... | collective-permute-start | bytes 1179656 | tf_op jit(solution)/shard_map/ppermute | solution.py:82
  16.5 15.0 %collective-permute-start.4 = (bf16[128,384]{1,0:T(8,128)(2,1)S(1)}, bf16[128,384]{1,0:T(8,128)(2,1)S(1)}, u32[]{:S(2)}, u32[]{:S(2)}) collective-permute-start(bf16[128,384]{1,0:T(8,128)(2,1)S(1)} %get-tuple-element.160), channel_id=1, source_target_pairs={{0,2},{1,3},{2,4},{3,5},{4,6},{5,7},{6,0},{7,1},{8,10},{9,11},{10,... | collective-permute-start | bytes 294920 | tf_op jit(solution)/shard_map/ppermute | solution.py:65
  17.2 14.3 %collective-permute-start.5 = (bf16[128,384]{1,0:T(8,128)(2,1)S(1)}, bf16[128,384]{1,0:T(8,128)(2,1)S(1)}, u32[]{:S(2)}, u32[]{:S(2)}) collective-permute-start(bf16[128,384]{1,0:T(8,128)(2,1)S(1)} %get-tuple-element.159), channel_id=1, source_target_pairs={{0,4},{1,5},{2,6},{3,7},{4,0},{5,1},{6,2},{7,3},{8,12},{9,13},{10,... | collective-permute-start | bytes 294920 | tf_op jit(solution)/shard_map/ppermute | solution.py:65
  18.6 12.9 %collective-permute-start.6 = (bf16[128,384]{1,0:T(8,128)(2,1)S(1)}, bf16[128,384]{1,0:T(8,128)(2,1)S(1)}, u32[]{:S(2)}, u32[]{:S(2)}) collective-permute-start(bf16[128,384]{1,0:T(8,128)(2,1)S(1)} %get-tuple-element.158), channel_id=1, source_target_pairs={{0,6},{1,7},{2,0},{3,1},{4,2},{5,3},{6,4},{7,5},{8,14},{9,15},{10,... | collective-permute-start | bytes 294920 | tf_op jit(solution)/shard_map/ppermute | solution.py:65
  20.4 10.4 %copy-start.10 = (bf16[512,384]{1,0:T(8,128)(2,1)}, bf16[512,384]{1,0:T(8,128)(2,1)S(1)}, u32[]{:S(2)}) copy-start(bf16[512,384]{1,0:T(8,128)(2,1)S(1)} %collective-permute-done.3.rest) | copy-start | bytes 1179652
  20.4 11.2 %copy-start.6 = (bf16[384,1536]{1,0:T(8,128)(2,1)S(1)}, bf16[384,1536]{1,0:T(8,128)(2,1)}, u32[]{:S(2)}) copy-start(bf16[384,1536]{1,0:T(8,128)(2,1)} %expand_weight.1) | copy-start | bytes 3538948
  20.4 11.2 %copy-start.7 = (bf16[1536,384]{1,0:T(8,128)(2,1)S(1)}, bf16[1536,384]{1,0:T(8,128)(2,1)}, u32[]{:S(2)}) copy-start(bf16[1536,384]{1,0:T(8,128)(2,1)} %shrink_weight.1) | copy-start | bytes 3538948
  20.4 11.2 %copy-start.12 = (bf16[384,384]{1,0:T(8,128)(2,1)S(1)}, bf16[384,384]{1,0:T(8,128)(2,1)}, u32[]{:S(2)}) copy-start(bf16[384,384]{1,0:T(8,128)(2,1)} %output_weight.1) | copy-start | bytes 884740
  31.5 9.8 %copy-start.15 = (bf16[768,1024]{1,0:T(8,128)(2,1)}, bf16[768,1024]{1,0:T(8,128)(2,1)S(1)}, u32[]{:S(2)}) copy-start(bf16[768,1024]{1,0:T(8,128)(2,1)S(1)} %get-tuple-element.97.key_value) | copy-start | bytes 4718596
  31.5 9.8 %copy-start.17 = (f32[384,512]{1,0:T(8,128)}, f32[384,512]{1,0:T(8,128)S(1)}, u32[]{:S(2)}) copy-start(f32[384,512]{1,0:T(8,128)S(1)} %get-tuple-element.98.attended_wide) | copy-start | bytes 2359300
  41.3 4.2 %collective-permute-start.10 = (bf16[1536,384]{1,0:T(8,128)(2,1)}, bf16[1536,384]{1,0:T(8,128)(2,1)}, u32[]{:S(2)}, u32[]{:S(2)}) collective-permute-start(bf16[1536,384]{1,0:T(8,128)(2,1)} %get-tuple-element.102), channel_id=1, source_target_pairs={{0,1},{1,0},{2,3},{3,2},{4,5},{5,4},{6,7},{7,6},{8,9},{9,8},{10,11... | collective-permute-start | bytes 3538952 | tf_op jit(solution)/shard_map/ppermute | solution.py:102
  41.4 9.1 %collective-permute-start.7 = (bf16[128,384]{1,0:T(8,128)(2,1)S(1)}, bf16[128,384]{1,0:T(8,128)(2,1)S(1)}, u32[]{:S(2)}, u32[]{:S(2)}) collective-permute-start(bf16[128,384]{1,0:T(8,128)(2,1)S(1)} %get-tuple-element.92), channel_id=1, source_target_pairs={{0,6},{1,7},{2,0},{3,1},{4,2},{5,3},{6,4},{7,5},{8,14},{9,15},{10,... | collective-permute-start | bytes 294920 | tf_op jit(solution)/shard_map/ppermute | solution.py:74
  42.7 19.9 %collective-permute-start.8 = (bf16[128,384]{1,0:T(8,128)(2,1)S(1)}, bf16[128,384]{1,0:T(8,128)(2,1)S(1)}, u32[]{:S(2)}, u32[]{:S(2)}) collective-permute-start(bf16[128,384]{1,0:T(8,128)(2,1)S(1)} %get-tuple-element.93), channel_id=1, source_target_pairs={{0,4},{1,5},{2,6},{3,7},{4,0},{5,1},{6,2},{7,3},{8,12},{9,13},{10,... | collective-permute-start | bytes 294920 | tf_op jit(solution)/shard_map/ppermute | solution.py:74
  43.6 19.0 %collective-permute-start.9 = (bf16[128,384]{1,0:T(8,128)(2,1)S(1)}, bf16[128,384]{1,0:T(8,128)(2,1)S(1)}, u32[]{:S(2)}, u32[]{:S(2)}) collective-permute-start(bf16[128,384]{1,0:T(8,128)(2,1)S(1)} %get-tuple-element.94), channel_id=1, source_target_pairs={{0,2},{1,3},{2,4},{3,5},{4,6},{5,7},{6,0},{7,1},{8,10},{9,11},{10,... | collective-permute-start | bytes 294920 | tf_op jit(solution)/shard_map/ppermute | solution.py:74
  45.5 5.5 %copy-start.16 = (bf16[768,1024]{1,0:T(8,128)(2,1)S(1)}, bf16[768,1024]{1,0:T(8,128)(2,1)}, u32[]{:S(2)}) copy-start(bf16[768,1024]{1,0:T(8,128)(2,1)} %copy-done.15) | copy-start | bytes 4718596
  45.5 5.5 %copy-start.18 = (f32[384,512]{1,0:T(8,128)S(1)}, f32[384,512]{1,0:T(8,128)}, u32[]{:S(2)}) copy-start(f32[384,512]{1,0:T(8,128)} %copy-done.17) | copy-start | bytes 2359300
  45.5 5.5 %copy-start.21 = (bf16[384,512]{1,0:T(8,128)(2,1)S(1)}, bf16[384,512]{1,0:T(8,128)(2,1)}, u32[]{:S(2)}) copy-start(bf16[384,512]{1,0:T(8,128)(2,1)} %get-tuple-element.103.grad_attended) | copy-start | bytes 1179652
  45.5 5.5 %copy-start.22 = (bf16[384,384]{1,0:T(8,128)(2,1)S(1)}, bf16[384,384]{1,0:T(8,128)(2,1)}, u32[]{:S(2)}) copy-start(bf16[384,384]{1,0:T(8,128)(2,1)} %get-tuple-element.104.packed_output) | copy-start | bytes 884740
  47.4 15.2 %collective-permute-start.11 = (bf16[384,384]{1,0:T(8,128)(2,1)S(1)}, bf16[384,384]{1,0:T(8,128)(2,1)S(1)}, u32[]{:S(2)}, u32[]{:S(2)}) collective-permute-start(bf16[384,384]{1,0:T(8,128)(2,1)S(1)} %get-tuple-element.154), channel_id=1, source_target_pairs={{0,8},{8,0},{16,24},{24,16},{1,9},{9,1},{17,25},{25,17},{2,10},{10... | collective-permute-start | bytes 884744 | tf_op jit(solution)/shard_map/ppermute | solution.py:116
  49.0 14.5 %collective-permute-start.12 = (bf16[384,384]{1,0:T(8,128)(2,1)S(1)}, bf16[384,384]{1,0:T(8,128)(2,1)S(1)}, u32[]{:S(2)}, u32[]{:S(2)}) collective-permute-start(bf16[384,384]{1,0:T(8,128)(2,1)S(1)} %get-tuple-element.153), channel_id=1, source_target_pairs={{0,16},{8,24},{16,0},{24,8},{1,17},{9,25},{17,1},{25,9},{2,18},{10... | collective-permute-start | bytes 884744 | tf_op jit(solution)/shard_map/ppermute | solution.py:116
  50.5 13.0 %collective-permute-start.13 = (bf16[384,384]{1,0:T(8,128)(2,1)S(1)}, bf16[384,384]{1,0:T(8,128)(2,1)S(1)}, u32[]{:S(2)}, u32[]{:S(2)}) collective-permute-start(bf16[384,384]{1,0:T(8,128)(2,1)S(1)} %get-tuple-element.152), channel_id=1, source_target_pairs={{0,24},{8,16},{16,8},{24,0},{1,25},{9,17},{17,9},{25,1},{2,26},{10... | collective-permute-start | bytes 884744 | tf_op jit(solution)/shard_map/ppermute | solution.py:116
  64.3 2.8 %collective-permute-start.14 = (bf16[1296,384]{1,0:T(8,128)(2,1)}, bf16[1296,384]{1,0:T(8,128)(2,1)S(1)}, u32[]{:S(2)}, u32[]{:S(2)}) collective-permute-start(bf16[1296,384]{1,0:T(8,128)(2,1)} %get-tuple-element.111), channel_id=1, source_target_pairs={{0,1},{1,0},{2,3},{3,2},{4,5},{5,4},{6,7},{7,6},{8,9},{9,8},{10,11... | collective-permute-start | bytes 2985992 | tf_op jit(solution)/shard_map/ppermute | solution.py:102
  64.3 6.6 %copy-start.26 = (bf16[384,384]{1,0:T(8,128)(2,1)S(1)}, bf16[384,384]{1,0:T(8,128)(2,1)}, u32[]{:S(2)}) copy-start(bf16[384,384]{1,0:T(8,128)(2,1)} %copy-done.25) | copy-start | bytes 884740
  64.3 6.6 %copy-start.28 = (bf16[384,384]{1,0:T(8,128)(2,1)S(1)}, bf16[384,384]{1,0:T(8,128)(2,1)}, u32[]{:S(2)}) copy-start(bf16[384,384]{1,0:T(8,128)(2,1)} %copy-done.27) | copy-start | bytes 884740
  64.3 6.6 %copy-start.30 = (bf16[384,384]{1,0:T(8,128)(2,1)S(1)}, bf16[384,384]{1,0:T(8,128)(2,1)}, u32[]{:S(2)}) copy-start(bf16[384,384]{1,0:T(8,128)(2,1)} %copy-done.29) | copy-start | bytes 884740
  67.4 7.4 %collective-permute-start.24 = (bf16[192,384]{1,0:T(8,128)(2,1)S(1)}, bf16[192,384]{1,0:T(8,128)(2,1)S(1)}, u32[]{:S(2)}, u32[]{:S(2)}) collective-permute-start(bf16[192,384]{1,0:T(8,128)(2,1)S(1)} %get-tuple-element.155), channel_id=1, source_target_pairs={{0,8},{8,0},{16,24},{24,16},{1,9},{9,1},{17,25},{25,17},{2,10},{10... | collective-permute-start | bytes 442376 | tf_op jit(solution)/shard_map/ppermute | solution.py:116
  68.6 8.1 %collective-permute-start.25 = (bf16[192,384]{1,0:T(8,128)(2,1)S(1)}, bf16[192,384]{1,0:T(8,128)(2,1)S(1)}, u32[]{:S(2)}, u32[]{:S(2)}) collective-permute-start(bf16[192,384]{1,0:T(8,128)(2,1)S(1)} %get-tuple-element.157), channel_id=1, source_target_pairs={{0,16},{8,24},{16,0},{24,8},{1,17},{9,25},{17,1},{25,9},{2,18},{10... | collective-permute-start | bytes 442376 | tf_op jit(solution)/shard_map/ppermute | solution.py:116
  69.6 7.8 %collective-permute-start.26 = (bf16[192,384]{1,0:T(8,128)(2,1)S(1)}, bf16[192,384]{1,0:T(8,128)(2,1)S(1)}, u32[]{:S(2)}, u32[]{:S(2)}) collective-permute-start(bf16[192,384]{1,0:T(8,128)(2,1)S(1)} %get-tuple-element.156), channel_id=1, source_target_pairs={{0,24},{8,16},{16,8},{24,0},{1,25},{9,17},{17,9},{25,1},{2,26},{10... | collective-permute-start | bytes 442376 | tf_op jit(solution)/shard_map/ppermute | solution.py:116
  72.0 20.8 %copy-start.3 = (f32[512,384]{1,0:T(8,128)S(1)}, f32[512,384]{1,0:T(8,128)}, u32[]{:S(2)}) copy-start(f32[512,384]{1,0:T(8,128)} %get-tuple-element.118.grad_residual) | copy-start | bytes 2359300
  72.1 7.0 %collective-permute-start.15 = (bf16[96,384]{1,0:T(8,128)(2,1)S(1)}, bf16[96,384]{1,0:T(8,128)(2,1)S(1)}, u32[]{:S(2)}, u32[]{:S(2)}) collective-permute-start(bf16[96,384]{1,0:T(8,128)(2,1)S(1)} %get-tuple-element.168), channel_id=1, source_target_pairs={{0,2},{1,3},{2,4},{3,5},{4,6},{5,7},{6,0},{7,1},{8,10},{9,11},{10,... | collective-permute-start | bytes 221192 | tf_op jit(solution)/shard_map/ppermute | solution.py:111
  72.8 7.9 %collective-permute-start.16 = (bf16[96,384]{1,0:T(8,128)(2,1)S(1)}, bf16[96,384]{1,0:T(8,128)(2,1)S(1)}, u32[]{:S(2)}, u32[]{:S(2)}) collective-permute-start(bf16[96,384]{1,0:T(8,128)(2,1)S(1)} %get-tuple-element.167), channel_id=1, source_target_pairs={{0,4},{1,5},{2,6},{3,7},{4,0},{5,1},{6,2},{7,3},{8,12},{9,13},{10,... | collective-permute-start | bytes 221192 | tf_op jit(solution)/shard_map/ppermute | solution.py:111
  74.8 6.0 %collective-permute-start.17 = (bf16[96,384]{1,0:T(8,128)(2,1)S(1)}, bf16[96,384]{1,0:T(8,128)(2,1)S(1)}, u32[]{:S(2)}, u32[]{:S(2)}) collective-permute-start(bf16[96,384]{1,0:T(8,128)(2,1)S(1)} %get-tuple-element.166), channel_id=1, source_target_pairs={{0,6},{1,7},{2,0},{3,1},{4,2},{5,3},{6,4},{7,5},{8,14},{9,15},{10,... | collective-permute-start | bytes 221192 | tf_op jit(solution)/shard_map/ppermute | solution.py:111
  80.8 6.9 %collective-permute-start.18 = (bf16[96,384]{1,0:T(8,128)(2,1)S(1)}, bf16[96,384]{1,0:T(8,128)(2,1)S(1)}, u32[]{:S(2)}, u32[]{:S(2)}) collective-permute-start(bf16[96,384]{1,0:T(8,128)(2,1)S(1)} %add_convert_fusion.4), channel_id=1, source_target_pairs={{0,2},{1,3},{2,4},{3,5},{4,6},{5,7},{6,0},{7,1},{8,10},{9,11},{10,... | collective-permute-start | bytes 221192 | tf_op jit(solution)/shard_map/ppermute | solution.py:111
  82.3 8.2 %collective-permute-start.19 = (bf16[96,384]{1,0:T(8,128)(2,1)S(1)}, bf16[96,384]{1,0:T(8,128)(2,1)S(1)}, u32[]{:S(2)}, u32[]{:S(2)}) collective-permute-start(bf16[96,384]{1,0:T(8,128)(2,1)S(1)} %add_convert_fusion.4), channel_id=1, source_target_pairs={{0,4},{1,5},{2,6},{3,7},{4,0},{5,1},{6,2},{7,3},{8,12},{9,13},{10,... | collective-permute-start | bytes 221192 | tf_op jit(solution)/shard_map/ppermute | solution.py:111
  84.4 6.2 %collective-permute-start.20 = (bf16[96,384]{1,0:T(8,128)(2,1)S(1)}, bf16[96,384]{1,0:T(8,128)(2,1)S(1)}, u32[]{:S(2)}, u32[]{:S(2)}) collective-permute-start(bf16[96,384]{1,0:T(8,128)(2,1)S(1)} %add_convert_fusion.4), channel_id=1, source_target_pairs={{0,6},{1,7},{2,0},{3,1},{4,2},{5,3},{6,4},{7,5},{8,14},{9,15},{10,... | collective-permute-start | bytes 221192 | tf_op jit(solution)/shard_map/ppermute | solution.py:111
  84.8 8.7 %collective-permute-start.27 = (bf16[48,384]{1,0:T(8,128)(2,1)S(1)}, bf16[48,384]{1,0:T(8,128)(2,1)S(1)}, u32[]{:S(2)}, u32[]{:S(2)}) collective-permute-start(bf16[48,384]{1,0:T(8,128)(2,1)S(1)} %get-tuple-element.170), channel_id=1, source_target_pairs={{0,2},{1,3},{2,4},{3,5},{4,6},{5,7},{6,0},{7,1},{8,10},{9,11},{10,... | collective-permute-start | bytes 110600 | tf_op jit(solution)/shard_map/ppermute | solution.py:111
  86.5 8.3 %collective-permute-start.28 = (bf16[48,384]{1,0:T(8,128)(2,1)S(1)}, bf16[48,384]{1,0:T(8,128)(2,1)S(1)}, u32[]{:S(2)}, u32[]{:S(2)}) collective-permute-start(bf16[48,384]{1,0:T(8,128)(2,1)S(1)} %get-tuple-element.172), channel_id=1, source_target_pairs={{0,4},{1,5},{2,6},{3,7},{4,0},{5,1},{6,2},{7,3},{8,12},{9,13},{10,... | collective-permute-start | bytes 110600 | tf_op jit(solution)/shard_map/ppermute | solution.py:111
  87.7 10.7 %collective-permute-start.29 = (bf16[48,384]{1,0:T(8,128)(2,1)S(1)}, bf16[48,384]{1,0:T(8,128)(2,1)S(1)}, u32[]{:S(2)}, u32[]{:S(2)}) collective-permute-start(bf16[48,384]{1,0:T(8,128)(2,1)S(1)} %get-tuple-element.171), channel_id=1, source_target_pairs={{0,6},{1,7},{2,0},{3,1},{4,2},{5,3},{6,4},{7,5},{8,14},{9,15},{10,... | collective-permute-start | bytes 110600 | tf_op jit(solution)/shard_map/ppermute | solution.py:111
  90.6 27.7 %collective-permute-start.36 = (bf16[384,384]{1,0:T(8,128)(2,1)S(1)}, bf16[384,384]{1,0:T(8,128)(2,1)S(1)}, u32[]{:S(2)}, u32[]{:S(2)}) collective-permute-start(bf16[384,384]{1,0:T(8,128)(2,1)S(1)} %pad_maximum_fusion.1.refs_0_), channel_id=1, source_target_pairs={{0,8},{8,0},{16,24},{24,16},{1,9},{9,1},{17,25},{25,17},{2,10},{10... | collective-permute-start | bytes 884744 | tf_op jit(solution)/shard_map/ppermute | solution.py:116
  91.8 26.5 %collective-permute-start.37 = (bf16[384,384]{1,0:T(8,128)(2,1)S(1)}, bf16[384,384]{1,0:T(8,128)(2,1)S(1)}, u32[]{:S(2)}, u32[]{:S(2)}) collective-permute-start(bf16[384,384]{1,0:T(8,128)(2,1)S(1)} %pad_maximum_fusion.1.refs_0_), channel_id=1, source_target_pairs={{0,16},{8,24},{16,0},{24,8},{1,17},{9,25},{17,1},{25,9},{2,18},{10... | collective-permute-start | bytes 884744 | tf_op jit(solution)/shard_map/ppermute | solution.py:116
  93.4 24.9 %collective-permute-start.38 = (bf16[384,384]{1,0:T(8,128)(2,1)S(1)}, bf16[384,384]{1,0:T(8,128)(2,1)S(1)}, u32[]{:S(2)}, u32[]{:S(2)}) collective-permute-start(bf16[384,384]{1,0:T(8,128)(2,1)S(1)} %pad_maximum_fusion.1.refs_0_), channel_id=1, source_target_pairs={{0,24},{8,16},{16,8},{24,0},{1,25},{9,17},{17,9},{25,1},{2,26},{10... | collective-permute-start | bytes 884744 | tf_op jit(solution)/shard_map/ppermute | solution.py:116
  94.9 10.9 %collective-permute-start.21 = (bf16[144,384]{1,0:T(8,128)(2,1)S(1)}, bf16[144,384]{1,0:T(8,128)(2,1)S(1)}, u32[]{:S(2)}, u32[]{:S(2)}) collective-permute-start(bf16[144,384]{1,0:T(8,128)(2,1)S(1)} %get-tuple-element.121), channel_id=1, source_target_pairs={{0,6},{1,7},{2,0},{3,1},{4,2},{5,3},{6,4},{7,5},{8,14},{9,15},{10,... | collective-permute-start | bytes 331784 | tf_op jit(solution)/shard_map/ppermute | solution.py:74
  98.4 6.3 %collective-permute-start.30 = (bf16[48,384]{1,0:T(8,128)(2,1)S(1)}, bf16[48,384]{1,0:T(8,128)(2,1)S(1)}, u32[]{:S(2)}, u32[]{:S(2)}) collective-permute-start(bf16[48,384]{1,0:T(8,128)(2,1)S(1)} %get-tuple-element.149), channel_id=1, source_target_pairs={{0,2},{1,3},{2,4},{3,5},{4,6},{5,7},{6,0},{7,1},{8,10},{9,11},{10,... | collective-permute-start | bytes 110600 | tf_op jit(solution)/shard_map/ppermute | solution.py:111
  104.7 8.7 %collective-permute-start.22 = (bf16[144,384]{1,0:T(8,128)(2,1)S(1)}, bf16[144,384]{1,0:T(8,128)(2,1)S(1)}, u32[]{:S(2)}, u32[]{:S(2)}) collective-permute-start(bf16[144,384]{1,0:T(8,128)(2,1)S(1)} %get-tuple-element.122), channel_id=1, source_target_pairs={{0,4},{1,5},{2,6},{3,7},{4,0},{5,1},{6,2},{7,3},{8,12},{9,13},{10,... | collective-permute-start | bytes 331784 | tf_op jit(solution)/shard_map/ppermute | solution.py:74
  105.7 7.7 %collective-permute-start.23 = (bf16[144,384]{1,0:T(8,128)(2,1)S(1)}, bf16[144,384]{1,0:T(8,128)(2,1)S(1)}, u32[]{:S(2)}, u32[]{:S(2)}) collective-permute-start(bf16[144,384]{1,0:T(8,128)(2,1)S(1)} %get-tuple-element.123), channel_id=1, source_target_pairs={{0,2},{1,3},{2,4},{3,5},{4,6},{5,7},{6,0},{7,1},{8,10},{9,11},{10,... | collective-permute-start | bytes 331784 | tf_op jit(solution)/shard_map/ppermute | solution.py:74
  113.4 4.9 %collective-permute-start.31 = (bf16[48,384]{1,0:T(8,128)(2,1)S(1)}, bf16[48,384]{1,0:T(8,128)(2,1)S(1)}, u32[]{:S(2)}, u32[]{:S(2)}) collective-permute-start(bf16[48,384]{1,0:T(8,128)(2,1)S(1)} %get-tuple-element.149), channel_id=1, source_target_pairs={{0,4},{1,5},{2,6},{3,7},{4,0},{5,1},{6,2},{7,3},{8,12},{9,13},{10,... | collective-permute-start | bytes 110600 | tf_op jit(solution)/shard_map/ppermute | solution.py:111
  113.4 4.9 %collective-permute-start.32 = (bf16[48,384]{1,0:T(8,128)(2,1)S(1)}, bf16[48,384]{1,0:T(8,128)(2,1)S(1)}, u32[]{:S(2)}, u32[]{:S(2)}) collective-permute-start(bf16[48,384]{1,0:T(8,128)(2,1)S(1)} %get-tuple-element.149), channel_id=1, source_target_pairs={{0,6},{1,7},{2,0},{3,1},{4,2},{5,3},{6,4},{7,5},{8,14},{9,15},{10,... | collective-permute-start | bytes 110600 | tf_op jit(solution)/shard_map/ppermute | solution.py:111
  118.3 2.4 %collective-permute-start.39 = (bf16[384,384]{1,0:T(8,128)(2,1)S(1)}, bf16[384,384]{1,0:T(8,128)(2,1)S(1)}, u32[]{:S(2)}, u32[]{:S(2)}) collective-permute-start(bf16[384,384]{1,0:T(8,128)(2,1)S(1)} %pad_maximum_fusion.1.refs_0_), channel_id=1, source_target_pairs={{0,1},{1,0},{2,3},{3,2},{4,5},{5,4},{6,7},{7,6},{8,9},{9,8},{10,11... | collective-permute-start | bytes 884744 | tf_op jit(solution)/shard_map/ppermute | solution.py:102
  118.4 3.2 %collective-permute-start.40 = (bf16[384,384]{1,0:T(8,128)(2,1)S(1)}, bf16[384,384]{1,0:T(8,128)(2,1)S(1)}, u32[]{:S(2)}, u32[]{:S(2)}) collective-permute-start(bf16[384,384]{1,0:T(8,128)(2,1)S(1)} %collective-permute-done.36.refs_1_), channel_id=1, source_target_pairs={{0,1},{1,0},{2,3},{3,2},{4,5},{5,4},{6,7},{7,6},{8,9},{9,8},{10,11... | collective-permute-start | bytes 884744 | tf_op jit(solution)/shard_map/ppermute | solution.py:102
  118.9 5.5 %collective-permute-start.41 = (bf16[384,384]{1,0:T(8,128)(2,1)S(1)}, bf16[384,384]{1,0:T(8,128)(2,1)S(1)}, u32[]{:S(2)}, u32[]{:S(2)}) collective-permute-start(bf16[384,384]{1,0:T(8,128)(2,1)S(1)} %collective-permute-done.37.refs_2_), channel_id=1, source_target_pairs={{0,1},{1,0},{2,3},{3,2},{4,5},{5,4},{6,7},{7,6},{8,9},{9,8},{10,11... | collective-permute-start | bytes 884744 | tf_op jit(solution)/shard_map/ppermute | solution.py:102
  119.0 5.3 %collective-permute-start.42 = (bf16[384,384]{1,0:T(8,128)(2,1)S(1)}, bf16[384,384]{1,0:T(8,128)(2,1)S(1)}, u32[]{:S(2)}, u32[]{:S(2)}) collective-permute-start(bf16[384,384]{1,0:T(8,128)(2,1)S(1)} %collective-permute-done.38.refs_3_), channel_id=1, source_target_pairs={{0,1},{1,0},{2,3},{3,2},{4,5},{5,4},{6,7},{7,6},{8,9},{9,8},{10,11... | collective-permute-start | bytes 884744 | tf_op jit(solution)/shard_map/ppermute | solution.py:102
  119.5 8.3 %collective-permute-start.33 = (bf16[208,384]{1,0:T(8,128)(2,1)S(1)}, bf16[208,384]{1,0:T(8,128)(2,1)S(1)}, u32[]{:S(2)}, u32[]{:S(2)}) collective-permute-start(bf16[208,384]{1,0:T(8,128)(2,1)S(1)} %constant_dynamic-update-slice_fusion.4.refs_0_), channel_id=1, source_target_pairs={{0,8},{8,0},{16,24},{24,16},{1,9},{9,1},{17,25},{25,17},{2,10},{10... | collective-permute-start | bytes 479240 | tf_op jit(solution)/shard_map/ppermute | solution.py:116
  120.7 7.9 %collective-permute-start.34 = (bf16[208,384]{1,0:T(8,128)(2,1)S(1)}, bf16[208,384]{1,0:T(8,128)(2,1)S(1)}, u32[]{:S(2)}, u32[]{:S(2)}) collective-permute-start(bf16[208,384]{1,0:T(8,128)(2,1)S(1)} %constant_dynamic-update-slice_fusion.4.refs_0_), channel_id=1, source_target_pairs={{0,16},{8,24},{16,0},{24,8},{1,17},{9,25},{17,1},{25,9},{2,18},{10... | collective-permute-start | bytes 479240 | tf_op jit(solution)/shard_map/ppermute | solution.py:116
  121.6 8.4 %collective-permute-start.35 = (bf16[208,384]{1,0:T(8,128)(2,1)S(1)}, bf16[208,384]{1,0:T(8,128)(2,1)S(1)}, u32[]{:S(2)}, u32[]{:S(2)}) collective-permute-start(bf16[208,384]{1,0:T(8,128)(2,1)S(1)} %constant_dynamic-update-slice_fusion.4.refs_0_), channel_id=1, source_target_pairs={{0,24},{8,16},{16,8},{24,0},{1,25},{9,17},{17,9},{25,1},{2,26},{10... | collective-permute-start | bytes 479240 | tf_op jit(solution)/shard_map/ppermute | solution.py:116
  124.4 6.7 %copy-start.1 = (bf16[384,2304]{1,0:T(8,128)(2,1)S(1)}, bf16[384,2304]{1,0:T(8,128)(2,1)}, u32[]{:S(2)}) copy-start(bf16[384,2304]{1,0:T(8,128)(2,1)} %refs_4_.1) | copy-start | bytes 5308420
  130.0 6.5 %collective-permute-start.43 = (bf16[208,384]{1,0:T(8,128)(2,1)S(1)}, bf16[208,384]{1,0:T(8,128)(2,1)S(1)}, u32[]{:S(2)}, u32[]{:S(2)}) collective-permute-start(bf16[208,384]{1,0:T(8,128)(2,1)S(1)} %constant_dynamic-update-slice_fusion.4.refs_0_), channel_id=1, source_target_pairs={{0,1},{1,0},{2,3},{3,2},{4,5},{5,4},{6,7},{7,6},{8,9},{9,8},{10,11... | collective-permute-start | bytes 479240 | tf_op jit(solution)/shard_map/ppermute | solution.py:102
  130.0 6.5 %collective-permute-start.44 = (bf16[208,384]{1,0:T(8,128)(2,1)S(1)}, bf16[208,384]{1,0:T(8,128)(2,1)S(1)}, u32[]{:S(2)}, u32[]{:S(2)}) collective-permute-start(bf16[208,384]{1,0:T(8,128)(2,1)S(1)} %collective-permute-done.33.refs_1_), channel_id=1, source_target_pairs={{0,1},{1,0},{2,3},{3,2},{4,5},{5,4},{6,7},{7,6},{8,9},{9,8},{10,11... | collective-permute-start | bytes 479240 | tf_op jit(solution)/shard_map/ppermute | solution.py:102
  130.5 6.0 %collective-permute-start.45 = (bf16[208,384]{1,0:T(8,128)(2,1)S(1)}, bf16[208,384]{1,0:T(8,128)(2,1)S(1)}, u32[]{:S(2)}, u32[]{:S(2)}) collective-permute-start(bf16[208,384]{1,0:T(8,128)(2,1)S(1)} %collective-permute-done.34.refs_2_), channel_id=1, source_target_pairs={{0,1},{1,0},{2,3},{3,2},{4,5},{5,4},{6,7},{7,6},{8,9},{9,8},{10,11... | collective-permute-start | bytes 479240 | tf_op jit(solution)/shard_map/ppermute | solution.py:102
  130.5 6.0 %collective-permute-start.46 = (bf16[208,384]{1,0:T(8,128)(2,1)S(1)}, bf16[208,384]{1,0:T(8,128)(2,1)S(1)}, u32[]{:S(2)}, u32[]{:S(2)}) collective-permute-start(bf16[208,384]{1,0:T(8,128)(2,1)S(1)} %collective-permute-done.35.refs_3_), channel_id=1, source_target_pairs={{0,1},{1,0},{2,3},{3,2},{4,5},{5,4},{6,7},{7,6},{8,9},{9,8},{10,11... | collective-permute-start | bytes 479240 | tf_op jit(solution)/shard_map/ppermute | solution.py:102
  (14 other events, 30.4 us)
where the time goes:
time: 139 us
  starting transfers between devices  49.3 us (35%)
  Pallas kernels  45.3 us (33%)
  waiting for transfers between devices  28.4 us (20%)
  local copies, waits for them, and re-layouts  10.1 us (7%)
  other arithmetic  3.87 us (3%)
  between operations  1.91 us (1%)
    ppermute x12, starting transfers between devices, plane_send(): lax.ppermute(values, 'grp', [(d, plane_at(d, step)) for d in range(grp_si...  14.3 us
    ppermute x12, waiting for transfers between devices, line_send(): lax.ppermute(values, 'seq', [(d, (d + 2 * step) % seq_size) for d in rang...  14.1 us
    ppermute x12, starting transfers between devices, line_send(): lax.ppermute(values, 'seq', [(d, (d + 2 * step) % seq_size) for d in rang...  13.1 us
    pallas_call x1, Pallas kernels, backward_attention(): pl.pallas_call(partial(backward_kernel, head_width, 1.0 / math.sqrt(head_...  11.6 us
    ppermute x6, starting transfers between devices, rows_to_owner(): lax.ppermute(block, 'seq', owner_shift(seq_size, owners, share, step))  10.9 us
    pallas_call x1, Pallas kernels, forward_attention(): pl.pallas_call(partial(forward_kernel, head_width, 1.0 / math.sqrt(head_w...  10.3 us
    pallas_call x1, Pallas kernels, middle(): pl.pallas_call(middle_kernel, grid=(1,), in_specs=[pl.BlockSpec(memory_sp...  9.68 us
    ppermute x6, starting transfers between devices, rows_from_owner(): lax.ppermute(pieces[step], 'seq', owner_shift(seq_size, owners, share, ow...  8.72 us
  transfers between devices with their start and end apart: 47, of which 12 were waited for; matrix products, arithmetic and copies ran while one was open for 6% of the time, Pallas kernels for 24%

commit v1 on v0

--- a/solution.py
+++ b/solution.py
@@ -67,13 +67,10 @@
     return pieces
 
 
-def rows_from_owner(pieces, share):
-    owners = len(pieces)
-    seq_size = lax.axis_size("seq")
-    return [pieces[0]] + [
-        lax.ppermute(pieces[step], "seq", owner_shift(seq_size, owners, share, owners - step))
-        for step in range(1, owners)
-    ]
+def rows_from_owner(blocks, share):
+    owners = blocks.shape[0]
+    groups = [[owner * share + rank for owner in range(owners)] for rank in range(share)]
+    return lax.all_to_all(blocks, "seq", 0, 0, axis_index_groups=groups)
 
 
 def share_rows(rows, rank, share):
@@ -162,6 +159,12 @@
 
 def send_line(parts):
     return [parts[0]] + [line_send(parts[step], step) for step in range(1, len(parts))]
+
+
+def line_exchange(values):
+    length = line_size()
+    groups = [list(range(core, 2 * length, 2)) for core in range(2)]
+    return lax.all_to_all(values, "seq", 0, 0, axis_index_groups=groups)
 
 
 def sum_line(values):
@@ -408,7 +411,7 @@
 
 def middle_kernel(
     place, own, attended, cotangent, mod, bias, output_weight, expand_weight, shrink_weight,
-    keep, send, packed_output, grad_attended, grad_residual, sums, *output,
+    keep, send, packed_output, grad_attended, grad_residual, sums, output,
 ):
     first_core = place[2] == 0
     rows, width = own.shape
@@ -445,9 +448,9 @@
         sums[7 + block : 8 + block, :] = column_sum(grad_hidden.astype(f32)) * share
         grad_mixed = grad_mixed + back_product(grad_hidden, expand_weight[:, part])
     result = (residual + row(GATE_TWO) * branch_two).astype(bf16)
-    count = rows // len(output)
-    for step in range(len(output)):
-        output[step][...] = result[step * count : (step + 1) * count, :]
+    owners, count = output.shape[:2]
+    for step in range(owners):
+        output[lax.rem(place[0] - step + owners, owners)] = result[step * count : (step + 1) * count, :]
     sums[5:6, :] = column_sum(wide * branch_two) * share
     sums[7 + blocks : 8 + blocks, :] = column_sum(grad_two.astype(f32)) * share
     sums[4:5, :] = column_sum(grad_mixed * normed) * share
@@ -476,7 +479,8 @@
         pltpu.HBM((width, rows), bf16),
         pltpu.HBM((rows, width), f32),
         jax.ShapeDtypeStruct((16, width), f32),
-    ] + [jax.ShapeDtypeStruct((rows // owners, width), bf16)] * owners
+        jax.ShapeDtypeStruct((owners, rows // owners, width), bf16),
+    ]
     return pl.pallas_call(
         middle_kernel,
         grid=(1,),
@@ -493,7 +497,8 @@
 
 def backward_kernel(
     head_width, score_scale, place, expo, query, key_value, attended_wide, inverse_total,
-    grad_attended, own, rest, mod, weight, packed_output, sums_in, keep, send, own_part, sums,
+    grad_attended, own, rest, mod, weight, packed_output, grad_residual, sums_in, keep, send,
+    rest_part, own_part, sums,
     grad_query, grad_key, grad_value,
 ):
     pair = pl.program_id(0)
@@ -528,7 +533,7 @@
         for at in range(0, rows + rest.shape[0], rows):
             here = slice(at, at + rows)
             source = own[...] if at == 0 else rest[at - rows : at, :]
-            normed = normalize(source.astype(f32))[0]
+            normed, inverse = normalize(source.astype(f32))
             mixed = (normed * scale + shift).astype(bf16)
             keys = jnp.concatenate([grad_key[pair, here, :] for pair in pairs], axis=1)
             values = jnp.concatenate([grad_value[pair, here, :] for pair in pairs], axis=1)
@@ -537,27 +542,31 @@
             )
             if at == 0:
                 part = part + inner(grad_query[...], weight[:width, :])
-                own_part[...] = part
+                back = normalize_back(part * scale, normed, inverse)
+                own_part[...] = (grad_residual[...] + back).astype(bf16)
                 packed_query = product(grad_query[...], mixed).T
             else:
-                send[2 * width + at - rows : 2 * width + at, :] = part.astype(bf16)
+                rest_part[at - rows : at, :] = part.astype(bf16)
             packed_key = packed_key + inner(mixed, keys)
             packed_value = packed_value + inner(mixed, values)
             total_shift = total_shift + column_sum(part)
             total_scale = total_scale + column_sum(part * normed)
         first_core = place[2] == 0
         packed = [packed_query * share, packed_key * share, packed_value * share, packed_output[...].astype(f32)]
-        for half in range(2):
-            here = slice(half * width, (half + 1) * width)
-            keep[here, :] = jnp.where(first_core, packed[half], packed[2 + half]).astype(bf16)
-            send[here, :] = jnp.where(first_core, packed[2 + half], packed[half]).astype(bf16)
+        half = width // 2
+        for at, matrix in enumerate(packed):
+            here = slice(at * half, (at + 1) * half)
+            keep[here, :] = jnp.where(first_core, matrix[:half], matrix[half:]).astype(bf16)
+            send[here, :] = jnp.where(first_core, matrix[half:], matrix[:half]).astype(bf16)
         sums[...] = sums_in[...]
         sums[0:1, :] = total_shift * share
         sums[1:2, :] = total_scale * share
-        send[2 * width + rest.shape[0] :, :] = sums[...].astype(bf16)
-
-
-def backward_attention(place, saved, grad_attended, own, rest, mod, weight, packed_output, sums):
+        rest_part[rest.shape[0] :, :] = sums[...].astype(bf16)
+
+
+def backward_attention(
+    place, saved, grad_attended, own, rest, mod, weight, packed_output, grad_residual, sums
+):
     expo, query, key_value, attended_wide, inverse_total = saved
     rows, width = own.shape
     key_count = rows + rest.shape[0]
@@ -565,14 +574,15 @@
     size = HEADS * rows * key_count
     operands = (
         query, key_value, attended_wide, inverse_total, grad_attended, own, rest, mod, weight,
-        packed_output, sums,
+        packed_output, grad_residual, sums,
     )
     specs = [whole(*item.shape) for item in operands]
     specs[3] = pl.BlockSpec((2, 1, rows), lambda p: (p, 0, 0))
     shapes = [
         jax.ShapeDtypeStruct((2 * width, width), bf16),
-        jax.ShapeDtypeStruct((2 * width + rest.shape[0] + sums.shape[0], width), bf16),
-        jax.ShapeDtypeStruct((rows, width), f32),
+        jax.ShapeDtypeStruct((2 * width, width), bf16),
+        jax.ShapeDtypeStruct((rest.shape[0] + sums.shape[0], width), bf16),
+        jax.ShapeDtypeStruct((rows, width), bf16),
         jax.ShapeDtypeStruct(sums.shape, f32),
     ]
     return pl.pallas_call(
@@ -598,175 +608,233 @@
     )(place, pltpu.with_memory_space_constraint(expo, pltpu.HBM), *operands)
 
 
-def finish_kernel(own, part, received, grad_residual, mod, sums, *results):
+def finish_kernel(place, own, part, received, mod, result):
     rows, width = own.shape
-    count = rows // len(results)
+    owners, count = result.shape[:2]
     normed, inverse = normalize(own[...].astype(f32))
-    first = received.shape[0] - rows - sums.shape[0]
-    grad = (part[...] + received[first : first + rows, :].astype(f32)) * (1.0 + mod[SCALE_ONE : SCALE_ONE + 1, :])
-    grad = (grad_residual[...] + normalize_back(grad, normed, inverse)).astype(bf16)
-    both = (sums[...] + received[first + rows :, :].astype(f32)).astype(bf16)
-    for step, result in enumerate(results):
-        result[:count, :] = grad[step * count : (step + 1) * count, :]
-        result[count:, :] = both
-
-
-def finish_rows(owners, own, part, received, grad_residual, mod, sums):
-    operands = (own, part, received, grad_residual, mod, sums)
-    shape = (own.shape[0] // owners + sums.shape[0], own.shape[1])
+    grad = received[:rows, :].astype(f32) * (1.0 + mod[SCALE_ONE : SCALE_ONE + 1, :])
+    grad = (part[...].astype(f32) + normalize_back(grad, normed, inverse)).astype(bf16)
+    for step in range(owners):
+        at = lax.rem(place[0] - step + owners, owners)
+        result[at] = grad[step * count : (step + 1) * count, :]
+
+
+def finish_rows(owners, place, own, part, received, mod):
+    operands = (own, part, received, mod)
+    shape = (owners, own.shape[0] // owners, own.shape[1])
     return pl.pallas_call(
         finish_kernel,
         grid=(1,),
-        in_specs=[whole(*item.shape) for item in operands],
-        out_specs=[whole(*shape)] * owners,
-        out_shape=[jax.ShapeDtypeStruct(shape, bf16)] * owners,
+        in_specs=[pl.BlockSpec(memory_space=pltpu.SMEM)] + [whole(*item.shape) for item in operands],
+        out_specs=whole(*shape),
+        out_shape=jax.ShapeDtypeStruct(shape, bf16),
         compiler_params=kernel_params(12),
         name="finish_rows",
-    )(*operands)
-
-
-def placed_kernel(owners, place, *refs):
-    pieces, result = refs[:owners], refs[owners]
-    for step in range(owners):
-        result[lax.rem(place[0] + step, owners)] = pieces[step][...]
-
-
-def placed(place, pieces):
-    owners = len(pieces)
-    shape = (owners,) + pieces[0].shape
+    )(place, *operands)
+
+
+def line_total_kernel(sums, received, *refs):
+    parts, result = refs[:-1], refs[-1]
+    count = parts[0].shape[0]
+    result[:count, :] = total([part[...] for part in parts]).astype(bf16)
+    below = received[received.shape[0] - sums.shape[0] :, :].astype(f32)
+    result[count:, :] = (sums[...] + below).astype(bf16)
+
+
+def line_total(parts, sums, received):
+    count, width = parts[0].shape
+    below = sums.shape[0]
     return pl.pallas_call(
-        partial(placed_kernel, owners),
+        line_total_kernel,
         grid=(1,),
-        in_specs=[pl.BlockSpec(memory_space=pltpu.SMEM)] + [whole(*item.shape) for item in pieces],
-        out_specs=whole(*shape),
-        out_shape=jax.ShapeDtypeStruct(shape, pieces[0].dtype),
+        in_specs=[whole(*item.shape) for item in [sums, received] + parts],
+        out_specs=whole(count + below, width),
+        out_shape=jax.ShapeDtypeStruct((count + below, width), bf16),
         compiler_params=kernel_params(8),
-        name="placed",
-    )(place, *pieces)
-
-
-def placed_sums_kernel(owners, place, lead, mod, *refs):
-    pieces, (result, vector) = refs[:owners], refs[owners:]
-    count = result.shape[1]
-    for step in range(owners):
-        result[lax.rem(place[0] + step, owners)] = pieces[step][:count, :].astype(f32)
-    below = total([piece[count:, :] for piece in pieces])
+        name="line_total",
+    )(sums, received, *parts)
+
+
+def with_lead(below, lead, mod):
     row = lax.broadcasted_iota(jnp.int32, below.shape, 0)
     below = jnp.where(row == 12, mod[EMBEDDING : EMBEDDING + 1, :], below)
-    below = jnp.where(row == 13, jnp.full(below.shape, lead[0]).astype(f32), below)
-    vector[...] = below.astype(bf16)
-
-
-def placed_sums(place, lead, mod, pieces):
-    owners = len(pieces)
-    below, width = 16, mod.shape[1]
-    shapes = [
-        jax.ShapeDtypeStruct((owners, pieces[0].shape[0] - below, width), f32),
-        jax.ShapeDtypeStruct((below, width), bf16),
-    ]
+    return jnp.where(row == 13, jnp.full(below.shape, lead).astype(f32), below).astype(bf16)
+
+
+def line_join_kernel(lead, mod, *refs):
+    parts, result = refs[:-1], refs[-1]
+    count = (result.shape[0] - 16) // len(parts)
+    for at, part in enumerate(parts):
+        result[at * count : (at + 1) * count, :] = part[:count, :]
+    below = total([part[count:, :] for part in parts])
+    result[len(parts) * count :, :] = with_lead(below, lead[0], mod)
+
+
+def line_join(lead, mod, parts):
+    rows, width = parts[0].shape
+    shape = (len(parts) * (rows - 16) + 16, width)
     return pl.pallas_call(
-        partial(placed_sums_kernel, owners),
+        line_join_kernel,
         grid=(1,),
-        in_specs=[pl.BlockSpec(memory_space=pltpu.SMEM)] * 2
-        + [whole(*mod.shape)]
-        + [whole(*item.shape) for item in pieces],
-        out_specs=[whole(*item.shape) for item in shapes],
-        out_shape=shapes,
+        in_specs=[pl.BlockSpec(memory_space=pltpu.SMEM)]
+        + [whole(*item.shape) for item in [mod] + parts],
+        out_specs=whole(*shape),
+        out_shape=jax.ShapeDtypeStruct(shape, bf16),
         compiler_params=kernel_params(8),
-        name="placed_sums",
-    )(place, lead, mod, *pieces)
-
-
-def ordered_kernel(grp_size, line, count, targets, place, *refs):
-    own, received, outputs = refs[:grp_size], refs[grp_size : 2 * grp_size], refs[2 * grp_size :]
-    width = own[0].shape[1]
-    core, group, at_line = place[2], place[3], place[4]
-
-    def write(side, ref, b):
-        for c in range(line):
-            from_c = lax.rem(at_line - c + line, line)
-            here = pl.ds(pl.multiple_of(from_c * count, count), count)
-            first = ((side * grp_size + b) * line + c) * count
-            output, row, column = targets[first // width]
-            row = row + first % width
-            outputs[output][row : row + count, column : column + width] = ref[here, :].astype(f32)
-
-    def choose(side, refs_here):
-        for step in range(grp_size):
-            for g in range(grp_size):
-                b = g ^ step if grp_size & (grp_size - 1) == 0 else (g - step) % grp_size
-
-                @pl.when(group == g)
-                def _():
-                    write(side, refs_here[step], b)
-
-    for side in range(2):
-
-        @pl.when(core == side)
-        def _():
-            choose(side, own)
-            choose(1 - side, received)
-
-
-def ordered(place, own, rows, targets, shapes):
+        name="line_join",
+    )(lead, mod, *parts)
+
+
+def picked(place, grp_size, own, received, side, b, write):
+    group = place[3]
+    for step in range(grp_size):
+        here = (group ^ b if grp_size & (grp_size - 1) == 0 else lax.rem(group - b + grp_size, grp_size)) == step
+        for ref, mine in ((own[step], True), (received[step], False)):
+
+            @pl.when(here & ((place[2] == side) == mine))
+            def _():
+                write(ref)
+
+
+def copy_line(place, line, count, ref, output, first):
+    for c in range(line):
+        from_c = lax.rem(place[4] - c + line, line)
+        here = pl.ds(pl.multiple_of(from_c * count, count), count)
+        output[first + c * count : first + (c + 1) * count, :] = ref[here, :].astype(f32)
+
+
+def first_sums_kernel(grp_size, line, place, *refs):
+    own, received = refs[:grp_size], refs[grp_size : 2 * grp_size]
+    refs = refs[2 * grp_size :]
+    weight, output, blocks = refs[:3]
+    shrink, expand, grad_weight, copied, rows, table, grad_bias = refs[3:10]
+    output_bias, expand_bias, shrink_bias, grad_lifted, sums = refs[10:]
+    b = pl.program_id(0)
+    width = table.shape[1]
+    count = own[0].shape[0] - 16
+    copied[...] = output[...]
+    rows[...] = blocks[...].astype(f32)
+    for side, target in enumerate((shrink, expand)):
+        write = lambda ref: copy_line(place, line, count // line, ref, target, 0)
+        picked(place, grp_size, own, received, side, b, write)
+
+    parts = [part[count:, :].astype(f32) for part in own]
+    pad = jnp.zeros((8 - grp_size, width), f32)
+    stacked = jnp.concatenate([part[12:13] for part in parts] + [pad])
+    gate = 1.0 / (1.0 + jnp.exp(-stacked))
+
+    @pl.when(b == 0)
+    def _():
+        sums[...] = total(parts)
+        grad_lifted[...] = jnp.zeros_like(grad_lifted)
+
+    @pl.when(b < 3)
+    def _():
+        lifted = (stacked * gate).astype(bf16)
+        line_of = lax.broadcasted_iota(jnp.int32, parts[0].shape, 0)
+        for i in range(2):
+            here = slice(i * width, (i + 1) * width)
+            picks = [column_sum(jnp.where(line_of == 2 * b + i, part, 0.0)) for part in parts]
+            picks = jnp.concatenate(picks + [pad]).astype(bf16)
+            grad_weight[:, here] = inner(lifted, picks)
+            grad_lifted[...] += back_product(picks, weight[:, here])
+
+    @pl.when(b == pl.num_programs(0) - 1)
+    def _():
+        for at in range(6):
+            grad_bias[at * width : (at + 1) * width] = sums[at]
+        output_bias[...] = sums[6]
+        for at in range(expand_bias.shape[0] // width):
+            expand_bias[at * width : (at + 1) * width] = sums[7 + at]
+        shrink_bias[...] = sums[7 + expand_bias.shape[0] // width]
+        grad_embedding = grad_lifted[...] * gate * (1.0 + stacked * (1.0 - gate))
+        lead = lax.broadcasted_iota(jnp.int32, (LEADS, width), 0).astype(f32)
+        table[...] = total(
+            [
+                jnp.where(lead == part[13:14], grad_embedding[p : p + 1], 0.0)
+                for p, part in enumerate(parts)
+            ]
+        )
+
+
+def first_sums(place, own, weight, output, blocks):
+    grp_size = len(own)
     line = 1 if line_size() > 4 else line_size()
     received = [swap_cores(part) for part in own]
-    shapes = [jax.ShapeDtypeStruct(shape, f32) for shape in shapes]
+    width = weight.shape[0]
+    hidden = grp_size * width
+    owners = blocks.shape[0]
+    block = pl.BlockSpec((owners // grp_size,) + blocks.shape[1:], lambda b: (b, 0, 0))
+    wide = pl.BlockSpec((width, 2 * width), lambda b: (0, jnp.minimum(b, 2)))
     return pl.pallas_call(
-        partial(ordered_kernel, len(own), line, rows // line, targets),
-        grid=(1,),
+        partial(first_sums_kernel, grp_size, line),
+        grid=(grp_size,),
         in_specs=[pl.BlockSpec(memory_space=pltpu.SMEM)]
-        + [whole(rows, part.shape[1]) for part in own + received],
-        out_specs=[whole(*item.shape) for item in shapes],
-        out_shape=shapes,
+        + [whole(*own[0].shape)] * (2 * grp_size)
+        + [wide, block, block],
+        out_specs=[
+            pl.BlockSpec((width, width), lambda b: (b, 0)),
+            pl.BlockSpec((width, width), lambda b: (0, b)),
+            wide,
+            block,
+            block,
+            whole(LEADS, width),
+            whole(6 * width),
+            whole(width),
+            whole(hidden),
+            whole(width),
+        ],
+        out_shape=[
+            jax.ShapeDtypeStruct((hidden, width), f32),
+            jax.ShapeDtypeStruct((width, hidden), f32),
+            jax.ShapeDtypeStruct(weight.shape, f32),
+            jax.ShapeDtypeStruct(output.shape, output.dtype),
+            jax.ShapeDtypeStruct(blocks.shape, f32),
+            jax.ShapeDtypeStruct((LEADS, width), f32),
+            jax.ShapeDtypeStruct((6 * width,), f32),
+            jax.ShapeDtypeStruct((width,), f32),
+            jax.ShapeDtypeStruct((hidden,), f32),
+            jax.ShapeDtypeStruct((width,), f32),
+        ],
+        scratch_shapes=[pltpu.VMEM((8, width), f32), pltpu.VMEM((16, width), f32)],
+        compiler_params=kernel_params(20),
+        name="first_sums",
+    )(place, *own, *received, weight, output, blocks)
+
+
+def second_sums_kernel(grp_size, line, place, *refs):
+    own, received = refs[:grp_size], refs[grp_size : 2 * grp_size]
+    attend, output = refs[2 * grp_size :]
+    b = pl.program_id(0)
+    half = output.shape[0] // 2
+    for target, chosen in ((attend, b < grp_size - 1), (output, b == grp_size - 1)):
+
+        @pl.when(chosen)
+        def _():
+            for side in range(2):
+                write = lambda ref: copy_line(place, line, half // line, ref, target, side * half)
+                picked(place, grp_size, own, received, side, b, write)
+
+
+def second_sums(place, own):
+    grp_size, width = len(own), own[0].shape[1]
+    line = 1 if line_size() > 4 else line_size()
+    received = [swap_cores(part) for part in own]
+    return pl.pallas_call(
+        partial(second_sums_kernel, grp_size, line),
+        grid=(grp_size,),
+        in_specs=[pl.BlockSpec(memory_space=pltpu.SMEM)] + [whole(*own[0].shape)] * (2 * grp_size),
+        out_specs=[
+            pl.BlockSpec((width, width), lambda b: (0, jnp.minimum(b, grp_size - 2))),
+            whole(width, width),
+        ],
+        out_shape=[
+            jax.ShapeDtypeStruct((width, 3 * width), f32),
+            jax.ShapeDtypeStruct((width, width), f32),
+        ],
         compiler_params=kernel_params(16),
-        name="ordered",
+        name="second_sums",
     )(place, *own, *received)
-
-
-def vectors_kernel(parts_count, *refs):
-    parts = [ref[...].astype(f32) for ref in refs[:parts_count]]
-    weight = refs[parts_count]
-    grad_weight, grad_bias, table, biases = refs[parts_count + 1 :]
-    width = parts[0].shape[1]
-    biases[...] = total([part[6:12] for part in parts])
-    stacked = jnp.concatenate([part[12:13] for part in parts] + [jnp.zeros((8 - parts_count, width), f32)])
-    gate = 1.0 / (1.0 + jnp.exp(-stacked))
-    lifted = (stacked * gate).astype(bf16).astype(f32).T
-    grad_lifted = jnp.zeros((8, width), f32)
-    for block in range(6):
-        rows = [part[block : block + 1] for part in parts]
-        here = slice(block * width, (block + 1) * width)
-        grad_weight[:, here] = total([lifted[:, p : p + 1] * row for p, row in enumerate(rows)])
-        grad_bias[:, here] = total(rows)
-        rows = jnp.concatenate(rows + [jnp.zeros((8 - parts_count, width), f32)])
-        high = rows.astype(bf16)
-        low = (rows - high.astype(f32)).astype(bf16)
-        grad_lifted = grad_lifted + back_product(high, weight[:, here]) + back_product(low, weight[:, here])
-    grad_embedding = grad_lifted * gate * (1.0 + stacked * (1.0 - gate))
-    lead = lax.broadcasted_iota(jnp.int32, (LEADS, width), 0).astype(f32)
-    table[...] = total(
-        [
-            jnp.where(lead == parts[p][13:14], grad_embedding[p : p + 1], 0.0)
-            for p in range(parts_count)
-        ]
-    )
-
-
-def vectors(parts, first, weight):
-    width = weight.shape[0]
-    shapes = [weight.shape, (1, weight.shape[1]), (LEADS, width), (6, width)]
-    shapes = [jax.ShapeDtypeStruct(shape, f32) for shape in shapes]
-    return pl.pallas_call(
-        partial(vectors_kernel, len(parts)),
-        grid=(1,),
-        in_specs=[pl.BlockSpec((16, width), lambda i: (first // 16, 0)) for _ in parts]
-        + [whole(*weight.shape)],
-        out_specs=[whole(*item.shape) for item in shapes],
-        out_shape=shapes,
-        compiler_params=kernel_params(16),
-        name="vectors",
-    )(*parts, weight)
 
 
 def long_forward(owner, rank, share, lengths, valid, own, rest, mod, weight):
@@ -800,7 +868,9 @@
     return ((probs, queries, keys, values, attended, normed, mixed), flat)
 
 
-def long_backward(place, saved, grad_attended, own, rest, mod, weight, packed_output, sums):
+def long_backward(
+    place, saved, grad_attended, own, rest, mod, weight, packed_output, grad_residual, sums
+):
     probs, queries, keys, values, attended, normed, mixed = saved
     rows, width = own.shape
     head_width = width // HEADS
@@ -819,18 +889,19 @@
     part = product(grad_key, weight[width : 2 * width]) + product(grad_value, weight[2 * width :])
     part = jnp.concatenate([part[:rows] + product(grad_query, weight[:width]), part[rows:]], axis=0)
     share = mod[SHARE]
-    first = jnp.concatenate([row_product(mixed[:rows], grad_query), row_product(mixed, grad_key)])
-    first = (first * share).astype(bf16)
-    second = jnp.concatenate(
-        [(row_product(mixed, grad_value) * share).astype(bf16), packed_output]
-    )
+    packed = [row_product(mixed[:rows], grad_query), row_product(mixed, grad_key), row_product(mixed, grad_value)]
+    packed = [(matrix * share).astype(bf16) for matrix in packed] + [packed_output]
+    half = width // 2
+    top = jnp.concatenate([matrix[:half] for matrix in packed])
+    bottom = jnp.concatenate([matrix[half:] for matrix in packed])
     first_core = place[2] == 0
-    keep = jnp.where(first_core, first, second)
-    send = jnp.where(first_core, second, first)
+    keep = jnp.where(first_core, top, bottom)
+    send = jnp.where(first_core, bottom, top)
     total_rows = jnp.stack([jnp.sum(part, axis=0), jnp.sum(part * normed, axis=0)]) * share
     sums = jnp.concatenate([total_rows, sums[2:]], axis=0)
-    send = jnp.concatenate([send, part[rows:].astype(bf16), sums.astype(bf16)])
-    return (keep, send, part[:rows], sums)
+    normed, inverse = normalize(own.astype(f32))
+    own_part = grad_residual + normalize_back(part[:rows] * (1.0 + mod[SCALE_ONE]), normed, inverse)
+    return (keep, send, part[rows:].astype(bf16), own_part.astype(bf16), sums)
 
 
 def on_device(
@@ -887,78 +958,68 @@
             owner, rank, share, lengths[0], valid_mask[0], own_tokens, rest_tokens, mod, weight
         )
     grad_out = jnp.concatenate(after_all(grad_pieces, attended), axis=0)
-    ff_keep, ff_send, packed_output, grad_attended, grad_residual, sums, *output_pieces = middle(
+    ff_keep, ff_send, packed_output, grad_attended, grad_residual, sums, output = middle(
         owners, where, own_tokens, attended, grad_out, mod, bias, output_weight, expand_weight,
         shrink_weight,
     )
-    output_pieces = rows_from_owner(output_pieces, share)
+    output = rows_from_owner(output, share)
     ff_core = low_total([ff_keep, swap_cores(ff_send)])
     ff_parts = send_plane(plane_parts(ff_core))
     grad_attended = after(grad_attended, ff_core)
     backward = backward_attention if short else long_backward
     held = backward(
-        where, saved, grad_attended, own_tokens, rest_tokens, mod, weight, packed_output, sums
+        where, saved, grad_attended, own_tokens, rest_tokens, mod, weight, packed_output,
+        grad_residual, sums,
     )
-    at_keep, send, own_part, sums = after_all(held, *ff_parts[1:], *output_pieces)
+    at_keep, at_send, rest_part, own_part, sums = after_all(held, *ff_parts[1:], output)
     ff_plane = low_total(ff_parts)
     line = line_size() <= 4
     if line:
         ff_parts = send_line(line_parts(ff_plane))
+    at_core = low_total([at_keep, swap_cores(at_send)])
     if share == 2:
-        received = swap_cores(send)
+        received = swap_cores(rest_part)
     else:
-        received = swap_cores(send[: 2 * width])
-        vector = sum_share(sums, share)
-        rest_part = return_rows(send[2 * width : -sums.shape[0]], rank, share)
-        received = jnp.concatenate([received, rest_part, (vector - sums).astype(bf16)])
-    at_core = low_total([at_keep, received[: 2 * width]])
+        received = return_rows(rest_part, rank, share)
     at_slices = plane_parts(at_core)
-    if line:
-        ff_parts = after_all(ff_parts, *at_slices)
+    finished = finish_rows(owners, where, own_tokens, own_part, after(received, ff_plane), mod)
+    finished = rows_from_owner(finished, share)
     at_parts = send_plane(at_slices)
     at_plane = low_total(at_parts)
     if line:
-        ff_line = low_total(ff_parts)
+        ff_parts = list(after_all(ff_parts, *at_slices))
+        ff_line = line_total(ff_parts, sums, received)
         ff_pieces = send_line([ff_line] * line_size())
-        at_line = low_total(send_line(line_parts(at_plane)))
+        ff_plane = line_join(lead_index, mod, ff_pieces)
+        at_line = low_total(after_all(send_line(line_parts(at_plane)), finished))
         at_pieces = send_line([at_line] * line_size())
     else:
+        vector = with_lead(lax.psum(sums, "seq"), lead_index[0], mod)
         ff_pieces = [sum_line(ff_plane)]
-        at_pieces = [sum_line(at_plane)]
-    finished = finish_rows(
-        owners, own_tokens, own_part, after(received, *ff_pieces), grad_residual, mod, sums
+        ff_plane = jnp.concatenate(ff_pieces + [vector])
+        at_line = sum_line(at_plane)
+        at_pieces = [at_line]
+    ff_parts = gather_plane(ff_plane)
+    at_parts = gather_plane(jnp.concatenate(at_pieces))
+    ff_parts = list(after_all(ff_parts, *at_pieces))
+    grad_shrink, grad_expand, grad_mod_weight, output, grad_tokens, grad_table, grad_mod_bias, *biases = (
+        first_sums(where, ff_parts, modulation_weight, output, finished)
     )
-    grad_pieces = rows_from_owner(finished, share)
-    ff_parts = gather_plane(jnp.concatenate(ff_pieces))
-    grad_tokens, vector = placed_sums(where, lead_index, mod, grad_pieces)
-    at_parts = gather_plane(jnp.concatenate(at_pieces + [vector]))
-    ff_parts = list(after_all(ff_parts, vector, *at_pieces))
-    ff_blocks = hidden_width // width
-    targets = [(0, i * width, 0) for i in range(ff_blocks)] + [(1, 0, i * width) for i in range(ff_blocks)]
-    grad_shrink, grad_expand = ordered(
-        where, ff_parts, ff_parts[0].shape[0], targets, [shrink_weight.shape, expand_weight.shape]
-    )
-    output = placed(where, after_all(output_pieces, vector))
-    at_parts = list(after_all(at_parts, grad_shrink, output))
-    targets = [(0, 0, i * width) for i in range(3)] + [(1, 0, 0)]
-    count = at_parts[0].shape[0] - vector.shape[0]
-    grad_attend, grad_output = ordered(
-        where, at_parts, count, targets, [attend_weight.shape, output_weight.shape]
-    )
-    grad_mod_weight, grad_mod_bias, grad_table, biases = vectors(at_parts, count, modulation_weight)
+    at_parts = list(after_all(at_parts, grad_shrink))
+    grad_attend, grad_output = second_sums(where, at_parts)
     return (
         output[None],
         grad_tokens[None],
         grad_table,
         grad_mod_weight,
-        grad_mod_bias.reshape(-1),
+        grad_mod_bias,
         grad_attend,
         grad_output,
         biases[0],
         grad_expand,
-        biases[1 : 1 + ff_blocks].reshape(-1),
+        biases[1],
         grad_shrink,
-        biases[1 + ff_blocks],
+        biases[2],
     )
 
 

time: 139 us -> 132 us (0.950)
  waiting for transfers between devices: 28.4 us -> 15.2 us
  starting transfers between devices: 49.3 us -> 57.9 us
  local copies, waits for them, and re-layouts: 10.1 us -> 8.08 us
  Pallas kernels: 45.3 us -> 43.3 us
    ppermute x12, starting transfers between devices: 13.1 us -> 21.9 us  [line_send(): lax.ppermute(values, 'seq', [(d, (d + 2 * step) % seq_size) for d in rang...]
    ppermute x6 -> x0, starting transfers between devices: 8.72 us -> none  [rows_from_owner(): lax.ppermute(pieces[step], 'seq', owner_shift(seq_size, owners, share, ow...]
    all_to_all x0 -> x2, starting transfers between devices: none -> 8.22 us  [rows_from_owner(): return lax.all_to_all(blocks, 'seq', 0, 0, axis_index_groups=groups)]
    ppermute x6 -> x0, waiting for transfers between devices: 7.65 us -> none  [rows_from_owner(): lax.ppermute(pieces[step], 'seq', owner_shift(seq_size, owners, share, ow...]
    ppermute x12, waiting for transfers between devices: 14.1 us -> 11.1 us  [line_send(): lax.ppermute(values, 'seq', [(d, (d + 2 * step) % seq_size) for d in rang...]
    pallas_call x6 -> x5, Pallas kernels: 12.8 us -> 10.9 us  [the longest x1 5.99 us: first_sums(): pl.pallas_call(partial(first_sums_kernel, grp_size, line), grid=(grp_size...]
    unnamed x68 -> x45, local copies, waits for them, and re-layouts: 4.57 us -> 2.97 us
    ppermute x10 -> x11, waiting for transfers between devices: 2.81 us -> 1.55 us  [swap_cores(): return lax.ppermute(values, 'seq', [(d, d ^ 1) for d in range(seq_size)])]
  transfers between devices with their start and end apart: 47 -> 44, of which waited for: 12 -> 14; matrix products, arithmetic and copies ran while one was open for 6% -> 6% of each run, Pallas kernels for 24% -> 24%
where the time goes in v1:
time: 132 us; the launch traced here: 131 us
  starting transfers between devices  57.9 us (44%)
  Pallas kernels  43.3 us (33%)
  waiting for transfers between devices  15.2 us (12%)
  local copies, waits for them, and re-layouts  8.08 us (6%)
  other arithmetic  4.5 us (3%)
  between operations  1.88 us (1%)
    ppermute x12, starting transfers between devices, line_send(): lax.ppermute(values, 'seq', [(d, (d + 2 * step) % seq_size) for d in rang...  21.9 us
    ppermute x12, starting transfers between devices, plane_send(): lax.ppermute(values, 'grp', [(d, plane_at(d, step)) for d in range(grp_si...  14.1 us
    pallas_call x1, Pallas kernels, backward_attention(): pl.pallas_call(partial(backward_kernel, head_width, 1.0 / math.sqrt(head_...  11.6 us
    ppermute x12, waiting for transfers between devices, line_send(): lax.ppermute(values, 'seq', [(d, (d + 2 * step) % seq_size) for d in rang...  11.1 us
    ppermute x6, starting transfers between devices, rows_to_owner(): lax.ppermute(block, 'seq', owner_shift(seq_size, owners, share, step))  10.9 us
    pallas_call x1, Pallas kernels, forward_attention(): pl.pallas_call(partial(forward_kernel, head_width, 1.0 / math.sqrt(head_w...  10.4 us
    pallas_call x1, Pallas kernels, middle(): pl.pallas_call(middle_kernel, grid=(1,), in_specs=[pl.BlockSpec(memory_sp...  9.51 us
    all_to_all x2, starting transfers between devices, rows_from_owner(): return lax.all_to_all(blocks, 'seq', 0, 0, axis_index_groups=groups)  8.22 us
  transfers between devices with their start and end apart: 44, of which 14 were waited for; matrix products, arithmetic and copies ran while one was open for 6% of the time, Pallas kernels for 24%

profile of v1, /device:TPU:0, one launch (start us, length us, event | category | flops | bytes accessed | tf_op | source)
XLA Modules:
  0.0 130.8 jit_solution(1324108547266944485)
XLA Ops:
  0.8 1.1 dynamic-slice_bitcast_fusion.4
  1.9 3.1 %collective-permute-start = (bf16[128,384]{1,0:T(8,128)(2,1)S(1)}, bf16[128,384]{1,0:T(8,128)(2,1)S(1)}, u32[]{:S(2)}, u32[]{:S(2)}) collective-permute-start(bf16[128,384]{1,0:T(8,128)(2,1)S(1)} %get-tuple-element.153), channel_id=1, source_target_pairs={{0,2},{1,3},{2,4},{3,5},{4,6},{5,7},{6,0},{7,1},{8,10},{9,11},{10,... | collective-permute-start | bytes 294920 | tf_op jit(solution)/shard_map/ppermute | solution.py:65
  5.0 2.6 %collective-permute-start.1 = (bf16[128,384]{1,0:T(8,128)(2,1)S(1)}, bf16[128,384]{1,0:T(8,128)(2,1)S(1)}, u32[]{:S(2)}, u32[]{:S(2)}) collective-permute-start(bf16[128,384]{1,0:T(8,128)(2,1)S(1)} %get-tuple-element.155), channel_id=1, source_target_pairs={{0,4},{1,5},{2,6},{3,7},{4,0},{5,1},{6,2},{7,3},{8,12},{9,13},{10,... | collective-permute-start | bytes 294920 | tf_op jit(solution)/shard_map/ppermute | solution.py:65
  7.6 1.3 %collective-permute-start.2 = (bf16[128,384]{1,0:T(8,128)(2,1)S(1)}, bf16[128,384]{1,0:T(8,128)(2,1)S(1)}, u32[]{:S(2)}, u32[]{:S(2)}) collective-permute-start(bf16[128,384]{1,0:T(8,128)(2,1)S(1)} %get-tuple-element.152), channel_id=1, source_target_pairs={{0,6},{1,7},{2,0},{3,1},{4,2},{5,3},{6,4},{7,5},{8,14},{9,15},{10,... | collective-permute-start | bytes 294920 | tf_op jit(solution)/shard_map/ppermute | solution.py:65
  8.9 0.7 concatenate.30
  9.6 0.7 concatenate.29
  10.3 0.7 concatenate.28
  11.0 0.7 concatenate.27
  12.5 1.5 %copy-done = bf16[384,2304]{1,0:T(8,128)(2,1)S(1)} copy-done((bf16[384,2304]{1,0:T(8,128)(2,1)S(1)}, bf16[384,2304]{1,0:T(8,128)(2,1)}, u32[]{:S(2)}) %copy-start) | copy-done | bytes 1769496
  13.9 0.7 copy-done.3
  14.6 0.7 copy-done.4
  15.3 0.9 prepare.1
  16.5 0.7 collective-permute-start.4
  17.2 1.4 %collective-permute-start.5 = (bf16[128,384]{1,0:T(8,128)(2,1)S(1)}, bf16[128,384]{1,0:T(8,128)(2,1)S(1)}, u32[]{:S(2)}, u32[]{:S(2)}) collective-permute-start(bf16[128,384]{1,0:T(8,128)(2,1)S(1)} %get-tuple-element.149), channel_id=1, source_target_pairs={{0,4},{1,5},{2,6},{3,7},{4,0},{5,1},{6,2},{7,3},{8,12},{9,13},{10,... | collective-permute-start | bytes 294920 | tf_op jit(solution)/shard_map/ppermute | solution.py:65
  18.6 1.7 %collective-permute-start.6 = (bf16[128,384]{1,0:T(8,128)(2,1)S(1)}, bf16[128,384]{1,0:T(8,128)(2,1)S(1)}, u32[]{:S(2)}, u32[]{:S(2)}) collective-permute-start(bf16[128,384]{1,0:T(8,128)(2,1)S(1)} %get-tuple-element.148), channel_id=1, source_target_pairs={{0,6},{1,7},{2,0},{3,1},{4,2},{5,3},{6,4},{7,5},{8,14},{9,15},{10,... | collective-permute-start | bytes 294920 | tf_op jit(solution)/shard_map/ppermute | solution.py:65
  20.4 10.4 %forward_attention.1 = (bf16[6,1024,512]{2,1,0:T(8,128)(2,1)}, bf16[384,512]{1,0:T(8,128)(2,1)S(1)}, bf16[768,1024]{1,0:T(8,128)(2,1)S(1)}, f32[384,512]{1,0:T(8...) custom-call(s32[5]{0:T(128)S(1)} %stack.17.place, s32[4,8]{1,0:T(4,128)S(1)} %bitcast.25, ...), custom_call_target="tpu_custom_call" | custom-call | flops 3221225472 | bytes 6291456 | tf_op jit(solution)/shard_map/forward_attention/pallas_call | solution.py:383
  30.9 9.5 %middle.1 = (bf16[1536,384]{1,0:T(8,128)(2,1)S(1)}, bf16[1536,384]{1,0:T(8,128)(2,1)}, bf16[384,384]{1,0:T(8,128)(2,1)}, bf16[384,512]{1,0:T(8,128)(2,1)}, f32[5...) custom-call(s32[5]{0:T(128)S(1)} %stack.17.place, ...), custom_call_target="tpu_custom_call" | custom-call | flops 4831838208 | bytes 16777216 | tf_op jit(solution)/shard_map/middle/pallas_call | solution.py:484
  40.5 3.7 %all-to-all-start = ((bf16[4,128,384]{2,1,0:T(8,128)(2,1)}), bf16[4,128,384]{2,1,0:T(8,128)(2,1)S(1)}, u32[]{:S(2)}, u32[]{:S(2)}) async-start(bf16[4,128,384]{2,1,0:T(8,128)(2,1)} %get-tuple-element.105), calls=%async_computation | async-start | bytes 786432 | tf_op jit(solution)/shard_map/all_to_all | solution.py:73
  44.2 1.7 %add_convert_fusion = bf16[1536,384]{1,0:T(8,128)(2,1)S(1)} fusion(bf16[1536,384]{1,0:T(8,128)(2,1)} %collective-permute-done.7, bf16[1536,384]{1,0:T(8,128)(2,1)S(1)} %get-tuple-element.94), kind=kLoop, calls=%fused_computation | loop fusion | flops 2359296 | bytes 3538944 | tf_op jit(solution)/shard_map/convert_element_type | solution.py:177
  46.0 0.9 constant_dynamic-slice_fusion.12
  46.9 1.5 %collective-permute-start.8 = (bf16[384,384]{1,0:T(8,128)(2,1)}, bf16[384,384]{1,0:T(8,128)(2,1)}, u32[]{:S(2)}, u32[]{:S(2)}) collective-permute-start(bf16[384,384]{1,0:T(8,128)(2,1)} %get-tuple-element.144), channel_id=1, source_target_pairs={{0,8},{8,0},{16,24},{24,16},{1,9},{9,1},{17,25},{25,17},{2,10},{10... | collective-permute-start | bytes 884744 | tf_op jit(solution)/shard_map/ppermute | solution.py:113
  48.4 1.5 %collective-permute-start.9 = (bf16[384,384]{1,0:T(8,128)(2,1)}, bf16[384,384]{1,0:T(8,128)(2,1)}, u32[]{:S(2)}, u32[]{:S(2)}) collective-permute-start(bf16[384,384]{1,0:T(8,128)(2,1)} %get-tuple-element.143), channel_id=1, source_target_pairs={{0,16},{8,24},{16,0},{24,8},{1,17},{9,25},{17,1},{25,9},{2,18},{10... | collective-permute-start | bytes 884744 | tf_op jit(solution)/shard_map/ppermute | solution.py:113
  49.9 0.5 collective-permute-start.10
  50.5 11.6 %backward_attention.1 = (bf16[768,384]{1,0:T(8,128)(2,1)S(1)}, bf16[768,384]{1,0:T(8,128)(2,1)}, bf16[528,384]{1,0:T(8,128)(2,1)S(1)}, bf16[512,384]{1,0:T(8,128)(2,1)S(1)}, f32[16,384]{1,0:T(8,128)S(1)}) custom-call(s32[5]{0:T(128)S(1)} %stack.17.place, bf16[6,1024,512]{2,1,0:T(8,128)(2,1)} %get-tuple-element.82.expo, ...), custom_call_target="tpu_custom_call" | custom-call | flops 6442450944 | bytes 6291456 | tf_op jit(solution)/shard_map/backward_attention/pallas_call | solution.py:588
  62.1 2.1 %collective-permute-done.9 = bf16[384,384]{1,0:T(8,128)(2,1)} collective-permute-done((bf16[384,384]{1,0:T(8,128)(2,1)}, bf16[384,384]{1,0:T(8,128)(2,1)}, u32[]{:S(2)}, u32[]{:S(2)}) %collective-permute-start.9) | collective-permute-done | bytes 294944 | tf_op jit(solution)/shard_map/ppermute | solution.py:113
  64.2 0.5 collective-permute-start.11
  64.7 1.4 %add_convert_fusion.2 = bf16[384,384]{1,0:T(8,128)(2,1)S(1)} fusion(bf16[384,384]{1,0:T(8,128)(2,1)} %collective-permute-done.10, bf16[384,384]{1,0:T(8,128)(2,1)} %collective-permute-done.9, bf16[384,384]{1,0:T(8,128)(2,1)} %collective-permute-done.8, bf16[1536,384]{1,0:T(8,128)(2,1)} %copy-done.19, s32[]{:T(128)S(6)} %select_n.134), kind=kLoop, calls=%fused_computation.2 | loop fusion | flops 1179648 | bytes 1474564 | tf_op jit(solution)/shard_map/convert_element_type | solution.py:177
  66.1 0.5 collective-permute-done.11.received
  66.5 1.8 %finish_rows.1 = bf16[4,128,384]{2,1,0:T(8,128)(2,1)} custom-call(s32[5]{0:T(128)S(1)} %stack.17.place, bf16[512,384]{1,0:T(8,128)(2,1)S(1)} %constant_dynamic-update-slice_fusion.own, bf16[512,384]{1,0:T(8,128)(2,1)S(1)} %get-tuple-element.114.part, bf16[528,384]{1,0:T(8,128)(2,1)S(1)} %collective-permute-done.11.received, f32[8,384]{1,0:T(8,128)S(1)} %get-tuple-element.76.mod), custom_call_target="tpu_custom_call" | custom-call | tf_op jit(solution)/shard_map/finish_rows/pallas_call | solution.py:625
  68.4 4.6 %all-to-all-start.1 = ((bf16[4,128,384]{2,1,0:T(8,128)(2,1)}), bf16[4,128,384]{2,1,0:T(8,128)(2,1)S(1)}, u32[]{:S(2)}, u32[]{:S(2)}) async-start(bf16[4,128,384]{2,1,0:T(8,128)(2,1)} %finish_rows.1), calls=%async_computation.1 | async-start | bytes 786432 | tf_op jit(solution)/shard_map/all_to_all | solution.py:73
  72.9 1.2 add_convert_fusion.1
  74.2 1.6 %collective-permute-start.24 = (bf16[192,384]{1,0:T(8,128)(2,1)S(1)}, bf16[192,384]{1,0:T(8,128)(2,1)S(1)}, u32[]{:S(2)}, u32[]{:S(2)}) collective-permute-start(bf16[192,384]{1,0:T(8,128)(2,1)S(1)} %get-tuple-element.146), channel_id=1, source_target_pairs={{0,24},{8,16},{16,8},{24,0},{1,25},{9,17},{17,9},{25,1},{2,26},{10... | collective-permute-start | bytes 442376 | tf_op jit(solution)/shard_map/ppermute | solution.py:113
  75.8 1.2 collective-permute-start.23
  77.0 0.8 collective-permute-start.22
  77.8 2.1 %collective-permute-start.12 = (bf16[96,384]{1,0:T(8,128)(2,1)S(1)}, bf16[96,384]{1,0:T(8,128)(2,1)S(1)}, u32[]{:S(2)}, u32[]{:S(2)}) collective-permute-start(bf16[96,384]{1,0:T(8,128)(2,1)S(1)} %get-tuple-element.158), channel_id=1, source_target_pairs={{0,2},{1,3},{2,4},{3,5},{4,6},{5,7},{6,0},{7,1},{8,10},{9,11},{10,... | collective-permute-start | bytes 221192 | tf_op jit(solution)/shard_map/ppermute | solution.py:108
  79.9 2.4 %collective-permute-start.13 = (bf16[96,384]{1,0:T(8,128)(2,1)S(1)}, bf16[96,384]{1,0:T(8,128)(2,1)S(1)}, u32[]{:S(2)}, u32[]{:S(2)}) collective-permute-start(bf16[96,384]{1,0:T(8,128)(2,1)S(1)} %get-tuple-element.157), channel_id=1, source_target_pairs={{0,4},{1,5},{2,6},{3,7},{4,0},{5,1},{6,2},{7,3},{8,12},{9,13},{10,... | collective-permute-start | bytes 221192 | tf_op jit(solution)/shard_map/ppermute | solution.py:108
  82.2 3.5 %collective-permute-start.14 = (bf16[96,384]{1,0:T(8,128)(2,1)S(1)}, bf16[96,384]{1,0:T(8,128)(2,1)S(1)}, u32[]{:S(2)}, u32[]{:S(2)}) collective-permute-start(bf16[96,384]{1,0:T(8,128)(2,1)S(1)} %get-tuple-element.156), channel_id=1, source_target_pairs={{0,6},{1,7},{2,0},{3,1},{4,2},{5,3},{6,4},{7,5},{8,14},{9,15},{10,... | collective-permute-start | bytes 221192 | tf_op jit(solution)/shard_map/ppermute | solution.py:108
  85.9 0.6 collective-permute-done.12.refs_1_
  86.4 4.1 %collective-permute-done.13.refs_2_ = bf16[96,384]{1,0:T(8,128)(2,1)S(1)} collective-permute-done((bf16[96,384]{1,0:T(8,128)(2,1)S(1)}, bf16[96,384]{1,0:T(8,128)(2,1)S(1)}, u32[]{:S(2)}, u32[]{:S(2)}) %collective-permute-start.13) | collective-permute-done | bytes 73760 | tf_op jit(solution)/shard_map/ppermute | solution.py:108
  90.6 1.4 %collective-permute-start.16 = (bf16[112,384]{1,0:T(8,128)(2,1)S(1)}, bf16[112,384]{1,0:T(8,128)(2,1)S(1)}, u32[]{:S(2)}, u32[]{:S(2)}) collective-permute-start(bf16[112,384]{1,0:T(8,128)(2,1)S(1)} %line_total.1.refs_0_), channel_id=1, source_target_pairs={{0,2},{1,3},{2,4},{3,5},{4,6},{5,7},{6,0},{7,1},{8,10},{9,11},{10,... | collective-permute-start | bytes 258056 | tf_op jit(solution)/shard_map/ppermute | solution.py:108
  92.0 1.5 %collective-permute-start.17 = (bf16[112,384]{1,0:T(8,128)(2,1)S(1)}, bf16[112,384]{1,0:T(8,128)(2,1)S(1)}, u32[]{:S(2)}, u32[]{:S(2)}) collective-permute-start(bf16[112,384]{1,0:T(8,128)(2,1)S(1)} %line_total.1.refs_0_), channel_id=1, source_target_pairs={{0,4},{1,5},{2,6},{3,7},{4,0},{5,1},{6,2},{7,3},{8,12},{9,13},{10,... | collective-permute-start | bytes 258056 | tf_op jit(solution)/shard_map/ppermute | solution.py:108
  93.5 1.0 collective-permute-start.18
  94.5 1.1 collective-permute-start.25
  95.5 1.5 %collective-permute-start.26 = (bf16[48,384]{1,0:T(8,128)(2,1)S(1)}, bf16[48,384]{1,0:T(8,128)(2,1)S(1)}, u32[]{:S(2)}, u32[]{:S(2)}) collective-permute-start(bf16[48,384]{1,0:T(8,128)(2,1)S(1)} %get-tuple-element.161), channel_id=1, source_target_pairs={{0,4},{1,5},{2,6},{3,7},{4,0},{5,1},{6,2},{7,3},{8,12},{9,13},{10,... | collective-permute-start | bytes 110600 | tf_op jit(solution)/shard_map/ppermute | solution.py:108
  97.1 2.4 %collective-permute-start.27 = (bf16[48,384]{1,0:T(8,128)(2,1)S(1)}, bf16[48,384]{1,0:T(8,128)(2,1)S(1)}, u32[]{:S(2)}, u32[]{:S(2)}) collective-permute-start(bf16[48,384]{1,0:T(8,128)(2,1)S(1)} %get-tuple-element.160), channel_id=1, source_target_pairs={{0,6},{1,7},{2,0},{3,1},{4,2},{5,3},{6,4},{7,5},{8,14},{9,15},{10,... | collective-permute-start | bytes 110600 | tf_op jit(solution)/shard_map/ppermute | solution.py:108
  99.5 1.7 %collective-permute-done.17.refs_2_ = bf16[112,384]{1,0:T(8,128)(2,1)S(1)} collective-permute-done((bf16[112,384]{1,0:T(8,128)(2,1)S(1)}, bf16[112,384]{1,0:T(8,128)(2,1)S(1)}, u32[]{:S(2)}, u32[]{:S(2)}) %collective-permute-start.17) | collective-permute-done | bytes 86048 | tf_op jit(solution)/shard_map/ppermute | solution.py:108
  101.2 1.3 collective-permute-start.19
  102.5 0.8 collective-permute-start.20
  103.3 1.4 %collective-permute-start.21 = (bf16[400,384]{1,0:T(8,128)(2,1)S(1)}, bf16[400,384]{1,0:T(8,128)(2,1)}, u32[]{:S(2)}, u32[]{:S(2)}) collective-permute-start(bf16[400,384]{1,0:T(8,128)(2,1)S(1)} %line_join.1.refs_0_), channel_id=1, source_target_pairs={{0,24},{8,16},{16,8},{24,0},{1,25},{9,17},{17,9},{25,1},{2,26},{10... | collective-permute-start | bytes 921608 | tf_op jit(solution)/shard_map/ppermute | solution.py:113
  104.8 2.5 %collective-permute-start.28 = (bf16[48,384]{1,0:T(8,128)(2,1)S(1)}, bf16[48,384]{1,0:T(8,128)(2,1)S(1)}, u32[]{:S(2)}, u32[]{:S(2)}) collective-permute-start(bf16[48,384]{1,0:T(8,128)(2,1)S(1)} %add_convert_fusion.4), channel_id=1, source_target_pairs={{0,2},{1,3},{2,4},{3,5},{4,6},{5,7},{6,0},{7,1},{8,10},{9,11},{10,... | collective-permute-start | bytes 110600 | tf_op jit(solution)/shard_map/ppermute | solution.py:108
  107.4 1.2 collective-permute-start.29
  108.6 2.1 %collective-permute-done.28 = bf16[48,384]{1,0:T(8,128)(2,1)S(1)} collective-permute-done((bf16[48,384]{1,0:T(8,128)(2,1)S(1)}, bf16[48,384]{1,0:T(8,128)(2,1)S(1)}, u32[]{:S(2)}, u32[]{:S(2)}) %collective-permute-start.28) | collective-permute-done | bytes 36896 | tf_op jit(solution)/shard_map/ppermute | solution.py:108
  110.6 1.3 %collective-permute-start.30 = (bf16[48,384]{1,0:T(8,128)(2,1)S(1)}, bf16[48,384]{1,0:T(8,128)(2,1)S(1)}, u32[]{:S(2)}, u32[]{:S(2)}) collective-permute-start(bf16[48,384]{1,0:T(8,128)(2,1)S(1)} %add_convert_fusion.4), channel_id=1, source_target_pairs={{0,6},{1,7},{2,0},{3,1},{4,2},{5,3},{6,4},{7,5},{8,14},{9,15},{10,... | collective-permute-start | bytes 110600 | tf_op jit(solution)/shard_map/ppermute | solution.py:108
  112.2 2.4 %collective-permute-done.30 = bf16[48,384]{1,0:T(8,128)(2,1)S(1)} collective-permute-done((bf16[48,384]{1,0:T(8,128)(2,1)S(1)}, bf16[48,384]{1,0:T(8,128)(2,1)S(1)}, u32[]{:S(2)}, u32[]{:S(2)}) %collective-permute-start.30) | collective-permute-done | bytes 36896 | tf_op jit(solution)/shard_map/ppermute | solution.py:108
  114.7 0.5 collective-permute-start.32
  115.3 0.4 collective-permute-start.34
  115.7 1.3 collective-permute-start.35
  117.0 0.8 collective-permute-start.36
  117.8 1.4 %collective-permute-start.37 = (bf16[192,384]{1,0:T(8,128)(2,1)S(1)}, bf16[192,384]{1,0:T(8,128)(2,1)S(1)}, u32[]{:S(2)}, u32[]{:S(2)}) collective-permute-start(bf16[192,384]{1,0:T(8,128)(2,1)S(1)} %pad_maximum_fusion.1.refs_0_), channel_id=1, source_target_pairs={{0,24},{8,16},{16,8},{24,0},{1,25},{9,17},{17,9},{25,1},{2,26},{10... | collective-permute-start | bytes 442376 | tf_op jit(solution)/shard_map/ppermute | solution.py:113
  119.3 6.0 %first_sums.1 = (f32[1536,384]{1,0:T(8,128)}, f32[384,1536]{1,0:T(8,128)}, f32[384,2304]{1,0:T(8,128)}, bf16[4,128,384]{2,1,0:T(8,128)(2,1)}, f32[4,128,384]{2,1...) custom-call(s32[5]{0:T(128)S(1)} %stack.17.place, ...), custom_call_target="tpu_custom_call" | custom-call | tf_op jit(solution)/shard_map/first_sums/pallas_call | solution.py:769
  125.3 0.4 collective-permute-done.37.refs_3_
  125.7 0.5 collective-permute-start.39
  126.2 0.5 collective-permute-start.41
  127.8 3.0 %second_sums.1 = (f32[384,1152]{1,0:T(8,128)}, f32[384,384]{1,0:T(8,128)}) custom-call(s32[5]{0:T(128)S(1)} %stack.17.place, bf16[192,384]{1,0:T(8,128)(2,1)S(1)} %pad_maximum_fusion.1.refs_0_, bf16[192,384]{1,0:T(8,128)(2,1)S(1)} %collective-permute-done.35.refs_1_, bf16[192,384]{1,0:T(8,128)(2,1)S(1)} %collective-permute-done.36.refs_2_, ...), custom_call_target="tpu_custom_call" | custom-call | tf_op jit(solution)/shard_map/second_sums/pallas_call | solution.py:823
  (98 shorter events, 2.4 us)
Async XLA Ops:
  0.6 11.8 %copy-start.2 = (bf16[384,1152]{1,0:T(8,128)(2,1)S(1)}, bf16[384,1152]{1,0:T(8,128)(2,1)}, u32[]{:S(2)}) copy-start(bf16[384,1152]{1,0:T(8,128)(2,1)} %attend_weight.1) | copy-start | bytes 2654212
  1.9 14.3 %collective-permute-start = (bf16[128,384]{1,0:T(8,128)(2,1)S(1)}, bf16[128,384]{1,0:T(8,128)(2,1)S(1)}, u32[]{:S(2)}, u32[]{:S(2)}) collective-permute-start(bf16[128,384]{1,0:T(8,128)(2,1)S(1)} %get-tuple-element.153), channel_id=1, source_target_pairs={{0,2},{1,3},{2,4},{3,5},{4,6},{5,7},{6,0},{7,1},{8,10},{9,11},{10,... | collective-permute-start | bytes 294920 | tf_op jit(solution)/shard_map/ppermute | solution.py:65
  5.0 11.3 %collective-permute-start.1 = (bf16[128,384]{1,0:T(8,128)(2,1)S(1)}, bf16[128,384]{1,0:T(8,128)(2,1)S(1)}, u32[]{:S(2)}, u32[]{:S(2)}) collective-permute-start(bf16[128,384]{1,0:T(8,128)(2,1)S(1)} %get-tuple-element.155), channel_id=1, source_target_pairs={{0,4},{1,5},{2,6},{3,7},{4,0},{5,1},{6,2},{7,3},{8,12},{9,13},{10,... | collective-permute-start | bytes 294920 | tf_op jit(solution)/shard_map/ppermute | solution.py:65
  7.6 8.7 %collective-permute-start.2 = (bf16[128,384]{1,0:T(8,128)(2,1)S(1)}, bf16[128,384]{1,0:T(8,128)(2,1)S(1)}, u32[]{:S(2)}, u32[]{:S(2)}) collective-permute-start(bf16[128,384]{1,0:T(8,128)(2,1)S(1)} %get-tuple-element.152), channel_id=1, source_target_pairs={{0,6},{1,7},{2,0},{3,1},{4,2},{5,3},{6,4},{7,5},{8,14},{9,15},{10,... | collective-permute-start | bytes 294920 | tf_op jit(solution)/shard_map/ppermute | solution.py:65
  12.4 1.5 %copy-start = (bf16[384,2304]{1,0:T(8,128)(2,1)S(1)}, bf16[384,2304]{1,0:T(8,128)(2,1)}, u32[]{:S(2)}) copy-start(bf16[384,2304]{1,0:T(8,128)(2,1)} %refs_8_.1) | copy-start | bytes 5308420
  13.9 0.7 copy-start.3
  15.3 1.2 copy-start.20
  16.2 14.6 %copy-start.7 = (bf16[1152,384]{1,0:T(8,128)(2,1)}, bf16[1152,384]{1,0:T(8,128)(2,1)S(1)}, u32[]{:S(2)}) copy-start(bf16[1152,384]{1,0:T(8,128)(2,1)S(1)} %get-tuple-element.81.weight) | copy-start | bytes 2654212
  16.2 4.2 %copy-start.10 = (s32[1,4,1024]{2,1,0:T(4,128)S(1)}, s32[1,4,1024]{2,1,0:T(4,128)}, u32[]{:S(2)}) copy-start(s32[1,4,1024]{2,1,0:T(4,128)} %param.19) | copy-start | bytes 49156
  16.2 4.2 %copy-start.11 = (s32[1,4,8]{2,1,0:T(4,128)S(1)}, s32[1,4,8]{2,1,0:T(4,128)}, u32[]{:S(2)}) copy-start(s32[1,4,8]{2,1,0:T(4,128)} %param.18) | copy-start | bytes 388
  16.4 4.0 %collective-permute-start.3 = (bf16[512,384]{1,0:T(8,128)(2,1)S(1)}, bf16[512,384]{1,0:T(8,128)(2,1)S(1)}, u32[]{:S(2)}, u32[]{:S(2)}) collective-permute-start(bf16[512,384]{1,0:T(8,128)(2,1)S(1)} %constant_dynamic-update-slice_fusion.own), channel_id=1, source_target_pairs={{0,1},{1,0},{2,3},{3,2},{4,5},{5,4},{6,7},{7,6},{8,9},{9,8},{10,11... | collective-permute-start | bytes 1179656 | tf_op jit(solution)/shard_map/ppermute | solution.py:79
  16.5 14.3 %collective-permute-start.4 = (bf16[128,384]{1,0:T(8,128)(2,1)S(1)}, bf16[128,384]{1,0:T(8,128)(2,1)S(1)}, u32[]{:S(2)}, u32[]{:S(2)}) collective-permute-start(bf16[128,384]{1,0:T(8,128)(2,1)S(1)} %get-tuple-element.150), channel_id=1, source_target_pairs={{0,2},{1,3},{2,4},{3,5},{4,6},{5,7},{6,0},{7,1},{8,10},{9,11},{10,... | collective-permute-start | bytes 294920 | tf_op jit(solution)/shard_map/ppermute | solution.py:65
  17.2 13.6 %collective-permute-start.5 = (bf16[128,384]{1,0:T(8,128)(2,1)S(1)}, bf16[128,384]{1,0:T(8,128)(2,1)S(1)}, u32[]{:S(2)}, u32[]{:S(2)}) collective-permute-start(bf16[128,384]{1,0:T(8,128)(2,1)S(1)} %get-tuple-element.149), channel_id=1, source_target_pairs={{0,4},{1,5},{2,6},{3,7},{4,0},{5,1},{6,2},{7,3},{8,12},{9,13},{10,... | collective-permute-start | bytes 294920 | tf_op jit(solution)/shard_map/ppermute | solution.py:65
  18.6 12.2 %collective-permute-start.6 = (bf16[128,384]{1,0:T(8,128)(2,1)S(1)}, bf16[128,384]{1,0:T(8,128)(2,1)S(1)}, u32[]{:S(2)}, u32[]{:S(2)}) collective-permute-start(bf16[128,384]{1,0:T(8,128)(2,1)S(1)} %get-tuple-element.148), channel_id=1, source_target_pairs={{0,6},{1,7},{2,0},{3,1},{4,2},{5,3},{6,4},{7,5},{8,14},{9,15},{10,... | collective-permute-start | bytes 294920 | tf_op jit(solution)/shard_map/ppermute | solution.py:65
  20.4 10.5 %copy-start.5 = (bf16[384,1536]{1,0:T(8,128)(2,1)S(1)}, bf16[384,1536]{1,0:T(8,128)(2,1)}, u32[]{:S(2)}) copy-start(bf16[384,1536]{1,0:T(8,128)(2,1)} %expand_weight.1) | copy-start | bytes 3538948
  20.4 10.5 %copy-start.6 = (bf16[1536,384]{1,0:T(8,128)(2,1)S(1)}, bf16[1536,384]{1,0:T(8,128)(2,1)}, u32[]{:S(2)}) copy-start(bf16[1536,384]{1,0:T(8,128)(2,1)} %shrink_weight.1) | copy-start | bytes 3538948
  20.4 10.5 %copy-start.9 = (bf16[384,384]{1,0:T(8,128)(2,1)S(1)}, bf16[384,384]{1,0:T(8,128)(2,1)}, u32[]{:S(2)}) copy-start(bf16[384,384]{1,0:T(8,128)(2,1)} %output_weight.1) | copy-start | bytes 884740
  30.8 9.6 %copy-start.12 = (bf16[768,1024]{1,0:T(8,128)(2,1)}, bf16[768,1024]{1,0:T(8,128)(2,1)S(1)}, u32[]{:S(2)}) copy-start(bf16[768,1024]{1,0:T(8,128)(2,1)S(1)} %get-tuple-element.84.key_value) | copy-start | bytes 4718596
  30.8 9.6 %copy-start.14 = (f32[384,512]{1,0:T(8,128)}, f32[384,512]{1,0:T(8,128)S(1)}, u32[]{:S(2)}) copy-start(f32[384,512]{1,0:T(8,128)S(1)} %get-tuple-element.85.attended_wide) | copy-start | bytes 2359300
  40.4 3.8 %collective-permute-start.7 = (bf16[1536,384]{1,0:T(8,128)(2,1)}, bf16[1536,384]{1,0:T(8,128)(2,1)}, u32[]{:S(2)}, u32[]{:S(2)}) collective-permute-start(bf16[1536,384]{1,0:T(8,128)(2,1)} %get-tuple-element.95), channel_id=1, source_target_pairs={{0,1},{1,0},{2,3},{3,2},{4,5},{5,4},{6,7},{7,6},{8,9},{9,8},{10,11... | collective-permute-start | bytes 3538952 | tf_op jit(solution)/shard_map/ppermute | solution.py:99
  40.5 21.5 %all-to-all-start = ((bf16[4,128,384]{2,1,0:T(8,128)(2,1)}), bf16[4,128,384]{2,1,0:T(8,128)(2,1)S(1)}, u32[]{:S(2)}, u32[]{:S(2)}) async-start(bf16[4,128,384]{2,1,0:T(8,128)(2,1)} %get-tuple-element.105), calls=%async_computation | async-start | bytes 786432 | tf_op jit(solution)/shard_map/all_to_all | solution.py:73
  44.2 6.2 %copy-start.13 = (bf16[768,1024]{1,0:T(8,128)(2,1)S(1)}, bf16[768,1024]{1,0:T(8,128)(2,1)}, u32[]{:S(2)}) copy-start(bf16[768,1024]{1,0:T(8,128)(2,1)} %copy-done.12) | copy-start | bytes 4718596
  44.2 6.2 %copy-start.16 = (f32[512,384]{1,0:T(8,128)S(1)}, f32[512,384]{1,0:T(8,128)}, u32[]{:S(2)}) copy-start(f32[512,384]{1,0:T(8,128)} %get-tuple-element.98.grad_residual) | copy-start | bytes 2359300
  44.2 6.2 %copy-start.17 = (bf16[384,512]{1,0:T(8,128)(2,1)S(1)}, bf16[384,512]{1,0:T(8,128)(2,1)}, u32[]{:S(2)}) copy-start(bf16[384,512]{1,0:T(8,128)(2,1)} %get-tuple-element.96.grad_attended) | copy-start | bytes 1179652
  44.2 6.2 %copy-start.18 = (bf16[384,384]{1,0:T(8,128)(2,1)S(1)}, bf16[384,384]{1,0:T(8,128)(2,1)}, u32[]{:S(2)}) copy-start(bf16[384,384]{1,0:T(8,128)(2,1)} %get-tuple-element.97.packed_output) | copy-start | bytes 884740
  46.0 4.5 %copy-start.19 = (bf16[1536,384]{1,0:T(8,128)(2,1)}, bf16[1536,384]{1,0:T(8,128)(2,1)S(1)}, u32[]{:S(2)}) copy-start(bf16[1536,384]{1,0:T(8,128)(2,1)S(1)} %add_convert_fusion) | copy-start | bytes 3538948
  46.0 4.5 %copy-start.8 = (bf16[1152,384]{1,0:T(8,128)(2,1)S(1)}, bf16[1152,384]{1,0:T(8,128)(2,1)}, u32[]{:S(2)}) copy-start(bf16[1152,384]{1,0:T(8,128)(2,1)} %copy-done.7) | copy-start | bytes 2654212
  46.0 4.5 %copy-start.15 = (f32[384,512]{1,0:T(8,128)S(1)}, f32[384,512]{1,0:T(8,128)}, u32[]{:S(2)}) copy-start(f32[384,512]{1,0:T(8,128)} %copy-done.14) | copy-start | bytes 2359300
  46.9 15.1 %collective-permute-start.8 = (bf16[384,384]{1,0:T(8,128)(2,1)}, bf16[384,384]{1,0:T(8,128)(2,1)}, u32[]{:S(2)}, u32[]{:S(2)}) collective-permute-start(bf16[384,384]{1,0:T(8,128)(2,1)} %get-tuple-element.144), channel_id=1, source_target_pairs={{0,8},{8,0},{16,24},{24,16},{1,9},{9,1},{17,25},{25,17},{2,10},{10... | collective-permute-start | bytes 884744 | tf_op jit(solution)/shard_map/ppermute | solution.py:113
  48.4 15.7 %collective-permute-start.9 = (bf16[384,384]{1,0:T(8,128)(2,1)}, bf16[384,384]{1,0:T(8,128)(2,1)}, u32[]{:S(2)}, u32[]{:S(2)}) collective-permute-start(bf16[384,384]{1,0:T(8,128)(2,1)} %get-tuple-element.143), channel_id=1, source_target_pairs={{0,16},{8,24},{16,0},{24,8},{1,17},{9,25},{17,1},{25,9},{2,18},{10... | collective-permute-start | bytes 884744 | tf_op jit(solution)/shard_map/ppermute | solution.py:113
  49.9 14.2 %collective-permute-start.10 = (bf16[384,384]{1,0:T(8,128)(2,1)S(1)}, bf16[384,384]{1,0:T(8,128)(2,1)}, u32[]{:S(2)}, u32[]{:S(2)}) collective-permute-start(bf16[384,384]{1,0:T(8,128)(2,1)S(1)} %get-tuple-element.142), channel_id=1, source_target_pairs={{0,24},{8,16},{16,8},{24,0},{1,25},{9,17},{17,9},{25,1},{2,26},{10... | collective-permute-start | bytes 884744 | tf_op jit(solution)/shard_map/ppermute | solution.py:113
  64.2 8.8 %collective-permute-start.15 = (bf16[768,384]{1,0:T(8,128)(2,1)}, bf16[768,384]{1,0:T(8,128)(2,1)}, u32[]{:S(2)}, u32[]{:S(2)}) collective-permute-start(bf16[768,384]{1,0:T(8,128)(2,1)} %get-tuple-element.109), channel_id=1, source_target_pairs={{0,1},{1,0},{2,3},{3,2},{4,5},{5,4},{6,7},{7,6},{8,9},{9,8},{10,11... | collective-permute-start | bytes 1769480 | tf_op jit(solution)/shard_map/ppermute | solution.py:99
  64.2 2.4 %collective-permute-start.11 = (bf16[528,384]{1,0:T(8,128)(2,1)S(1)}, bf16[528,384]{1,0:T(8,128)(2,1)S(1)}, u32[]{:S(2)}, u32[]{:S(2)}) collective-permute-start(bf16[528,384]{1,0:T(8,128)(2,1)S(1)} %get-tuple-element.107), channel_id=1, source_target_pairs={{0,1},{1,0},{2,3},{3,2},{4,5},{5,4},{6,7},{7,6},{8,9},{9,8},{10,11... | collective-permute-start | bytes 1216520 | tf_op jit(solution)/shard_map/ppermute | solution.py:99
  68.4 36.4 %all-to-all-start.1 = ((bf16[4,128,384]{2,1,0:T(8,128)(2,1)}), bf16[4,128,384]{2,1,0:T(8,128)(2,1)S(1)}, u32[]{:S(2)}, u32[]{:S(2)}) async-start(bf16[4,128,384]{2,1,0:T(8,128)(2,1)} %finish_rows.1), calls=%async_computation.1 | async-start | bytes 786432 | tf_op jit(solution)/shard_map/all_to_all | solution.py:73
  74.2 8.0 %collective-permute-start.24 = (bf16[192,384]{1,0:T(8,128)(2,1)S(1)}, bf16[192,384]{1,0:T(8,128)(2,1)S(1)}, u32[]{:S(2)}, u32[]{:S(2)}) collective-permute-start(bf16[192,384]{1,0:T(8,128)(2,1)S(1)} %get-tuple-element.146), channel_id=1, source_target_pairs={{0,24},{8,16},{16,8},{24,0},{1,25},{9,17},{17,9},{25,1},{2,26},{10... | collective-permute-start | bytes 442376 | tf_op jit(solution)/shard_map/ppermute | solution.py:113
  75.8 10.0 %collective-permute-start.23 = (bf16[192,384]{1,0:T(8,128)(2,1)S(1)}, bf16[192,384]{1,0:T(8,128)(2,1)S(1)}, u32[]{:S(2)}, u32[]{:S(2)}) collective-permute-start(bf16[192,384]{1,0:T(8,128)(2,1)S(1)} %get-tuple-element.147), channel_id=1, source_target_pairs={{0,16},{8,24},{16,0},{24,8},{1,17},{9,25},{17,1},{25,9},{2,18},{10... | collective-permute-start | bytes 442376 | tf_op jit(solution)/shard_map/ppermute | solution.py:113
  77.0 8.8 %collective-permute-start.22 = (bf16[192,384]{1,0:T(8,128)(2,1)S(1)}, bf16[192,384]{1,0:T(8,128)(2,1)S(1)}, u32[]{:S(2)}, u32[]{:S(2)}) collective-permute-start(bf16[192,384]{1,0:T(8,128)(2,1)S(1)} %get-tuple-element.145), channel_id=1, source_target_pairs={{0,8},{8,0},{16,24},{24,16},{1,9},{9,1},{17,25},{25,17},{2,10},{10... | collective-permute-start | bytes 442376 | tf_op jit(solution)/shard_map/ppermute | solution.py:113
  77.8 8.6 %collective-permute-start.12 = (bf16[96,384]{1,0:T(8,128)(2,1)S(1)}, bf16[96,384]{1,0:T(8,128)(2,1)S(1)}, u32[]{:S(2)}, u32[]{:S(2)}) collective-permute-start(bf16[96,384]{1,0:T(8,128)(2,1)S(1)} %get-tuple-element.158), channel_id=1, source_target_pairs={{0,2},{1,3},{2,4},{3,5},{4,6},{5,7},{6,0},{7,1},{8,10},{9,11},{10,... | collective-permute-start | bytes 221192 | tf_op jit(solution)/shard_map/ppermute | solution.py:108
  79.9 10.6 %collective-permute-start.13 = (bf16[96,384]{1,0:T(8,128)(2,1)S(1)}, bf16[96,384]{1,0:T(8,128)(2,1)S(1)}, u32[]{:S(2)}, u32[]{:S(2)}) collective-permute-start(bf16[96,384]{1,0:T(8,128)(2,1)S(1)} %get-tuple-element.157), channel_id=1, source_target_pairs={{0,4},{1,5},{2,6},{3,7},{4,0},{5,1},{6,2},{7,3},{8,12},{9,13},{10,... | collective-permute-start | bytes 221192 | tf_op jit(solution)/shard_map/ppermute | solution.py:108
  82.2 8.3 %collective-permute-start.14 = (bf16[96,384]{1,0:T(8,128)(2,1)S(1)}, bf16[96,384]{1,0:T(8,128)(2,1)S(1)}, u32[]{:S(2)}, u32[]{:S(2)}) collective-permute-start(bf16[96,384]{1,0:T(8,128)(2,1)S(1)} %get-tuple-element.156), channel_id=1, source_target_pairs={{0,6},{1,7},{2,0},{3,1},{4,2},{5,3},{6,4},{7,5},{8,14},{9,15},{10,... | collective-permute-start | bytes 221192 | tf_op jit(solution)/shard_map/ppermute | solution.py:108
  85.9 33.4 %copy-start.1 = (bf16[384,2304]{1,0:T(8,128)(2,1)S(1)}, bf16[384,2304]{1,0:T(8,128)(2,1)}, u32[]{:S(2)}) copy-start(bf16[384,2304]{1,0:T(8,128)(2,1)} %refs_8_.1) | copy-start | bytes 5308420
  90.6 6.5 %collective-permute-start.16 = (bf16[112,384]{1,0:T(8,128)(2,1)S(1)}, bf16[112,384]{1,0:T(8,128)(2,1)S(1)}, u32[]{:S(2)}, u32[]{:S(2)}) collective-permute-start(bf16[112,384]{1,0:T(8,128)(2,1)S(1)} %line_total.1.refs_0_), channel_id=1, source_target_pairs={{0,2},{1,3},{2,4},{3,5},{4,6},{5,7},{6,0},{7,1},{8,10},{9,11},{10,... | collective-permute-start | bytes 258056 | tf_op jit(solution)/shard_map/ppermute | solution.py:108
  92.0 9.2 %collective-permute-start.17 = (bf16[112,384]{1,0:T(8,128)(2,1)S(1)}, bf16[112,384]{1,0:T(8,128)(2,1)S(1)}, u32[]{:S(2)}, u32[]{:S(2)}) collective-permute-start(bf16[112,384]{1,0:T(8,128)(2,1)S(1)} %line_total.1.refs_0_), channel_id=1, source_target_pairs={{0,4},{1,5},{2,6},{3,7},{4,0},{5,1},{6,2},{7,3},{8,12},{9,13},{10,... | collective-permute-start | bytes 258056 | tf_op jit(solution)/shard_map/ppermute | solution.py:108
  93.5 7.7 %collective-permute-start.18 = (bf16[112,384]{1,0:T(8,128)(2,1)S(1)}, bf16[112,384]{1,0:T(8,128)(2,1)S(1)}, u32[]{:S(2)}, u32[]{:S(2)}) collective-permute-start(bf16[112,384]{1,0:T(8,128)(2,1)S(1)} %line_total.1.refs_0_), channel_id=1, source_target_pairs={{0,6},{1,7},{2,0},{3,1},{4,2},{5,3},{6,4},{7,5},{8,14},{9,15},{10,... | collective-permute-start | bytes 258056 | tf_op jit(solution)/shard_map/ppermute | solution.py:108
  94.5 8.9 %collective-permute-start.25 = (bf16[48,384]{1,0:T(8,128)(2,1)S(1)}, bf16[48,384]{1,0:T(8,128)(2,1)S(1)}, u32[]{:S(2)}, u32[]{:S(2)}) collective-permute-start(bf16[48,384]{1,0:T(8,128)(2,1)S(1)} %get-tuple-element.162), channel_id=1, source_target_pairs={{0,2},{1,3},{2,4},{3,5},{4,6},{5,7},{6,0},{7,1},{8,10},{9,11},{10,... | collective-permute-start | bytes 110600 | tf_op jit(solution)/shard_map/ppermute | solution.py:108
  95.5 9.2 %collective-permute-start.26 = (bf16[48,384]{1,0:T(8,128)(2,1)S(1)}, bf16[48,384]{1,0:T(8,128)(2,1)S(1)}, u32[]{:S(2)}, u32[]{:S(2)}) collective-permute-start(bf16[48,384]{1,0:T(8,128)(2,1)S(1)} %get-tuple-element.161), channel_id=1, source_target_pairs={{0,4},{1,5},{2,6},{3,7},{4,0},{5,1},{6,2},{7,3},{8,12},{9,13},{10,... | collective-permute-start | bytes 110600 | tf_op jit(solution)/shard_map/ppermute | solution.py:108
  97.1 7.7 %collective-permute-start.27 = (bf16[48,384]{1,0:T(8,128)(2,1)S(1)}, bf16[48,384]{1,0:T(8,128)(2,1)S(1)}, u32[]{:S(2)}, u32[]{:S(2)}) collective-permute-start(bf16[48,384]{1,0:T(8,128)(2,1)S(1)} %get-tuple-element.160), channel_id=1, source_target_pairs={{0,6},{1,7},{2,0},{3,1},{4,2},{5,3},{6,4},{7,5},{8,14},{9,15},{10,... | collective-permute-start | bytes 110600 | tf_op jit(solution)/shard_map/ppermute | solution.py:108
  101.2 13.4 %collective-permute-start.19 = (bf16[400,384]{1,0:T(8,128)(2,1)S(1)}, bf16[400,384]{1,0:T(8,128)(2,1)S(1)}, u32[]{:S(2)}, u32[]{:S(2)}) collective-permute-start(bf16[400,384]{1,0:T(8,128)(2,1)S(1)} %line_join.1.refs_0_), channel_id=1, source_target_pairs={{0,8},{8,0},{16,24},{24,16},{1,9},{9,1},{17,25},{25,17},{2,10},{10... | collective-permute-start | bytes 921608 | tf_op jit(solution)/shard_map/ppermute | solution.py:113
  102.5 12.1 %collective-permute-start.20 = (bf16[400,384]{1,0:T(8,128)(2,1)S(1)}, bf16[400,384]{1,0:T(8,128)(2,1)}, u32[]{:S(2)}, u32[]{:S(2)}) collective-permute-start(bf16[400,384]{1,0:T(8,128)(2,1)S(1)} %line_join.1.refs_0_), channel_id=1, source_target_pairs={{0,16},{8,24},{16,0},{24,8},{1,17},{9,25},{17,1},{25,9},{2,18},{10... | collective-permute-start | bytes 921608 | tf_op jit(solution)/shard_map/ppermute | solution.py:113
  103.3 11.3 %collective-permute-start.21 = (bf16[400,384]{1,0:T(8,128)(2,1)S(1)}, bf16[400,384]{1,0:T(8,128)(2,1)}, u32[]{:S(2)}, u32[]{:S(2)}) collective-permute-start(bf16[400,384]{1,0:T(8,128)(2,1)S(1)} %line_join.1.refs_0_), channel_id=1, source_target_pairs={{0,24},{8,16},{16,8},{24,0},{1,25},{9,17},{17,9},{25,1},{2,26},{10... | collective-permute-start | bytes 921608 | tf_op jit(solution)/shard_map/ppermute | solution.py:113
  104.8 5.8 %collective-permute-start.28 = (bf16[48,384]{1,0:T(8,128)(2,1)S(1)}, bf16[48,384]{1,0:T(8,128)(2,1)S(1)}, u32[]{:S(2)}, u32[]{:S(2)}) collective-permute-start(bf16[48,384]{1,0:T(8,128)(2,1)S(1)} %add_convert_fusion.4), channel_id=1, source_target_pairs={{0,2},{1,3},{2,4},{3,5},{4,6},{5,7},{6,0},{7,1},{8,10},{9,11},{10,... | collective-permute-start | bytes 110600 | tf_op jit(solution)/shard_map/ppermute | solution.py:108
  107.4 4.9 %collective-permute-start.29 = (bf16[48,384]{1,0:T(8,128)(2,1)S(1)}, bf16[48,384]{1,0:T(8,128)(2,1)S(1)}, u32[]{:S(2)}, u32[]{:S(2)}) collective-permute-start(bf16[48,384]{1,0:T(8,128)(2,1)S(1)} %add_convert_fusion.4), channel_id=1, source_target_pairs={{0,4},{1,5},{2,6},{3,7},{4,0},{5,1},{6,2},{7,3},{8,12},{9,13},{10,... | collective-permute-start | bytes 110600 | tf_op jit(solution)/shard_map/ppermute | solution.py:108
  110.6 4.0 %collective-permute-start.30 = (bf16[48,384]{1,0:T(8,128)(2,1)S(1)}, bf16[48,384]{1,0:T(8,128)(2,1)S(1)}, u32[]{:S(2)}, u32[]{:S(2)}) collective-permute-start(bf16[48,384]{1,0:T(8,128)(2,1)S(1)} %add_convert_fusion.4), channel_id=1, source_target_pairs={{0,6},{1,7},{2,0},{3,1},{4,2},{5,3},{6,4},{7,5},{8,14},{9,15},{10,... | collective-permute-start | bytes 110600 | tf_op jit(solution)/shard_map/ppermute | solution.py:108
  114.6 2.4 %collective-permute-start.31 = (bf16[400,384]{1,0:T(8,128)(2,1)S(1)}, bf16[400,384]{1,0:T(8,128)(2,1)S(1)}, u32[]{:S(2)}, u32[]{:S(2)}) collective-permute-start(bf16[400,384]{1,0:T(8,128)(2,1)S(1)} %line_join.1.refs_0_), channel_id=1, source_target_pairs={{0,1},{1,0},{2,3},{3,2},{4,5},{5,4},{6,7},{7,6},{8,9},{9,8},{10,11... | collective-permute-start | bytes 921608 | tf_op jit(solution)/shard_map/ppermute | solution.py:99
  114.7 3.2 %collective-permute-start.32 = (bf16[400,384]{1,0:T(8,128)(2,1)S(1)}, bf16[400,384]{1,0:T(8,128)(2,1)S(1)}, u32[]{:S(2)}, u32[]{:S(2)}) collective-permute-start(bf16[400,384]{1,0:T(8,128)(2,1)S(1)} %collective-permute-done.19.refs_1_), channel_id=1, source_target_pairs={{0,1},{1,0},{2,3},{3,2},{4,5},{5,4},{6,7},{7,6},{8,9},{9,8},{10,11... | collective-permute-start | bytes 921608 | tf_op jit(solution)/shard_map/ppermute | solution.py:99
  115.2 4.1 %collective-permute-start.33 = (bf16[400,384]{1,0:T(8,128)(2,1)}, bf16[400,384]{1,0:T(8,128)(2,1)S(1)}, u32[]{:S(2)}, u32[]{:S(2)}) collective-permute-start(bf16[400,384]{1,0:T(8,128)(2,1)} %collective-permute-done.20.refs_2_), channel_id=1, source_target_pairs={{0,1},{1,0},{2,3},{3,2},{4,5},{5,4},{6,7},{7,6},{8,9},{9,8},{10,11... | collective-permute-start | bytes 921608 | tf_op jit(solution)/shard_map/ppermute | solution.py:99
  115.3 4.0 %collective-permute-start.34 = (bf16[400,384]{1,0:T(8,128)(2,1)}, bf16[400,384]{1,0:T(8,128)(2,1)S(1)}, u32[]{:S(2)}, u32[]{:S(2)}) collective-permute-start(bf16[400,384]{1,0:T(8,128)(2,1)} %collective-permute-done.21.refs_3_), channel_id=1, source_target_pairs={{0,1},{1,0},{2,3},{3,2},{4,5},{5,4},{6,7},{7,6},{8,9},{9,8},{10,11... | collective-permute-start | bytes 921608 | tf_op jit(solution)/shard_map/ppermute | solution.py:99
  115.7 9.6 %collective-permute-start.35 = (bf16[192,384]{1,0:T(8,128)(2,1)S(1)}, bf16[192,384]{1,0:T(8,128)(2,1)S(1)}, u32[]{:S(2)}, u32[]{:S(2)}) collective-permute-start(bf16[192,384]{1,0:T(8,128)(2,1)S(1)} %pad_maximum_fusion.1.refs_0_), channel_id=1, source_target_pairs={{0,8},{8,0},{16,24},{24,16},{1,9},{9,1},{17,25},{25,17},{2,10},{10... | collective-permute-start | bytes 442376 | tf_op jit(solution)/shard_map/ppermute | solution.py:113
  117.0 8.3 %collective-permute-start.36 = (bf16[192,384]{1,0:T(8,128)(2,1)S(1)}, bf16[192,384]{1,0:T(8,128)(2,1)S(1)}, u32[]{:S(2)}, u32[]{:S(2)}) collective-permute-start(bf16[192,384]{1,0:T(8,128)(2,1)S(1)} %pad_maximum_fusion.1.refs_0_), channel_id=1, source_target_pairs={{0,16},{8,24},{16,0},{24,8},{1,17},{9,25},{17,1},{25,9},{2,18},{10... | collective-permute-start | bytes 442376 | tf_op jit(solution)/shard_map/ppermute | solution.py:113
  117.8 7.9 %collective-permute-start.37 = (bf16[192,384]{1,0:T(8,128)(2,1)S(1)}, bf16[192,384]{1,0:T(8,128)(2,1)S(1)}, u32[]{:S(2)}, u32[]{:S(2)}) collective-permute-start(bf16[192,384]{1,0:T(8,128)(2,1)S(1)} %pad_maximum_fusion.1.refs_0_), channel_id=1, source_target_pairs={{0,24},{8,16},{16,8},{24,0},{1,25},{9,17},{17,9},{25,1},{2,26},{10... | collective-permute-start | bytes 442376 | tf_op jit(solution)/shard_map/ppermute | solution.py:113
  125.7 1.4 %collective-permute-start.38 = (bf16[192,384]{1,0:T(8,128)(2,1)S(1)}, bf16[192,384]{1,0:T(8,128)(2,1)S(1)}, u32[]{:S(2)}, u32[]{:S(2)}) collective-permute-start(bf16[192,384]{1,0:T(8,128)(2,1)S(1)} %pad_maximum_fusion.1.refs_0_), channel_id=1, source_target_pairs={{0,1},{1,0},{2,3},{3,2},{4,5},{5,4},{6,7},{7,6},{8,9},{9,8},{10,11... | collective-permute-start | bytes 442376 | tf_op jit(solution)/shard_map/ppermute | solution.py:99
  125.7 1.6 %collective-permute-start.39 = (bf16[192,384]{1,0:T(8,128)(2,1)S(1)}, bf16[192,384]{1,0:T(8,128)(2,1)S(1)}, u32[]{:S(2)}, u32[]{:S(2)}) collective-permute-start(bf16[192,384]{1,0:T(8,128)(2,1)S(1)} %collective-permute-done.35.refs_1_), channel_id=1, source_target_pairs={{0,1},{1,0},{2,3},{3,2},{4,5},{5,4},{6,7},{7,6},{8,9},{9,8},{10,11... | collective-permute-start | bytes 442376 | tf_op jit(solution)/shard_map/ppermute | solution.py:99
  126.2 1.4 %collective-permute-start.40 = (bf16[192,384]{1,0:T(8,128)(2,1)S(1)}, bf16[192,384]{1,0:T(8,128)(2,1)S(1)}, u32[]{:S(2)}, u32[]{:S(2)}) collective-permute-start(bf16[192,384]{1,0:T(8,128)(2,1)S(1)} %collective-permute-done.36.refs_2_), channel_id=1, source_target_pairs={{0,1},{1,0},{2,3},{3,2},{4,5},{5,4},{6,7},{7,6},{8,9},{9,8},{10,11... | collective-permute-start | bytes 442376 | tf_op jit(solution)/shard_map/ppermute | solution.py:99
  126.2 1.6 %collective-permute-start.41 = (bf16[192,384]{1,0:T(8,128)(2,1)S(1)}, bf16[192,384]{1,0:T(8,128)(2,1)S(1)}, u32[]{:S(2)}, u32[]{:S(2)}) collective-permute-start(bf16[192,384]{1,0:T(8,128)(2,1)S(1)} %collective-permute-done.37.refs_3_), channel_id=1, source_target_pairs={{0,1},{1,0},{2,3},{3,2},{4,5},{5,4},{6,7},{7,6},{8,9},{9,8},{10,11... | collective-permute-start | bytes 442376 | tf_op jit(solution)/shard_map/ppermute | solution.py:99
  (1 other events, 0.7 us)

commit v2 on v1

--- a/solution.py
+++ b/solution.py
@@ -51,8 +51,16 @@
     return result
 
 
-def owner_shift(seq_size, owners, share, step):
-    return [(d, ((d // share + step) % owners) * share + d % share) for d in range(seq_size)]
+def away(index, size, step):
+    return index ^ step if size & (size - 1) == 0 else (index + step) % size
+
+
+def back(index, size, step):
+    return index ^ step if size & (size - 1) == 0 else (index - step) % size
+
+
+def owner_pairs(seq_size, owners, share, step):
+    return [(d, away(d // share, owners, step) * share + d % share) for d in range(seq_size)]
 
 
 def rows_to_owner(blocks, owner, share):
@@ -60,11 +68,19 @@
     seq_size = lax.axis_size("seq")
     pieces = []
     for step in range(owners):
-        block = lax.dynamic_index_in_dim(blocks, (owner + step) % owners, 0, False)
+        block = lax.dynamic_index_in_dim(blocks, away(owner, owners, step), 0, False)
         if step:
-            block = lax.ppermute(block, "seq", owner_shift(seq_size, owners, share, step))
+            block = lax.ppermute(block, "seq", owner_pairs(seq_size, owners, share, step))
         pieces.append(block)
     return pieces
+
+
+def pieces_from_owner(pieces, share):
+    owners, seq_size = len(pieces), lax.axis_size("seq")
+    return [pieces[0]] + [
+        lax.ppermute(pieces[step], "seq", owner_pairs(seq_size, owners, share, step))
+        for step in range(1, owners)
+    ]
 
 
 def rows_from_owner(blocks, share):
@@ -105,26 +121,12 @@
 
 def line_send(values, step):
     seq_size = lax.axis_size("seq")
-    return lax.ppermute(values, "seq", [(d, (d + 2 * step) % seq_size) for d in range(seq_size)])
+    return lax.ppermute(values, "seq", owner_pairs(seq_size, seq_size // 2, 2, step))
 
 
 def plane_send(values, step):
     grp_size = lax.axis_size("grp")
-    return lax.ppermute(values, "grp", [(d, plane_at(d, step)) for d in range(grp_size)])
-
-
-def plane_at(group, step):
-    grp_size = lax.axis_size("grp")
-    if grp_size & (grp_size - 1) == 0:
-        return group ^ step
-    return (group + step) % grp_size
-
-
-def plane_back(group, other):
-    grp_size = lax.axis_size("grp")
-    if grp_size & (grp_size - 1) == 0:
-        return group ^ other
-    return (group - other) % grp_size
+    return lax.ppermute(values, "grp", [(d, away(d, grp_size, step)) for d in range(grp_size)])
 
 
 def rows_at(values, at, count):
@@ -139,7 +141,7 @@
     grp_size = lax.axis_size("grp")
     group = lax.axis_index("grp")
     count = values.shape[0] // grp_size
-    return [rows_at(values, plane_at(group, step), count) for step in range(grp_size)]
+    return [rows_at(values, away(group, grp_size, step), count) for step in range(grp_size)]
 
 
 def send_plane(parts):
@@ -154,7 +156,7 @@
     length = line_size()
     place = lax.axis_index("seq") // 2
     count = values.shape[0] // length
-    return [rows_at(values, (place + step) % length, count) for step in range(length)]
+    return [rows_at(values, away(place, length, step), count) for step in range(length)]
 
 
 def send_line(parts):
@@ -334,7 +336,7 @@
             return sum((positions >= end).astype(jnp.int32) for end in ends)
 
         def block_at(r, step):
-            return lax.rem(owner - step + owners, owners) * share + lax.rem(rank + r, share)
+            return back(owner, owners, step) * share + lax.rem(rank + r, share)
 
         lane = lax.broadcasted_iota(jnp.int32, (1, count), 1)
         query_pos = jnp.concatenate(
@@ -356,18 +358,20 @@
                 at = (r * owners + step) * count
                 bias[at : at + count, :] = jnp.where(allow, 0.0, MASKED)
 
-    for i in range(2):
-        first = pl.multiple_of((2 * pair + i) * head_width, head_width)
+    heads = [pl.multiple_of((2 * pair + i) * head_width, head_width) for i in range(2)]
+    scores = []
+    for first in heads:
         here = pl.ds(first, head_width)
         scaled = (query[here, :].astype(f32) * score_scale).astype(bf16)
-        scores = inner(key_value[here, :], scaled) + bias[...]
-        wide = jnp.exp(scores - jnp.max(scores, axis=0, keepdims=True))
+        scores.append(inner(key_value[here, :], scaled) + bias[...])
+    for i, first in enumerate(heads):
+        wide = jnp.exp(scores[i] - jnp.max(scores[i], axis=0, keepdims=True))
         inverse = 1.0 / column_sum(wide)
         low = wide.astype(bf16)
         expo[i] = low
         inverse_total[i] = inverse
         values = key_value[pl.ds(pl.multiple_of(width + first, head_width), head_width), :]
-        attended_wide[here, :] = product(values, low) * inverse
+        attended_wide[pl.ds(first, head_width), :] = product(values, low) * inverse
 
     @pl.when(pair == pl.num_programs(0) - 1)
     def _():
@@ -450,7 +454,7 @@
     result = (residual + row(GATE_TWO) * branch_two).astype(bf16)
     owners, count = output.shape[:2]
     for step in range(owners):
-        output[lax.rem(place[0] - step + owners, owners)] = result[step * count : (step + 1) * count, :]
+        output[back(place[0], owners, step)] = result[step * count : (step + 1) * count, :]
     sums[5:6, :] = column_sum(wide * branch_two) * share
     sums[7 + blocks : 8 + blocks, :] = column_sum(grad_two.astype(f32)) * share
     sums[4:5, :] = column_sum(grad_mixed * normed) * share
@@ -608,41 +612,47 @@
     )(place, pltpu.with_memory_space_constraint(expo, pltpu.HBM), *operands)
 
 
-def finish_kernel(place, own, part, received, mod, result):
+def finish_kernel(owners, own, part, received, mod, *refs):
+    parts, results = refs[:-owners], refs[-owners:]
     rows, width = own.shape
-    owners, count = result.shape[:2]
+    count = rows // owners
     normed, inverse = normalize(own[...].astype(f32))
     grad = received[:rows, :].astype(f32) * (1.0 + mod[SCALE_ONE : SCALE_ONE + 1, :])
     grad = (part[...].astype(f32) + normalize_back(grad, normed, inverse)).astype(bf16)
-    for step in range(owners):
-        at = lax.rem(place[0] - step + owners, owners)
-        result[at] = grad[step * count : (step + 1) * count, :]
-
-
-def finish_rows(owners, place, own, part, received, mod):
-    operands = (own, part, received, mod)
-    shape = (owners, own.shape[0] // owners, own.shape[1])
+    for step, result in enumerate(results):
+        result[:count, :] = grad[step * count : (step + 1) * count, :]
+    if parts:
+        summed = total([ref[...] for ref in parts]).astype(bf16)
+        for result in results:
+            result[count:, :] = summed
+
+
+def finish_rows(owners, own, part, received, mod, parts):
+    operands = [own, part, received, mod] + parts
+    shape = (own.shape[0] // owners + (parts[0].shape[0] if parts else 0), own.shape[1])
     return pl.pallas_call(
-        finish_kernel,
+        partial(finish_kernel, owners),
         grid=(1,),
-        in_specs=[pl.BlockSpec(memory_space=pltpu.SMEM)] + [whole(*item.shape) for item in operands],
-        out_specs=whole(*shape),
-        out_shape=jax.ShapeDtypeStruct(shape, bf16),
+        in_specs=[whole(*item.shape) for item in operands],
+        out_specs=[whole(*shape)] * owners,
+        out_shape=[jax.ShapeDtypeStruct(shape, bf16)] * owners,
         compiler_params=kernel_params(12),
         name="finish_rows",
-    )(place, *operands)
+    )(*operands)
 
 
 def line_total_kernel(sums, received, *refs):
     parts, result = refs[:-1], refs[-1]
-    count = parts[0].shape[0]
+    count = parts[0].shape[-2]
+    if len(parts[0].shape) == 3:
+        parts = [parts[0].at[at] for at in range(parts[0].shape[0])]
     result[:count, :] = total([part[...] for part in parts]).astype(bf16)
     below = received[received.shape[0] - sums.shape[0] :, :].astype(f32)
     result[count:, :] = (sums[...] + below).astype(bf16)
 
 
 def line_total(parts, sums, received):
-    count, width = parts[0].shape
+    count, width = parts[0].shape[-2:]
     below = sums.shape[0]
     return pl.pallas_call(
         line_total_kernel,
@@ -688,7 +698,7 @@
 def picked(place, grp_size, own, received, side, b, write):
     group = place[3]
     for step in range(grp_size):
-        here = (group ^ b if grp_size & (grp_size - 1) == 0 else lax.rem(group - b + grp_size, grp_size)) == step
+        here = back(group, grp_size, b) == step
         for ref, mine in ((own[step], True), (received[step], False)):
 
             @pl.when(here & ((place[2] == side) == mine))
@@ -698,22 +708,29 @@
 
 def copy_line(place, line, count, ref, output, first):
     for c in range(line):
-        from_c = lax.rem(place[4] - c + line, line)
-        here = pl.ds(pl.multiple_of(from_c * count, count), count)
+        from_c = back(place[4], line, c) if line > 1 else 0
+        here = pl.ds(pl.multiple_of(from_c * count, count), count) if line > 1 else slice(0, count)
         output[first + c * count : first + (c + 1) * count, :] = ref[here, :].astype(f32)
 
 
 def first_sums_kernel(grp_size, line, place, *refs):
     own, received = refs[:grp_size], refs[grp_size : 2 * grp_size]
     refs = refs[2 * grp_size :]
-    weight, output, blocks = refs[:3]
-    shrink, expand, grad_weight, copied, rows, table, grad_bias = refs[3:10]
-    output_bias, expand_bias, shrink_bias, grad_lifted, sums = refs[10:]
+    weight, output = refs[:2]
+    owners = len(refs) - 14
+    pieces, refs = refs[2 : 2 + owners], refs[2 + owners :]
+    shrink, expand, grad_weight, copied, rows, table, grad_bias = refs[:7]
+    output_bias, expand_bias, shrink_bias, grad_lifted, sums = refs[7:]
     b = pl.program_id(0)
     width = table.shape[1]
     count = own[0].shape[0] - 16
     copied[...] = output[...]
-    rows[...] = blocks[...].astype(f32)
+    for step, piece in enumerate(pieces):
+
+        @pl.when(back(place[0], owners, step) == b)
+        def _():
+            rows[0] = piece[: rows.shape[1], :].astype(f32)
+
     for side, target in enumerate((shrink, expand)):
         write = lambda ref: copy_line(place, line, count // line, ref, target, 0)
         picked(place, grp_size, own, received, side, b, write)
@@ -757,21 +774,21 @@
         )
 
 
-def first_sums(place, own, weight, output, blocks):
+def first_sums(place, own, weight, output, pieces):
     grp_size = len(own)
     line = 1 if line_size() > 4 else line_size()
     received = [swap_cores(part) for part in own]
     width = weight.shape[0]
     hidden = grp_size * width
-    owners = blocks.shape[0]
-    block = pl.BlockSpec((owners // grp_size,) + blocks.shape[1:], lambda b: (b, 0, 0))
+    block = pl.BlockSpec((1,) + output.shape[1:], lambda b: (b, 0, 0))
     wide = pl.BlockSpec((width, 2 * width), lambda b: (0, jnp.minimum(b, 2)))
     return pl.pallas_call(
         partial(first_sums_kernel, grp_size, line),
         grid=(grp_size,),
         in_specs=[pl.BlockSpec(memory_space=pltpu.SMEM)]
         + [whole(*own[0].shape)] * (2 * grp_size)
-        + [wide, block, block],
+        + [wide, block]
+        + [whole(*item.shape) for item in pieces],
         out_specs=[
             pl.BlockSpec((width, width), lambda b: (b, 0)),
             pl.BlockSpec((width, width), lambda b: (0, b)),
@@ -789,7 +806,7 @@
             jax.ShapeDtypeStruct((width, hidden), f32),
             jax.ShapeDtypeStruct(weight.shape, f32),
             jax.ShapeDtypeStruct(output.shape, output.dtype),
-            jax.ShapeDtypeStruct(blocks.shape, f32),
+            jax.ShapeDtypeStruct(output.shape, f32),
             jax.ShapeDtypeStruct((LEADS, width), f32),
             jax.ShapeDtypeStruct((6 * width,), f32),
             jax.ShapeDtypeStruct((width,), f32),
@@ -799,7 +816,7 @@
         scratch_shapes=[pltpu.VMEM((8, width), f32), pltpu.VMEM((16, width), f32)],
         compiler_params=kernel_params(20),
         name="first_sums",
-    )(place, *own, *received, weight, output, blocks)
+    )(place, *own, *received, weight, output, *pieces)
 
 
 def second_sums_kernel(grp_size, line, place, *refs):
@@ -843,7 +860,7 @@
     count = rows // owners
     steps = jnp.arange(owners, dtype=jnp.int32)
     ranks = (rank + jnp.arange(share, dtype=jnp.int32)) % share
-    blocks = (((owner - steps) % owners)[None, :] * share + ranks[:, None]).reshape(-1, 1)
+    blocks = (back(owner, owners, steps)[None, :] * share + ranks[:, None]).reshape(-1, 1)
     key_pos = blocks * count + jnp.arange(count, dtype=jnp.int32)[None, :]
     doc_ends = jnp.cumsum(lax.dynamic_index_in_dim(lengths, owner, 0, False))
     key_seg = sum((key_pos >= doc_ends[doc]).astype(jnp.int32) for doc in range(doc_ends.shape[0]))
@@ -975,35 +992,36 @@
     ff_plane = low_total(ff_parts)
     line = line_size() <= 4
     if line:
-        ff_parts = send_line(line_parts(ff_plane))
+        ff_parts = [line_exchange(ff_plane.reshape(line_size(), -1, width))]
     at_core = low_total([at_keep, swap_cores(at_send)])
     if share == 2:
         received = swap_cores(rest_part)
     else:
         received = return_rows(rest_part, rank, share)
     at_slices = plane_parts(at_core)
-    finished = finish_rows(owners, where, own_tokens, own_part, after(received, ff_plane), mod)
-    finished = rows_from_owner(finished, share)
     at_parts = send_plane(at_slices)
-    at_plane = low_total(at_parts)
     if line:
         ff_parts = list(after_all(ff_parts, *at_slices))
         ff_line = line_total(ff_parts, sums, received)
+        at_parts = after_all(at_parts, ff_line)
+    at_plane = low_total(at_parts)
+    if line:
         ff_pieces = send_line([ff_line] * line_size())
         ff_plane = line_join(lead_index, mod, ff_pieces)
-        at_line = low_total(after_all(send_line(line_parts(at_plane)), finished))
-        at_pieces = send_line([at_line] * line_size())
+        at_line = send_line(line_parts(at_plane))
     else:
         vector = with_lead(lax.psum(sums, "seq"), lead_index[0], mod)
         ff_pieces = [sum_line(ff_plane)]
         ff_plane = jnp.concatenate(ff_pieces + [vector])
-        at_line = sum_line(at_plane)
-        at_pieces = [at_line]
+        at_line = []
+    pieces = finish_rows(owners, own_tokens, own_part, received, mod, at_line)
+    pieces = pieces_from_owner(pieces, share)
+    at_pieces = [piece[block_rows:] for piece in pieces] if line else [sum_line(at_plane)]
     ff_parts = gather_plane(ff_plane)
     at_parts = gather_plane(jnp.concatenate(at_pieces))
-    ff_parts = list(after_all(ff_parts, *at_pieces))
+    ff_parts = list(after_all(ff_parts, *pieces))
     grad_shrink, grad_expand, grad_mod_weight, output, grad_tokens, grad_table, grad_mod_bias, *biases = (
-        first_sums(where, ff_parts, modulation_weight, output, finished)
+        first_sums(where, ff_parts, modulation_weight, output, pieces)
     )
     at_parts = list(after_all(at_parts, grad_shrink))
     grad_attend, grad_output = second_sums(where, at_parts)

time: 132 us -> 126 us (0.955)
  starting transfers between devices: 57.9 us -> 50.8 us
  waiting for transfers between devices: 15.2 us -> 19.4 us
  Pallas kernels: 43.3 us -> 40.3 us
    ppermute x30 -> x27, starting transfers between devices: 46.9 us -> 38.4 us  [the longest x12 14.1 us: plane_send(): lax.ppermute(values, 'grp', [(d, away(d, grp_size, step)) for d in range(...]
    all_to_all x0 -> x1, waiting for transfers between devices: none -> 4.93 us  [line_exchange(): return lax.all_to_all(values, 'seq', 0, 0, axis_index_groups=groups)]
    all_to_all x0 -> x1, starting transfers between devices: none -> 4.8 us  [line_exchange(): return lax.all_to_all(values, 'seq', 0, 0, axis_index_groups=groups)]
    all_to_all x2 -> x1, starting transfers between devices: 8.22 us -> 4.76 us  [rows_from_owner(): return lax.all_to_all(blocks, 'seq', 0, 0, axis_index_groups=groups)]
    convert_element_type x5 -> x4, other arithmetic: 4.42 us -> 5.1 us  [low_total(): return total(parts).astype(bf16)]
    ppermute x30 -> x27, waiting for transfers between devices: 13.6 us -> 13.4 us  [the longest x3 8.22 us: pieces_from_owner(): lax.ppermute(pieces[step], 'seq', owner_pairs(seq_size, owners, share, st...]
    unnamed x45 -> x53, local copies, waits for them, and re-layouts: 2.97 us -> 2.99 us
  transfers between devices with their start and end apart: 44 -> 41, of which waited for: 14 -> 12; matrix products, arithmetic and copies ran while one was open for 6% -> 7% of each run, Pallas kernels for 24% -> 22%
where the time goes in v2:
time: 126 us
  starting transfers between devices  50.8 us (40%)
  Pallas kernels  40.3 us (32%)
  waiting for transfers between devices  19.4 us (15%)
  local copies, waits for them, and re-layouts  8.1 us (6%)
  other arithmetic  5.19 us (4%)
  between operations  1.88 us (1%)
    ppermute x12, starting transfers between devices, plane_send(): lax.ppermute(values, 'grp', [(d, away(d, grp_size, step)) for d in range(...  14.1 us
    pallas_call x1, Pallas kernels, backward_attention(): pl.pallas_call(partial(backward_kernel, head_width, 1.0 / math.sqrt(head_...  10.8 us
    ppermute x6, starting transfers between devices, rows_to_owner(): lax.ppermute(block, 'seq', owner_pairs(seq_size, owners, share, step))  10.1 us
    pallas_call x1, Pallas kernels, forward_attention(): pl.pallas_call(partial(forward_kernel, head_width, 1.0 / math.sqrt(head_w...  9.94 us
    pallas_call x1, Pallas kernels, middle(): pl.pallas_call(middle_kernel, grid=(1,), in_specs=[pl.BlockSpec(memory_sp...  9.53 us
    ppermute x6, starting transfers between devices, line_send(): lax.ppermute(values, 'seq', owner_pairs(seq_size, seq_size // 2, 2, step))  8.89 us
    ppermute x3, waiting for transfers between devices, pieces_from_owner(): lax.ppermute(pieces[step], 'seq', owner_pairs(seq_size, owners, share, st...  8.22 us
    pallas_call x1, Pallas kernels, first_sums(): pl.pallas_call(partial(first_sums_kernel, grp_size, line), grid=(grp_size...  5.51 us
  transfers between devices with their start and end apart: 41, of which 12 were waited for; matrix products, arithmetic and copies ran while one was open for 7% of the time, Pallas kernels for 22%

profile of v2, /device:TPU:0, one launch (start us, length us, event | category | flops | bytes accessed | tf_op | source)
XLA Modules:
  0.0 125.6 jit_solution(9005880545586288739)
XLA Ops:
  0.7 1.2 dynamic-slice_bitcast_fusion.4
  1.8 3.1 %collective-permute-start = (bf16[128,384]{1,0:T(8,128)(2,1)S(1)}, bf16[128,384]{1,0:T(8,128)(2,1)S(1)}, u32[]{:S(2)}, u32[]{:S(2)}) collective-permute-start(bf16[128,384]{1,0:T(8,128)(2,1)S(1)} %get-tuple-element.152), channel_id=1, source_target_pairs={{0,2},{1,3},{2,0},{3,1},{4,6},{5,7},{6,4},{7,5},{8,10},{9,11},{10,... | collective-permute-start | bytes 294920 | tf_op jit(solution)/shard_map/ppermute | solution.py:73
  4.9 2.6 %collective-permute-start.1 = (bf16[128,384]{1,0:T(8,128)(2,1)S(1)}, bf16[128,384]{1,0:T(8,128)(2,1)S(1)}, u32[]{:S(2)}, u32[]{:S(2)}) collective-permute-start(bf16[128,384]{1,0:T(8,128)(2,1)S(1)} %get-tuple-element.154), channel_id=1, source_target_pairs={{0,4},{1,5},{2,6},{3,7},{4,0},{5,1},{6,2},{7,3},{8,12},{9,13},{10,... | collective-permute-start | bytes 294920 | tf_op jit(solution)/shard_map/ppermute | solution.py:73
  7.5 0.7 concatenate.30
  8.2 0.7 concatenate.29
  8.9 0.7 concatenate.28
  9.6 0.7 concatenate.27
  11.0 0.1 stack.17.place
  11.1 1.5 %copy-done = bf16[384,2304]{1,0:T(8,128)(2,1)S(1)} copy-done((bf16[384,2304]{1,0:T(8,128)(2,1)S(1)}, bf16[384,2304]{1,0:T(8,128)(2,1)}, u32[]{:S(2)}) %copy-start) | copy-done | bytes 1769496
  12.5 0.7 copy-done.3
  13.2 0.7 copy-done.4
  13.9 0.9 prepare.1
  14.9 0.5 collective-permute-done.1
  15.6 1.7 %collective-permute-start.4 = (bf16[128,384]{1,0:T(8,128)(2,1)S(1)}, bf16[128,384]{1,0:T(8,128)(2,1)S(1)}, u32[]{:S(2)}, u32[]{:S(2)}) collective-permute-start(bf16[128,384]{1,0:T(8,128)(2,1)S(1)} %get-tuple-element.149), channel_id=1, source_target_pairs={{0,2},{1,3},{2,0},{3,1},{4,6},{5,7},{6,4},{7,5},{8,10},{9,11},{10,... | collective-permute-start | bytes 294920 | tf_op jit(solution)/shard_map/ppermute | solution.py:73
  17.3 2.3 %collective-permute-start.5 = (bf16[128,384]{1,0:T(8,128)(2,1)S(1)}, bf16[128,384]{1,0:T(8,128)(2,1)S(1)}, u32[]{:S(2)}, u32[]{:S(2)}) collective-permute-start(bf16[128,384]{1,0:T(8,128)(2,1)S(1)} %get-tuple-element.148), channel_id=1, source_target_pairs={{0,4},{1,5},{2,6},{3,7},{4,0},{5,1},{6,2},{7,3},{8,12},{9,13},{10,... | collective-permute-start | bytes 294920 | tf_op jit(solution)/shard_map/ppermute | solution.py:73
  19.6 0.5 collective-permute-start.6
  20.1 9.9 %forward_attention.1 = (bf16[6,1024,512]{2,1,0:T(8,128)(2,1)}, bf16[384,512]{1,0:T(8,128)(2,1)S(1)}, bf16[768,1024]{1,0:T(8,128)(2,1)S(1)}, f32[384,512]{1,0:T(8...) custom-call(s32[5]{0:T(128)S(1)} %stack.17.place, s32[4,8]{1,0:T(4,128)S(1)} %bitcast.26, ...), custom_call_target="tpu_custom_call" | custom-call | flops 3221225472 | bytes 6291456 | tf_op jit(solution)/shard_map/forward_attention/pallas_call | solution.py:387
  30.2 9.5 %middle.1 = (bf16[1536,384]{1,0:T(8,128)(2,1)S(1)}, bf16[1536,384]{1,0:T(8,128)(2,1)}, bf16[384,384]{1,0:T(8,128)(2,1)}, bf16[384,512]{1,0:T(8,128)(2,1)}, f32[5...) custom-call(s32[5]{0:T(128)S(1)} %stack.17.place, ...), custom_call_target="tpu_custom_call" | custom-call | flops 4831838208 | bytes 16777216 | tf_op jit(solution)/shard_map/middle/pallas_call | solution.py:488
  39.8 4.8 %all-to-all-start = ((bf16[4,128,384]{2,1,0:T(8,128)(2,1)}), bf16[4,128,384]{2,1,0:T(8,128)(2,1)S(1)}, u32[]{:S(2)}, u32[]{:S(2)}) async-start(bf16[4,128,384]{2,1,0:T(8,128)(2,1)} %get-tuple-element.105), calls=%async_computation | async-start | bytes 786432 | tf_op jit(solution)/shard_map/all_to_all | solution.py:89
  44.6 1.7 %add_convert_fusion = bf16[1536,384]{1,0:T(8,128)(2,1)S(1)} fusion(bf16[1536,384]{1,0:T(8,128)(2,1)} %collective-permute-done.7, bf16[1536,384]{1,0:T(8,128)(2,1)S(1)} %get-tuple-element.94), kind=kLoop, calls=%fused_computation | loop fusion | flops 2359296 | bytes 3538944 | tf_op jit(solution)/shard_map/convert_element_type | solution.py:179
  46.4 0.9 constant_dynamic-slice_fusion.8
  47.3 1.5 %collective-permute-start.8 = (bf16[384,384]{1,0:T(8,128)(2,1)}, bf16[384,384]{1,0:T(8,128)(2,1)}, u32[]{:S(2)}, u32[]{:S(2)}) collective-permute-start(bf16[384,384]{1,0:T(8,128)(2,1)} %get-tuple-element.142), channel_id=1, source_target_pairs={{0,8},{8,0},{16,24},{24,16},{1,9},{9,1},{17,25},{25,17},{2,10},{10... | collective-permute-start | bytes 884744 | tf_op jit(solution)/shard_map/ppermute | solution.py:129
  48.8 1.5 %collective-permute-start.9 = (bf16[384,384]{1,0:T(8,128)(2,1)}, bf16[384,384]{1,0:T(8,128)(2,1)}, u32[]{:S(2)}, u32[]{:S(2)}) collective-permute-start(bf16[384,384]{1,0:T(8,128)(2,1)} %get-tuple-element.141), channel_id=1, source_target_pairs={{0,16},{8,24},{16,0},{24,8},{1,17},{9,25},{17,1},{25,9},{2,18},{10... | collective-permute-start | bytes 884744 | tf_op jit(solution)/shard_map/ppermute | solution.py:129
  50.4 0.5 collective-permute-start.10
  50.9 10.8 %backward_attention.1 = (bf16[768,384]{1,0:T(8,128)(2,1)S(1)}, bf16[768,384]{1,0:T(8,128)(2,1)S(1)}, bf16[528,384]{1,0:T(8,128)(2,1)S(1)}, bf16[512,384]{1,0:T(8,128)(2,1)S(1)}, f32[16,384]{1,0:T(8,128)S(1)}) custom-call(s32[5]{0:T(128)S(1)} %stack.17.place, bf16[6,1024,512]{2,1,0:T(8,128)(2,1)} %get-tuple-element.82.expo, bf16[384,512]{1,0:T(8,128)(2,1)S(1)} %copy-done.20, ...), custom_call_target="tpu_custom_call" | custom-call | flops 6442450944 | bytes 6291456 | tf_op jit(solution)/shard_map/backward_attention/pallas_call | solution.py:592
  61.7 2.6 %collective-permute-done.9 = bf16[384,384]{1,0:T(8,128)(2,1)} collective-permute-done((bf16[384,384]{1,0:T(8,128)(2,1)}, bf16[384,384]{1,0:T(8,128)(2,1)}, u32[]{:S(2)}, u32[]{:S(2)}) %collective-permute-start.9) | collective-permute-done | bytes 294944 | tf_op jit(solution)/shard_map/ppermute | solution.py:129
  64.3 0.5 collective-permute-start.11
  64.8 2.1 %add_convert_fusion.2 = bf16[384,384]{1,0:T(8,128)(2,1)} fusion(bf16[384,384]{1,0:T(8,128)(2,1)} %collective-permute-done.10, bf16[384,384]{1,0:T(8,128)(2,1)} %collective-permute-done.9, bf16[384,384]{1,0:T(8,128)(2,1)} %collective-permute-done.8, bf16[1536,384]{1,0:T(8,128)(2,1)} %copy-done.23, s32[]{:T(128)S(6)} %select_n.77), kind=kLoop, calls=%fused_computation.2 | loop fusion | flops 1179648 | bytes 1474564 | tf_op jit(solution)/shard_map/convert_element_type | solution.py:179
  66.9 4.8 %all-to-all-start.1 = ((bf16[4,96,384]{2,1,0:T(8,128)(2,1)}), bf16[4,96,384]{2,1,0:T(8,128)(2,1)S(1)}, u32[]{:S(2)}, u32[]{:S(2)}) async-start(bf16[4,96,384]{2,1,0:T(8,128)(2,1)} %bitcast.27), calls=%async_computation.1 | async-start | bytes 589824 | tf_op jit(solution)/shard_map/all_to_all | solution.py:169
  71.7 1.2 add_convert_fusion.1
  73.0 1.3 %collective-permute-start.19 = (bf16[192,384]{1,0:T(8,128)(2,1)S(1)}, bf16[192,384]{1,0:T(8,128)(2,1)S(1)}, u32[]{:S(2)}, u32[]{:S(2)}) collective-permute-start(bf16[192,384]{1,0:T(8,128)(2,1)S(1)} %get-tuple-element.145), channel_id=1, source_target_pairs={{0,8},{8,0},{16,24},{24,16},{1,9},{9,1},{17,25},{25,17},{2,10},{10... | collective-permute-start | bytes 442376 | tf_op jit(solution)/shard_map/ppermute | solution.py:129
  74.3 0.8 collective-permute-start.20
  75.1 1.4 %collective-permute-start.21 = (bf16[192,384]{1,0:T(8,128)(2,1)S(1)}, bf16[192,384]{1,0:T(8,128)(2,1)S(1)}, u32[]{:S(2)}, u32[]{:S(2)}) collective-permute-start(bf16[192,384]{1,0:T(8,128)(2,1)S(1)} %get-tuple-element.143), channel_id=1, source_target_pairs={{0,24},{8,16},{16,8},{24,0},{1,25},{9,17},{17,9},{25,1},{2,26},{10... | collective-permute-start | bytes 442376 | tf_op jit(solution)/shard_map/ppermute | solution.py:129
  76.5 4.9 %all-to-all-done.1.refs_0_ = bf16[4,96,384]{2,1,0:T(8,128)(2,1)S(1)} async-done(((bf16[4,96,384]{2,1,0:T(8,128)(2,1)}), bf16[4,96,384]{2,1,0:T(8,128)(2,1)S(1)}, u32[]{:S(2)}, u32[]{:S(2)}) %all-to-all-start.1) | async-done | bytes 294944 | tf_op jit(solution)/shard_map/all_to_all | solution.py:169
  81.6 2.0 %collective-permute-start.14 = (bf16[112,384]{1,0:T(8,128)(2,1)S(1)}, bf16[112,384]{1,0:T(8,128)(2,1)S(1)}, u32[]{:S(2)}, u32[]{:S(2)}) collective-permute-start(bf16[112,384]{1,0:T(8,128)(2,1)S(1)} %line_total.1.refs_0_), channel_id=1, source_target_pairs={{0,4},{1,5},{2,6},{3,7},{4,0},{5,1},{6,2},{7,3},{8,12},{9,13},{10,... | collective-permute-start | bytes 258056 | tf_op jit(solution)/shard_map/ppermute | solution.py:124
  83.6 2.4 %collective-permute-start.15 = (bf16[112,384]{1,0:T(8,128)(2,1)S(1)}, bf16[112,384]{1,0:T(8,128)(2,1)S(1)}, u32[]{:S(2)}, u32[]{:S(2)}) collective-permute-start(bf16[112,384]{1,0:T(8,128)(2,1)S(1)} %line_total.1.refs_0_), channel_id=1, source_target_pairs={{0,6},{1,7},{2,4},{3,5},{4,2},{5,3},{6,0},{7,1},{8,14},{9,15},{10,... | collective-permute-start | bytes 258056 | tf_op jit(solution)/shard_map/ppermute | solution.py:124
  86.2 2.0 %collective-permute-start.23 = (bf16[48,384]{1,0:T(8,128)(2,1)S(1)}, bf16[48,384]{1,0:T(8,128)(2,1)S(1)}, u32[]{:S(2)}, u32[]{:S(2)}) collective-permute-start(bf16[48,384]{1,0:T(8,128)(2,1)S(1)} %get-tuple-element.156), channel_id=1, source_target_pairs={{0,4},{1,5},{2,6},{3,7},{4,0},{5,1},{6,2},{7,3},{8,12},{9,13},{10,... | collective-permute-start | bytes 110600 | tf_op jit(solution)/shard_map/ppermute | solution.py:124
  88.2 2.4 %collective-permute-start.24 = (bf16[48,384]{1,0:T(8,128)(2,1)S(1)}, bf16[48,384]{1,0:T(8,128)(2,1)S(1)}, u32[]{:S(2)}, u32[]{:S(2)}) collective-permute-start(bf16[48,384]{1,0:T(8,128)(2,1)S(1)} %get-tuple-element.155), channel_id=1, source_target_pairs={{0,6},{1,7},{2,4},{3,5},{4,2},{5,3},{6,0},{7,1},{8,14},{9,15},{10,... | collective-permute-start | bytes 110600 | tf_op jit(solution)/shard_map/ppermute | solution.py:124
  90.6 0.7 collective-permute-done.14.refs_2_
  91.3 1.3 %collective-permute-start.16 = (bf16[400,384]{1,0:T(8,128)(2,1)S(1)}, bf16[400,384]{1,0:T(8,128)(2,1)S(1)}, u32[]{:S(2)}, u32[]{:S(2)}) collective-permute-start(bf16[400,384]{1,0:T(8,128)(2,1)S(1)} %line_join.1.refs_0_), channel_id=1, source_target_pairs={{0,8},{8,0},{16,24},{24,16},{1,9},{9,1},{17,25},{25,17},{2,10},{10... | collective-permute-start | bytes 921608 | tf_op jit(solution)/shard_map/ppermute | solution.py:129
  92.6 0.8 collective-permute-start.17
  93.4 1.4 %collective-permute-start.18 = (bf16[400,384]{1,0:T(8,128)(2,1)S(1)}, bf16[400,384]{1,0:T(8,128)(2,1)S(1)}, u32[]{:S(2)}, u32[]{:S(2)}) collective-permute-start(bf16[400,384]{1,0:T(8,128)(2,1)S(1)} %line_join.1.refs_0_), channel_id=1, source_target_pairs={{0,24},{8,16},{16,8},{24,0},{1,25},{9,17},{17,9},{25,1},{2,26},{10... | collective-permute-start | bytes 921608 | tf_op jit(solution)/shard_map/ppermute | solution.py:129
  94.8 0.6 finish_rows.1
  95.4 2.1 %collective-permute-start.25 = (bf16[176,384]{1,0:T(8,128)(2,1)S(1)}, bf16[176,384]{1,0:T(8,128)(2,1)S(1)}, u32[]{:S(2)}, u32[]{:S(2)}) collective-permute-start(bf16[176,384]{1,0:T(8,128)(2,1)S(1)} %get-tuple-element.117), channel_id=1, source_target_pairs={{0,2},{1,3},{2,0},{3,1},{4,6},{5,7},{6,4},{7,5},{8,10},{9,11},{10,... | collective-permute-start | bytes 405512 | tf_op jit(solution)/shard_map/ppermute | solution.py:81
  97.6 0.8 collective-permute-start.26
  98.4 3.6 %collective-permute-done.25.refs_11_ = bf16[176,384]{1,0:T(8,128)(2,1)S(1)} collective-permute-done((bf16[176,384]{1,0:T(8,128)(2,1)S(1)}, bf16[176,384]{1,0:T(8,128)(2,1)S(1)}, u32[]{:S(2)}, u32[]{:S(2)}) %collective-permute-start.25) | collective-permute-done | bytes 135200 | tf_op jit(solution)/shard_map/ppermute | solution.py:81
  102.0 2.3 %collective-permute-start.27 = (bf16[176,384]{1,0:T(8,128)(2,1)S(1)}, bf16[176,384]{1,0:T(8,128)(2,1)S(1)}, u32[]{:S(2)}, u32[]{:S(2)}) collective-permute-start(bf16[176,384]{1,0:T(8,128)(2,1)S(1)} %get-tuple-element.119), channel_id=1, source_target_pairs={{0,6},{1,7},{2,4},{3,5},{4,2},{5,3},{6,0},{7,1},{8,14},{9,15},{10,... | collective-permute-start | bytes 405512 | tf_op jit(solution)/shard_map/ppermute | solution.py:81
  104.3 0.6 collective-permute-done.26.refs_12_
  104.9 4.0 %collective-permute-done.27.refs_13_ = bf16[176,384]{1,0:T(8,128)(2,1)S(1)} collective-permute-done((bf16[176,384]{1,0:T(8,128)(2,1)S(1)}, bf16[176,384]{1,0:T(8,128)(2,1)S(1)}, u32[]{:S(2)}, u32[]{:S(2)}) %collective-permute-start.27) | collective-permute-done | bytes 135200 | tf_op jit(solution)/shard_map/ppermute | solution.py:81
  109.0 0.5 collective-permute-start.29
  109.5 0.1 collective-permute-start.30
  109.6 0.4 collective-permute-start.31
  110.1 1.3 %collective-permute-start.32 = (bf16[192,384]{1,0:T(8,128)(2,1)S(1)}, bf16[192,384]{1,0:T(8,128)(2,1)S(1)}, u32[]{:S(2)}, u32[]{:S(2)}) collective-permute-start(bf16[192,384]{1,0:T(8,128)(2,1)S(1)} %pad_maximum_fusion.1.refs_0_), channel_id=1, source_target_pairs={{0,8},{8,0},{16,24},{24,16},{1,9},{9,1},{17,25},{25,17},{2,10},{10... | collective-permute-start | bytes 442376 | tf_op jit(solution)/shard_map/ppermute | solution.py:129
  111.4 1.2 collective-permute-start.33
  112.6 1.1 collective-permute-start.34
  113.7 5.5 %first_sums.1 = (f32[1536,384]{1,0:T(8,128)}, f32[384,1536]{1,0:T(8,128)}, f32[384,2304]{1,0:T(8,128)}, bf16[4,128,384]{2,1,0:T(8,128)(2,1)}, f32[4,128,384]{2,1...) custom-call(s32[5]{0:T(128)S(1)} %stack.17.place, ...), custom_call_target="tpu_custom_call" | custom-call | tf_op jit(solution)/shard_map/first_sums/pallas_call | solution.py:785
  119.2 1.3 %collective-permute-done.34.refs_3_ = bf16[192,384]{1,0:T(8,128)(2,1)S(1)} collective-permute-done((bf16[192,384]{1,0:T(8,128)(2,1)S(1)}, bf16[192,384]{1,0:T(8,128)(2,1)S(1)}, u32[]{:S(2)}, u32[]{:S(2)}) %collective-permute-start.34) | collective-permute-done | bytes 147488 | tf_op jit(solution)/shard_map/ppermute | solution.py:129
  120.5 0.5 collective-permute-start.36
  121.1 0.5 collective-permute-start.38
  121.6 0.3 collective-permute-done.35.refs_4_
  121.9 0.2 collective-permute-done.36.refs_5_
  122.1 0.3 collective-permute-done.37.refs_6_
  122.4 0.2 collective-permute-done.38.refs_7_
  122.6 3.0 %second_sums.1 = (f32[384,1152]{1,0:T(8,128)}, f32[384,384]{1,0:T(8,128)}) custom-call(s32[5]{0:T(128)S(1)} %stack.17.place, bf16[192,384]{1,0:T(8,128)(2,1)S(1)} %pad_maximum_fusion.1.refs_0_, bf16[192,384]{1,0:T(8,128)(2,1)S(1)} %collective-permute-done.32.refs_1_, bf16[192,384]{1,0:T(8,128)(2,1)S(1)} %collective-permute-done.33.refs_2_, ...), custom_call_target="tpu_custom_call" | custom-call | tf_op jit(solution)/shard_map/second_sums/pallas_call | solution.py:840
  (102 shorter events, 1.1 us)
Async XLA Ops:
  0.6 10.4 %copy-start.2 = (bf16[384,1152]{1,0:T(8,128)(2,1)S(1)}, bf16[384,1152]{1,0:T(8,128)(2,1)}, u32[]{:S(2)}) copy-start(bf16[384,1152]{1,0:T(8,128)(2,1)} %attend_weight.1) | copy-start | bytes 2654212
  1.8 13.0 %collective-permute-start = (bf16[128,384]{1,0:T(8,128)(2,1)S(1)}, bf16[128,384]{1,0:T(8,128)(2,1)S(1)}, u32[]{:S(2)}, u32[]{:S(2)}) collective-permute-start(bf16[128,384]{1,0:T(8,128)(2,1)S(1)} %get-tuple-element.152), channel_id=1, source_target_pairs={{0,2},{1,3},{2,0},{3,1},{4,6},{5,7},{6,4},{7,5},{8,10},{9,11},{10,... | collective-permute-start | bytes 294920 | tf_op jit(solution)/shard_map/ppermute | solution.py:73
  4.9 10.4 %collective-permute-start.1 = (bf16[128,384]{1,0:T(8,128)(2,1)S(1)}, bf16[128,384]{1,0:T(8,128)(2,1)S(1)}, u32[]{:S(2)}, u32[]{:S(2)}) collective-permute-start(bf16[128,384]{1,0:T(8,128)(2,1)S(1)} %get-tuple-element.154), channel_id=1, source_target_pairs={{0,4},{1,5},{2,6},{3,7},{4,0},{5,1},{6,2},{7,3},{8,12},{9,13},{10,... | collective-permute-start | bytes 294920 | tf_op jit(solution)/shard_map/ppermute | solution.py:73
  7.5 7.8 %collective-permute-start.2 = (bf16[128,384]{1,0:T(8,128)(2,1)S(1)}, bf16[128,384]{1,0:T(8,128)(2,1)S(1)}, u32[]{:S(2)}, u32[]{:S(2)}) collective-permute-start(bf16[128,384]{1,0:T(8,128)(2,1)S(1)} %get-tuple-element.151), channel_id=1, source_target_pairs={{0,6},{1,7},{2,4},{3,5},{4,2},{5,3},{6,0},{7,1},{8,14},{9,15},{10,... | collective-permute-start | bytes 294920 | tf_op jit(solution)/shard_map/ppermute | solution.py:73
  11.1 1.5 %copy-start = (bf16[384,2304]{1,0:T(8,128)(2,1)S(1)}, bf16[384,2304]{1,0:T(8,128)(2,1)}, u32[]{:S(2)}) copy-start(bf16[384,2304]{1,0:T(8,128)(2,1)} %refs_8_.1) | copy-start | bytes 5308420
  13.9 1.6 %copy-start.24 = (bf16[1,4,128,384]{3,2,1,0:T(8,128)(2,1)S(1)}, bf16[1,4,128,384]{3,2,1,0:T(8,128)(2,1)}, u32[]{:S(2)}) copy-start(bf16[1,4,128,384]{3,2,1,0:T(8,128)(2,1)} %param.17) | copy-start | bytes 1179652
  14.8 15.2 %copy-start.7 = (bf16[1152,384]{1,0:T(8,128)(2,1)}, bf16[1152,384]{1,0:T(8,128)(2,1)S(1)}, u32[]{:S(2)}) copy-start(bf16[1152,384]{1,0:T(8,128)(2,1)S(1)} %get-tuple-element.81.weight) | copy-start | bytes 2654212
  14.8 5.2 %copy-start.12 = (s32[1,4,1024]{2,1,0:T(4,128)S(1)}, s32[1,4,1024]{2,1,0:T(4,128)}, u32[]{:S(2)}) copy-start(s32[1,4,1024]{2,1,0:T(4,128)} %param.19) | copy-start | bytes 49156
  14.8 5.2 %copy-start.13 = (s32[1,4,8]{2,1,0:T(4,128)S(1)}, s32[1,4,8]{2,1,0:T(4,128)}, u32[]{:S(2)}) copy-start(s32[1,4,8]{2,1,0:T(4,128)} %param.18) | copy-start | bytes 388
  15.5 4.6 %collective-permute-start.3 = (bf16[512,384]{1,0:T(8,128)(2,1)S(1)}, bf16[512,384]{1,0:T(8,128)(2,1)S(1)}, u32[]{:S(2)}, u32[]{:S(2)}) collective-permute-start(bf16[512,384]{1,0:T(8,128)(2,1)S(1)} %constant_dynamic-update-slice_fusion.own), channel_id=1, source_target_pairs={{0,1},{1,0},{2,3},{3,2},{4,5},{5,4},{6,7},{7,6},{8,9},{9,8},{10,11... | collective-permute-start | bytes 1179656 | tf_op jit(solution)/shard_map/ppermute | solution.py:95
  15.6 14.5 %collective-permute-start.4 = (bf16[128,384]{1,0:T(8,128)(2,1)S(1)}, bf16[128,384]{1,0:T(8,128)(2,1)S(1)}, u32[]{:S(2)}, u32[]{:S(2)}) collective-permute-start(bf16[128,384]{1,0:T(8,128)(2,1)S(1)} %get-tuple-element.149), channel_id=1, source_target_pairs={{0,2},{1,3},{2,0},{3,1},{4,6},{5,7},{6,4},{7,5},{8,10},{9,11},{10,... | collective-permute-start | bytes 294920 | tf_op jit(solution)/shard_map/ppermute | solution.py:73
  17.3 12.8 %collective-permute-start.5 = (bf16[128,384]{1,0:T(8,128)(2,1)S(1)}, bf16[128,384]{1,0:T(8,128)(2,1)S(1)}, u32[]{:S(2)}, u32[]{:S(2)}) collective-permute-start(bf16[128,384]{1,0:T(8,128)(2,1)S(1)} %get-tuple-element.148), channel_id=1, source_target_pairs={{0,4},{1,5},{2,6},{3,7},{4,0},{5,1},{6,2},{7,3},{8,12},{9,13},{10,... | collective-permute-start | bytes 294920 | tf_op jit(solution)/shard_map/ppermute | solution.py:73
  19.6 10.5 %collective-permute-start.6 = (bf16[128,384]{1,0:T(8,128)(2,1)S(1)}, bf16[128,384]{1,0:T(8,128)(2,1)S(1)}, u32[]{:S(2)}, u32[]{:S(2)}) collective-permute-start(bf16[128,384]{1,0:T(8,128)(2,1)S(1)} %get-tuple-element.147), channel_id=1, source_target_pairs={{0,6},{1,7},{2,4},{3,5},{4,2},{5,3},{6,0},{7,1},{8,14},{9,15},{10,... | collective-permute-start | bytes 294920 | tf_op jit(solution)/shard_map/ppermute | solution.py:73
  20.1 10.0 %copy-start.9 = (bf16[512,384]{1,0:T(8,128)(2,1)}, bf16[512,384]{1,0:T(8,128)(2,1)S(1)}, u32[]{:S(2)}) copy-start(bf16[512,384]{1,0:T(8,128)(2,1)S(1)} %collective-permute-done.3.rest) | copy-start | bytes 1179652
  20.1 10.1 %copy-start.5 = (bf16[384,1536]{1,0:T(8,128)(2,1)S(1)}, bf16[384,1536]{1,0:T(8,128)(2,1)}, u32[]{:S(2)}) copy-start(bf16[384,1536]{1,0:T(8,128)(2,1)} %expand_weight.1) | copy-start | bytes 3538948
  20.1 10.1 %copy-start.6 = (bf16[1536,384]{1,0:T(8,128)(2,1)S(1)}, bf16[1536,384]{1,0:T(8,128)(2,1)}, u32[]{:S(2)}) copy-start(bf16[1536,384]{1,0:T(8,128)(2,1)} %shrink_weight.1) | copy-start | bytes 3538948
  20.1 10.1 %copy-start.11 = (bf16[384,384]{1,0:T(8,128)(2,1)S(1)}, bf16[384,384]{1,0:T(8,128)(2,1)}, u32[]{:S(2)}) copy-start(bf16[384,384]{1,0:T(8,128)(2,1)} %output_weight.1) | copy-start | bytes 884740
  30.1 9.7 %copy-start.14 = (bf16[768,1024]{1,0:T(8,128)(2,1)}, bf16[768,1024]{1,0:T(8,128)(2,1)S(1)}, u32[]{:S(2)}) copy-start(bf16[768,1024]{1,0:T(8,128)(2,1)S(1)} %get-tuple-element.84.key_value) | copy-start | bytes 4718596
  30.1 9.7 %copy-start.16 = (f32[384,512]{1,0:T(8,128)}, f32[384,512]{1,0:T(8,128)S(1)}, u32[]{:S(2)}) copy-start(f32[384,512]{1,0:T(8,128)S(1)} %get-tuple-element.85.attended_wide) | copy-start | bytes 2359300
  30.1 9.7 %copy-start.19 = (bf16[384,512]{1,0:T(8,128)(2,1)}, bf16[384,512]{1,0:T(8,128)(2,1)S(1)}, u32[]{:S(2)}) copy-start(bf16[384,512]{1,0:T(8,128)(2,1)S(1)} %get-tuple-element.83.query) | copy-start | bytes 1179652
  39.7 4.9 %collective-permute-start.7 = (bf16[1536,384]{1,0:T(8,128)(2,1)}, bf16[1536,384]{1,0:T(8,128)(2,1)}, u32[]{:S(2)}, u32[]{:S(2)}) collective-permute-start(bf16[1536,384]{1,0:T(8,128)(2,1)} %get-tuple-element.95), channel_id=1, source_target_pairs={{0,1},{1,0},{2,3},{3,2},{4,5},{5,4},{6,7},{7,6},{8,9},{9,8},{10,11... | collective-permute-start | bytes 3538952 | tf_op jit(solution)/shard_map/ppermute | solution.py:115
  39.8 11.0 %copy-start.22 = (bf16[384,384]{1,0:T(8,128)(2,1)S(1)}, bf16[384,384]{1,0:T(8,128)(2,1)}, u32[]{:S(2)}) copy-start(bf16[384,384]{1,0:T(8,128)(2,1)} %get-tuple-element.97.packed_output) | copy-start | bytes 884740
  39.8 21.8 %all-to-all-start = ((bf16[4,128,384]{2,1,0:T(8,128)(2,1)}), bf16[4,128,384]{2,1,0:T(8,128)(2,1)S(1)}, u32[]{:S(2)}, u32[]{:S(2)}) async-start(bf16[4,128,384]{2,1,0:T(8,128)(2,1)} %get-tuple-element.105), calls=%async_computation | async-start | bytes 786432 | tf_op jit(solution)/shard_map/all_to_all | solution.py:89
  44.6 6.2 %copy-start.15 = (bf16[768,1024]{1,0:T(8,128)(2,1)S(1)}, bf16[768,1024]{1,0:T(8,128)(2,1)}, u32[]{:S(2)}) copy-start(bf16[768,1024]{1,0:T(8,128)(2,1)} %copy-done.14) | copy-start | bytes 4718596
  44.6 6.2 %copy-start.17 = (f32[384,512]{1,0:T(8,128)S(1)}, f32[384,512]{1,0:T(8,128)}, u32[]{:S(2)}) copy-start(f32[384,512]{1,0:T(8,128)} %copy-done.16) | copy-start | bytes 2359300
  44.6 6.2 %copy-start.18 = (f32[512,384]{1,0:T(8,128)S(1)}, f32[512,384]{1,0:T(8,128)}, u32[]{:S(2)}) copy-start(f32[512,384]{1,0:T(8,128)} %get-tuple-element.98.grad_residual) | copy-start | bytes 2359300
  44.6 6.2 %copy-start.21 = (bf16[384,512]{1,0:T(8,128)(2,1)S(1)}, bf16[384,512]{1,0:T(8,128)(2,1)}, u32[]{:S(2)}) copy-start(bf16[384,512]{1,0:T(8,128)(2,1)} %get-tuple-element.96.grad_attended) | copy-start | bytes 1179652
  46.4 4.5 %copy-start.23 = (bf16[1536,384]{1,0:T(8,128)(2,1)}, bf16[1536,384]{1,0:T(8,128)(2,1)S(1)}, u32[]{:S(2)}) copy-start(bf16[1536,384]{1,0:T(8,128)(2,1)S(1)} %add_convert_fusion) | copy-start | bytes 3538948
  46.4 4.5 %copy-start.8 = (bf16[1152,384]{1,0:T(8,128)(2,1)S(1)}, bf16[1152,384]{1,0:T(8,128)(2,1)}, u32[]{:S(2)}) copy-start(bf16[1152,384]{1,0:T(8,128)(2,1)} %copy-done.7) | copy-start | bytes 2654212
  46.4 4.5 %copy-start.10 = (bf16[512,384]{1,0:T(8,128)(2,1)S(1)}, bf16[512,384]{1,0:T(8,128)(2,1)}, u32[]{:S(2)}) copy-start(bf16[512,384]{1,0:T(8,128)(2,1)} %copy-done.9) | copy-start | bytes 1179652
  46.4 4.5 %copy-start.20 = (bf16[384,512]{1,0:T(8,128)(2,1)S(1)}, bf16[384,512]{1,0:T(8,128)(2,1)}, u32[]{:S(2)}) copy-start(bf16[384,512]{1,0:T(8,128)(2,1)} %copy-done.19) | copy-start | bytes 1179652
  47.3 14.4 %collective-permute-start.8 = (bf16[384,384]{1,0:T(8,128)(2,1)}, bf16[384,384]{1,0:T(8,128)(2,1)}, u32[]{:S(2)}, u32[]{:S(2)}) collective-permute-start(bf16[384,384]{1,0:T(8,128)(2,1)} %get-tuple-element.142), channel_id=1, source_target_pairs={{0,8},{8,0},{16,24},{24,16},{1,9},{9,1},{17,25},{25,17},{2,10},{10... | collective-permute-start | bytes 884744 | tf_op jit(solution)/shard_map/ppermute | solution.py:129
  48.8 15.4 %collective-permute-start.9 = (bf16[384,384]{1,0:T(8,128)(2,1)}, bf16[384,384]{1,0:T(8,128)(2,1)}, u32[]{:S(2)}, u32[]{:S(2)}) collective-permute-start(bf16[384,384]{1,0:T(8,128)(2,1)} %get-tuple-element.141), channel_id=1, source_target_pairs={{0,16},{8,24},{16,0},{24,8},{1,17},{9,25},{17,1},{25,9},{2,18},{10... | collective-permute-start | bytes 884744 | tf_op jit(solution)/shard_map/ppermute | solution.py:129
  50.4 13.9 %collective-permute-start.10 = (bf16[384,384]{1,0:T(8,128)(2,1)S(1)}, bf16[384,384]{1,0:T(8,128)(2,1)}, u32[]{:S(2)}, u32[]{:S(2)}) collective-permute-start(bf16[384,384]{1,0:T(8,128)(2,1)S(1)} %get-tuple-element.140), channel_id=1, source_target_pairs={{0,24},{8,16},{16,8},{24,0},{1,25},{9,17},{17,9},{25,1},{2,26},{10... | collective-permute-start | bytes 884744 | tf_op jit(solution)/shard_map/ppermute | solution.py:129
  64.3 7.4 %collective-permute-start.12 = (bf16[768,384]{1,0:T(8,128)(2,1)S(1)}, bf16[768,384]{1,0:T(8,128)(2,1)}, u32[]{:S(2)}, u32[]{:S(2)}) collective-permute-start(bf16[768,384]{1,0:T(8,128)(2,1)S(1)} %get-tuple-element.109), channel_id=1, source_target_pairs={{0,1},{1,0},{2,3},{3,2},{4,5},{5,4},{6,7},{7,6},{8,9},{9,8},{10,11... | collective-permute-start | bytes 1769480 | tf_op jit(solution)/shard_map/ppermute | solution.py:115
  64.3 17.2 %collective-permute-start.11 = (bf16[528,384]{1,0:T(8,128)(2,1)S(1)}, bf16[528,384]{1,0:T(8,128)(2,1)S(1)}, u32[]{:S(2)}, u32[]{:S(2)}) collective-permute-start(bf16[528,384]{1,0:T(8,128)(2,1)S(1)} %get-tuple-element.107), channel_id=1, source_target_pairs={{0,1},{1,0},{2,3},{3,2},{4,5},{5,4},{6,7},{7,6},{8,9},{9,8},{10,11... | collective-permute-start | bytes 1216520 | tf_op jit(solution)/shard_map/ppermute | solution.py:115
  66.9 14.6 %all-to-all-start.1 = ((bf16[4,96,384]{2,1,0:T(8,128)(2,1)}), bf16[4,96,384]{2,1,0:T(8,128)(2,1)S(1)}, u32[]{:S(2)}, u32[]{:S(2)}) async-start(bf16[4,96,384]{2,1,0:T(8,128)(2,1)} %bitcast.27), calls=%async_computation.1 | async-start | bytes 589824 | tf_op jit(solution)/shard_map/all_to_all | solution.py:169
  73.0 10.6 %collective-permute-start.19 = (bf16[192,384]{1,0:T(8,128)(2,1)S(1)}, bf16[192,384]{1,0:T(8,128)(2,1)S(1)}, u32[]{:S(2)}, u32[]{:S(2)}) collective-permute-start(bf16[192,384]{1,0:T(8,128)(2,1)S(1)} %get-tuple-element.145), channel_id=1, source_target_pairs={{0,8},{8,0},{16,24},{24,16},{1,9},{9,1},{17,25},{25,17},{2,10},{10... | collective-permute-start | bytes 442376 | tf_op jit(solution)/shard_map/ppermute | solution.py:129
  74.3 11.7 %collective-permute-start.20 = (bf16[192,384]{1,0:T(8,128)(2,1)S(1)}, bf16[192,384]{1,0:T(8,128)(2,1)S(1)}, u32[]{:S(2)}, u32[]{:S(2)}) collective-permute-start(bf16[192,384]{1,0:T(8,128)(2,1)S(1)} %get-tuple-element.144), channel_id=1, source_target_pairs={{0,16},{8,24},{16,0},{24,8},{1,17},{9,25},{17,1},{25,9},{2,18},{10... | collective-permute-start | bytes 442376 | tf_op jit(solution)/shard_map/ppermute | solution.py:129
  75.1 10.9 %collective-permute-start.21 = (bf16[192,384]{1,0:T(8,128)(2,1)S(1)}, bf16[192,384]{1,0:T(8,128)(2,1)S(1)}, u32[]{:S(2)}, u32[]{:S(2)}) collective-permute-start(bf16[192,384]{1,0:T(8,128)(2,1)S(1)} %get-tuple-element.143), channel_id=1, source_target_pairs={{0,24},{8,16},{16,8},{24,0},{1,25},{9,17},{17,9},{25,1},{2,26},{10... | collective-permute-start | bytes 442376 | tf_op jit(solution)/shard_map/ppermute | solution.py:129
  81.5 6.6 %collective-permute-start.13 = (bf16[112,384]{1,0:T(8,128)(2,1)S(1)}, bf16[112,384]{1,0:T(8,128)(2,1)S(1)}, u32[]{:S(2)}, u32[]{:S(2)}) collective-permute-start(bf16[112,384]{1,0:T(8,128)(2,1)S(1)} %line_total.1.refs_0_), channel_id=1, source_target_pairs={{0,2},{1,3},{2,0},{3,1},{4,6},{5,7},{6,4},{7,5},{8,10},{9,11},{10,... | collective-permute-start | bytes 258056 | tf_op jit(solution)/shard_map/ppermute | solution.py:124
  81.6 9.6 %collective-permute-start.14 = (bf16[112,384]{1,0:T(8,128)(2,1)S(1)}, bf16[112,384]{1,0:T(8,128)(2,1)S(1)}, u32[]{:S(2)}, u32[]{:S(2)}) collective-permute-start(bf16[112,384]{1,0:T(8,128)(2,1)S(1)} %line_total.1.refs_0_), channel_id=1, source_target_pairs={{0,4},{1,5},{2,6},{3,7},{4,0},{5,1},{6,2},{7,3},{8,12},{9,13},{10,... | collective-permute-start | bytes 258056 | tf_op jit(solution)/shard_map/ppermute | solution.py:124
  83.6 7.7 %collective-permute-start.15 = (bf16[112,384]{1,0:T(8,128)(2,1)S(1)}, bf16[112,384]{1,0:T(8,128)(2,1)S(1)}, u32[]{:S(2)}, u32[]{:S(2)}) collective-permute-start(bf16[112,384]{1,0:T(8,128)(2,1)S(1)} %line_total.1.refs_0_), channel_id=1, source_target_pairs={{0,6},{1,7},{2,4},{3,5},{4,2},{5,3},{6,0},{7,1},{8,14},{9,15},{10,... | collective-permute-start | bytes 258056 | tf_op jit(solution)/shard_map/ppermute | solution.py:124
  86.1 7.3 %collective-permute-start.22 = (bf16[48,384]{1,0:T(8,128)(2,1)S(1)}, bf16[48,384]{1,0:T(8,128)(2,1)S(1)}, u32[]{:S(2)}, u32[]{:S(2)}) collective-permute-start(bf16[48,384]{1,0:T(8,128)(2,1)S(1)} %get-tuple-element.157), channel_id=1, source_target_pairs={{0,2},{1,3},{2,0},{3,1},{4,6},{5,7},{6,4},{7,5},{8,10},{9,11},{10,... | collective-permute-start | bytes 110600 | tf_op jit(solution)/shard_map/ppermute | solution.py:124
  86.2 8.7 %collective-permute-start.23 = (bf16[48,384]{1,0:T(8,128)(2,1)S(1)}, bf16[48,384]{1,0:T(8,128)(2,1)S(1)}, u32[]{:S(2)}, u32[]{:S(2)}) collective-permute-start(bf16[48,384]{1,0:T(8,128)(2,1)S(1)} %get-tuple-element.156), channel_id=1, source_target_pairs={{0,4},{1,5},{2,6},{3,7},{4,0},{5,1},{6,2},{7,3},{8,12},{9,13},{10,... | collective-permute-start | bytes 110600 | tf_op jit(solution)/shard_map/ppermute | solution.py:124
  88.2 25.5 %copy-start.1 = (bf16[384,2304]{1,0:T(8,128)(2,1)S(1)}, bf16[384,2304]{1,0:T(8,128)(2,1)}, u32[]{:S(2)}) copy-start(bf16[384,2304]{1,0:T(8,128)(2,1)} %refs_8_.1) | copy-start | bytes 5308420
  88.2 6.7 %collective-permute-start.24 = (bf16[48,384]{1,0:T(8,128)(2,1)S(1)}, bf16[48,384]{1,0:T(8,128)(2,1)S(1)}, u32[]{:S(2)}, u32[]{:S(2)}) collective-permute-start(bf16[48,384]{1,0:T(8,128)(2,1)S(1)} %get-tuple-element.155), channel_id=1, source_target_pairs={{0,6},{1,7},{2,4},{3,5},{4,2},{5,3},{6,0},{7,1},{8,14},{9,15},{10,... | collective-permute-start | bytes 110600 | tf_op jit(solution)/shard_map/ppermute | solution.py:124
  91.3 17.6 %collective-permute-start.16 = (bf16[400,384]{1,0:T(8,128)(2,1)S(1)}, bf16[400,384]{1,0:T(8,128)(2,1)S(1)}, u32[]{:S(2)}, u32[]{:S(2)}) collective-permute-start(bf16[400,384]{1,0:T(8,128)(2,1)S(1)} %line_join.1.refs_0_), channel_id=1, source_target_pairs={{0,8},{8,0},{16,24},{24,16},{1,9},{9,1},{17,25},{25,17},{2,10},{10... | collective-permute-start | bytes 921608 | tf_op jit(solution)/shard_map/ppermute | solution.py:129
  92.6 16.4 %collective-permute-start.17 = (bf16[400,384]{1,0:T(8,128)(2,1)S(1)}, bf16[400,384]{1,0:T(8,128)(2,1)S(1)}, u32[]{:S(2)}, u32[]{:S(2)}) collective-permute-start(bf16[400,384]{1,0:T(8,128)(2,1)S(1)} %line_join.1.refs_0_), channel_id=1, source_target_pairs={{0,16},{8,24},{16,0},{24,8},{1,17},{9,25},{17,1},{25,9},{2,18},{10... | collective-permute-start | bytes 921608 | tf_op jit(solution)/shard_map/ppermute | solution.py:129
  93.4 15.5 %collective-permute-start.18 = (bf16[400,384]{1,0:T(8,128)(2,1)S(1)}, bf16[400,384]{1,0:T(8,128)(2,1)S(1)}, u32[]{:S(2)}, u32[]{:S(2)}) collective-permute-start(bf16[400,384]{1,0:T(8,128)(2,1)S(1)} %line_join.1.refs_0_), channel_id=1, source_target_pairs={{0,24},{8,16},{16,8},{24,0},{1,25},{9,17},{17,9},{25,1},{2,26},{10... | collective-permute-start | bytes 921608 | tf_op jit(solution)/shard_map/ppermute | solution.py:129
  95.4 6.6 %collective-permute-start.25 = (bf16[176,384]{1,0:T(8,128)(2,1)S(1)}, bf16[176,384]{1,0:T(8,128)(2,1)S(1)}, u32[]{:S(2)}, u32[]{:S(2)}) collective-permute-start(bf16[176,384]{1,0:T(8,128)(2,1)S(1)} %get-tuple-element.117), channel_id=1, source_target_pairs={{0,2},{1,3},{2,0},{3,1},{4,6},{5,7},{6,4},{7,5},{8,10},{9,11},{10,... | collective-permute-start | bytes 405512 | tf_op jit(solution)/shard_map/ppermute | solution.py:81
  97.6 7.4 %collective-permute-start.26 = (bf16[176,384]{1,0:T(8,128)(2,1)S(1)}, bf16[176,384]{1,0:T(8,128)(2,1)S(1)}, u32[]{:S(2)}, u32[]{:S(2)}) collective-permute-start(bf16[176,384]{1,0:T(8,128)(2,1)S(1)} %get-tuple-element.118), channel_id=1, source_target_pairs={{0,4},{1,5},{2,6},{3,7},{4,0},{5,1},{6,2},{7,3},{8,12},{9,13},{10,... | collective-permute-start | bytes 405512 | tf_op jit(solution)/shard_map/ppermute | solution.py:81
  102.0 6.9 %collective-permute-start.27 = (bf16[176,384]{1,0:T(8,128)(2,1)S(1)}, bf16[176,384]{1,0:T(8,128)(2,1)S(1)}, u32[]{:S(2)}, u32[]{:S(2)}) collective-permute-start(bf16[176,384]{1,0:T(8,128)(2,1)S(1)} %get-tuple-element.119), channel_id=1, source_target_pairs={{0,6},{1,7},{2,4},{3,5},{4,2},{5,3},{6,0},{7,1},{8,14},{9,15},{10,... | collective-permute-start | bytes 405512 | tf_op jit(solution)/shard_map/ppermute | solution.py:81
  108.9 2.5 %collective-permute-start.28 = (bf16[400,384]{1,0:T(8,128)(2,1)S(1)}, bf16[400,384]{1,0:T(8,128)(2,1)S(1)}, u32[]{:S(2)}, u32[]{:S(2)}) collective-permute-start(bf16[400,384]{1,0:T(8,128)(2,1)S(1)} %line_join.1.refs_0_), channel_id=1, source_target_pairs={{0,1},{1,0},{2,3},{3,2},{4,5},{5,4},{6,7},{7,6},{8,9},{9,8},{10,11... | collective-permute-start | bytes 921608 | tf_op jit(solution)/shard_map/ppermute | solution.py:115
  109.0 3.5 %collective-permute-start.29 = (bf16[400,384]{1,0:T(8,128)(2,1)S(1)}, bf16[400,384]{1,0:T(8,128)(2,1)S(1)}, u32[]{:S(2)}, u32[]{:S(2)}) collective-permute-start(bf16[400,384]{1,0:T(8,128)(2,1)S(1)} %collective-permute-done.16.refs_1_), channel_id=1, source_target_pairs={{0,1},{1,0},{2,3},{3,2},{4,5},{5,4},{6,7},{7,6},{8,9},{9,8},{10,11... | collective-permute-start | bytes 921608 | tf_op jit(solution)/shard_map/ppermute | solution.py:115
  109.5 4.1 %collective-permute-start.30 = (bf16[400,384]{1,0:T(8,128)(2,1)S(1)}, bf16[400,384]{1,0:T(8,128)(2,1)S(1)}, u32[]{:S(2)}, u32[]{:S(2)}) collective-permute-start(bf16[400,384]{1,0:T(8,128)(2,1)S(1)} %collective-permute-done.17.refs_2_), channel_id=1, source_target_pairs={{0,1},{1,0},{2,3},{3,2},{4,5},{5,4},{6,7},{7,6},{8,9},{9,8},{10,11... | collective-permute-start | bytes 921608 | tf_op jit(solution)/shard_map/ppermute | solution.py:115
  109.6 4.1 %collective-permute-start.31 = (bf16[400,384]{1,0:T(8,128)(2,1)S(1)}, bf16[400,384]{1,0:T(8,128)(2,1)S(1)}, u32[]{:S(2)}, u32[]{:S(2)}) collective-permute-start(bf16[400,384]{1,0:T(8,128)(2,1)S(1)} %collective-permute-done.18.refs_3_), channel_id=1, source_target_pairs={{0,1},{1,0},{2,3},{3,2},{4,5},{5,4},{6,7},{7,6},{8,9},{9,8},{10,11... | collective-permute-start | bytes 921608 | tf_op jit(solution)/shard_map/ppermute | solution.py:115
  110.1 9.1 %collective-permute-start.32 = (bf16[192,384]{1,0:T(8,128)(2,1)S(1)}, bf16[192,384]{1,0:T(8,128)(2,1)S(1)}, u32[]{:S(2)}, u32[]{:S(2)}) collective-permute-start(bf16[192,384]{1,0:T(8,128)(2,1)S(1)} %pad_maximum_fusion.1.refs_0_), channel_id=1, source_target_pairs={{0,8},{8,0},{16,24},{24,16},{1,9},{9,1},{17,25},{25,17},{2,10},{10... | collective-permute-start | bytes 442376 | tf_op jit(solution)/shard_map/ppermute | solution.py:129
  111.4 7.8 %collective-permute-start.33 = (bf16[192,384]{1,0:T(8,128)(2,1)S(1)}, bf16[192,384]{1,0:T(8,128)(2,1)S(1)}, u32[]{:S(2)}, u32[]{:S(2)}) collective-permute-start(bf16[192,384]{1,0:T(8,128)(2,1)S(1)} %pad_maximum_fusion.1.refs_0_), channel_id=1, source_target_pairs={{0,16},{8,24},{16,0},{24,8},{1,17},{9,25},{17,1},{25,9},{2,18},{10... | collective-permute-start | bytes 442376 | tf_op jit(solution)/shard_map/ppermute | solution.py:129
  112.6 8.0 %collective-permute-start.34 = (bf16[192,384]{1,0:T(8,128)(2,1)S(1)}, bf16[192,384]{1,0:T(8,128)(2,1)S(1)}, u32[]{:S(2)}, u32[]{:S(2)}) collective-permute-start(bf16[192,384]{1,0:T(8,128)(2,1)S(1)} %pad_maximum_fusion.1.refs_0_), channel_id=1, source_target_pairs={{0,24},{8,16},{16,8},{24,0},{1,25},{9,17},{17,9},{25,1},{2,26},{10... | collective-permute-start | bytes 442376 | tf_op jit(solution)/shard_map/ppermute | solution.py:129
  120.5 1.4 %collective-permute-start.35 = (bf16[192,384]{1,0:T(8,128)(2,1)S(1)}, bf16[192,384]{1,0:T(8,128)(2,1)S(1)}, u32[]{:S(2)}, u32[]{:S(2)}) collective-permute-start(bf16[192,384]{1,0:T(8,128)(2,1)S(1)} %pad_maximum_fusion.1.refs_0_), channel_id=1, source_target_pairs={{0,1},{1,0},{2,3},{3,2},{4,5},{5,4},{6,7},{7,6},{8,9},{9,8},{10,11... | collective-permute-start | bytes 442376 | tf_op jit(solution)/shard_map/ppermute | solution.py:115
  120.5 1.6 %collective-permute-start.36 = (bf16[192,384]{1,0:T(8,128)(2,1)S(1)}, bf16[192,384]{1,0:T(8,128)(2,1)S(1)}, u32[]{:S(2)}, u32[]{:S(2)}) collective-permute-start(bf16[192,384]{1,0:T(8,128)(2,1)S(1)} %collective-permute-done.32.refs_1_), channel_id=1, source_target_pairs={{0,1},{1,0},{2,3},{3,2},{4,5},{5,4},{6,7},{7,6},{8,9},{9,8},{10,11... | collective-permute-start | bytes 442376 | tf_op jit(solution)/shard_map/ppermute | solution.py:115
  121.1 1.4 %collective-permute-start.37 = (bf16[192,384]{1,0:T(8,128)(2,1)S(1)}, bf16[192,384]{1,0:T(8,128)(2,1)S(1)}, u32[]{:S(2)}, u32[]{:S(2)}) collective-permute-start(bf16[192,384]{1,0:T(8,128)(2,1)S(1)} %collective-permute-done.33.refs_2_), channel_id=1, source_target_pairs={{0,1},{1,0},{2,3},{3,2},{4,5},{5,4},{6,7},{7,6},{8,9},{9,8},{10,11... | collective-permute-start | bytes 442376 | tf_op jit(solution)/shard_map/ppermute | solution.py:115
  121.1 1.6 %collective-permute-start.38 = (bf16[192,384]{1,0:T(8,128)(2,1)S(1)}, bf16[192,384]{1,0:T(8,128)(2,1)S(1)}, u32[]{:S(2)}, u32[]{:S(2)}) collective-permute-start(bf16[192,384]{1,0:T(8,128)(2,1)S(1)} %collective-permute-done.34.refs_3_), channel_id=1, source_target_pairs={{0,1},{1,0},{2,3},{3,2},{4,5},{5,4},{6,7},{7,6},{8,9},{9,8},{10,11... | collective-permute-start | bytes 442376 | tf_op jit(solution)/shard_map/ppermute | solution.py:115
  (2 other events, 1.3 us)

commit v3 on v2

--- a/solution.py
+++ b/solution.py
@@ -301,7 +301,7 @@
         in_specs=[pl.BlockSpec(memory_space=pltpu.SMEM)] * 3 + [whole(*item.shape) for item in operands],
         out_specs=[whole(*item.shape) for item in shapes],
         out_shape=shapes,
-        compiler_params=kernel_params(12),
+        compiler_params=kernel_params(8),
         name="prepare",
     )(place, lead, counts, *operands)
 
@@ -405,7 +405,7 @@
             jax.ShapeDtypeStruct((rows, width), bf16),
         ],
         scratch_shapes=[pltpu.VMEM((key_count, rows), f32)],
-        compiler_params=kernel_params(20),
+        compiler_params=kernel_params(22),
         cost_estimate=pl.CostEstimate(
             flops=16 * size * head_width, bytes_accessed=2 * size, transcendentals=size
         ),
@@ -431,26 +431,25 @@
     wide = cotangent[...].astype(f32)
     grad_two = (wide * row(GATE_TWO)).astype(bf16)
     sums[...] = jnp.zeros_like(sums)
-    branch_two = jnp.zeros((rows, width), f32) + bias_row(7 + blocks)
-    grad_mixed = jnp.zeros((rows, width), f32)
+    hidden = product(mixed, expand_weight[...]) + bias[:, 7 * width : (7 + blocks) * width]
+    square = hidden * hidden
+    bent = jnp.tanh(GELU_RATE * hidden * (1.0 + GELU_CUBE * square))
+    half = 0.5 + 0.5 * bent
+    slope = half + 0.5 * hidden * (1.0 - bent * bent) * (
+        GELU_RATE + (3.0 * GELU_CUBE * GELU_RATE) * square
+    )
+    active = (hidden * half).astype(bf16)
+    branch_two = product(active, shrink_weight[...]) + bias_row(7 + blocks)
+    grad_hidden = (back_product(grad_two, shrink_weight[...]) * slope).astype(bf16)
+    grad_mixed = back_product(grad_hidden, expand_weight[...])
+    hidden_sum = column_sum(grad_hidden.astype(f32))
     for block in range(blocks):
         part = slice(block * width, (block + 1) * width)
-        hidden = product(mixed, expand_weight[:, part]) + bias_row(7 + block)
-        square = hidden * hidden
-        bent = jnp.tanh(GELU_RATE * hidden * (1.0 + GELU_CUBE * square))
-        half = 0.5 + 0.5 * bent
-        slope = half + 0.5 * hidden * (1.0 - bent * bent) * (
-            GELU_RATE + (3.0 * GELU_CUBE * GELU_RATE) * square
-        )
-        active = (hidden * half).astype(bf16)
-        branch_two = branch_two + product(active, shrink_weight[part, :])
-        grad_hidden = (back_product(grad_two, shrink_weight[part, :]) * slope).astype(bf16)
-        grad_shrink = inner(active, grad_two) * share
-        grad_expand = inner(mixed, grad_hidden) * share
+        grad_shrink = inner(active[:, part], grad_two) * share
+        grad_expand = inner(mixed, grad_hidden[:, part]) * share
         keep[part, :] = jnp.where(first_core, grad_shrink, grad_expand).astype(bf16)
         send[part, :] = jnp.where(first_core, grad_expand, grad_shrink).astype(bf16)
-        sums[7 + block : 8 + block, :] = column_sum(grad_hidden.astype(f32)) * share
-        grad_mixed = grad_mixed + back_product(grad_hidden, expand_weight[:, part])
+        sums[7 + block : 8 + block, :] = hidden_sum[:, part] * share
     result = (residual + row(GATE_TWO) * branch_two).astype(bf16)
     owners, count = output.shape[:2]
     for step in range(owners):
@@ -491,7 +490,7 @@
         in_specs=[pl.BlockSpec(memory_space=pltpu.SMEM)] + [whole(*item.shape) for item in operands],
         out_specs=[whole(*item.shape) for item in shapes],
         out_shape=shapes,
-        compiler_params=kernel_params(16),
+        compiler_params=kernel_params(20),
         cost_estimate=pl.CostEstimate(
             flops=16 * rows * width * hidden, bytes_accessed=2**24, transcendentals=rows * hidden
         ),
@@ -583,9 +582,9 @@
     specs = [whole(*item.shape) for item in operands]
     specs[3] = pl.BlockSpec((2, 1, rows), lambda p: (p, 0, 0))
     shapes = [
+        pltpu.HBM((2 * width, width), bf16),
         jax.ShapeDtypeStruct((2 * width, width), bf16),
-        jax.ShapeDtypeStruct((2 * width, width), bf16),
-        jax.ShapeDtypeStruct((rest.shape[0] + sums.shape[0], width), bf16),
+        pltpu.HBM((rest.shape[0] + sums.shape[0], width), bf16),
         jax.ShapeDtypeStruct((rows, width), bf16),
         jax.ShapeDtypeStruct(sums.shape, f32),
     ]
@@ -641,6 +640,43 @@
     )(*operands)
 
 
+def pair_parts_kernel(grp_size, place, kept, received, *results):
+    count = results[0].shape[0]
+    for step, result in enumerate(results):
+        here = pl.ds(pl.multiple_of(away(place[3], grp_size, step) * count, count), count)
+        result[...] = total([kept[here, :], received[here, :]]).astype(bf16)
+
+
+def pair_parts(place, kept, received):
+    grp_size = lax.axis_size("grp")
+    shape = (kept.shape[0] // grp_size, kept.shape[1])
+    return pl.pallas_call(
+        partial(pair_parts_kernel, grp_size),
+        grid=(1,),
+        in_specs=[pl.BlockSpec(memory_space=pltpu.SMEM)] + [whole(*kept.shape)] * 2,
+        out_specs=[whole(*shape)] * grp_size,
+        out_shape=[jax.ShapeDtypeStruct(shape, bf16)] * grp_size,
+        compiler_params=kernel_params(12),
+        name="pair_parts",
+    )(place, kept, received)
+
+
+def sum_parts_kernel(*refs):
+    refs[-1][...] = total([ref[...] for ref in refs[:-1]]).astype(bf16)
+
+
+def sum_parts(parts):
+    return pl.pallas_call(
+        sum_parts_kernel,
+        grid=(1,),
+        in_specs=[whole(*parts[0].shape)] * len(parts),
+        out_specs=whole(*parts[0].shape),
+        out_shape=jax.ShapeDtypeStruct(parts[0].shape, bf16),
+        compiler_params=kernel_params(8),
+        name="sum_parts",
+    )(*parts)
+
+
 def line_total_kernel(sums, received, *refs):
     parts, result = refs[:-1], refs[-1]
     count = parts[0].shape[-2]
@@ -660,7 +696,7 @@
         in_specs=[whole(*item.shape) for item in [sums, received] + parts],
         out_specs=whole(count + below, width),
         out_shape=jax.ShapeDtypeStruct((count + below, width), bf16),
-        compiler_params=kernel_params(8),
+        compiler_params=kernel_params(4),
         name="line_total",
     )(sums, received, *parts)
 
@@ -814,7 +850,7 @@
             jax.ShapeDtypeStruct((width,), f32),
         ],
         scratch_shapes=[pltpu.VMEM((8, width), f32), pltpu.VMEM((16, width), f32)],
-        compiler_params=kernel_params(20),
+        compiler_params=kernel_params(16),
         name="first_sums",
     )(place, *own, *received, weight, output, *pieces)
 
@@ -822,33 +858,34 @@
 def second_sums_kernel(grp_size, line, place, *refs):
     own, received = refs[:grp_size], refs[grp_size : 2 * grp_size]
     attend, output = refs[2 * grp_size :]
-    b = pl.program_id(0)
-    half = output.shape[0] // 2
-    for target, chosen in ((attend, b < grp_size - 1), (output, b == grp_size - 1)):
-
-        @pl.when(chosen)
-        def _():
-            for side in range(2):
-                write = lambda ref: copy_line(place, line, half // line, ref, target, side * half)
-                picked(place, grp_size, own, received, side, b, write)
+    width = output.shape[0]
+    half = width // 2
+    for group in range(grp_size):
+        for core in range(2):
+
+            @pl.when((place[3] == group) & (place[2] == core))
+            def _():
+                for b in range(grp_size):
+                    step = back(group, grp_size, b)
+                    for side, parts in ((core, own), (1 - core, received)):
+                        if b < grp_size - 1:
+                            target = attend.at[:, b * width : (b + 1) * width]
+                        else:
+                            target = output
+                        copy_line(place, line, half // line, parts[step], target, side * half)
 
 
 def second_sums(place, own):
     grp_size, width = len(own), own[0].shape[1]
     line = 1 if line_size() > 4 else line_size()
     received = [swap_cores(part) for part in own]
+    shapes = [(width, (grp_size - 1) * width), (width, width)]
     return pl.pallas_call(
         partial(second_sums_kernel, grp_size, line),
-        grid=(grp_size,),
+        grid=(1,),
         in_specs=[pl.BlockSpec(memory_space=pltpu.SMEM)] + [whole(*own[0].shape)] * (2 * grp_size),
-        out_specs=[
-            pl.BlockSpec((width, width), lambda b: (0, jnp.minimum(b, grp_size - 2))),
-            whole(width, width),
-        ],
-        out_shape=[
-            jax.ShapeDtypeStruct((width, 3 * width), f32),
-            jax.ShapeDtypeStruct((width, width), f32),
-        ],
+        out_specs=[whole(*shape) for shape in shapes],
+        out_shape=[jax.ShapeDtypeStruct(shape, f32) for shape in shapes],
         compiler_params=kernel_params(16),
         name="second_sums",
     )(place, *own, *received)
@@ -956,7 +993,7 @@
     token_pieces = rows_to_owner(tokens[0], owner, share)
 
     bias = [modulation_bias, output_bias, expand_bias, shrink_bias]
-    bias = jnp.concatenate(bias).astype(f32)[None]
+    bias = after(jnp.concatenate(bias).astype(f32))[None]
     mod, weight = prepare(
         where, lead_index, sample_counts, lead_table, modulation_weight, bias, attend_weight,
         owners * seq_length,
@@ -989,7 +1026,7 @@
         grad_residual, sums,
     )
     at_keep, at_send, rest_part, own_part, sums = after_all(held, *ff_parts[1:], output)
-    ff_plane = low_total(ff_parts)
+    ff_plane = sum_parts(ff_parts)
     line = line_size() <= 4
     if line:
         ff_parts = [line_exchange(ff_plane.reshape(line_size(), -1, width))]

time: 126 us -> 121 us (0.960)
  local copies, waits for them, and re-layouts: 8.1 us -> 5.39 us
    concatenate x4 -> x0, local copies, waits for them, and re-layouts: 2.75 us -> none  [on_device(): bias = jnp.concatenate(bias).astype(f32)[None]]
    ppermute x6, waiting for transfers between devices: 0.52 us -> 2.53 us  [rows_to_owner(): lax.ppermute(block, 'seq', owner_pairs(seq_size, owners, share, step))]
    convert_element_type x4 -> x3, other arithmetic: 5.1 us -> 3.23 us  [low_total(): return total(parts).astype(bf16)]
    pallas_call x1 -> x2, Pallas kernels: 3.01 us -> 3.03 us  [the longest x1 2.17 us: second_sums(): pl.pallas_call(partial(second_sums_kernel, grp_size, line), grid=(1,), in...]
    unnamed x53 -> x51, local copies, waits for them, and re-layouts: 2.99 us -> 2.98 us
  transfers between devices with their start and end apart: 41 -> 41, of which waited for: 12 -> 12; matrix products, arithmetic and copies ran while one was open for 7% -> 4% of each run, Pallas kernels for 22% -> 24%
where the time goes in v3:
time: 121 us
  starting transfers between devices  49.6 us (41%)
  Pallas kernels  40.2 us (33%)
  waiting for transfers between devices  20 us (17%)
  local copies, waits for them, and re-layouts  5.39 us (4%)
  other arithmetic  4.04 us (3%)
  between operations  1.84 us (2%)
    ppermute x12, starting transfers between devices, plane_send(): lax.ppermute(values, 'grp', [(d, away(d, grp_size, step)) for d in range(...  14.2 us
    pallas_call x1, Pallas kernels, backward_attention(): pl.pallas_call(partial(backward_kernel, head_width, 1.0 / math.sqrt(head_...  11.7 us
    ppermute x6, starting transfers between devices, rows_to_owner(): lax.ppermute(block, 'seq', owner_pairs(seq_size, owners, share, step))  10.1 us
    pallas_call x1, Pallas kernels, forward_attention(): pl.pallas_call(partial(forward_kernel, head_width, 1.0 / math.sqrt(head_w...  9.95 us
    ppermute x6, starting transfers between devices, line_send(): lax.ppermute(values, 'seq', owner_pairs(seq_size, seq_size // 2, 2, step))  8.89 us
    pallas_call x1, Pallas kernels, middle(): pl.pallas_call(middle_kernel, grid=(1,), in_specs=[pl.BlockSpec(memory_sp...  8.41 us
    ppermute x3, waiting for transfers between devices, pieces_from_owner(): lax.ppermute(pieces[step], 'seq', owner_pairs(seq_size, owners, share, st...  8.22 us
    pallas_call x1, Pallas kernels, first_sums(): pl.pallas_call(partial(first_sums_kernel, grp_size, line), grid=(grp_size...  5.51 us
  transfers between devices with their start and end apart: 41, of which 12 were waited for; matrix products, arithmetic and copies ran while one was open for 4% of the time, Pallas kernels for 24%

profile of v3, /device:TPU:0, one launch (start us, length us, event | category | flops | bytes accessed | tf_op | source)
XLA Modules:
  0.0 121.0 jit_solution(12219631659130090099)
XLA Ops:
  0.7 1.2 dynamic-slice_bitcast_fusion.4
  1.8 3.1 %collective-permute-start = (bf16[128,384]{1,0:T(8,128)(2,1)S(1)}, bf16[128,384]{1,0:T(8,128)(2,1)S(1)}, u32[]{:S(2)}, u32[]{:S(2)}) collective-permute-start(bf16[128,384]{1,0:T(8,128)(2,1)S(1)} %get-tuple-element.153), channel_id=1, source_target_pairs={{0,2},{1,3},{2,0},{3,1},{4,6},{5,7},{6,4},{7,5},{8,10},{9,11},{10,... | collective-permute-start | bytes 294920 | tf_op jit(solution)/shard_map/ppermute | solution.py:73
  4.9 2.6 %collective-permute-start.1 = (bf16[128,384]{1,0:T(8,128)(2,1)S(1)}, bf16[128,384]{1,0:T(8,128)(2,1)S(1)}, u32[]{:S(2)}, u32[]{:S(2)}) collective-permute-start(bf16[128,384]{1,0:T(8,128)(2,1)S(1)} %get-tuple-element.155), channel_id=1, source_target_pairs={{0,4},{1,5},{2,6},{3,7},{4,0},{5,1},{6,2},{7,3},{8,12},{9,13},{10,... | collective-permute-start | bytes 294920 | tf_op jit(solution)/shard_map/ppermute | solution.py:73
  8.2 0.8 maximum_convert_fusion
  9.0 0.1 stack.17.place
  9.1 1.5 %copy-done = bf16[384,2304]{1,0:T(8,128)(2,1)S(1)} copy-done((bf16[384,2304]{1,0:T(8,128)(2,1)S(1)}, bf16[384,2304]{1,0:T(8,128)(2,1)}, u32[]{:S(2)}) %copy-start) | copy-done | bytes 1769496
  10.5 0.7 copy-done.3
  11.2 0.7 copy-done.4
  11.9 0.9 prepare.1
  12.8 2.5 %collective-permute-done.1 = bf16[128,384]{1,0:T(8,128)(2,1)S(1)} collective-permute-done((bf16[128,384]{1,0:T(8,128)(2,1)S(1)}, bf16[128,384]{1,0:T(8,128)(2,1)S(1)}, u32[]{:S(2)}, u32[]{:S(2)}) %collective-permute-start.1) | collective-permute-done | bytes 98336 | tf_op jit(solution)/shard_map/ppermute | solution.py:73
  15.6 1.7 %collective-permute-start.4 = (bf16[128,384]{1,0:T(8,128)(2,1)S(1)}, bf16[128,384]{1,0:T(8,128)(2,1)S(1)}, u32[]{:S(2)}, u32[]{:S(2)}) collective-permute-start(bf16[128,384]{1,0:T(8,128)(2,1)S(1)} %get-tuple-element.150), channel_id=1, source_target_pairs={{0,2},{1,3},{2,0},{3,1},{4,6},{5,7},{6,4},{7,5},{8,10},{9,11},{10,... | collective-permute-start | bytes 294920 | tf_op jit(solution)/shard_map/ppermute | solution.py:73
  17.3 1.4 %collective-permute-start.5 = (bf16[128,384]{1,0:T(8,128)(2,1)S(1)}, bf16[128,384]{1,0:T(8,128)(2,1)S(1)}, u32[]{:S(2)}, u32[]{:S(2)}) collective-permute-start(bf16[128,384]{1,0:T(8,128)(2,1)S(1)} %get-tuple-element.149), channel_id=1, source_target_pairs={{0,4},{1,5},{2,6},{3,7},{4,0},{5,1},{6,2},{7,3},{8,12},{9,13},{10,... | collective-permute-start | bytes 294920 | tf_op jit(solution)/shard_map/ppermute | solution.py:73
  18.7 1.3 %collective-permute-start.6 = (bf16[128,384]{1,0:T(8,128)(2,1)S(1)}, bf16[128,384]{1,0:T(8,128)(2,1)S(1)}, u32[]{:S(2)}, u32[]{:S(2)}) collective-permute-start(bf16[128,384]{1,0:T(8,128)(2,1)S(1)} %get-tuple-element.148), channel_id=1, source_target_pairs={{0,6},{1,7},{2,4},{3,5},{4,2},{5,3},{6,0},{7,1},{8,14},{9,15},{10,... | collective-permute-start | bytes 294920 | tf_op jit(solution)/shard_map/ppermute | solution.py:73
  20.1 10.0 %forward_attention.1 = (bf16[6,1024,512]{2,1,0:T(8,128)(2,1)}, bf16[384,512]{1,0:T(8,128)(2,1)S(1)}, bf16[768,1024]{1,0:T(8,128)(2,1)S(1)}, f32[384,512]{1,0:T(8...) custom-call(s32[5]{0:T(128)S(1)} %stack.17.place, s32[4,8]{1,0:T(4,128)S(1)} %bitcast.26, ...), custom_call_target="tpu_custom_call" | custom-call | flops 3221225472 | bytes 6291456 | tf_op jit(solution)/shard_map/forward_attention/pallas_call | solution.py:387
  30.2 8.4 %middle.1 = (bf16[1536,384]{1,0:T(8,128)(2,1)S(1)}, bf16[1536,384]{1,0:T(8,128)(2,1)}, bf16[384,384]{1,0:T(8,128)(2,1)}, bf16[384,512]{1,0:T(8,128)(2,1)}, f32[5...) custom-call(s32[5]{0:T(128)S(1)} %stack.17.place, ...), custom_call_target="tpu_custom_call" | custom-call | flops 4831838208 | bytes 16777216 | tf_op jit(solution)/shard_map/middle/pallas_call | solution.py:487
  38.6 0.1 collective-permute-start.7
  38.7 3.8 %all-to-all-start = ((bf16[4,128,384]{2,1,0:T(8,128)(2,1)}), bf16[4,128,384]{2,1,0:T(8,128)(2,1)S(1)}, u32[]{:S(2)}, u32[]{:S(2)}) async-start(bf16[4,128,384]{2,1,0:T(8,128)(2,1)} %get-tuple-element.105), calls=%async_computation | async-start | bytes 786432 | tf_op jit(solution)/shard_map/all_to_all | solution.py:89
  42.5 1.8 %add_convert_fusion = bf16[1536,384]{1,0:T(8,128)(2,1)S(1)} fusion(bf16[1536,384]{1,0:T(8,128)(2,1)} %collective-permute-done.7, bf16[1536,384]{1,0:T(8,128)(2,1)S(1)} %get-tuple-element.94), kind=kLoop, calls=%fused_computation | loop fusion | flops 2359296 | bytes 3538944 | tf_op jit(solution)/shard_map/convert_element_type | solution.py:179
  44.3 1.0 constant_dynamic-slice_fusion.8
  45.3 1.5 %collective-permute-start.8 = (bf16[384,384]{1,0:T(8,128)(2,1)}, bf16[384,384]{1,0:T(8,128)(2,1)S(1)}, u32[]{:S(2)}, u32[]{:S(2)}) collective-permute-start(bf16[384,384]{1,0:T(8,128)(2,1)} %get-tuple-element.143), channel_id=1, source_target_pairs={{0,8},{8,0},{16,24},{24,16},{1,9},{9,1},{17,25},{25,17},{2,10},{10... | collective-permute-start | bytes 884744 | tf_op jit(solution)/shard_map/ppermute | solution.py:129
  46.8 1.5 %collective-permute-start.9 = (bf16[384,384]{1,0:T(8,128)(2,1)}, bf16[384,384]{1,0:T(8,128)(2,1)S(1)}, u32[]{:S(2)}, u32[]{:S(2)}) collective-permute-start(bf16[384,384]{1,0:T(8,128)(2,1)} %get-tuple-element.142), channel_id=1, source_target_pairs={{0,16},{8,24},{16,0},{24,8},{1,17},{9,25},{17,1},{25,9},{2,18},{10... | collective-permute-start | bytes 884744 | tf_op jit(solution)/shard_map/ppermute | solution.py:129
  48.3 0.5 collective-permute-start.10
  48.9 11.7 %backward_attention.1 = (bf16[768,384]{1,0:T(8,128)(2,1)}, bf16[768,384]{1,0:T(8,128)(2,1)S(1)}, bf16[528,384]{1,0:T(8,128)(2,1)}, bf16[512,384]{1,0:T(8,128)(2,1)S(1)}, f32[16,384]{1,0:T(8,128)S(1)}) custom-call(s32[5]{0:T(128)S(1)} %stack.17.place, bf16[6,1024,512]{2,1,0:T(8,128)(2,1)} %get-tuple-element.82.expo, bf16[384,512]{1,0:T(8,128)(2,1)S(1)} %copy-done.20, ...), custom_call_target="tpu_custom_call" | custom-call | flops 6442450944 | bytes 6291456 | tf_op jit(solution)/shard_map/backward_attention/pallas_call | solution.py:591
  60.6 1.7 %collective-permute-done.9.refs_2_ = bf16[384,384]{1,0:T(8,128)(2,1)S(1)} collective-permute-done((bf16[384,384]{1,0:T(8,128)(2,1)}, bf16[384,384]{1,0:T(8,128)(2,1)S(1)}, u32[]{:S(2)}, u32[]{:S(2)}) %collective-permute-start.9) | collective-permute-done | bytes 294944 | tf_op jit(solution)/shard_map/ppermute | solution.py:129
  62.3 0.5 collective-permute-start.11
  62.9 0.9 sum_parts.1
  63.7 4.6 %all-to-all-start.1 = ((bf16[4,96,384]{2,1,0:T(8,128)(2,1)}), bf16[4,96,384]{2,1,0:T(8,128)(2,1)S(1)}, u32[]{:S(2)}, u32[]{:S(2)}) async-start(bf16[4,96,384]{2,1,0:T(8,128)(2,1)} %bitcast.14), calls=%async_computation.1 | async-start | bytes 589824 | tf_op jit(solution)/shard_map/all_to_all | solution.py:169
  68.3 1.4 %add_convert_fusion.1 = bf16[768,384]{1,0:T(8,128)(2,1)S(1)} fusion(bf16[768,384]{1,0:T(8,128)(2,1)} %collective-permute-done.12, bf16[768,384]{1,0:T(8,128)(2,1)} %get-tuple-element.108), kind=kLoop, calls=%fused_computation.1 | loop fusion | flops 1179648 | bytes 1769472 | tf_op jit(solution)/shard_map/convert_element_type | solution.py:179
  69.7 0.1 constant_dynamic-slice_fusion.4
  69.8 1.3 %collective-permute-start.19 = (bf16[192,384]{1,0:T(8,128)(2,1)S(1)}, bf16[192,384]{1,0:T(8,128)(2,1)S(1)}, u32[]{:S(2)}, u32[]{:S(2)}) collective-permute-start(bf16[192,384]{1,0:T(8,128)(2,1)S(1)} %get-tuple-element.146), channel_id=1, source_target_pairs={{0,8},{8,0},{16,24},{24,16},{1,9},{9,1},{17,25},{25,17},{2,10},{10... | collective-permute-start | bytes 442376 | tf_op jit(solution)/shard_map/ppermute | solution.py:129
  71.1 0.8 collective-permute-start.20
  71.9 1.4 %collective-permute-start.21 = (bf16[192,384]{1,0:T(8,128)(2,1)S(1)}, bf16[192,384]{1,0:T(8,128)(2,1)S(1)}, u32[]{:S(2)}, u32[]{:S(2)}) collective-permute-start(bf16[192,384]{1,0:T(8,128)(2,1)S(1)} %get-tuple-element.144), channel_id=1, source_target_pairs={{0,24},{8,16},{16,8},{24,0},{1,25},{9,17},{17,9},{25,1},{2,26},{10... | collective-permute-start | bytes 442376 | tf_op jit(solution)/shard_map/ppermute | solution.py:129
  73.4 4.8 %all-to-all-done.1.refs_0_ = bf16[4,96,384]{2,1,0:T(8,128)(2,1)S(1)} async-done(((bf16[4,96,384]{2,1,0:T(8,128)(2,1)}), bf16[4,96,384]{2,1,0:T(8,128)(2,1)S(1)}, u32[]{:S(2)}, u32[]{:S(2)}) %all-to-all-start.1) | async-done | bytes 294944 | tf_op jit(solution)/shard_map/all_to_all | solution.py:169
  78.2 2.0 %collective-permute-start.14 = (bf16[112,384]{1,0:T(8,128)(2,1)S(1)}, bf16[112,384]{1,0:T(8,128)(2,1)S(1)}, u32[]{:S(2)}, u32[]{:S(2)}) collective-permute-start(bf16[112,384]{1,0:T(8,128)(2,1)S(1)} %line_total.1.refs_0_), channel_id=1, source_target_pairs={{0,4},{1,5},{2,6},{3,7},{4,0},{5,1},{6,2},{7,3},{8,12},{9,13},{10,... | collective-permute-start | bytes 258056 | tf_op jit(solution)/shard_map/ppermute | solution.py:124
  80.2 2.4 %collective-permute-start.15 = (bf16[112,384]{1,0:T(8,128)(2,1)S(1)}, bf16[112,384]{1,0:T(8,128)(2,1)S(1)}, u32[]{:S(2)}, u32[]{:S(2)}) collective-permute-start(bf16[112,384]{1,0:T(8,128)(2,1)S(1)} %line_total.1.refs_0_), channel_id=1, source_target_pairs={{0,6},{1,7},{2,4},{3,5},{4,2},{5,3},{6,0},{7,1},{8,14},{9,15},{10,... | collective-permute-start | bytes 258056 | tf_op jit(solution)/shard_map/ppermute | solution.py:124
  82.6 0.1 add_convert_fusion.2
  82.8 2.0 %collective-permute-start.23 = (bf16[48,384]{1,0:T(8,128)(2,1)S(1)}, bf16[48,384]{1,0:T(8,128)(2,1)S(1)}, u32[]{:S(2)}, u32[]{:S(2)}) collective-permute-start(bf16[48,384]{1,0:T(8,128)(2,1)S(1)} %get-tuple-element.157), channel_id=1, source_target_pairs={{0,4},{1,5},{2,6},{3,7},{4,0},{5,1},{6,2},{7,3},{8,12},{9,13},{10,... | collective-permute-start | bytes 110600 | tf_op jit(solution)/shard_map/ppermute | solution.py:124
  84.8 2.4 %collective-permute-start.24 = (bf16[48,384]{1,0:T(8,128)(2,1)S(1)}, bf16[48,384]{1,0:T(8,128)(2,1)S(1)}, u32[]{:S(2)}, u32[]{:S(2)}) collective-permute-start(bf16[48,384]{1,0:T(8,128)(2,1)S(1)} %get-tuple-element.156), channel_id=1, source_target_pairs={{0,6},{1,7},{2,4},{3,5},{4,2},{5,3},{6,0},{7,1},{8,14},{9,15},{10,... | collective-permute-start | bytes 110600 | tf_op jit(solution)/shard_map/ppermute | solution.py:124
  87.2 0.7 collective-permute-done.14.refs_2_
  87.9 1.3 %collective-permute-start.16 = (bf16[400,384]{1,0:T(8,128)(2,1)S(1)}, bf16[400,384]{1,0:T(8,128)(2,1)S(1)}, u32[]{:S(2)}, u32[]{:S(2)}) collective-permute-start(bf16[400,384]{1,0:T(8,128)(2,1)S(1)} %line_join.1.refs_0_), channel_id=1, source_target_pairs={{0,8},{8,0},{16,24},{24,16},{1,9},{9,1},{17,25},{25,17},{2,10},{10... | collective-permute-start | bytes 921608 | tf_op jit(solution)/shard_map/ppermute | solution.py:129
  89.2 0.8 collective-permute-start.17
  90.0 1.4 %collective-permute-start.18 = (bf16[400,384]{1,0:T(8,128)(2,1)S(1)}, bf16[400,384]{1,0:T(8,128)(2,1)S(1)}, u32[]{:S(2)}, u32[]{:S(2)}) collective-permute-start(bf16[400,384]{1,0:T(8,128)(2,1)S(1)} %line_join.1.refs_0_), channel_id=1, source_target_pairs={{0,24},{8,16},{16,8},{24,0},{1,25},{9,17},{17,9},{25,1},{2,26},{10... | collective-permute-start | bytes 921608 | tf_op jit(solution)/shard_map/ppermute | solution.py:129
  91.5 0.6 finish_rows.1
  92.1 2.1 %collective-permute-start.25 = (bf16[176,384]{1,0:T(8,128)(2,1)S(1)}, bf16[176,384]{1,0:T(8,128)(2,1)S(1)}, u32[]{:S(2)}, u32[]{:S(2)}) collective-permute-start(bf16[176,384]{1,0:T(8,128)(2,1)S(1)} %get-tuple-element.117), channel_id=1, source_target_pairs={{0,2},{1,3},{2,0},{3,1},{4,6},{5,7},{6,4},{7,5},{8,10},{9,11},{10,... | collective-permute-start | bytes 405512 | tf_op jit(solution)/shard_map/ppermute | solution.py:81
  94.2 0.8 collective-permute-start.26
  95.0 3.6 %collective-permute-done.25.refs_11_ = bf16[176,384]{1,0:T(8,128)(2,1)S(1)} collective-permute-done((bf16[176,384]{1,0:T(8,128)(2,1)S(1)}, bf16[176,384]{1,0:T(8,128)(2,1)S(1)}, u32[]{:S(2)}, u32[]{:S(2)}) %collective-permute-start.25) | collective-permute-done | bytes 135200 | tf_op jit(solution)/shard_map/ppermute | solution.py:81
  98.7 2.3 %collective-permute-start.27 = (bf16[176,384]{1,0:T(8,128)(2,1)S(1)}, bf16[176,384]{1,0:T(8,128)(2,1)S(1)}, u32[]{:S(2)}, u32[]{:S(2)}) collective-permute-start(bf16[176,384]{1,0:T(8,128)(2,1)S(1)} %get-tuple-element.119), channel_id=1, source_target_pairs={{0,6},{1,7},{2,4},{3,5},{4,2},{5,3},{6,0},{7,1},{8,14},{9,15},{10,... | collective-permute-start | bytes 405512 | tf_op jit(solution)/shard_map/ppermute | solution.py:81
  101.0 0.6 collective-permute-done.26.refs_12_
  101.6 4.0 %collective-permute-done.27.refs_13_ = bf16[176,384]{1,0:T(8,128)(2,1)S(1)} collective-permute-done((bf16[176,384]{1,0:T(8,128)(2,1)S(1)}, bf16[176,384]{1,0:T(8,128)(2,1)S(1)}, u32[]{:S(2)}, u32[]{:S(2)}) %collective-permute-start.27) | collective-permute-done | bytes 135200 | tf_op jit(solution)/shard_map/ppermute | solution.py:81
  105.7 0.5 collective-permute-start.29
  106.2 0.1 collective-permute-start.30
  106.2 0.4 collective-permute-start.31
  106.7 1.3 %collective-permute-start.32 = (bf16[192,384]{1,0:T(8,128)(2,1)S(1)}, bf16[192,384]{1,0:T(8,128)(2,1)S(1)}, u32[]{:S(2)}, u32[]{:S(2)}) collective-permute-start(bf16[192,384]{1,0:T(8,128)(2,1)S(1)} %pad_maximum_fusion.1.refs_0_), channel_id=1, source_target_pairs={{0,8},{8,0},{16,24},{24,16},{1,9},{9,1},{17,25},{25,17},{2,10},{10... | collective-permute-start | bytes 442376 | tf_op jit(solution)/shard_map/ppermute | solution.py:129
  108.0 0.8 collective-permute-start.33
  108.9 1.4 %collective-permute-start.34 = (bf16[192,384]{1,0:T(8,128)(2,1)S(1)}, bf16[192,384]{1,0:T(8,128)(2,1)S(1)}, u32[]{:S(2)}, u32[]{:S(2)}) collective-permute-start(bf16[192,384]{1,0:T(8,128)(2,1)S(1)} %pad_maximum_fusion.1.refs_0_), channel_id=1, source_target_pairs={{0,24},{8,16},{16,8},{24,0},{1,25},{9,17},{17,9},{25,1},{2,26},{10... | collective-permute-start | bytes 442376 | tf_op jit(solution)/shard_map/ppermute | solution.py:129
  110.3 5.5 %first_sums.1 = (f32[1536,384]{1,0:T(8,128)}, f32[384,1536]{1,0:T(8,128)}, f32[384,2304]{1,0:T(8,128)}, bf16[4,128,384]{2,1,0:T(8,128)(2,1)}, f32[4,128,384]{2,1...) custom-call(s32[5]{0:T(128)S(1)} %stack.17.place, ...), custom_call_target="tpu_custom_call" | custom-call | tf_op jit(solution)/shard_map/first_sums/pallas_call | solution.py:821
  115.8 0.9 collective-permute-done.34.refs_3_
  116.8 0.5 collective-permute-start.36
  117.3 0.5 collective-permute-start.38
  117.8 0.3 collective-permute-done.35.refs_4_
  118.1 0.2 collective-permute-done.36.refs_5_
  118.3 0.3 collective-permute-done.37.refs_6_
  118.6 0.2 collective-permute-done.38.refs_7_
  118.8 2.2 %second_sums.1 = (f32[384,1152]{1,0:T(8,128)}, f32[384,384]{1,0:T(8,128)}) custom-call(s32[5]{0:T(128)S(1)} %stack.17.place, bf16[192,384]{1,0:T(8,128)(2,1)S(1)} %pad_maximum_fusion.1.refs_0_, bf16[192,384]{1,0:T(8,128)(2,1)S(1)} %collective-permute-done.32.refs_1_, bf16[192,384]{1,0:T(8,128)(2,1)S(1)} %collective-permute-done.33.refs_2_, ...), custom_call_target="tpu_custom_call" | custom-call | tf_op jit(solution)/shard_map/second_sums/pallas_call | solution.py:883
  (97 shorter events, 0.8 us)
Async XLA Ops:
  0.6 8.4 %copy-start.2 = (bf16[384,1152]{1,0:T(8,128)(2,1)S(1)}, bf16[384,1152]{1,0:T(8,128)(2,1)}, u32[]{:S(2)}) copy-start(bf16[384,1152]{1,0:T(8,128)(2,1)} %attend_weight.1) | copy-start | bytes 2654212
  1.8 11.0 %collective-permute-start = (bf16[128,384]{1,0:T(8,128)(2,1)S(1)}, bf16[128,384]{1,0:T(8,128)(2,1)S(1)}, u32[]{:S(2)}, u32[]{:S(2)}) collective-permute-start(bf16[128,384]{1,0:T(8,128)(2,1)S(1)} %get-tuple-element.153), channel_id=1, source_target_pairs={{0,2},{1,3},{2,0},{3,1},{4,6},{5,7},{6,4},{7,5},{8,10},{9,11},{10,... | collective-permute-start | bytes 294920 | tf_op jit(solution)/shard_map/ppermute | solution.py:73
  4.9 10.4 %collective-permute-start.1 = (bf16[128,384]{1,0:T(8,128)(2,1)S(1)}, bf16[128,384]{1,0:T(8,128)(2,1)S(1)}, u32[]{:S(2)}, u32[]{:S(2)}) collective-permute-start(bf16[128,384]{1,0:T(8,128)(2,1)S(1)} %get-tuple-element.155), channel_id=1, source_target_pairs={{0,4},{1,5},{2,6},{3,7},{4,0},{5,1},{6,2},{7,3},{8,12},{9,13},{10,... | collective-permute-start | bytes 294920 | tf_op jit(solution)/shard_map/ppermute | solution.py:73
  7.5 7.8 %collective-permute-start.2 = (bf16[128,384]{1,0:T(8,128)(2,1)S(1)}, bf16[128,384]{1,0:T(8,128)(2,1)S(1)}, u32[]{:S(2)}, u32[]{:S(2)}) collective-permute-start(bf16[128,384]{1,0:T(8,128)(2,1)S(1)} %get-tuple-element.152), channel_id=1, source_target_pairs={{0,6},{1,7},{2,4},{3,5},{4,2},{5,3},{6,0},{7,1},{8,14},{9,15},{10,... | collective-permute-start | bytes 294920 | tf_op jit(solution)/shard_map/ppermute | solution.py:73
  9.0 1.5 %copy-start = (bf16[384,2304]{1,0:T(8,128)(2,1)S(1)}, bf16[384,2304]{1,0:T(8,128)(2,1)}, u32[]{:S(2)}) copy-start(bf16[384,2304]{1,0:T(8,128)(2,1)} %refs_8_.1) | copy-start | bytes 5308420
  10.5 0.7 copy-start.3
  11.9 3.7 %copy-start.23 = (bf16[1,4,128,384]{3,2,1,0:T(8,128)(2,1)S(1)}, bf16[1,4,128,384]{3,2,1,0:T(8,128)(2,1)}, u32[]{:S(2)}) copy-start(bf16[1,4,128,384]{3,2,1,0:T(8,128)(2,1)} %param.17) | copy-start | bytes 1179652
  12.8 17.3 %copy-start.7 = (bf16[1152,384]{1,0:T(8,128)(2,1)}, bf16[1152,384]{1,0:T(8,128)(2,1)S(1)}, u32[]{:S(2)}) copy-start(bf16[1152,384]{1,0:T(8,128)(2,1)S(1)} %get-tuple-element.81.weight) | copy-start | bytes 2654212
  12.8 7.3 %copy-start.12 = (s32[1,4,1024]{2,1,0:T(4,128)S(1)}, s32[1,4,1024]{2,1,0:T(4,128)}, u32[]{:S(2)}) copy-start(s32[1,4,1024]{2,1,0:T(4,128)} %param.19) | copy-start | bytes 49156
  12.8 7.3 %copy-start.13 = (s32[1,4,8]{2,1,0:T(4,128)S(1)}, s32[1,4,8]{2,1,0:T(4,128)}, u32[]{:S(2)}) copy-start(s32[1,4,8]{2,1,0:T(4,128)} %param.18) | copy-start | bytes 388
  15.5 4.6 %collective-permute-start.3 = (bf16[512,384]{1,0:T(8,128)(2,1)S(1)}, bf16[512,384]{1,0:T(8,128)(2,1)S(1)}, u32[]{:S(2)}, u32[]{:S(2)}) collective-permute-start(bf16[512,384]{1,0:T(8,128)(2,1)S(1)} %constant_dynamic-update-slice_fusion.own), channel_id=1, source_target_pairs={{0,1},{1,0},{2,3},{3,2},{4,5},{5,4},{6,7},{7,6},{8,9},{9,8},{10,11... | collective-permute-start | bytes 1179656 | tf_op jit(solution)/shard_map/ppermute | solution.py:95
  15.6 14.5 %collective-permute-start.4 = (bf16[128,384]{1,0:T(8,128)(2,1)S(1)}, bf16[128,384]{1,0:T(8,128)(2,1)S(1)}, u32[]{:S(2)}, u32[]{:S(2)}) collective-permute-start(bf16[128,384]{1,0:T(8,128)(2,1)S(1)} %get-tuple-element.150), channel_id=1, source_target_pairs={{0,2},{1,3},{2,0},{3,1},{4,6},{5,7},{6,4},{7,5},{8,10},{9,11},{10,... | collective-permute-start | bytes 294920 | tf_op jit(solution)/shard_map/ppermute | solution.py:73
  17.3 12.8 %collective-permute-start.5 = (bf16[128,384]{1,0:T(8,128)(2,1)S(1)}, bf16[128,384]{1,0:T(8,128)(2,1)S(1)}, u32[]{:S(2)}, u32[]{:S(2)}) collective-permute-start(bf16[128,384]{1,0:T(8,128)(2,1)S(1)} %get-tuple-element.149), channel_id=1, source_target_pairs={{0,4},{1,5},{2,6},{3,7},{4,0},{5,1},{6,2},{7,3},{8,12},{9,13},{10,... | collective-permute-start | bytes 294920 | tf_op jit(solution)/shard_map/ppermute | solution.py:73
  18.7 11.4 %collective-permute-start.6 = (bf16[128,384]{1,0:T(8,128)(2,1)S(1)}, bf16[128,384]{1,0:T(8,128)(2,1)S(1)}, u32[]{:S(2)}, u32[]{:S(2)}) collective-permute-start(bf16[128,384]{1,0:T(8,128)(2,1)S(1)} %get-tuple-element.148), channel_id=1, source_target_pairs={{0,6},{1,7},{2,4},{3,5},{4,2},{5,3},{6,0},{7,1},{8,14},{9,15},{10,... | collective-permute-start | bytes 294920 | tf_op jit(solution)/shard_map/ppermute | solution.py:73
  20.1 10.0 %copy-start.9 = (bf16[512,384]{1,0:T(8,128)(2,1)}, bf16[512,384]{1,0:T(8,128)(2,1)S(1)}, u32[]{:S(2)}) copy-start(bf16[512,384]{1,0:T(8,128)(2,1)S(1)} %collective-permute-done.3.rest) | copy-start | bytes 1179652
  20.1 10.1 %copy-start.5 = (bf16[384,1536]{1,0:T(8,128)(2,1)S(1)}, bf16[384,1536]{1,0:T(8,128)(2,1)}, u32[]{:S(2)}) copy-start(bf16[384,1536]{1,0:T(8,128)(2,1)} %expand_weight.1) | copy-start | bytes 3538948
  20.1 10.1 %copy-start.6 = (bf16[1536,384]{1,0:T(8,128)(2,1)S(1)}, bf16[1536,384]{1,0:T(8,128)(2,1)}, u32[]{:S(2)}) copy-start(bf16[1536,384]{1,0:T(8,128)(2,1)} %shrink_weight.1) | copy-start | bytes 3538948
  20.1 10.1 %copy-start.11 = (bf16[384,384]{1,0:T(8,128)(2,1)S(1)}, bf16[384,384]{1,0:T(8,128)(2,1)}, u32[]{:S(2)}) copy-start(bf16[384,384]{1,0:T(8,128)(2,1)} %output_weight.1) | copy-start | bytes 884740
  30.1 8.6 %copy-start.14 = (bf16[768,1024]{1,0:T(8,128)(2,1)}, bf16[768,1024]{1,0:T(8,128)(2,1)S(1)}, u32[]{:S(2)}) copy-start(bf16[768,1024]{1,0:T(8,128)(2,1)S(1)} %get-tuple-element.84.key_value) | copy-start | bytes 4718596
  30.1 8.6 %copy-start.16 = (f32[384,512]{1,0:T(8,128)}, f32[384,512]{1,0:T(8,128)S(1)}, u32[]{:S(2)}) copy-start(f32[384,512]{1,0:T(8,128)S(1)} %get-tuple-element.85.attended_wide) | copy-start | bytes 2359300
  30.1 8.5 %copy-start.19 = (bf16[384,512]{1,0:T(8,128)(2,1)}, bf16[384,512]{1,0:T(8,128)(2,1)S(1)}, u32[]{:S(2)}) copy-start(bf16[384,512]{1,0:T(8,128)(2,1)S(1)} %get-tuple-element.83.query) | copy-start | bytes 1179652
  38.6 3.9 %collective-permute-start.7 = (bf16[1536,384]{1,0:T(8,128)(2,1)}, bf16[1536,384]{1,0:T(8,128)(2,1)}, u32[]{:S(2)}, u32[]{:S(2)}) collective-permute-start(bf16[1536,384]{1,0:T(8,128)(2,1)} %get-tuple-element.95), channel_id=1, source_target_pairs={{0,1},{1,0},{2,3},{3,2},{4,5},{5,4},{6,7},{7,6},{8,9},{9,8},{10,11... | collective-permute-start | bytes 3538952 | tf_op jit(solution)/shard_map/ppermute | solution.py:115
  38.7 21.8 %all-to-all-start = ((bf16[4,128,384]{2,1,0:T(8,128)(2,1)}), bf16[4,128,384]{2,1,0:T(8,128)(2,1)S(1)}, u32[]{:S(2)}, u32[]{:S(2)}) async-start(bf16[4,128,384]{2,1,0:T(8,128)(2,1)} %get-tuple-element.105), calls=%async_computation | async-start | bytes 786432 | tf_op jit(solution)/shard_map/all_to_all | solution.py:89
  42.5 6.3 %copy-start.15 = (bf16[768,1024]{1,0:T(8,128)(2,1)S(1)}, bf16[768,1024]{1,0:T(8,128)(2,1)}, u32[]{:S(2)}) copy-start(bf16[768,1024]{1,0:T(8,128)(2,1)} %copy-done.14) | copy-start | bytes 4718596
  42.5 6.3 %copy-start.18 = (f32[512,384]{1,0:T(8,128)S(1)}, f32[512,384]{1,0:T(8,128)}, u32[]{:S(2)}) copy-start(f32[512,384]{1,0:T(8,128)} %get-tuple-element.98.grad_residual) | copy-start | bytes 2359300
  42.5 6.3 %copy-start.20 = (bf16[384,512]{1,0:T(8,128)(2,1)S(1)}, bf16[384,512]{1,0:T(8,128)(2,1)}, u32[]{:S(2)}) copy-start(bf16[384,512]{1,0:T(8,128)(2,1)} %copy-done.19) | copy-start | bytes 1179652
  42.5 6.3 %copy-start.21 = (bf16[384,512]{1,0:T(8,128)(2,1)S(1)}, bf16[384,512]{1,0:T(8,128)(2,1)}, u32[]{:S(2)}) copy-start(bf16[384,512]{1,0:T(8,128)(2,1)} %get-tuple-element.96.grad_attended) | copy-start | bytes 1179652
  44.3 4.5 %copy-start.8 = (bf16[1152,384]{1,0:T(8,128)(2,1)S(1)}, bf16[1152,384]{1,0:T(8,128)(2,1)}, u32[]{:S(2)}) copy-start(bf16[1152,384]{1,0:T(8,128)(2,1)} %copy-done.7) | copy-start | bytes 2654212
  44.3 4.5 %copy-start.10 = (bf16[512,384]{1,0:T(8,128)(2,1)S(1)}, bf16[512,384]{1,0:T(8,128)(2,1)}, u32[]{:S(2)}) copy-start(bf16[512,384]{1,0:T(8,128)(2,1)} %copy-done.9) | copy-start | bytes 1179652
  44.3 4.5 %copy-start.17 = (f32[384,512]{1,0:T(8,128)S(1)}, f32[384,512]{1,0:T(8,128)}, u32[]{:S(2)}) copy-start(f32[384,512]{1,0:T(8,128)} %copy-done.16) | copy-start | bytes 2359300
  44.3 4.5 %copy-start.22 = (bf16[384,384]{1,0:T(8,128)(2,1)S(1)}, bf16[384,384]{1,0:T(8,128)(2,1)}, u32[]{:S(2)}) copy-start(bf16[384,384]{1,0:T(8,128)(2,1)} %get-tuple-element.97.packed_output) | copy-start | bytes 884740
  45.3 15.3 %collective-permute-start.8 = (bf16[384,384]{1,0:T(8,128)(2,1)}, bf16[384,384]{1,0:T(8,128)(2,1)S(1)}, u32[]{:S(2)}, u32[]{:S(2)}) collective-permute-start(bf16[384,384]{1,0:T(8,128)(2,1)} %get-tuple-element.143), channel_id=1, source_target_pairs={{0,8},{8,0},{16,24},{24,16},{1,9},{9,1},{17,25},{25,17},{2,10},{10... | collective-permute-start | bytes 884744 | tf_op jit(solution)/shard_map/ppermute | solution.py:129
  46.8 15.5 %collective-permute-start.9 = (bf16[384,384]{1,0:T(8,128)(2,1)}, bf16[384,384]{1,0:T(8,128)(2,1)S(1)}, u32[]{:S(2)}, u32[]{:S(2)}) collective-permute-start(bf16[384,384]{1,0:T(8,128)(2,1)} %get-tuple-element.142), channel_id=1, source_target_pairs={{0,16},{8,24},{16,0},{24,8},{1,17},{9,25},{17,1},{25,9},{2,18},{10... | collective-permute-start | bytes 884744 | tf_op jit(solution)/shard_map/ppermute | solution.py:129
  48.3 14.0 %collective-permute-start.10 = (bf16[384,384]{1,0:T(8,128)(2,1)}, bf16[384,384]{1,0:T(8,128)(2,1)S(1)}, u32[]{:S(2)}, u32[]{:S(2)}) collective-permute-start(bf16[384,384]{1,0:T(8,128)(2,1)} %get-tuple-element.141), channel_id=1, source_target_pairs={{0,24},{8,16},{16,8},{24,0},{1,25},{9,17},{17,9},{25,1},{2,26},{10... | collective-permute-start | bytes 884744 | tf_op jit(solution)/shard_map/ppermute | solution.py:129
  62.3 6.0 %collective-permute-start.12 = (bf16[768,384]{1,0:T(8,128)(2,1)S(1)}, bf16[768,384]{1,0:T(8,128)(2,1)}, u32[]{:S(2)}, u32[]{:S(2)}) collective-permute-start(bf16[768,384]{1,0:T(8,128)(2,1)S(1)} %get-tuple-element.109), channel_id=1, source_target_pairs={{0,1},{1,0},{2,3},{3,2},{4,5},{5,4},{6,7},{7,6},{8,9},{9,8},{10,11... | collective-permute-start | bytes 1769480 | tf_op jit(solution)/shard_map/ppermute | solution.py:115
  62.3 15.8 %collective-permute-start.11 = (bf16[528,384]{1,0:T(8,128)(2,1)}, bf16[528,384]{1,0:T(8,128)(2,1)S(1)}, u32[]{:S(2)}, u32[]{:S(2)}) collective-permute-start(bf16[528,384]{1,0:T(8,128)(2,1)} %get-tuple-element.107), channel_id=1, source_target_pairs={{0,1},{1,0},{2,3},{3,2},{4,5},{5,4},{6,7},{7,6},{8,9},{9,8},{10,11... | collective-permute-start | bytes 1216520 | tf_op jit(solution)/shard_map/ppermute | solution.py:115
  63.7 14.4 %all-to-all-start.1 = ((bf16[4,96,384]{2,1,0:T(8,128)(2,1)}), bf16[4,96,384]{2,1,0:T(8,128)(2,1)S(1)}, u32[]{:S(2)}, u32[]{:S(2)}) async-start(bf16[4,96,384]{2,1,0:T(8,128)(2,1)} %bitcast.14), calls=%async_computation.1 | async-start | bytes 589824 | tf_op jit(solution)/shard_map/all_to_all | solution.py:169
  69.8 10.4 %collective-permute-start.19 = (bf16[192,384]{1,0:T(8,128)(2,1)S(1)}, bf16[192,384]{1,0:T(8,128)(2,1)S(1)}, u32[]{:S(2)}, u32[]{:S(2)}) collective-permute-start(bf16[192,384]{1,0:T(8,128)(2,1)S(1)} %get-tuple-element.146), channel_id=1, source_target_pairs={{0,8},{8,0},{16,24},{24,16},{1,9},{9,1},{17,25},{25,17},{2,10},{10... | collective-permute-start | bytes 442376 | tf_op jit(solution)/shard_map/ppermute | solution.py:129
  71.1 11.5 %collective-permute-start.20 = (bf16[192,384]{1,0:T(8,128)(2,1)S(1)}, bf16[192,384]{1,0:T(8,128)(2,1)S(1)}, u32[]{:S(2)}, u32[]{:S(2)}) collective-permute-start(bf16[192,384]{1,0:T(8,128)(2,1)S(1)} %get-tuple-element.145), channel_id=1, source_target_pairs={{0,16},{8,24},{16,0},{24,8},{1,17},{9,25},{17,1},{25,9},{2,18},{10... | collective-permute-start | bytes 442376 | tf_op jit(solution)/shard_map/ppermute | solution.py:129
  71.9 10.7 %collective-permute-start.21 = (bf16[192,384]{1,0:T(8,128)(2,1)S(1)}, bf16[192,384]{1,0:T(8,128)(2,1)S(1)}, u32[]{:S(2)}, u32[]{:S(2)}) collective-permute-start(bf16[192,384]{1,0:T(8,128)(2,1)S(1)} %get-tuple-element.144), channel_id=1, source_target_pairs={{0,24},{8,16},{16,8},{24,0},{1,25},{9,17},{17,9},{25,1},{2,26},{10... | collective-permute-start | bytes 442376 | tf_op jit(solution)/shard_map/ppermute | solution.py:129
  78.2 6.6 %collective-permute-start.13 = (bf16[112,384]{1,0:T(8,128)(2,1)S(1)}, bf16[112,384]{1,0:T(8,128)(2,1)S(1)}, u32[]{:S(2)}, u32[]{:S(2)}) collective-permute-start(bf16[112,384]{1,0:T(8,128)(2,1)S(1)} %line_total.1.refs_0_), channel_id=1, source_target_pairs={{0,2},{1,3},{2,0},{3,1},{4,6},{5,7},{6,4},{7,5},{8,10},{9,11},{10,... | collective-permute-start | bytes 258056 | tf_op jit(solution)/shard_map/ppermute | solution.py:124
  78.2 9.6 %collective-permute-start.14 = (bf16[112,384]{1,0:T(8,128)(2,1)S(1)}, bf16[112,384]{1,0:T(8,128)(2,1)S(1)}, u32[]{:S(2)}, u32[]{:S(2)}) collective-permute-start(bf16[112,384]{1,0:T(8,128)(2,1)S(1)} %line_total.1.refs_0_), channel_id=1, source_target_pairs={{0,4},{1,5},{2,6},{3,7},{4,0},{5,1},{6,2},{7,3},{8,12},{9,13},{10,... | collective-permute-start | bytes 258056 | tf_op jit(solution)/shard_map/ppermute | solution.py:124
  80.2 7.7 %collective-permute-start.15 = (bf16[112,384]{1,0:T(8,128)(2,1)S(1)}, bf16[112,384]{1,0:T(8,128)(2,1)S(1)}, u32[]{:S(2)}, u32[]{:S(2)}) collective-permute-start(bf16[112,384]{1,0:T(8,128)(2,1)S(1)} %line_total.1.refs_0_), channel_id=1, source_target_pairs={{0,6},{1,7},{2,4},{3,5},{4,2},{5,3},{6,0},{7,1},{8,14},{9,15},{10,... | collective-permute-start | bytes 258056 | tf_op jit(solution)/shard_map/ppermute | solution.py:124
  82.7 7.3 %collective-permute-start.22 = (bf16[48,384]{1,0:T(8,128)(2,1)S(1)}, bf16[48,384]{1,0:T(8,128)(2,1)S(1)}, u32[]{:S(2)}, u32[]{:S(2)}) collective-permute-start(bf16[48,384]{1,0:T(8,128)(2,1)S(1)} %get-tuple-element.158), channel_id=1, source_target_pairs={{0,2},{1,3},{2,0},{3,1},{4,6},{5,7},{6,4},{7,5},{8,10},{9,11},{10,... | collective-permute-start | bytes 110600 | tf_op jit(solution)/shard_map/ppermute | solution.py:124
  82.8 8.7 %collective-permute-start.23 = (bf16[48,384]{1,0:T(8,128)(2,1)S(1)}, bf16[48,384]{1,0:T(8,128)(2,1)S(1)}, u32[]{:S(2)}, u32[]{:S(2)}) collective-permute-start(bf16[48,384]{1,0:T(8,128)(2,1)S(1)} %get-tuple-element.157), channel_id=1, source_target_pairs={{0,4},{1,5},{2,6},{3,7},{4,0},{5,1},{6,2},{7,3},{8,12},{9,13},{10,... | collective-permute-start | bytes 110600 | tf_op jit(solution)/shard_map/ppermute | solution.py:124
  84.8 25.5 %copy-start.1 = (bf16[384,2304]{1,0:T(8,128)(2,1)S(1)}, bf16[384,2304]{1,0:T(8,128)(2,1)}, u32[]{:S(2)}) copy-start(bf16[384,2304]{1,0:T(8,128)(2,1)} %refs_8_.1) | copy-start | bytes 5308420
  84.8 6.7 %collective-permute-start.24 = (bf16[48,384]{1,0:T(8,128)(2,1)S(1)}, bf16[48,384]{1,0:T(8,128)(2,1)S(1)}, u32[]{:S(2)}, u32[]{:S(2)}) collective-permute-start(bf16[48,384]{1,0:T(8,128)(2,1)S(1)} %get-tuple-element.156), channel_id=1, source_target_pairs={{0,6},{1,7},{2,4},{3,5},{4,2},{5,3},{6,0},{7,1},{8,14},{9,15},{10,... | collective-permute-start | bytes 110600 | tf_op jit(solution)/shard_map/ppermute | solution.py:124
  87.9 17.6 %collective-permute-start.16 = (bf16[400,384]{1,0:T(8,128)(2,1)S(1)}, bf16[400,384]{1,0:T(8,128)(2,1)S(1)}, u32[]{:S(2)}, u32[]{:S(2)}) collective-permute-start(bf16[400,384]{1,0:T(8,128)(2,1)S(1)} %line_join.1.refs_0_), channel_id=1, source_target_pairs={{0,8},{8,0},{16,24},{24,16},{1,9},{9,1},{17,25},{25,17},{2,10},{10... | collective-permute-start | bytes 921608 | tf_op jit(solution)/shard_map/ppermute | solution.py:129
  89.2 16.4 %collective-permute-start.17 = (bf16[400,384]{1,0:T(8,128)(2,1)S(1)}, bf16[400,384]{1,0:T(8,128)(2,1)S(1)}, u32[]{:S(2)}, u32[]{:S(2)}) collective-permute-start(bf16[400,384]{1,0:T(8,128)(2,1)S(1)} %line_join.1.refs_0_), channel_id=1, source_target_pairs={{0,16},{8,24},{16,0},{24,8},{1,17},{9,25},{17,1},{25,9},{2,18},{10... | collective-permute-start | bytes 921608 | tf_op jit(solution)/shard_map/ppermute | solution.py:129
  90.0 15.5 %collective-permute-start.18 = (bf16[400,384]{1,0:T(8,128)(2,1)S(1)}, bf16[400,384]{1,0:T(8,128)(2,1)S(1)}, u32[]{:S(2)}, u32[]{:S(2)}) collective-permute-start(bf16[400,384]{1,0:T(8,128)(2,1)S(1)} %line_join.1.refs_0_), channel_id=1, source_target_pairs={{0,24},{8,16},{16,8},{24,0},{1,25},{9,17},{17,9},{25,1},{2,26},{10... | collective-permute-start | bytes 921608 | tf_op jit(solution)/shard_map/ppermute | solution.py:129
  92.1 6.6 %collective-permute-start.25 = (bf16[176,384]{1,0:T(8,128)(2,1)S(1)}, bf16[176,384]{1,0:T(8,128)(2,1)S(1)}, u32[]{:S(2)}, u32[]{:S(2)}) collective-permute-start(bf16[176,384]{1,0:T(8,128)(2,1)S(1)} %get-tuple-element.117), channel_id=1, source_target_pairs={{0,2},{1,3},{2,0},{3,1},{4,6},{5,7},{6,4},{7,5},{8,10},{9,11},{10,... | collective-permute-start | bytes 405512 | tf_op jit(solution)/shard_map/ppermute | solution.py:81
  94.2 7.4 %collective-permute-start.26 = (bf16[176,384]{1,0:T(8,128)(2,1)S(1)}, bf16[176,384]{1,0:T(8,128)(2,1)S(1)}, u32[]{:S(2)}, u32[]{:S(2)}) collective-permute-start(bf16[176,384]{1,0:T(8,128)(2,1)S(1)} %get-tuple-element.118), channel_id=1, source_target_pairs={{0,4},{1,5},{2,6},{3,7},{4,0},{5,1},{6,2},{7,3},{8,12},{9,13},{10,... | collective-permute-start | bytes 405512 | tf_op jit(solution)/shard_map/ppermute | solution.py:81
  98.7 6.9 %collective-permute-start.27 = (bf16[176,384]{1,0:T(8,128)(2,1)S(1)}, bf16[176,384]{1,0:T(8,128)(2,1)S(1)}, u32[]{:S(2)}, u32[]{:S(2)}) collective-permute-start(bf16[176,384]{1,0:T(8,128)(2,1)S(1)} %get-tuple-element.119), channel_id=1, source_target_pairs={{0,6},{1,7},{2,4},{3,5},{4,2},{5,3},{6,0},{7,1},{8,14},{9,15},{10,... | collective-permute-start | bytes 405512 | tf_op jit(solution)/shard_map/ppermute | solution.py:81
  105.6 2.5 %collective-permute-start.28 = (bf16[400,384]{1,0:T(8,128)(2,1)S(1)}, bf16[400,384]{1,0:T(8,128)(2,1)S(1)}, u32[]{:S(2)}, u32[]{:S(2)}) collective-permute-start(bf16[400,384]{1,0:T(8,128)(2,1)S(1)} %line_join.1.refs_0_), channel_id=1, source_target_pairs={{0,1},{1,0},{2,3},{3,2},{4,5},{5,4},{6,7},{7,6},{8,9},{9,8},{10,11... | collective-permute-start | bytes 921608 | tf_op jit(solution)/shard_map/ppermute | solution.py:115
  105.7 3.2 %collective-permute-start.29 = (bf16[400,384]{1,0:T(8,128)(2,1)S(1)}, bf16[400,384]{1,0:T(8,128)(2,1)S(1)}, u32[]{:S(2)}, u32[]{:S(2)}) collective-permute-start(bf16[400,384]{1,0:T(8,128)(2,1)S(1)} %collective-permute-done.16.refs_1_), channel_id=1, source_target_pairs={{0,1},{1,0},{2,3},{3,2},{4,5},{5,4},{6,7},{7,6},{8,9},{9,8},{10,11... | collective-permute-start | bytes 921608 | tf_op jit(solution)/shard_map/ppermute | solution.py:115
  106.2 4.1 %collective-permute-start.30 = (bf16[400,384]{1,0:T(8,128)(2,1)S(1)}, bf16[400,384]{1,0:T(8,128)(2,1)S(1)}, u32[]{:S(2)}, u32[]{:S(2)}) collective-permute-start(bf16[400,384]{1,0:T(8,128)(2,1)S(1)} %collective-permute-done.17.refs_2_), channel_id=1, source_target_pairs={{0,1},{1,0},{2,3},{3,2},{4,5},{5,4},{6,7},{7,6},{8,9},{9,8},{10,11... | collective-permute-start | bytes 921608 | tf_op jit(solution)/shard_map/ppermute | solution.py:115
  106.2 4.1 %collective-permute-start.31 = (bf16[400,384]{1,0:T(8,128)(2,1)S(1)}, bf16[400,384]{1,0:T(8,128)(2,1)S(1)}, u32[]{:S(2)}, u32[]{:S(2)}) collective-permute-start(bf16[400,384]{1,0:T(8,128)(2,1)S(1)} %collective-permute-done.18.refs_3_), channel_id=1, source_target_pairs={{0,1},{1,0},{2,3},{3,2},{4,5},{5,4},{6,7},{7,6},{8,9},{9,8},{10,11... | collective-permute-start | bytes 921608 | tf_op jit(solution)/shard_map/ppermute | solution.py:115
  106.7 9.1 %collective-permute-start.32 = (bf16[192,384]{1,0:T(8,128)(2,1)S(1)}, bf16[192,384]{1,0:T(8,128)(2,1)S(1)}, u32[]{:S(2)}, u32[]{:S(2)}) collective-permute-start(bf16[192,384]{1,0:T(8,128)(2,1)S(1)} %pad_maximum_fusion.1.refs_0_), channel_id=1, source_target_pairs={{0,8},{8,0},{16,24},{24,16},{1,9},{9,1},{17,25},{25,17},{2,10},{10... | collective-permute-start | bytes 442376 | tf_op jit(solution)/shard_map/ppermute | solution.py:129
  108.0 7.8 %collective-permute-start.33 = (bf16[192,384]{1,0:T(8,128)(2,1)S(1)}, bf16[192,384]{1,0:T(8,128)(2,1)S(1)}, u32[]{:S(2)}, u32[]{:S(2)}) collective-permute-start(bf16[192,384]{1,0:T(8,128)(2,1)S(1)} %pad_maximum_fusion.1.refs_0_), channel_id=1, source_target_pairs={{0,16},{8,24},{16,0},{24,8},{1,17},{9,25},{17,1},{25,9},{2,18},{10... | collective-permute-start | bytes 442376 | tf_op jit(solution)/shard_map/ppermute | solution.py:129
  108.9 7.9 %collective-permute-start.34 = (bf16[192,384]{1,0:T(8,128)(2,1)S(1)}, bf16[192,384]{1,0:T(8,128)(2,1)S(1)}, u32[]{:S(2)}, u32[]{:S(2)}) collective-permute-start(bf16[192,384]{1,0:T(8,128)(2,1)S(1)} %pad_maximum_fusion.1.refs_0_), channel_id=1, source_target_pairs={{0,24},{8,16},{16,8},{24,0},{1,25},{9,17},{17,9},{25,1},{2,26},{10... | collective-permute-start | bytes 442376 | tf_op jit(solution)/shard_map/ppermute | solution.py:129
  116.7 1.4 %collective-permute-start.35 = (bf16[192,384]{1,0:T(8,128)(2,1)S(1)}, bf16[192,384]{1,0:T(8,128)(2,1)S(1)}, u32[]{:S(2)}, u32[]{:S(2)}) collective-permute-start(bf16[192,384]{1,0:T(8,128)(2,1)S(1)} %pad_maximum_fusion.1.refs_0_), channel_id=1, source_target_pairs={{0,1},{1,0},{2,3},{3,2},{4,5},{5,4},{6,7},{7,6},{8,9},{9,8},{10,11... | collective-permute-start | bytes 442376 | tf_op jit(solution)/shard_map/ppermute | solution.py:115
  116.8 1.6 %collective-permute-start.36 = (bf16[192,384]{1,0:T(8,128)(2,1)S(1)}, bf16[192,384]{1,0:T(8,128)(2,1)S(1)}, u32[]{:S(2)}, u32[]{:S(2)}) collective-permute-start(bf16[192,384]{1,0:T(8,128)(2,1)S(1)} %collective-permute-done.32.refs_1_), channel_id=1, source_target_pairs={{0,1},{1,0},{2,3},{3,2},{4,5},{5,4},{6,7},{7,6},{8,9},{9,8},{10,11... | collective-permute-start | bytes 442376 | tf_op jit(solution)/shard_map/ppermute | solution.py:115
  117.3 1.4 %collective-permute-start.37 = (bf16[192,384]{1,0:T(8,128)(2,1)S(1)}, bf16[192,384]{1,0:T(8,128)(2,1)S(1)}, u32[]{:S(2)}, u32[]{:S(2)}) collective-permute-start(bf16[192,384]{1,0:T(8,128)(2,1)S(1)} %collective-permute-done.33.refs_2_), channel_id=1, source_target_pairs={{0,1},{1,0},{2,3},{3,2},{4,5},{5,4},{6,7},{7,6},{8,9},{9,8},{10,11... | collective-permute-start | bytes 442376 | tf_op jit(solution)/shard_map/ppermute | solution.py:115
  117.3 1.6 %collective-permute-start.38 = (bf16[192,384]{1,0:T(8,128)(2,1)S(1)}, bf16[192,384]{1,0:T(8,128)(2,1)S(1)}, u32[]{:S(2)}, u32[]{:S(2)}) collective-permute-start(bf16[192,384]{1,0:T(8,128)(2,1)S(1)} %collective-permute-done.34.refs_3_), channel_id=1, source_target_pairs={{0,1},{1,0},{2,3},{3,2},{4,5},{5,4},{6,7},{7,6},{8,9},{9,8},{10,11... | collective-permute-start | bytes 442376 | tf_op jit(solution)/shard_map/ppermute | solution.py:115
  (1 other events, 0.7 us)

commit v4 on v3

--- a/solution.py
+++ b/solution.py
@@ -63,12 +63,14 @@
     return [(d, away(d // share, owners, step) * share + d % share) for d in range(seq_size)]
 
 
-def rows_to_owner(blocks, owner, share):
+def rows_to_owner(blocks, owner, share, earlier=None):
     owners = blocks.shape[0]
     seq_size = lax.axis_size("seq")
     pieces = []
     for step in range(owners):
         block = lax.dynamic_index_in_dim(blocks, away(owner, owners, step), 0, False)
+        if step and earlier:
+            block = after(block, earlier[step])
         if step:
             block = lax.ppermute(block, "seq", owner_pairs(seq_size, owners, share, step))
         pieces.append(block)
@@ -998,8 +1000,8 @@
         where, lead_index, sample_counts, lead_table, modulation_weight, bias, attend_weight,
         owners * seq_length,
     )
-    grad_pieces = rows_to_owner(after(cotangent[0], mod), owner, share)
-    token_pieces = after_all(token_pieces, mod)
+    grad_pieces = rows_to_owner(cotangent[0], owner, share, {step: bias if step in (1,) else mod for step in range(1, owners)})
+    token_pieces = after_all(token_pieces, mod, grad_pieces[1])
     own_tokens = jnp.concatenate(token_pieces, axis=0)
     rest_tokens = share_rows(own_tokens, rank, share)
     short = seq_length <= 2048

time: 121 us -> 121 us (level)
  local copies, waits for them, and re-layouts: 5.39 us -> 4.06 us
    unnamed x51, local copies, waits for them, and re-layouts: 2.98 us -> 1.63 us
  transfers between devices with their start and end apart: 41 -> 41, of which waited for: 12 -> 13; matrix products, arithmetic and copies ran while one was open for 4% -> 4% of each run, Pallas kernels for 24% -> 25%
where the time goes in v4:
time: 121 us
  starting transfers between devices  50 us (41%)
  Pallas kernels  40.2 us (33%)
  waiting for transfers between devices  20.4 us (17%)
  local copies, waits for them, and re-layouts  4.06 us (3%)
  other arithmetic  4 us (3%)
  between operations  1.84 us (2%)
    ppermute x12, starting transfers between devices, plane_send(): lax.ppermute(values, 'grp', [(d, away(d, grp_size, step)) for d in range(...  14.2 us
    pallas_call x1, Pallas kernels, backward_attention(): pl.pallas_call(partial(backward_kernel, head_width, 1.0 / math.sqrt(head_...  11.7 us
    ppermute x6, starting transfers between devices, rows_to_owner(): lax.ppermute(block, 'seq', owner_pairs(seq_size, owners, share, step))  10.6 us
    pallas_call x1, Pallas kernels, forward_attention(): pl.pallas_call(partial(forward_kernel, head_width, 1.0 / math.sqrt(head_w...  9.96 us
    ppermute x6, starting transfers between devices, line_send(): lax.ppermute(values, 'seq', owner_pairs(seq_size, seq_size // 2, 2, step))  8.89 us
    pallas_call x1, Pallas kernels, middle(): pl.pallas_call(middle_kernel, grid=(1,), in_specs=[pl.BlockSpec(memory_sp...  8.44 us
    ppermute x3, waiting for transfers between devices, pieces_from_owner(): lax.ppermute(pieces[step], 'seq', owner_pairs(seq_size, owners, share, st...  8.22 us
    pallas_call x1, Pallas kernels, first_sums(): pl.pallas_call(partial(first_sums_kernel, grp_size, line), grid=(grp_size...  5.51 us
  transfers between devices with their start and end apart: 41, of which 13 were waited for; matrix products, arithmetic and copies ran while one was open for 4% of the time, Pallas kernels for 25%

profile of v4, /device:TPU:0, one launch (start us, length us, event | category | flops | bytes accessed | tf_op | source)
XLA Modules:
  0.0 120.5 jit_solution(202102311174824183)
XLA Ops:
  0.7 1.2 dynamic-slice_bitcast_fusion.4
  1.9 3.1 %collective-permute-start = (bf16[128,384]{1,0:T(8,128)(2,1)S(1)}, bf16[128,384]{1,0:T(8,128)(2,1)S(1)}, u32[]{:S(2)}, u32[]{:S(2)}) collective-permute-start(bf16[128,384]{1,0:T(8,128)(2,1)S(1)} %get-tuple-element.157), channel_id=1, source_target_pairs={{0,2},{1,3},{2,0},{3,1},{4,6},{5,7},{6,4},{7,5},{8,10},{9,11},{10,... | collective-permute-start | bytes 294920 | tf_op jit(solution)/shard_map/ppermute | solution.py:75
  5.0 2.6 %collective-permute-start.1 = (bf16[128,384]{1,0:T(8,128)(2,1)S(1)}, bf16[128,384]{1,0:T(8,128)(2,1)S(1)}, u32[]{:S(2)}, u32[]{:S(2)}) collective-permute-start(bf16[128,384]{1,0:T(8,128)(2,1)S(1)} %get-tuple-element.159), channel_id=1, source_target_pairs={{0,4},{1,5},{2,6},{3,7},{4,0},{5,1},{6,2},{7,3},{8,12},{9,13},{10,... | collective-permute-start | bytes 294920 | tf_op jit(solution)/shard_map/ppermute | solution.py:75
  7.6 0.7 maximum_convert_fusion
  8.4 1.0 collective-permute-start.3
  10.0 0.1 stack.17.place
  10.1 1.5 %copy-done = bf16[384,2304]{1,0:T(8,128)(2,1)S(1)} copy-done((bf16[384,2304]{1,0:T(8,128)(2,1)S(1)}, bf16[384,2304]{1,0:T(8,128)(2,1)}, u32[]{:S(2)}) %copy-start) | copy-done | bytes 1769496
  11.6 0.9 prepare.1
  12.6 2.8 %collective-permute-done.1 = bf16[128,384]{1,0:T(8,128)(2,1)S(1)} collective-permute-done((bf16[128,384]{1,0:T(8,128)(2,1)S(1)}, bf16[128,384]{1,0:T(8,128)(2,1)S(1)}, u32[]{:S(2)}, u32[]{:S(2)}) %collective-permute-start.1) | collective-permute-done | bytes 98336 | tf_op jit(solution)/shard_map/ppermute | solution.py:75
  15.4 0.1 collective-permute-done.3
  15.6 0.1 collective-permute-start.4
  15.7 2.6 %collective-permute-start.5 = (bf16[128,384]{1,0:T(8,128)(2,1)S(1)}, bf16[128,384]{1,0:T(8,128)(2,1)S(1)}, u32[]{:S(2)}, u32[]{:S(2)}) collective-permute-start(bf16[128,384]{1,0:T(8,128)(2,1)S(1)} %get-tuple-element.91), channel_id=1, source_target_pairs={{0,4},{1,5},{2,6},{3,7},{4,0},{5,1},{6,2},{7,3},{8,12},{9,13},{10,... | collective-permute-start | bytes 294920 | tf_op jit(solution)/shard_map/ppermute | solution.py:75
  18.3 1.3 %collective-permute-start.6 = (bf16[128,384]{1,0:T(8,128)(2,1)S(1)}, bf16[128,384]{1,0:T(8,128)(2,1)S(1)}, u32[]{:S(2)}, u32[]{:S(2)}) collective-permute-start(bf16[128,384]{1,0:T(8,128)(2,1)S(1)} %get-tuple-element.92), channel_id=1, source_target_pairs={{0,6},{1,7},{2,4},{3,5},{4,2},{5,3},{6,0},{7,1},{8,14},{9,15},{10,... | collective-permute-start | bytes 294920 | tf_op jit(solution)/shard_map/ppermute | solution.py:75
  19.7 10.0 %forward_attention.1 = (bf16[6,1024,512]{2,1,0:T(8,128)(2,1)}, bf16[384,512]{1,0:T(8,128)(2,1)S(1)}, bf16[768,1024]{1,0:T(8,128)(2,1)S(1)}, f32[384,512]{1,0:T(8...) custom-call(s32[5]{0:T(128)S(1)} %stack.17.place, s32[4,8]{1,0:T(4,128)S(1)} %bitcast.25, ...), custom_call_target="tpu_custom_call" | custom-call | flops 3221225472 | bytes 6291456 | tf_op jit(solution)/shard_map/forward_attention/pallas_call | solution.py:389
  29.8 8.4 %middle.1 = (bf16[1536,384]{1,0:T(8,128)(2,1)S(1)}, bf16[1536,384]{1,0:T(8,128)(2,1)}, bf16[384,384]{1,0:T(8,128)(2,1)}, bf16[384,512]{1,0:T(8,128)(2,1)}, f32[5...) custom-call(s32[5]{0:T(128)S(1)} %stack.17.place, ...), custom_call_target="tpu_custom_call" | custom-call | flops 4831838208 | bytes 16777216 | tf_op jit(solution)/shard_map/middle/pallas_call | solution.py:489
  38.2 0.1 collective-permute-start.7
  38.3 3.7 %all-to-all-start = ((bf16[4,128,384]{2,1,0:T(8,128)(2,1)}), bf16[4,128,384]{2,1,0:T(8,128)(2,1)S(1)}, u32[]{:S(2)}, u32[]{:S(2)}) async-start(bf16[4,128,384]{2,1,0:T(8,128)(2,1)} %get-tuple-element.109), calls=%async_computation | async-start | bytes 786432 | tf_op jit(solution)/shard_map/all_to_all | solution.py:91
  42.1 1.7 %add_convert_fusion = bf16[1536,384]{1,0:T(8,128)(2,1)S(1)} fusion(bf16[1536,384]{1,0:T(8,128)(2,1)} %collective-permute-done.7, bf16[1536,384]{1,0:T(8,128)(2,1)S(1)} %get-tuple-element.98), kind=kLoop, calls=%fused_computation | loop fusion | flops 2359296 | bytes 3538944 | tf_op jit(solution)/shard_map/convert_element_type | solution.py:181
  43.9 1.0 constant_dynamic-slice_fusion.8
  44.8 1.5 %collective-permute-start.8 = (bf16[384,384]{1,0:T(8,128)(2,1)}, bf16[384,384]{1,0:T(8,128)(2,1)S(1)}, u32[]{:S(2)}, u32[]{:S(2)}) collective-permute-start(bf16[384,384]{1,0:T(8,128)(2,1)} %get-tuple-element.147), channel_id=1, source_target_pairs={{0,8},{8,0},{16,24},{24,16},{1,9},{9,1},{17,25},{25,17},{2,10},{10... | collective-permute-start | bytes 884744 | tf_op jit(solution)/shard_map/ppermute | solution.py:131
  46.3 1.5 %collective-permute-start.9 = (bf16[384,384]{1,0:T(8,128)(2,1)}, bf16[384,384]{1,0:T(8,128)(2,1)S(1)}, u32[]{:S(2)}, u32[]{:S(2)}) collective-permute-start(bf16[384,384]{1,0:T(8,128)(2,1)} %get-tuple-element.146), channel_id=1, source_target_pairs={{0,16},{8,24},{16,0},{24,8},{1,17},{9,25},{17,1},{25,9},{2,18},{10... | collective-permute-start | bytes 884744 | tf_op jit(solution)/shard_map/ppermute | solution.py:131
  47.9 0.5 collective-permute-start.10
  48.4 11.7 %backward_attention.1 = (bf16[768,384]{1,0:T(8,128)(2,1)}, bf16[768,384]{1,0:T(8,128)(2,1)S(1)}, bf16[528,384]{1,0:T(8,128)(2,1)}, bf16[512,384]{1,0:T(8,128)(2,1)S(1)}, f32[16,384]{1,0:T(8,128)S(1)}) custom-call(s32[5]{0:T(128)S(1)} %stack.17.place, bf16[6,1024,512]{2,1,0:T(8,128)(2,1)} %get-tuple-element.85.expo, bf16[384,512]{1,0:T(8,128)(2,1)S(1)} %copy-done.20, ...), custom_call_target="tpu_custom_call" | custom-call | flops 6442450944 | bytes 6291456 | tf_op jit(solution)/shard_map/backward_attention/pallas_call | solution.py:593
  60.1 1.7 %collective-permute-done.9.refs_2_ = bf16[384,384]{1,0:T(8,128)(2,1)S(1)} collective-permute-done((bf16[384,384]{1,0:T(8,128)(2,1)}, bf16[384,384]{1,0:T(8,128)(2,1)S(1)}, u32[]{:S(2)}, u32[]{:S(2)}) %collective-permute-start.9) | collective-permute-done | bytes 294944 | tf_op jit(solution)/shard_map/ppermute | solution.py:131
  61.9 0.5 collective-permute-start.11
  62.4 0.9 sum_parts.1
  63.3 4.6 %all-to-all-start.1 = ((bf16[4,96,384]{2,1,0:T(8,128)(2,1)}), bf16[4,96,384]{2,1,0:T(8,128)(2,1)S(1)}, u32[]{:S(2)}, u32[]{:S(2)}) async-start(bf16[4,96,384]{2,1,0:T(8,128)(2,1)} %bitcast.13), calls=%async_computation.1 | async-start | bytes 589824 | tf_op jit(solution)/shard_map/all_to_all | solution.py:171
  67.9 1.4 %add_convert_fusion.1 = bf16[768,384]{1,0:T(8,128)(2,1)S(1)} fusion(bf16[768,384]{1,0:T(8,128)(2,1)} %collective-permute-done.12, bf16[768,384]{1,0:T(8,128)(2,1)} %get-tuple-element.112), kind=kLoop, calls=%fused_computation.1 | loop fusion | flops 1179648 | bytes 1769472 | tf_op jit(solution)/shard_map/convert_element_type | solution.py:181
  69.2 0.1 constant_dynamic-slice_fusion.4
  69.3 1.3 %collective-permute-start.19 = (bf16[192,384]{1,0:T(8,128)(2,1)S(1)}, bf16[192,384]{1,0:T(8,128)(2,1)S(1)}, u32[]{:S(2)}, u32[]{:S(2)}) collective-permute-start(bf16[192,384]{1,0:T(8,128)(2,1)S(1)} %get-tuple-element.150), channel_id=1, source_target_pairs={{0,8},{8,0},{16,24},{24,16},{1,9},{9,1},{17,25},{25,17},{2,10},{10... | collective-permute-start | bytes 442376 | tf_op jit(solution)/shard_map/ppermute | solution.py:131
  70.6 0.8 collective-permute-start.20
  71.5 1.4 %collective-permute-start.21 = (bf16[192,384]{1,0:T(8,128)(2,1)S(1)}, bf16[192,384]{1,0:T(8,128)(2,1)S(1)}, u32[]{:S(2)}, u32[]{:S(2)}) collective-permute-start(bf16[192,384]{1,0:T(8,128)(2,1)S(1)} %get-tuple-element.148), channel_id=1, source_target_pairs={{0,24},{8,16},{16,8},{24,0},{1,25},{9,17},{17,9},{25,1},{2,26},{10... | collective-permute-start | bytes 442376 | tf_op jit(solution)/shard_map/ppermute | solution.py:131
  72.9 4.8 %all-to-all-done.1.refs_0_ = bf16[4,96,384]{2,1,0:T(8,128)(2,1)S(1)} async-done(((bf16[4,96,384]{2,1,0:T(8,128)(2,1)}), bf16[4,96,384]{2,1,0:T(8,128)(2,1)S(1)}, u32[]{:S(2)}, u32[]{:S(2)}) %all-to-all-start.1) | async-done | bytes 294944 | tf_op jit(solution)/shard_map/all_to_all | solution.py:171
  77.8 2.0 %collective-permute-start.14 = (bf16[112,384]{1,0:T(8,128)(2,1)S(1)}, bf16[112,384]{1,0:T(8,128)(2,1)S(1)}, u32[]{:S(2)}, u32[]{:S(2)}) collective-permute-start(bf16[112,384]{1,0:T(8,128)(2,1)S(1)} %line_total.1.refs_0_), channel_id=1, source_target_pairs={{0,4},{1,5},{2,6},{3,7},{4,0},{5,1},{6,2},{7,3},{8,12},{9,13},{10,... | collective-permute-start | bytes 258056 | tf_op jit(solution)/shard_map/ppermute | solution.py:126
  79.7 2.4 %collective-permute-start.15 = (bf16[112,384]{1,0:T(8,128)(2,1)S(1)}, bf16[112,384]{1,0:T(8,128)(2,1)S(1)}, u32[]{:S(2)}, u32[]{:S(2)}) collective-permute-start(bf16[112,384]{1,0:T(8,128)(2,1)S(1)} %line_total.1.refs_0_), channel_id=1, source_target_pairs={{0,6},{1,7},{2,4},{3,5},{4,2},{5,3},{6,0},{7,1},{8,14},{9,15},{10,... | collective-permute-start | bytes 258056 | tf_op jit(solution)/shard_map/ppermute | solution.py:126
  82.2 0.1 add_convert_fusion.2
  82.3 2.0 %collective-permute-start.23 = (bf16[48,384]{1,0:T(8,128)(2,1)S(1)}, bf16[48,384]{1,0:T(8,128)(2,1)S(1)}, u32[]{:S(2)}, u32[]{:S(2)}) collective-permute-start(bf16[48,384]{1,0:T(8,128)(2,1)S(1)} %get-tuple-element.161), channel_id=1, source_target_pairs={{0,4},{1,5},{2,6},{3,7},{4,0},{5,1},{6,2},{7,3},{8,12},{9,13},{10,... | collective-permute-start | bytes 110600 | tf_op jit(solution)/shard_map/ppermute | solution.py:126
  84.3 2.4 %collective-permute-start.24 = (bf16[48,384]{1,0:T(8,128)(2,1)S(1)}, bf16[48,384]{1,0:T(8,128)(2,1)S(1)}, u32[]{:S(2)}, u32[]{:S(2)}) collective-permute-start(bf16[48,384]{1,0:T(8,128)(2,1)S(1)} %get-tuple-element.160), channel_id=1, source_target_pairs={{0,6},{1,7},{2,4},{3,5},{4,2},{5,3},{6,0},{7,1},{8,14},{9,15},{10,... | collective-permute-start | bytes 110600 | tf_op jit(solution)/shard_map/ppermute | solution.py:126
  86.7 0.7 collective-permute-done.14.refs_2_
  87.5 1.3 %collective-permute-start.16 = (bf16[400,384]{1,0:T(8,128)(2,1)S(1)}, bf16[400,384]{1,0:T(8,128)(2,1)S(1)}, u32[]{:S(2)}, u32[]{:S(2)}) collective-permute-start(bf16[400,384]{1,0:T(8,128)(2,1)S(1)} %line_join.1.refs_0_), channel_id=1, source_target_pairs={{0,8},{8,0},{16,24},{24,16},{1,9},{9,1},{17,25},{25,17},{2,10},{10... | collective-permute-start | bytes 921608 | tf_op jit(solution)/shard_map/ppermute | solution.py:131
  88.8 0.8 collective-permute-start.17
  89.6 1.4 %collective-permute-start.18 = (bf16[400,384]{1,0:T(8,128)(2,1)S(1)}, bf16[400,384]{1,0:T(8,128)(2,1)S(1)}, u32[]{:S(2)}, u32[]{:S(2)}) collective-permute-start(bf16[400,384]{1,0:T(8,128)(2,1)S(1)} %line_join.1.refs_0_), channel_id=1, source_target_pairs={{0,24},{8,16},{16,8},{24,0},{1,25},{9,17},{17,9},{25,1},{2,26},{10... | collective-permute-start | bytes 921608 | tf_op jit(solution)/shard_map/ppermute | solution.py:131
  91.0 0.6 finish_rows.1
  91.6 2.1 %collective-permute-start.25 = (bf16[176,384]{1,0:T(8,128)(2,1)S(1)}, bf16[176,384]{1,0:T(8,128)(2,1)S(1)}, u32[]{:S(2)}, u32[]{:S(2)}) collective-permute-start(bf16[176,384]{1,0:T(8,128)(2,1)S(1)} %get-tuple-element.121), channel_id=1, source_target_pairs={{0,2},{1,3},{2,0},{3,1},{4,6},{5,7},{6,4},{7,5},{8,10},{9,11},{10,... | collective-permute-start | bytes 405512 | tf_op jit(solution)/shard_map/ppermute | solution.py:83
  93.7 0.8 collective-permute-start.26
  94.6 3.6 %collective-permute-done.25.refs_11_ = bf16[176,384]{1,0:T(8,128)(2,1)S(1)} collective-permute-done((bf16[176,384]{1,0:T(8,128)(2,1)S(1)}, bf16[176,384]{1,0:T(8,128)(2,1)S(1)}, u32[]{:S(2)}, u32[]{:S(2)}) %collective-permute-start.25) | collective-permute-done | bytes 135200 | tf_op jit(solution)/shard_map/ppermute | solution.py:83
  98.2 2.3 %collective-permute-start.27 = (bf16[176,384]{1,0:T(8,128)(2,1)S(1)}, bf16[176,384]{1,0:T(8,128)(2,1)S(1)}, u32[]{:S(2)}, u32[]{:S(2)}) collective-permute-start(bf16[176,384]{1,0:T(8,128)(2,1)S(1)} %get-tuple-element.123), channel_id=1, source_target_pairs={{0,6},{1,7},{2,4},{3,5},{4,2},{5,3},{6,0},{7,1},{8,14},{9,15},{10,... | collective-permute-start | bytes 405512 | tf_op jit(solution)/shard_map/ppermute | solution.py:83
  100.5 0.6 collective-permute-done.26.refs_12_
  101.1 4.0 %collective-permute-done.27.refs_13_ = bf16[176,384]{1,0:T(8,128)(2,1)S(1)} collective-permute-done((bf16[176,384]{1,0:T(8,128)(2,1)S(1)}, bf16[176,384]{1,0:T(8,128)(2,1)S(1)}, u32[]{:S(2)}, u32[]{:S(2)}) %collective-permute-start.27) | collective-permute-done | bytes 135200 | tf_op jit(solution)/shard_map/ppermute | solution.py:83
  105.2 0.5 collective-permute-start.29
  105.7 0.1 collective-permute-start.30
  105.8 0.4 collective-permute-start.31
  106.3 1.3 %collective-permute-start.32 = (bf16[192,384]{1,0:T(8,128)(2,1)S(1)}, bf16[192,384]{1,0:T(8,128)(2,1)S(1)}, u32[]{:S(2)}, u32[]{:S(2)}) collective-permute-start(bf16[192,384]{1,0:T(8,128)(2,1)S(1)} %pad_maximum_fusion.1.refs_0_), channel_id=1, source_target_pairs={{0,8},{8,0},{16,24},{24,16},{1,9},{9,1},{17,25},{25,17},{2,10},{10... | collective-permute-start | bytes 442376 | tf_op jit(solution)/shard_map/ppermute | solution.py:131
  107.6 0.8 collective-permute-start.33
  108.4 1.4 %collective-permute-start.34 = (bf16[192,384]{1,0:T(8,128)(2,1)S(1)}, bf16[192,384]{1,0:T(8,128)(2,1)S(1)}, u32[]{:S(2)}, u32[]{:S(2)}) collective-permute-start(bf16[192,384]{1,0:T(8,128)(2,1)S(1)} %pad_maximum_fusion.1.refs_0_), channel_id=1, source_target_pairs={{0,24},{8,16},{16,8},{24,0},{1,25},{9,17},{17,9},{25,1},{2,26},{10... | collective-permute-start | bytes 442376 | tf_op jit(solution)/shard_map/ppermute | solution.py:131
  109.8 5.5 %first_sums.1 = (f32[1536,384]{1,0:T(8,128)}, f32[384,1536]{1,0:T(8,128)}, f32[384,2304]{1,0:T(8,128)}, bf16[4,128,384]{2,1,0:T(8,128)(2,1)}, f32[4,128,384]{2,1...) custom-call(s32[5]{0:T(128)S(1)} %stack.17.place, ...), custom_call_target="tpu_custom_call" | custom-call | tf_op jit(solution)/shard_map/first_sums/pallas_call | solution.py:823
  115.4 0.9 collective-permute-done.34.refs_3_
  116.3 0.5 collective-permute-start.36
  116.8 0.5 collective-permute-start.38
  117.3 0.3 collective-permute-done.35.refs_4_
  117.7 0.2 collective-permute-done.36.refs_5_
  117.9 0.3 collective-permute-done.37.refs_6_
  118.2 0.2 collective-permute-done.38.refs_7_
  118.4 2.2 %second_sums.1 = (f32[384,1152]{1,0:T(8,128)}, f32[384,384]{1,0:T(8,128)}) custom-call(s32[5]{0:T(128)S(1)} %stack.17.place, bf16[192,384]{1,0:T(8,128)(2,1)S(1)} %pad_maximum_fusion.1.refs_0_, bf16[192,384]{1,0:T(8,128)(2,1)S(1)} %collective-permute-done.32.refs_1_, bf16[192,384]{1,0:T(8,128)(2,1)S(1)} %collective-permute-done.33.refs_2_, ...), custom_call_target="tpu_custom_call" | custom-call | tf_op jit(solution)/shard_map/second_sums/pallas_call | solution.py:885
  (97 shorter events, 0.7 us)
Async XLA Ops:
  0.6 7.7 %copy-start.23 = (bf16[1,4,128,384]{3,2,1,0:T(8,128)(2,1)S(1)}, bf16[1,4,128,384]{3,2,1,0:T(8,128)(2,1)}, u32[]{:S(2)}) copy-start(bf16[1,4,128,384]{3,2,1,0:T(8,128)(2,1)} %param.17) | copy-start | bytes 1179652
  0.7 9.5 %copy-start.4 = (s32[4]{0:T(128)S(1)}, s32[4]{0:T(128)}, u32[]{:S(2)}) copy-start(s32[4]{0:T(128)} %counts.1) | copy-start | bytes 52
  0.7 9.5 %copy-start.3 = (bf16[8,384]{1,0:T(8,128)(2,1)S(1)}, bf16[8,384]{1,0:T(8,128)(2,1)}, u32[]{:S(2)}) copy-start(bf16[8,384]{1,0:T(8,128)(2,1)} %table.1) | copy-start | bytes 18436
  0.7 9.5 %copy-start.2 = (bf16[384,1152]{1,0:T(8,128)(2,1)S(1)}, bf16[384,1152]{1,0:T(8,128)(2,1)}, u32[]{:S(2)}) copy-start(bf16[384,1152]{1,0:T(8,128)(2,1)} %attend_weight.1) | copy-start | bytes 2654212
  1.9 10.7 %collective-permute-start = (bf16[128,384]{1,0:T(8,128)(2,1)S(1)}, bf16[128,384]{1,0:T(8,128)(2,1)S(1)}, u32[]{:S(2)}, u32[]{:S(2)}) collective-permute-start(bf16[128,384]{1,0:T(8,128)(2,1)S(1)} %get-tuple-element.157), channel_id=1, source_target_pairs={{0,2},{1,3},{2,0},{3,1},{4,6},{5,7},{6,4},{7,5},{8,10},{9,11},{10,... | collective-permute-start | bytes 294920 | tf_op jit(solution)/shard_map/ppermute | solution.py:75
  5.0 10.4 %collective-permute-start.1 = (bf16[128,384]{1,0:T(8,128)(2,1)S(1)}, bf16[128,384]{1,0:T(8,128)(2,1)S(1)}, u32[]{:S(2)}, u32[]{:S(2)}) collective-permute-start(bf16[128,384]{1,0:T(8,128)(2,1)S(1)} %get-tuple-element.159), channel_id=1, source_target_pairs={{0,4},{1,5},{2,6},{3,7},{4,0},{5,1},{6,2},{7,3},{8,12},{9,13},{10,... | collective-permute-start | bytes 294920 | tf_op jit(solution)/shard_map/ppermute | solution.py:75
  7.6 7.8 %collective-permute-start.2 = (bf16[128,384]{1,0:T(8,128)(2,1)S(1)}, bf16[128,384]{1,0:T(8,128)(2,1)S(1)}, u32[]{:S(2)}, u32[]{:S(2)}) collective-permute-start(bf16[128,384]{1,0:T(8,128)(2,1)S(1)} %get-tuple-element.156), channel_id=1, source_target_pairs={{0,6},{1,7},{2,4},{3,5},{4,2},{5,3},{6,0},{7,1},{8,14},{9,15},{10,... | collective-permute-start | bytes 294920 | tf_op jit(solution)/shard_map/ppermute | solution.py:75
  8.4 7.1 %collective-permute-start.3 = (bf16[128,384]{1,0:T(8,128)(2,1)S(1)}, bf16[128,384]{1,0:T(8,128)(2,1)S(1)}, u32[]{:S(2)}, u32[]{:S(2)}) collective-permute-start(bf16[128,384]{1,0:T(8,128)(2,1)S(1)} %get-tuple-element.79), channel_id=1, source_target_pairs={{0,2},{1,3},{2,0},{3,1},{4,6},{5,7},{6,4},{7,5},{8,10},{9,11},{10,... | collective-permute-start | bytes 294920 | tf_op jit(solution)/shard_map/ppermute | solution.py:75
  11.6 8.0 %copy-start.12 = (s32[1,4,1024]{2,1,0:T(4,128)S(1)}, s32[1,4,1024]{2,1,0:T(4,128)}, u32[]{:S(2)}) copy-start(s32[1,4,1024]{2,1,0:T(4,128)} %param.19) | copy-start | bytes 49156
  11.6 8.0 %copy-start.13 = (s32[1,4,8]{2,1,0:T(4,128)S(1)}, s32[1,4,8]{2,1,0:T(4,128)}, u32[]{:S(2)}) copy-start(s32[1,4,8]{2,1,0:T(4,128)} %param.18) | copy-start | bytes 388
  12.6 17.1 %copy-start.7 = (bf16[1152,384]{1,0:T(8,128)(2,1)}, bf16[1152,384]{1,0:T(8,128)(2,1)S(1)}, u32[]{:S(2)}) copy-start(bf16[1152,384]{1,0:T(8,128)(2,1)S(1)} %get-tuple-element.84.weight) | copy-start | bytes 2654212
  15.6 4.0 %collective-permute-start.4 = (bf16[512,384]{1,0:T(8,128)(2,1)S(1)}, bf16[512,384]{1,0:T(8,128)(2,1)S(1)}, u32[]{:S(2)}, u32[]{:S(2)}) collective-permute-start(bf16[512,384]{1,0:T(8,128)(2,1)S(1)} %constant_dynamic-update-slice_fusion.own), channel_id=1, source_target_pairs={{0,1},{1,0},{2,3},{3,2},{4,5},{5,4},{6,7},{7,6},{8,9},{9,8},{10,11... | collective-permute-start | bytes 1179656 | tf_op jit(solution)/shard_map/ppermute | solution.py:97
  15.7 14.0 %collective-permute-start.5 = (bf16[128,384]{1,0:T(8,128)(2,1)S(1)}, bf16[128,384]{1,0:T(8,128)(2,1)S(1)}, u32[]{:S(2)}, u32[]{:S(2)}) collective-permute-start(bf16[128,384]{1,0:T(8,128)(2,1)S(1)} %get-tuple-element.91), channel_id=1, source_target_pairs={{0,4},{1,5},{2,6},{3,7},{4,0},{5,1},{6,2},{7,3},{8,12},{9,13},{10,... | collective-permute-start | bytes 294920 | tf_op jit(solution)/shard_map/ppermute | solution.py:75
  18.3 11.4 %collective-permute-start.6 = (bf16[128,384]{1,0:T(8,128)(2,1)S(1)}, bf16[128,384]{1,0:T(8,128)(2,1)S(1)}, u32[]{:S(2)}, u32[]{:S(2)}) collective-permute-start(bf16[128,384]{1,0:T(8,128)(2,1)S(1)} %get-tuple-element.92), channel_id=1, source_target_pairs={{0,6},{1,7},{2,4},{3,5},{4,2},{5,3},{6,0},{7,1},{8,14},{9,15},{10,... | collective-permute-start | bytes 294920 | tf_op jit(solution)/shard_map/ppermute | solution.py:75
  19.6 10.0 %copy-start.9 = (bf16[512,384]{1,0:T(8,128)(2,1)}, bf16[512,384]{1,0:T(8,128)(2,1)S(1)}, u32[]{:S(2)}) copy-start(bf16[512,384]{1,0:T(8,128)(2,1)S(1)} %collective-permute-done.4.rest) | copy-start | bytes 1179652
  19.6 10.1 %copy-start.5 = (bf16[384,1536]{1,0:T(8,128)(2,1)S(1)}, bf16[384,1536]{1,0:T(8,128)(2,1)}, u32[]{:S(2)}) copy-start(bf16[384,1536]{1,0:T(8,128)(2,1)} %expand_weight.1) | copy-start | bytes 3538948
  19.7 10.1 %copy-start.6 = (bf16[1536,384]{1,0:T(8,128)(2,1)S(1)}, bf16[1536,384]{1,0:T(8,128)(2,1)}, u32[]{:S(2)}) copy-start(bf16[1536,384]{1,0:T(8,128)(2,1)} %shrink_weight.1) | copy-start | bytes 3538948
  19.7 10.1 %copy-start.11 = (bf16[384,384]{1,0:T(8,128)(2,1)S(1)}, bf16[384,384]{1,0:T(8,128)(2,1)}, u32[]{:S(2)}) copy-start(bf16[384,384]{1,0:T(8,128)(2,1)} %output_weight.1) | copy-start | bytes 884740
  29.6 8.6 %copy-start.14 = (bf16[768,1024]{1,0:T(8,128)(2,1)}, bf16[768,1024]{1,0:T(8,128)(2,1)S(1)}, u32[]{:S(2)}) copy-start(bf16[768,1024]{1,0:T(8,128)(2,1)S(1)} %get-tuple-element.87.key_value) | copy-start | bytes 4718596
  29.6 8.6 %copy-start.16 = (f32[384,512]{1,0:T(8,128)}, f32[384,512]{1,0:T(8,128)S(1)}, u32[]{:S(2)}) copy-start(f32[384,512]{1,0:T(8,128)S(1)} %get-tuple-element.88.attended_wide) | copy-start | bytes 2359300
  29.7 8.6 %copy-start.19 = (bf16[384,512]{1,0:T(8,128)(2,1)}, bf16[384,512]{1,0:T(8,128)(2,1)S(1)}, u32[]{:S(2)}) copy-start(bf16[384,512]{1,0:T(8,128)(2,1)S(1)} %get-tuple-element.86.query) | copy-start | bytes 1179652
  38.2 3.8 %collective-permute-start.7 = (bf16[1536,384]{1,0:T(8,128)(2,1)}, bf16[1536,384]{1,0:T(8,128)(2,1)}, u32[]{:S(2)}, u32[]{:S(2)}) collective-permute-start(bf16[1536,384]{1,0:T(8,128)(2,1)} %get-tuple-element.99), channel_id=1, source_target_pairs={{0,1},{1,0},{2,3},{3,2},{4,5},{5,4},{6,7},{7,6},{8,9},{9,8},{10,11... | collective-permute-start | bytes 3538952 | tf_op jit(solution)/shard_map/ppermute | solution.py:117
  38.3 21.8 %all-to-all-start = ((bf16[4,128,384]{2,1,0:T(8,128)(2,1)}), bf16[4,128,384]{2,1,0:T(8,128)(2,1)S(1)}, u32[]{:S(2)}, u32[]{:S(2)}) async-start(bf16[4,128,384]{2,1,0:T(8,128)(2,1)} %get-tuple-element.109), calls=%async_computation | async-start | bytes 786432 | tf_op jit(solution)/shard_map/all_to_all | solution.py:91
  42.1 6.3 %copy-start.15 = (bf16[768,1024]{1,0:T(8,128)(2,1)S(1)}, bf16[768,1024]{1,0:T(8,128)(2,1)}, u32[]{:S(2)}) copy-start(bf16[768,1024]{1,0:T(8,128)(2,1)} %copy-done.14) | copy-start | bytes 4718596
  42.1 6.3 %copy-start.18 = (f32[512,384]{1,0:T(8,128)S(1)}, f32[512,384]{1,0:T(8,128)}, u32[]{:S(2)}) copy-start(f32[512,384]{1,0:T(8,128)} %get-tuple-element.102.grad_residual) | copy-start | bytes 2359300
  42.1 6.3 %copy-start.20 = (bf16[384,512]{1,0:T(8,128)(2,1)S(1)}, bf16[384,512]{1,0:T(8,128)(2,1)}, u32[]{:S(2)}) copy-start(bf16[384,512]{1,0:T(8,128)(2,1)} %copy-done.19) | copy-start | bytes 1179652
  42.1 6.3 %copy-start.21 = (bf16[384,512]{1,0:T(8,128)(2,1)S(1)}, bf16[384,512]{1,0:T(8,128)(2,1)}, u32[]{:S(2)}) copy-start(bf16[384,512]{1,0:T(8,128)(2,1)} %get-tuple-element.100.grad_attended) | copy-start | bytes 1179652
  43.8 4.5 %copy-start.8 = (bf16[1152,384]{1,0:T(8,128)(2,1)S(1)}, bf16[1152,384]{1,0:T(8,128)(2,1)}, u32[]{:S(2)}) copy-start(bf16[1152,384]{1,0:T(8,128)(2,1)} %copy-done.7) | copy-start | bytes 2654212
  43.8 4.5 %copy-start.10 = (bf16[512,384]{1,0:T(8,128)(2,1)S(1)}, bf16[512,384]{1,0:T(8,128)(2,1)}, u32[]{:S(2)}) copy-start(bf16[512,384]{1,0:T(8,128)(2,1)} %copy-done.9) | copy-start | bytes 1179652
  43.9 4.5 %copy-start.17 = (f32[384,512]{1,0:T(8,128)S(1)}, f32[384,512]{1,0:T(8,128)}, u32[]{:S(2)}) copy-start(f32[384,512]{1,0:T(8,128)} %copy-done.16) | copy-start | bytes 2359300
  43.9 4.5 %copy-start.22 = (bf16[384,384]{1,0:T(8,128)(2,1)S(1)}, bf16[384,384]{1,0:T(8,128)(2,1)}, u32[]{:S(2)}) copy-start(bf16[384,384]{1,0:T(8,128)(2,1)} %get-tuple-element.101.packed_output) | copy-start | bytes 884740
  44.8 15.3 %collective-permute-start.8 = (bf16[384,384]{1,0:T(8,128)(2,1)}, bf16[384,384]{1,0:T(8,128)(2,1)S(1)}, u32[]{:S(2)}, u32[]{:S(2)}) collective-permute-start(bf16[384,384]{1,0:T(8,128)(2,1)} %get-tuple-element.147), channel_id=1, source_target_pairs={{0,8},{8,0},{16,24},{24,16},{1,9},{9,1},{17,25},{25,17},{2,10},{10... | collective-permute-start | bytes 884744 | tf_op jit(solution)/shard_map/ppermute | solution.py:131
  46.3 15.5 %collective-permute-start.9 = (bf16[384,384]{1,0:T(8,128)(2,1)}, bf16[384,384]{1,0:T(8,128)(2,1)S(1)}, u32[]{:S(2)}, u32[]{:S(2)}) collective-permute-start(bf16[384,384]{1,0:T(8,128)(2,1)} %get-tuple-element.146), channel_id=1, source_target_pairs={{0,16},{8,24},{16,0},{24,8},{1,17},{9,25},{17,1},{25,9},{2,18},{10... | collective-permute-start | bytes 884744 | tf_op jit(solution)/shard_map/ppermute | solution.py:131
  47.9 14.0 %collective-permute-start.10 = (bf16[384,384]{1,0:T(8,128)(2,1)}, bf16[384,384]{1,0:T(8,128)(2,1)S(1)}, u32[]{:S(2)}, u32[]{:S(2)}) collective-permute-start(bf16[384,384]{1,0:T(8,128)(2,1)} %get-tuple-element.145), channel_id=1, source_target_pairs={{0,24},{8,16},{16,8},{24,0},{1,25},{9,17},{17,9},{25,1},{2,26},{10... | collective-permute-start | bytes 884744 | tf_op jit(solution)/shard_map/ppermute | solution.py:131
  61.9 6.0 %collective-permute-start.12 = (bf16[768,384]{1,0:T(8,128)(2,1)S(1)}, bf16[768,384]{1,0:T(8,128)(2,1)}, u32[]{:S(2)}, u32[]{:S(2)}) collective-permute-start(bf16[768,384]{1,0:T(8,128)(2,1)S(1)} %get-tuple-element.113), channel_id=1, source_target_pairs={{0,1},{1,0},{2,3},{3,2},{4,5},{5,4},{6,7},{7,6},{8,9},{9,8},{10,11... | collective-permute-start | bytes 1769480 | tf_op jit(solution)/shard_map/ppermute | solution.py:117
  61.9 15.8 %collective-permute-start.11 = (bf16[528,384]{1,0:T(8,128)(2,1)}, bf16[528,384]{1,0:T(8,128)(2,1)S(1)}, u32[]{:S(2)}, u32[]{:S(2)}) collective-permute-start(bf16[528,384]{1,0:T(8,128)(2,1)} %get-tuple-element.111), channel_id=1, source_target_pairs={{0,1},{1,0},{2,3},{3,2},{4,5},{5,4},{6,7},{7,6},{8,9},{9,8},{10,11... | collective-permute-start | bytes 1216520 | tf_op jit(solution)/shard_map/ppermute | solution.py:117
  63.3 14.4 %all-to-all-start.1 = ((bf16[4,96,384]{2,1,0:T(8,128)(2,1)}), bf16[4,96,384]{2,1,0:T(8,128)(2,1)S(1)}, u32[]{:S(2)}, u32[]{:S(2)}) async-start(bf16[4,96,384]{2,1,0:T(8,128)(2,1)} %bitcast.13), calls=%async_computation.1 | async-start | bytes 589824 | tf_op jit(solution)/shard_map/all_to_all | solution.py:171
  69.3 10.4 %collective-permute-start.19 = (bf16[192,384]{1,0:T(8,128)(2,1)S(1)}, bf16[192,384]{1,0:T(8,128)(2,1)S(1)}, u32[]{:S(2)}, u32[]{:S(2)}) collective-permute-start(bf16[192,384]{1,0:T(8,128)(2,1)S(1)} %get-tuple-element.150), channel_id=1, source_target_pairs={{0,8},{8,0},{16,24},{24,16},{1,9},{9,1},{17,25},{25,17},{2,10},{10... | collective-permute-start | bytes 442376 | tf_op jit(solution)/shard_map/ppermute | solution.py:131
  70.6 11.5 %collective-permute-start.20 = (bf16[192,384]{1,0:T(8,128)(2,1)S(1)}, bf16[192,384]{1,0:T(8,128)(2,1)S(1)}, u32[]{:S(2)}, u32[]{:S(2)}) collective-permute-start(bf16[192,384]{1,0:T(8,128)(2,1)S(1)} %get-tuple-element.149), channel_id=1, source_target_pairs={{0,16},{8,24},{16,0},{24,8},{1,17},{9,25},{17,1},{25,9},{2,18},{10... | collective-permute-start | bytes 442376 | tf_op jit(solution)/shard_map/ppermute | solution.py:131
  71.5 10.7 %collective-permute-start.21 = (bf16[192,384]{1,0:T(8,128)(2,1)S(1)}, bf16[192,384]{1,0:T(8,128)(2,1)S(1)}, u32[]{:S(2)}, u32[]{:S(2)}) collective-permute-start(bf16[192,384]{1,0:T(8,128)(2,1)S(1)} %get-tuple-element.148), channel_id=1, source_target_pairs={{0,24},{8,16},{16,8},{24,0},{1,25},{9,17},{17,9},{25,1},{2,26},{10... | collective-permute-start | bytes 442376 | tf_op jit(solution)/shard_map/ppermute | solution.py:131
  77.7 6.6 %collective-permute-start.13 = (bf16[112,384]{1,0:T(8,128)(2,1)S(1)}, bf16[112,384]{1,0:T(8,128)(2,1)S(1)}, u32[]{:S(2)}, u32[]{:S(2)}) collective-permute-start(bf16[112,384]{1,0:T(8,128)(2,1)S(1)} %line_total.1.refs_0_), channel_id=1, source_target_pairs={{0,2},{1,3},{2,0},{3,1},{4,6},{5,7},{6,4},{7,5},{8,10},{9,11},{10,... | collective-permute-start | bytes 258056 | tf_op jit(solution)/shard_map/ppermute | solution.py:126
  77.8 9.6 %collective-permute-start.14 = (bf16[112,384]{1,0:T(8,128)(2,1)S(1)}, bf16[112,384]{1,0:T(8,128)(2,1)S(1)}, u32[]{:S(2)}, u32[]{:S(2)}) collective-permute-start(bf16[112,384]{1,0:T(8,128)(2,1)S(1)} %line_total.1.refs_0_), channel_id=1, source_target_pairs={{0,4},{1,5},{2,6},{3,7},{4,0},{5,1},{6,2},{7,3},{8,12},{9,13},{10,... | collective-permute-start | bytes 258056 | tf_op jit(solution)/shard_map/ppermute | solution.py:126
  79.7 7.7 %collective-permute-start.15 = (bf16[112,384]{1,0:T(8,128)(2,1)S(1)}, bf16[112,384]{1,0:T(8,128)(2,1)S(1)}, u32[]{:S(2)}, u32[]{:S(2)}) collective-permute-start(bf16[112,384]{1,0:T(8,128)(2,1)S(1)} %line_total.1.refs_0_), channel_id=1, source_target_pairs={{0,6},{1,7},{2,4},{3,5},{4,2},{5,3},{6,0},{7,1},{8,14},{9,15},{10,... | collective-permute-start | bytes 258056 | tf_op jit(solution)/shard_map/ppermute | solution.py:126
  82.3 7.3 %collective-permute-start.22 = (bf16[48,384]{1,0:T(8,128)(2,1)S(1)}, bf16[48,384]{1,0:T(8,128)(2,1)S(1)}, u32[]{:S(2)}, u32[]{:S(2)}) collective-permute-start(bf16[48,384]{1,0:T(8,128)(2,1)S(1)} %get-tuple-element.162), channel_id=1, source_target_pairs={{0,2},{1,3},{2,0},{3,1},{4,6},{5,7},{6,4},{7,5},{8,10},{9,11},{10,... | collective-permute-start | bytes 110600 | tf_op jit(solution)/shard_map/ppermute | solution.py:126
  82.3 8.7 %collective-permute-start.23 = (bf16[48,384]{1,0:T(8,128)(2,1)S(1)}, bf16[48,384]{1,0:T(8,128)(2,1)S(1)}, u32[]{:S(2)}, u32[]{:S(2)}) collective-permute-start(bf16[48,384]{1,0:T(8,128)(2,1)S(1)} %get-tuple-element.161), channel_id=1, source_target_pairs={{0,4},{1,5},{2,6},{3,7},{4,0},{5,1},{6,2},{7,3},{8,12},{9,13},{10,... | collective-permute-start | bytes 110600 | tf_op jit(solution)/shard_map/ppermute | solution.py:126
  84.3 25.5 %copy-start.1 = (bf16[384,2304]{1,0:T(8,128)(2,1)S(1)}, bf16[384,2304]{1,0:T(8,128)(2,1)}, u32[]{:S(2)}) copy-start(bf16[384,2304]{1,0:T(8,128)(2,1)} %refs_8_.1) | copy-start | bytes 5308420
  84.3 6.7 %collective-permute-start.24 = (bf16[48,384]{1,0:T(8,128)(2,1)S(1)}, bf16[48,384]{1,0:T(8,128)(2,1)S(1)}, u32[]{:S(2)}, u32[]{:S(2)}) collective-permute-start(bf16[48,384]{1,0:T(8,128)(2,1)S(1)} %get-tuple-element.160), channel_id=1, source_target_pairs={{0,6},{1,7},{2,4},{3,5},{4,2},{5,3},{6,0},{7,1},{8,14},{9,15},{10,... | collective-permute-start | bytes 110600 | tf_op jit(solution)/shard_map/ppermute | solution.py:126
  87.5 17.6 %collective-permute-start.16 = (bf16[400,384]{1,0:T(8,128)(2,1)S(1)}, bf16[400,384]{1,0:T(8,128)(2,1)S(1)}, u32[]{:S(2)}, u32[]{:S(2)}) collective-permute-start(bf16[400,384]{1,0:T(8,128)(2,1)S(1)} %line_join.1.refs_0_), channel_id=1, source_target_pairs={{0,8},{8,0},{16,24},{24,16},{1,9},{9,1},{17,25},{25,17},{2,10},{10... | collective-permute-start | bytes 921608 | tf_op jit(solution)/shard_map/ppermute | solution.py:131
  88.8 16.3 %collective-permute-start.17 = (bf16[400,384]{1,0:T(8,128)(2,1)S(1)}, bf16[400,384]{1,0:T(8,128)(2,1)S(1)}, u32[]{:S(2)}, u32[]{:S(2)}) collective-permute-start(bf16[400,384]{1,0:T(8,128)(2,1)S(1)} %line_join.1.refs_0_), channel_id=1, source_target_pairs={{0,16},{8,24},{16,0},{24,8},{1,17},{9,25},{17,1},{25,9},{2,18},{10... | collective-permute-start | bytes 921608 | tf_op jit(solution)/shard_map/ppermute | solution.py:131
  89.6 15.5 %collective-permute-start.18 = (bf16[400,384]{1,0:T(8,128)(2,1)S(1)}, bf16[400,384]{1,0:T(8,128)(2,1)S(1)}, u32[]{:S(2)}, u32[]{:S(2)}) collective-permute-start(bf16[400,384]{1,0:T(8,128)(2,1)S(1)} %line_join.1.refs_0_), channel_id=1, source_target_pairs={{0,24},{8,16},{16,8},{24,0},{1,25},{9,17},{17,9},{25,1},{2,26},{10... | collective-permute-start | bytes 921608 | tf_op jit(solution)/shard_map/ppermute | solution.py:131
  91.6 6.6 %collective-permute-start.25 = (bf16[176,384]{1,0:T(8,128)(2,1)S(1)}, bf16[176,384]{1,0:T(8,128)(2,1)S(1)}, u32[]{:S(2)}, u32[]{:S(2)}) collective-permute-start(bf16[176,384]{1,0:T(8,128)(2,1)S(1)} %get-tuple-element.121), channel_id=1, source_target_pairs={{0,2},{1,3},{2,0},{3,1},{4,6},{5,7},{6,4},{7,5},{8,10},{9,11},{10,... | collective-permute-start | bytes 405512 | tf_op jit(solution)/shard_map/ppermute | solution.py:83
  93.7 7.4 %collective-permute-start.26 = (bf16[176,384]{1,0:T(8,128)(2,1)S(1)}, bf16[176,384]{1,0:T(8,128)(2,1)S(1)}, u32[]{:S(2)}, u32[]{:S(2)}) collective-permute-start(bf16[176,384]{1,0:T(8,128)(2,1)S(1)} %get-tuple-element.122), channel_id=1, source_target_pairs={{0,4},{1,5},{2,6},{3,7},{4,0},{5,1},{6,2},{7,3},{8,12},{9,13},{10,... | collective-permute-start | bytes 405512 | tf_op jit(solution)/shard_map/ppermute | solution.py:83
  98.2 6.9 %collective-permute-start.27 = (bf16[176,384]{1,0:T(8,128)(2,1)S(1)}, bf16[176,384]{1,0:T(8,128)(2,1)S(1)}, u32[]{:S(2)}, u32[]{:S(2)}) collective-permute-start(bf16[176,384]{1,0:T(8,128)(2,1)S(1)} %get-tuple-element.123), channel_id=1, source_target_pairs={{0,6},{1,7},{2,4},{3,5},{4,2},{5,3},{6,0},{7,1},{8,14},{9,15},{10,... | collective-permute-start | bytes 405512 | tf_op jit(solution)/shard_map/ppermute | solution.py:83
  105.1 2.5 %collective-permute-start.28 = (bf16[400,384]{1,0:T(8,128)(2,1)S(1)}, bf16[400,384]{1,0:T(8,128)(2,1)S(1)}, u32[]{:S(2)}, u32[]{:S(2)}) collective-permute-start(bf16[400,384]{1,0:T(8,128)(2,1)S(1)} %line_join.1.refs_0_), channel_id=1, source_target_pairs={{0,1},{1,0},{2,3},{3,2},{4,5},{5,4},{6,7},{7,6},{8,9},{9,8},{10,11... | collective-permute-start | bytes 921608 | tf_op jit(solution)/shard_map/ppermute | solution.py:117
  105.2 3.2 %collective-permute-start.29 = (bf16[400,384]{1,0:T(8,128)(2,1)S(1)}, bf16[400,384]{1,0:T(8,128)(2,1)S(1)}, u32[]{:S(2)}, u32[]{:S(2)}) collective-permute-start(bf16[400,384]{1,0:T(8,128)(2,1)S(1)} %collective-permute-done.16.refs_1_), channel_id=1, source_target_pairs={{0,1},{1,0},{2,3},{3,2},{4,5},{5,4},{6,7},{7,6},{8,9},{9,8},{10,11... | collective-permute-start | bytes 921608 | tf_op jit(solution)/shard_map/ppermute | solution.py:117
  105.7 4.1 %collective-permute-start.30 = (bf16[400,384]{1,0:T(8,128)(2,1)S(1)}, bf16[400,384]{1,0:T(8,128)(2,1)S(1)}, u32[]{:S(2)}, u32[]{:S(2)}) collective-permute-start(bf16[400,384]{1,0:T(8,128)(2,1)S(1)} %collective-permute-done.17.refs_2_), channel_id=1, source_target_pairs={{0,1},{1,0},{2,3},{3,2},{4,5},{5,4},{6,7},{7,6},{8,9},{9,8},{10,11... | collective-permute-start | bytes 921608 | tf_op jit(solution)/shard_map/ppermute | solution.py:117
  105.8 4.1 %collective-permute-start.31 = (bf16[400,384]{1,0:T(8,128)(2,1)S(1)}, bf16[400,384]{1,0:T(8,128)(2,1)S(1)}, u32[]{:S(2)}, u32[]{:S(2)}) collective-permute-start(bf16[400,384]{1,0:T(8,128)(2,1)S(1)} %collective-permute-done.18.refs_3_), channel_id=1, source_target_pairs={{0,1},{1,0},{2,3},{3,2},{4,5},{5,4},{6,7},{7,6},{8,9},{9,8},{10,11... | collective-permute-start | bytes 921608 | tf_op jit(solution)/shard_map/ppermute | solution.py:117
  106.3 9.1 %collective-permute-start.32 = (bf16[192,384]{1,0:T(8,128)(2,1)S(1)}, bf16[192,384]{1,0:T(8,128)(2,1)S(1)}, u32[]{:S(2)}, u32[]{:S(2)}) collective-permute-start(bf16[192,384]{1,0:T(8,128)(2,1)S(1)} %pad_maximum_fusion.1.refs_0_), channel_id=1, source_target_pairs={{0,8},{8,0},{16,24},{24,16},{1,9},{9,1},{17,25},{25,17},{2,10},{10... | collective-permute-start | bytes 442376 | tf_op jit(solution)/shard_map/ppermute | solution.py:131
  107.6 7.8 %collective-permute-start.33 = (bf16[192,384]{1,0:T(8,128)(2,1)S(1)}, bf16[192,384]{1,0:T(8,128)(2,1)S(1)}, u32[]{:S(2)}, u32[]{:S(2)}) collective-permute-start(bf16[192,384]{1,0:T(8,128)(2,1)S(1)} %pad_maximum_fusion.1.refs_0_), channel_id=1, source_target_pairs={{0,16},{8,24},{16,0},{24,8},{1,17},{9,25},{17,1},{25,9},{2,18},{10... | collective-permute-start | bytes 442376 | tf_op jit(solution)/shard_map/ppermute | solution.py:131
  108.4 7.9 %collective-permute-start.34 = (bf16[192,384]{1,0:T(8,128)(2,1)S(1)}, bf16[192,384]{1,0:T(8,128)(2,1)S(1)}, u32[]{:S(2)}, u32[]{:S(2)}) collective-permute-start(bf16[192,384]{1,0:T(8,128)(2,1)S(1)} %pad_maximum_fusion.1.refs_0_), channel_id=1, source_target_pairs={{0,24},{8,16},{16,8},{24,0},{1,25},{9,17},{17,9},{25,1},{2,26},{10... | collective-permute-start | bytes 442376 | tf_op jit(solution)/shard_map/ppermute | solution.py:131
  116.3 1.4 %collective-permute-start.35 = (bf16[192,384]{1,0:T(8,128)(2,1)S(1)}, bf16[192,384]{1,0:T(8,128)(2,1)S(1)}, u32[]{:S(2)}, u32[]{:S(2)}) collective-permute-start(bf16[192,384]{1,0:T(8,128)(2,1)S(1)} %pad_maximum_fusion.1.refs_0_), channel_id=1, source_target_pairs={{0,1},{1,0},{2,3},{3,2},{4,5},{5,4},{6,7},{7,6},{8,9},{9,8},{10,11... | collective-permute-start | bytes 442376 | tf_op jit(solution)/shard_map/ppermute | solution.py:117
  116.3 1.6 %collective-permute-start.36 = (bf16[192,384]{1,0:T(8,128)(2,1)S(1)}, bf16[192,384]{1,0:T(8,128)(2,1)S(1)}, u32[]{:S(2)}, u32[]{:S(2)}) collective-permute-start(bf16[192,384]{1,0:T(8,128)(2,1)S(1)} %collective-permute-done.32.refs_1_), channel_id=1, source_target_pairs={{0,1},{1,0},{2,3},{3,2},{4,5},{5,4},{6,7},{7,6},{8,9},{9,8},{10,11... | collective-permute-start | bytes 442376 | tf_op jit(solution)/shard_map/ppermute | solution.py:117
  116.8 1.4 %collective-permute-start.37 = (bf16[192,384]{1,0:T(8,128)(2,1)S(1)}, bf16[192,384]{1,0:T(8,128)(2,1)S(1)}, u32[]{:S(2)}, u32[]{:S(2)}) collective-permute-start(bf16[192,384]{1,0:T(8,128)(2,1)S(1)} %collective-permute-done.33.refs_2_), channel_id=1, source_target_pairs={{0,1},{1,0},{2,3},{3,2},{4,5},{5,4},{6,7},{7,6},{8,9},{9,8},{10,11... | collective-permute-start | bytes 442376 | tf_op jit(solution)/shard_map/ppermute | solution.py:117
  116.8 1.6 %collective-permute-start.38 = (bf16[192,384]{1,0:T(8,128)(2,1)S(1)}, bf16[192,384]{1,0:T(8,128)(2,1)S(1)}, u32[]{:S(2)}, u32[]{:S(2)}) collective-permute-start(bf16[192,384]{1,0:T(8,128)(2,1)S(1)} %collective-permute-done.34.refs_3_), channel_id=1, source_target_pairs={{0,1},{1,0},{2,3},{3,2},{4,5},{5,4},{6,7},{7,6},{8,9},{9,8},{10,11... | collective-permute-start | bytes 442376 | tf_op jit(solution)/shard_map/ppermute | solution.py:117
  (1 other events, 1.5 us)

commit v5 on v4

--- a/solution.py
+++ b/solution.py
@@ -812,10 +812,10 @@
         )
 
 
-def first_sums(place, own, weight, output, pieces):
+def first_sums(place, own, first, weight, output, pieces):
     grp_size = len(own)
     line = 1 if line_size() > 4 else line_size()
-    received = [swap_cores(part) for part in own]
+    received = [first] + [swap_cores(part) for part in own[1:]]
     width = weight.shape[0]
     hidden = grp_size * width
     block = pl.BlockSpec((1,) + output.shape[1:], lambda b: (b, 0, 0))
@@ -877,10 +877,10 @@
                         copy_line(place, line, half // line, parts[step], target, side * half)
 
 
-def second_sums(place, own):
+def second_sums(place, own, first):
     grp_size, width = len(own), own[0].shape[1]
     line = 1 if line_size() > 4 else line_size()
-    received = [swap_cores(part) for part in own]
+    received = [first] + [swap_cores(part) for part in own[1:]]
     shapes = [(width, (grp_size - 1) * width), (width, width)]
     return pl.pallas_call(
         partial(second_sums_kernel, grp_size, line),
@@ -1057,13 +1057,16 @@
     pieces = pieces_from_owner(pieces, share)
     at_pieces = [piece[block_rows:] for piece in pieces] if line else [sum_line(at_plane)]
     ff_parts = gather_plane(ff_plane)
-    at_parts = gather_plane(jnp.concatenate(at_pieces))
+    ff_first = swap_cores(ff_plane)
+    at_held = jnp.concatenate(at_pieces)
+    at_parts = gather_plane(at_held)
+    at_first = swap_cores(at_held)
     ff_parts = list(after_all(ff_parts, *pieces))
     grad_shrink, grad_expand, grad_mod_weight, output, grad_tokens, grad_table, grad_mod_bias, *biases = (
-        first_sums(where, ff_parts, modulation_weight, output, pieces)
+        first_sums(where, ff_parts, ff_first, modulation_weight, output, pieces)
     )
     at_parts = list(after_all(at_parts, grad_shrink))
-    grad_attend, grad_output = second_sums(where, at_parts)
+    grad_attend, grad_output = second_sums(where, at_parts, at_first)
     return (
         output[None],
         grad_tokens[None],

time: 121 us -> 121 us (level)
  transfers between devices with their start and end apart: 41 -> 41, of which waited for: 13 -> 12; matrix products, arithmetic and copies ran while one was open for 4% -> 4% of each run, Pallas kernels for 25% -> 25%
where the time goes in v5:
time: 121 us; the launch traced here: 120 us
  starting transfers between devices  49.1 us (41%)
  Pallas kernels  40.2 us (33%)
  waiting for transfers between devices  21 us (17%)
  local copies, waits for them, and re-layouts  4.06 us (3%)
  other arithmetic  4 us (3%)
  between operations  1.85 us (2%)
    ppermute x12, starting transfers between devices, plane_send(): lax.ppermute(values, 'grp', [(d, away(d, grp_size, step)) for d in range(...  14.2 us
    pallas_call x1, Pallas kernels, backward_attention(): pl.pallas_call(partial(backward_kernel, head_width, 1.0 / math.sqrt(head_...  11.7 us
    ppermute x6, starting transfers between devices, rows_to_owner(): lax.ppermute(block, 'seq', owner_pairs(seq_size, owners, share, step))  10.6 us
    pallas_call x1, Pallas kernels, forward_attention(): pl.pallas_call(partial(forward_kernel, head_width, 1.0 / math.sqrt(head_w...  9.96 us
    ppermute x6, starting transfers between devices, line_send(): lax.ppermute(values, 'seq', owner_pairs(seq_size, seq_size // 2, 2, step))  8.89 us
    pallas_call x1, Pallas kernels, middle(): pl.pallas_call(middle_kernel, grid=(1,), in_specs=[pl.BlockSpec(memory_sp...  8.44 us
    ppermute x3, waiting for transfers between devices, pieces_from_owner(): lax.ppermute(pieces[step], 'seq', owner_pairs(seq_size, owners, share, st...  8.22 us
    pallas_call x1, Pallas kernels, first_sums(): pl.pallas_call(partial(first_sums_kernel, grp_size, line), grid=(grp_size...  5.51 us
  transfers between devices with their start and end apart: 41, of which 12 were waited for; matrix products, arithmetic and copies ran while one was open for 4% of the time, Pallas kernels for 25%

profile of v5, /device:TPU:0, one launch (start us, length us, event | category | flops | bytes accessed | tf_op | source)
XLA Modules:
  0.0 120.3 jit_solution(1747134522000376498)
XLA Ops:
  0.7 1.2 dynamic-slice_bitcast_fusion.4
  1.9 3.1 %collective-permute-start = (bf16[128,384]{1,0:T(8,128)(2,1)S(1)}, bf16[128,384]{1,0:T(8,128)(2,1)S(1)}, u32[]{:S(2)}, u32[]{:S(2)}) collective-permute-start(bf16[128,384]{1,0:T(8,128)(2,1)S(1)} %get-tuple-element.157), channel_id=1, source_target_pairs={{0,2},{1,3},{2,0},{3,1},{4,6},{5,7},{6,4},{7,5},{8,10},{9,11},{10,... | collective-permute-start | bytes 294920 | tf_op jit(solution)/shard_map/ppermute | solution.py:75
  5.0 2.6 %collective-permute-start.1 = (bf16[128,384]{1,0:T(8,128)(2,1)S(1)}, bf16[128,384]{1,0:T(8,128)(2,1)S(1)}, u32[]{:S(2)}, u32[]{:S(2)}) collective-permute-start(bf16[128,384]{1,0:T(8,128)(2,1)S(1)} %get-tuple-element.159), channel_id=1, source_target_pairs={{0,4},{1,5},{2,6},{3,7},{4,0},{5,1},{6,2},{7,3},{8,12},{9,13},{10,... | collective-permute-start | bytes 294920 | tf_op jit(solution)/shard_map/ppermute | solution.py:75
  7.6 0.7 maximum_convert_fusion
  8.4 1.0 collective-permute-start.3
  10.0 0.1 stack.17.place
  10.1 1.5 %copy-done = bf16[384,2304]{1,0:T(8,128)(2,1)S(1)} copy-done((bf16[384,2304]{1,0:T(8,128)(2,1)S(1)}, bf16[384,2304]{1,0:T(8,128)(2,1)}, u32[]{:S(2)}) %copy-start) | copy-done | bytes 1769496
  11.6 0.9 prepare.1
  12.6 2.8 %collective-permute-done.1 = bf16[128,384]{1,0:T(8,128)(2,1)S(1)} collective-permute-done((bf16[128,384]{1,0:T(8,128)(2,1)S(1)}, bf16[128,384]{1,0:T(8,128)(2,1)S(1)}, u32[]{:S(2)}, u32[]{:S(2)}) %collective-permute-start.1) | collective-permute-done | bytes 98336 | tf_op jit(solution)/shard_map/ppermute | solution.py:75
  15.4 0.1 collective-permute-done.3
  15.6 0.1 collective-permute-start.4
  15.7 2.6 %collective-permute-start.5 = (bf16[128,384]{1,0:T(8,128)(2,1)S(1)}, bf16[128,384]{1,0:T(8,128)(2,1)S(1)}, u32[]{:S(2)}, u32[]{:S(2)}) collective-permute-start(bf16[128,384]{1,0:T(8,128)(2,1)S(1)} %get-tuple-element.91), channel_id=1, source_target_pairs={{0,4},{1,5},{2,6},{3,7},{4,0},{5,1},{6,2},{7,3},{8,12},{9,13},{10,... | collective-permute-start | bytes 294920 | tf_op jit(solution)/shard_map/ppermute | solution.py:75
  18.3 1.3 %collective-permute-start.6 = (bf16[128,384]{1,0:T(8,128)(2,1)S(1)}, bf16[128,384]{1,0:T(8,128)(2,1)S(1)}, u32[]{:S(2)}, u32[]{:S(2)}) collective-permute-start(bf16[128,384]{1,0:T(8,128)(2,1)S(1)} %get-tuple-element.92), channel_id=1, source_target_pairs={{0,6},{1,7},{2,4},{3,5},{4,2},{5,3},{6,0},{7,1},{8,14},{9,15},{10,... | collective-permute-start | bytes 294920 | tf_op jit(solution)/shard_map/ppermute | solution.py:75
  19.7 10.0 %forward_attention.1 = (bf16[6,1024,512]{2,1,0:T(8,128)(2,1)}, bf16[384,512]{1,0:T(8,128)(2,1)S(1)}, bf16[768,1024]{1,0:T(8,128)(2,1)S(1)}, f32[384,512]{1,0:T(8...) custom-call(s32[5]{0:T(128)S(1)} %stack.17.place, s32[4,8]{1,0:T(4,128)S(1)} %bitcast.25, ...), custom_call_target="tpu_custom_call" | custom-call | flops 3221225472 | bytes 6291456 | tf_op jit(solution)/shard_map/forward_attention/pallas_call | solution.py:389
  29.8 8.4 %middle.1 = (bf16[1536,384]{1,0:T(8,128)(2,1)S(1)}, bf16[1536,384]{1,0:T(8,128)(2,1)}, bf16[384,384]{1,0:T(8,128)(2,1)}, bf16[384,512]{1,0:T(8,128)(2,1)}, f32[5...) custom-call(s32[5]{0:T(128)S(1)} %stack.17.place, ...), custom_call_target="tpu_custom_call" | custom-call | flops 4831838208 | bytes 16777216 | tf_op jit(solution)/shard_map/middle/pallas_call | solution.py:489
  38.2 0.1 collective-permute-start.7
  38.3 3.7 %all-to-all-start = ((bf16[4,128,384]{2,1,0:T(8,128)(2,1)}), bf16[4,128,384]{2,1,0:T(8,128)(2,1)S(1)}, u32[]{:S(2)}, u32[]{:S(2)}) async-start(bf16[4,128,384]{2,1,0:T(8,128)(2,1)} %get-tuple-element.109), calls=%async_computation | async-start | bytes 786432 | tf_op jit(solution)/shard_map/all_to_all | solution.py:91
  42.1 1.7 %add_convert_fusion = bf16[1536,384]{1,0:T(8,128)(2,1)S(1)} fusion(bf16[1536,384]{1,0:T(8,128)(2,1)} %collective-permute-done.7, bf16[1536,384]{1,0:T(8,128)(2,1)S(1)} %get-tuple-element.98), kind=kLoop, calls=%fused_computation | loop fusion | flops 2359296 | bytes 3538944 | tf_op jit(solution)/shard_map/convert_element_type | solution.py:181
  43.9 1.0 constant_dynamic-slice_fusion.8
  44.8 1.5 %collective-permute-start.8 = (bf16[384,384]{1,0:T(8,128)(2,1)}, bf16[384,384]{1,0:T(8,128)(2,1)S(1)}, u32[]{:S(2)}, u32[]{:S(2)}) collective-permute-start(bf16[384,384]{1,0:T(8,128)(2,1)} %get-tuple-element.147), channel_id=1, source_target_pairs={{0,8},{8,0},{16,24},{24,16},{1,9},{9,1},{17,25},{25,17},{2,10},{10... | collective-permute-start | bytes 884744 | tf_op jit(solution)/shard_map/ppermute | solution.py:131
  46.3 1.5 %collective-permute-start.9 = (bf16[384,384]{1,0:T(8,128)(2,1)}, bf16[384,384]{1,0:T(8,128)(2,1)S(1)}, u32[]{:S(2)}, u32[]{:S(2)}) collective-permute-start(bf16[384,384]{1,0:T(8,128)(2,1)} %get-tuple-element.146), channel_id=1, source_target_pairs={{0,16},{8,24},{16,0},{24,8},{1,17},{9,25},{17,1},{25,9},{2,18},{10... | collective-permute-start | bytes 884744 | tf_op jit(solution)/shard_map/ppermute | solution.py:131
  47.9 0.5 collective-permute-start.10
  48.4 11.7 %backward_attention.1 = (bf16[768,384]{1,0:T(8,128)(2,1)}, bf16[768,384]{1,0:T(8,128)(2,1)S(1)}, bf16[528,384]{1,0:T(8,128)(2,1)}, bf16[512,384]{1,0:T(8,128)(2,1)S(1)}, f32[16,384]{1,0:T(8,128)S(1)}) custom-call(s32[5]{0:T(128)S(1)} %stack.17.place, bf16[6,1024,512]{2,1,0:T(8,128)(2,1)} %get-tuple-element.85.expo, bf16[384,512]{1,0:T(8,128)(2,1)S(1)} %copy-done.20, ...), custom_call_target="tpu_custom_call" | custom-call | flops 6442450944 | bytes 6291456 | tf_op jit(solution)/shard_map/backward_attention/pallas_call | solution.py:593
  60.1 1.7 %collective-permute-done.9.refs_2_ = bf16[384,384]{1,0:T(8,128)(2,1)S(1)} collective-permute-done((bf16[384,384]{1,0:T(8,128)(2,1)}, bf16[384,384]{1,0:T(8,128)(2,1)S(1)}, u32[]{:S(2)}, u32[]{:S(2)}) %collective-permute-start.9) | collective-permute-done | bytes 294944 | tf_op jit(solution)/shard_map/ppermute | solution.py:131
  61.9 0.5 collective-permute-start.11
  62.4 0.9 sum_parts.1
  63.3 4.6 %all-to-all-start.1 = ((bf16[4,96,384]{2,1,0:T(8,128)(2,1)}), bf16[4,96,384]{2,1,0:T(8,128)(2,1)S(1)}, u32[]{:S(2)}, u32[]{:S(2)}) async-start(bf16[4,96,384]{2,1,0:T(8,128)(2,1)} %bitcast.13), calls=%async_computation.1 | async-start | bytes 589824 | tf_op jit(solution)/shard_map/all_to_all | solution.py:171
  67.9 1.4 %add_convert_fusion.1 = bf16[768,384]{1,0:T(8,128)(2,1)S(1)} fusion(bf16[768,384]{1,0:T(8,128)(2,1)} %collective-permute-done.12, bf16[768,384]{1,0:T(8,128)(2,1)} %get-tuple-element.112), kind=kLoop, calls=%fused_computation.1 | loop fusion | flops 1179648 | bytes 1769472 | tf_op jit(solution)/shard_map/convert_element_type | solution.py:181
  69.2 0.1 constant_dynamic-slice_fusion.4
  69.3 1.3 %collective-permute-start.19 = (bf16[192,384]{1,0:T(8,128)(2,1)S(1)}, bf16[192,384]{1,0:T(8,128)(2,1)S(1)}, u32[]{:S(2)}, u32[]{:S(2)}) collective-permute-start(bf16[192,384]{1,0:T(8,128)(2,1)S(1)} %get-tuple-element.150), channel_id=1, source_target_pairs={{0,8},{8,0},{16,24},{24,16},{1,9},{9,1},{17,25},{25,17},{2,10},{10... | collective-permute-start | bytes 442376 | tf_op jit(solution)/shard_map/ppermute | solution.py:131
  70.6 0.8 collective-permute-start.20
  71.5 1.4 %collective-permute-start.21 = (bf16[192,384]{1,0:T(8,128)(2,1)S(1)}, bf16[192,384]{1,0:T(8,128)(2,1)S(1)}, u32[]{:S(2)}, u32[]{:S(2)}) collective-permute-start(bf16[192,384]{1,0:T(8,128)(2,1)S(1)} %get-tuple-element.148), channel_id=1, source_target_pairs={{0,24},{8,16},{16,8},{24,0},{1,25},{9,17},{17,9},{25,1},{2,26},{10... | collective-permute-start | bytes 442376 | tf_op jit(solution)/shard_map/ppermute | solution.py:131
  72.9 4.8 %all-to-all-done.1.refs_0_ = bf16[4,96,384]{2,1,0:T(8,128)(2,1)S(1)} async-done(((bf16[4,96,384]{2,1,0:T(8,128)(2,1)}), bf16[4,96,384]{2,1,0:T(8,128)(2,1)S(1)}, u32[]{:S(2)}, u32[]{:S(2)}) %all-to-all-start.1) | async-done | bytes 294944 | tf_op jit(solution)/shard_map/all_to_all | solution.py:171
  77.7 0.1 collective-permute-start.13
  77.8 2.0 %collective-permute-start.14 = (bf16[112,384]{1,0:T(8,128)(2,1)S(1)}, bf16[112,384]{1,0:T(8,128)(2,1)S(1)}, u32[]{:S(2)}, u32[]{:S(2)}) collective-permute-start(bf16[112,384]{1,0:T(8,128)(2,1)S(1)} %line_total.1.refs_0_), channel_id=1, source_target_pairs={{0,4},{1,5},{2,6},{3,7},{4,0},{5,1},{6,2},{7,3},{8,12},{9,13},{10,... | collective-permute-start | bytes 258056 | tf_op jit(solution)/shard_map/ppermute | solution.py:126
  79.7 2.4 %collective-permute-start.15 = (bf16[112,384]{1,0:T(8,128)(2,1)S(1)}, bf16[112,384]{1,0:T(8,128)(2,1)S(1)}, u32[]{:S(2)}, u32[]{:S(2)}) collective-permute-start(bf16[112,384]{1,0:T(8,128)(2,1)S(1)} %line_total.1.refs_0_), channel_id=1, source_target_pairs={{0,6},{1,7},{2,4},{3,5},{4,2},{5,3},{6,0},{7,1},{8,14},{9,15},{10,... | collective-permute-start | bytes 258056 | tf_op jit(solution)/shard_map/ppermute | solution.py:126
  82.2 0.1 add_convert_fusion.2
  82.3 0.1 collective-permute-start.22
  82.3 2.0 %collective-permute-start.23 = (bf16[48,384]{1,0:T(8,128)(2,1)S(1)}, bf16[48,384]{1,0:T(8,128)(2,1)S(1)}, u32[]{:S(2)}, u32[]{:S(2)}) collective-permute-start(bf16[48,384]{1,0:T(8,128)(2,1)S(1)} %get-tuple-element.161), channel_id=1, source_target_pairs={{0,4},{1,5},{2,6},{3,7},{4,0},{5,1},{6,2},{7,3},{8,12},{9,13},{10,... | collective-permute-start | bytes 110600 | tf_op jit(solution)/shard_map/ppermute | solution.py:126
  84.3 2.4 %collective-permute-start.24 = (bf16[48,384]{1,0:T(8,128)(2,1)S(1)}, bf16[48,384]{1,0:T(8,128)(2,1)S(1)}, u32[]{:S(2)}, u32[]{:S(2)}) collective-permute-start(bf16[48,384]{1,0:T(8,128)(2,1)S(1)} %get-tuple-element.160), channel_id=1, source_target_pairs={{0,6},{1,7},{2,4},{3,5},{4,2},{5,3},{6,0},{7,1},{8,14},{9,15},{10,... | collective-permute-start | bytes 110600 | tf_op jit(solution)/shard_map/ppermute | solution.py:126
  86.7 0.7 collective-permute-done.14.refs_2_
  87.5 1.3 %collective-permute-start.16 = (bf16[400,384]{1,0:T(8,128)(2,1)S(1)}, bf16[400,384]{1,0:T(8,128)(2,1)S(1)}, u32[]{:S(2)}, u32[]{:S(2)}) collective-permute-start(bf16[400,384]{1,0:T(8,128)(2,1)S(1)} %line_join.1.refs_0_), channel_id=1, source_target_pairs={{0,8},{8,0},{16,24},{24,16},{1,9},{9,1},{17,25},{25,17},{2,10},{10... | collective-permute-start | bytes 921608 | tf_op jit(solution)/shard_map/ppermute | solution.py:131
  88.8 0.8 collective-permute-start.17
  89.6 1.4 %collective-permute-start.18 = (bf16[400,384]{1,0:T(8,128)(2,1)S(1)}, bf16[400,384]{1,0:T(8,128)(2,1)S(1)}, u32[]{:S(2)}, u32[]{:S(2)}) collective-permute-start(bf16[400,384]{1,0:T(8,128)(2,1)S(1)} %line_join.1.refs_0_), channel_id=1, source_target_pairs={{0,24},{8,16},{16,8},{24,0},{1,25},{9,17},{17,9},{25,1},{2,26},{10... | collective-permute-start | bytes 921608 | tf_op jit(solution)/shard_map/ppermute | solution.py:131
  91.0 0.6 finish_rows.1
  91.6 2.1 %collective-permute-start.25 = (bf16[176,384]{1,0:T(8,128)(2,1)S(1)}, bf16[176,384]{1,0:T(8,128)(2,1)S(1)}, u32[]{:S(2)}, u32[]{:S(2)}) collective-permute-start(bf16[176,384]{1,0:T(8,128)(2,1)S(1)} %get-tuple-element.121), channel_id=1, source_target_pairs={{0,2},{1,3},{2,0},{3,1},{4,6},{5,7},{6,4},{7,5},{8,10},{9,11},{10,... | collective-permute-start | bytes 405512 | tf_op jit(solution)/shard_map/ppermute | solution.py:83
  93.7 0.8 collective-permute-start.26
  94.6 3.6 %collective-permute-done.25.refs_11_ = bf16[176,384]{1,0:T(8,128)(2,1)S(1)} collective-permute-done((bf16[176,384]{1,0:T(8,128)(2,1)S(1)}, bf16[176,384]{1,0:T(8,128)(2,1)S(1)}, u32[]{:S(2)}, u32[]{:S(2)}) %collective-permute-start.25) | collective-permute-done | bytes 135200 | tf_op jit(solution)/shard_map/ppermute | solution.py:83
  98.2 2.3 %collective-permute-start.27 = (bf16[176,384]{1,0:T(8,128)(2,1)S(1)}, bf16[176,384]{1,0:T(8,128)(2,1)S(1)}, u32[]{:S(2)}, u32[]{:S(2)}) collective-permute-start(bf16[176,384]{1,0:T(8,128)(2,1)S(1)} %get-tuple-element.123), channel_id=1, source_target_pairs={{0,6},{1,7},{2,4},{3,5},{4,2},{5,3},{6,0},{7,1},{8,14},{9,15},{10,... | collective-permute-start | bytes 405512 | tf_op jit(solution)/shard_map/ppermute | solution.py:83
  100.5 0.6 collective-permute-done.26.refs_12_
  101.1 4.0 %collective-permute-done.27.refs_13_ = bf16[176,384]{1,0:T(8,128)(2,1)S(1)} collective-permute-done((bf16[176,384]{1,0:T(8,128)(2,1)S(1)}, bf16[176,384]{1,0:T(8,128)(2,1)S(1)}, u32[]{:S(2)}, u32[]{:S(2)}) %collective-permute-start.27) | collective-permute-done | bytes 135200 | tf_op jit(solution)/shard_map/ppermute | solution.py:83
  105.1 0.1 collective-permute-start.29
  105.2 0.5 collective-permute-start.30
  105.7 0.1 collective-permute-start.31
  105.8 1.3 %collective-permute-start.32 = (bf16[192,384]{1,0:T(8,128)(2,1)S(1)}, bf16[192,384]{1,0:T(8,128)(2,1)S(1)}, u32[]{:S(2)}, u32[]{:S(2)}) collective-permute-start(bf16[192,384]{1,0:T(8,128)(2,1)S(1)} %pad_maximum_fusion.1.refs_0_), channel_id=1, source_target_pairs={{0,8},{8,0},{16,24},{24,16},{1,9},{9,1},{17,25},{25,17},{2,10},{10... | collective-permute-start | bytes 442376 | tf_op jit(solution)/shard_map/ppermute | solution.py:131
  107.1 0.8 collective-permute-start.33
  108.0 1.4 %collective-permute-start.34 = (bf16[192,384]{1,0:T(8,128)(2,1)S(1)}, bf16[192,384]{1,0:T(8,128)(2,1)S(1)}, u32[]{:S(2)}, u32[]{:S(2)}) collective-permute-start(bf16[192,384]{1,0:T(8,128)(2,1)S(1)} %pad_maximum_fusion.1.refs_0_), channel_id=1, source_target_pairs={{0,24},{8,16},{16,8},{24,0},{1,25},{9,17},{17,9},{25,1},{2,26},{10... | collective-permute-start | bytes 442376 | tf_op jit(solution)/shard_map/ppermute | solution.py:131
  109.4 5.5 %first_sums.1 = (f32[1536,384]{1,0:T(8,128)}, f32[384,1536]{1,0:T(8,128)}, f32[384,2304]{1,0:T(8,128)}, bf16[4,128,384]{2,1,0:T(8,128)(2,1)}, f32[4,128,384]{2,1...) custom-call(s32[5]{0:T(128)S(1)} %stack.17.place, ...), custom_call_target="tpu_custom_call" | custom-call | tf_op jit(solution)/shard_map/first_sums/pallas_call | solution.py:823
  115.0 1.3 %collective-permute-done.34.refs_3_ = bf16[192,384]{1,0:T(8,128)(2,1)S(1)} collective-permute-done((bf16[192,384]{1,0:T(8,128)(2,1)S(1)}, bf16[192,384]{1,0:T(8,128)(2,1)S(1)}, u32[]{:S(2)}, u32[]{:S(2)}) %collective-permute-start.34) | collective-permute-done | bytes 147488 | tf_op jit(solution)/shard_map/ppermute | solution.py:131
  116.2 0.5 collective-permute-start.37
  116.7 0.9 collective-permute-done.36.refs_5_
  117.6 0.2 collective-permute-done.37.refs_6_
  117.8 0.3 collective-permute-done.38.refs_7_
  118.1 2.2 %second_sums.1 = (f32[384,1152]{1,0:T(8,128)}, f32[384,384]{1,0:T(8,128)}) custom-call(s32[5]{0:T(128)S(1)} %stack.17.place, bf16[192,384]{1,0:T(8,128)(2,1)S(1)} %pad_maximum_fusion.1.refs_0_, bf16[192,384]{1,0:T(8,128)(2,1)S(1)} %collective-permute-done.32.refs_1_, bf16[192,384]{1,0:T(8,128)(2,1)S(1)} %collective-permute-done.33.refs_2_, ...), custom_call_target="tpu_custom_call" | custom-call | tf_op jit(solution)/shard_map/second_sums/pallas_call | solution.py:885
  (97 shorter events, 0.5 us)
Async XLA Ops:
  0.6 7.7 %copy-start.23 = (bf16[1,4,128,384]{3,2,1,0:T(8,128)(2,1)S(1)}, bf16[1,4,128,384]{3,2,1,0:T(8,128)(2,1)}, u32[]{:S(2)}) copy-start(bf16[1,4,128,384]{3,2,1,0:T(8,128)(2,1)} %param.17) | copy-start | bytes 1179652
  0.7 9.5 %copy-start.4 = (s32[4]{0:T(128)S(1)}, s32[4]{0:T(128)}, u32[]{:S(2)}) copy-start(s32[4]{0:T(128)} %counts.1) | copy-start | bytes 52
  0.7 9.5 %copy-start.3 = (bf16[8,384]{1,0:T(8,128)(2,1)S(1)}, bf16[8,384]{1,0:T(8,128)(2,1)}, u32[]{:S(2)}) copy-start(bf16[8,384]{1,0:T(8,128)(2,1)} %table.1) | copy-start | bytes 18436
  0.7 9.5 %copy-start.2 = (bf16[384,1152]{1,0:T(8,128)(2,1)S(1)}, bf16[384,1152]{1,0:T(8,128)(2,1)}, u32[]{:S(2)}) copy-start(bf16[384,1152]{1,0:T(8,128)(2,1)} %attend_weight.1) | copy-start | bytes 2654212
  1.9 10.7 %collective-permute-start = (bf16[128,384]{1,0:T(8,128)(2,1)S(1)}, bf16[128,384]{1,0:T(8,128)(2,1)S(1)}, u32[]{:S(2)}, u32[]{:S(2)}) collective-permute-start(bf16[128,384]{1,0:T(8,128)(2,1)S(1)} %get-tuple-element.157), channel_id=1, source_target_pairs={{0,2},{1,3},{2,0},{3,1},{4,6},{5,7},{6,4},{7,5},{8,10},{9,11},{10,... | collective-permute-start | bytes 294920 | tf_op jit(solution)/shard_map/ppermute | solution.py:75
  5.0 10.4 %collective-permute-start.1 = (bf16[128,384]{1,0:T(8,128)(2,1)S(1)}, bf16[128,384]{1,0:T(8,128)(2,1)S(1)}, u32[]{:S(2)}, u32[]{:S(2)}) collective-permute-start(bf16[128,384]{1,0:T(8,128)(2,1)S(1)} %get-tuple-element.159), channel_id=1, source_target_pairs={{0,4},{1,5},{2,6},{3,7},{4,0},{5,1},{6,2},{7,3},{8,12},{9,13},{10,... | collective-permute-start | bytes 294920 | tf_op jit(solution)/shard_map/ppermute | solution.py:75
  7.6 7.8 %collective-permute-start.2 = (bf16[128,384]{1,0:T(8,128)(2,1)S(1)}, bf16[128,384]{1,0:T(8,128)(2,1)S(1)}, u32[]{:S(2)}, u32[]{:S(2)}) collective-permute-start(bf16[128,384]{1,0:T(8,128)(2,1)S(1)} %get-tuple-element.156), channel_id=1, source_target_pairs={{0,6},{1,7},{2,4},{3,5},{4,2},{5,3},{6,0},{7,1},{8,14},{9,15},{10,... | collective-permute-start | bytes 294920 | tf_op jit(solution)/shard_map/ppermute | solution.py:75
  8.4 7.1 %collective-permute-start.3 = (bf16[128,384]{1,0:T(8,128)(2,1)S(1)}, bf16[128,384]{1,0:T(8,128)(2,1)S(1)}, u32[]{:S(2)}, u32[]{:S(2)}) collective-permute-start(bf16[128,384]{1,0:T(8,128)(2,1)S(1)} %get-tuple-element.79), channel_id=1, source_target_pairs={{0,2},{1,3},{2,0},{3,1},{4,6},{5,7},{6,4},{7,5},{8,10},{9,11},{10,... | collective-permute-start | bytes 294920 | tf_op jit(solution)/shard_map/ppermute | solution.py:75
  11.6 8.0 %copy-start.12 = (s32[1,4,1024]{2,1,0:T(4,128)S(1)}, s32[1,4,1024]{2,1,0:T(4,128)}, u32[]{:S(2)}) copy-start(s32[1,4,1024]{2,1,0:T(4,128)} %param.19) | copy-start | bytes 49156
  11.6 8.0 %copy-start.13 = (s32[1,4,8]{2,1,0:T(4,128)S(1)}, s32[1,4,8]{2,1,0:T(4,128)}, u32[]{:S(2)}) copy-start(s32[1,4,8]{2,1,0:T(4,128)} %param.18) | copy-start | bytes 388
  12.6 17.1 %copy-start.7 = (bf16[1152,384]{1,0:T(8,128)(2,1)}, bf16[1152,384]{1,0:T(8,128)(2,1)S(1)}, u32[]{:S(2)}) copy-start(bf16[1152,384]{1,0:T(8,128)(2,1)S(1)} %get-tuple-element.84.weight) | copy-start | bytes 2654212
  15.6 4.0 %collective-permute-start.4 = (bf16[512,384]{1,0:T(8,128)(2,1)S(1)}, bf16[512,384]{1,0:T(8,128)(2,1)S(1)}, u32[]{:S(2)}, u32[]{:S(2)}) collective-permute-start(bf16[512,384]{1,0:T(8,128)(2,1)S(1)} %constant_dynamic-update-slice_fusion.own), channel_id=1, source_target_pairs={{0,1},{1,0},{2,3},{3,2},{4,5},{5,4},{6,7},{7,6},{8,9},{9,8},{10,11... | collective-permute-start | bytes 1179656 | tf_op jit(solution)/shard_map/ppermute | solution.py:97
  15.7 14.0 %collective-permute-start.5 = (bf16[128,384]{1,0:T(8,128)(2,1)S(1)}, bf16[128,384]{1,0:T(8,128)(2,1)S(1)}, u32[]{:S(2)}, u32[]{:S(2)}) collective-permute-start(bf16[128,384]{1,0:T(8,128)(2,1)S(1)} %get-tuple-element.91), channel_id=1, source_target_pairs={{0,4},{1,5},{2,6},{3,7},{4,0},{5,1},{6,2},{7,3},{8,12},{9,13},{10,... | collective-permute-start | bytes 294920 | tf_op jit(solution)/shard_map/ppermute | solution.py:75
  18.3 11.4 %collective-permute-start.6 = (bf16[128,384]{1,0:T(8,128)(2,1)S(1)}, bf16[128,384]{1,0:T(8,128)(2,1)S(1)}, u32[]{:S(2)}, u32[]{:S(2)}) collective-permute-start(bf16[128,384]{1,0:T(8,128)(2,1)S(1)} %get-tuple-element.92), channel_id=1, source_target_pairs={{0,6},{1,7},{2,4},{3,5},{4,2},{5,3},{6,0},{7,1},{8,14},{9,15},{10,... | collective-permute-start | bytes 294920 | tf_op jit(solution)/shard_map/ppermute | solution.py:75
  19.6 10.0 %copy-start.9 = (bf16[512,384]{1,0:T(8,128)(2,1)}, bf16[512,384]{1,0:T(8,128)(2,1)S(1)}, u32[]{:S(2)}) copy-start(bf16[512,384]{1,0:T(8,128)(2,1)S(1)} %collective-permute-done.4.rest) | copy-start | bytes 1179652
  19.6 10.1 %copy-start.5 = (bf16[384,1536]{1,0:T(8,128)(2,1)S(1)}, bf16[384,1536]{1,0:T(8,128)(2,1)}, u32[]{:S(2)}) copy-start(bf16[384,1536]{1,0:T(8,128)(2,1)} %expand_weight.1) | copy-start | bytes 3538948
  19.7 10.1 %copy-start.6 = (bf16[1536,384]{1,0:T(8,128)(2,1)S(1)}, bf16[1536,384]{1,0:T(8,128)(2,1)}, u32[]{:S(2)}) copy-start(bf16[1536,384]{1,0:T(8,128)(2,1)} %shrink_weight.1) | copy-start | bytes 3538948
  19.7 10.1 %copy-start.11 = (bf16[384,384]{1,0:T(8,128)(2,1)S(1)}, bf16[384,384]{1,0:T(8,128)(2,1)}, u32[]{:S(2)}) copy-start(bf16[384,384]{1,0:T(8,128)(2,1)} %output_weight.1) | copy-start | bytes 884740
  29.6 8.6 %copy-start.14 = (bf16[768,1024]{1,0:T(8,128)(2,1)}, bf16[768,1024]{1,0:T(8,128)(2,1)S(1)}, u32[]{:S(2)}) copy-start(bf16[768,1024]{1,0:T(8,128)(2,1)S(1)} %get-tuple-element.87.key_value) | copy-start | bytes 4718596
  29.6 8.6 %copy-start.16 = (f32[384,512]{1,0:T(8,128)}, f32[384,512]{1,0:T(8,128)S(1)}, u32[]{:S(2)}) copy-start(f32[384,512]{1,0:T(8,128)S(1)} %get-tuple-element.88.attended_wide) | copy-start | bytes 2359300
  29.7 8.6 %copy-start.19 = (bf16[384,512]{1,0:T(8,128)(2,1)}, bf16[384,512]{1,0:T(8,128)(2,1)S(1)}, u32[]{:S(2)}) copy-start(bf16[384,512]{1,0:T(8,128)(2,1)S(1)} %get-tuple-element.86.query) | copy-start | bytes 1179652
  38.2 3.8 %collective-permute-start.7 = (bf16[1536,384]{1,0:T(8,128)(2,1)}, bf16[1536,384]{1,0:T(8,128)(2,1)}, u32[]{:S(2)}, u32[]{:S(2)}) collective-permute-start(bf16[1536,384]{1,0:T(8,128)(2,1)} %get-tuple-element.99), channel_id=1, source_target_pairs={{0,1},{1,0},{2,3},{3,2},{4,5},{5,4},{6,7},{7,6},{8,9},{9,8},{10,11... | collective-permute-start | bytes 3538952 | tf_op jit(solution)/shard_map/ppermute | solution.py:117
  38.3 21.8 %all-to-all-start = ((bf16[4,128,384]{2,1,0:T(8,128)(2,1)}), bf16[4,128,384]{2,1,0:T(8,128)(2,1)S(1)}, u32[]{:S(2)}, u32[]{:S(2)}) async-start(bf16[4,128,384]{2,1,0:T(8,128)(2,1)} %get-tuple-element.109), calls=%async_computation | async-start | bytes 786432 | tf_op jit(solution)/shard_map/all_to_all | solution.py:91
  42.1 6.3 %copy-start.15 = (bf16[768,1024]{1,0:T(8,128)(2,1)S(1)}, bf16[768,1024]{1,0:T(8,128)(2,1)}, u32[]{:S(2)}) copy-start(bf16[768,1024]{1,0:T(8,128)(2,1)} %copy-done.14) | copy-start | bytes 4718596
  42.1 6.3 %copy-start.18 = (f32[512,384]{1,0:T(8,128)S(1)}, f32[512,384]{1,0:T(8,128)}, u32[]{:S(2)}) copy-start(f32[512,384]{1,0:T(8,128)} %get-tuple-element.102.grad_residual) | copy-start | bytes 2359300
  42.1 6.3 %copy-start.20 = (bf16[384,512]{1,0:T(8,128)(2,1)S(1)}, bf16[384,512]{1,0:T(8,128)(2,1)}, u32[]{:S(2)}) copy-start(bf16[384,512]{1,0:T(8,128)(2,1)} %copy-done.19) | copy-start | bytes 1179652
  42.1 6.3 %copy-start.21 = (bf16[384,512]{1,0:T(8,128)(2,1)S(1)}, bf16[384,512]{1,0:T(8,128)(2,1)}, u32[]{:S(2)}) copy-start(bf16[384,512]{1,0:T(8,128)(2,1)} %get-tuple-element.100.grad_attended) | copy-start | bytes 1179652
  43.8 4.5 %copy-start.8 = (bf16[1152,384]{1,0:T(8,128)(2,1)S(1)}, bf16[1152,384]{1,0:T(8,128)(2,1)}, u32[]{:S(2)}) copy-start(bf16[1152,384]{1,0:T(8,128)(2,1)} %copy-done.7) | copy-start | bytes 2654212
  43.8 4.5 %copy-start.10 = (bf16[512,384]{1,0:T(8,128)(2,1)S(1)}, bf16[512,384]{1,0:T(8,128)(2,1)}, u32[]{:S(2)}) copy-start(bf16[512,384]{1,0:T(8,128)(2,1)} %copy-done.9) | copy-start | bytes 1179652
  43.9 4.5 %copy-start.17 = (f32[384,512]{1,0:T(8,128)S(1)}, f32[384,512]{1,0:T(8,128)}, u32[]{:S(2)}) copy-start(f32[384,512]{1,0:T(8,128)} %copy-done.16) | copy-start | bytes 2359300
  43.9 4.5 %copy-start.22 = (bf16[384,384]{1,0:T(8,128)(2,1)S(1)}, bf16[384,384]{1,0:T(8,128)(2,1)}, u32[]{:S(2)}) copy-start(bf16[384,384]{1,0:T(8,128)(2,1)} %get-tuple-element.101.packed_output) | copy-start | bytes 884740
  44.8 15.3 %collective-permute-start.8 = (bf16[384,384]{1,0:T(8,128)(2,1)}, bf16[384,384]{1,0:T(8,128)(2,1)S(1)}, u32[]{:S(2)}, u32[]{:S(2)}) collective-permute-start(bf16[384,384]{1,0:T(8,128)(2,1)} %get-tuple-element.147), channel_id=1, source_target_pairs={{0,8},{8,0},{16,24},{24,16},{1,9},{9,1},{17,25},{25,17},{2,10},{10... | collective-permute-start | bytes 884744 | tf_op jit(solution)/shard_map/ppermute | solution.py:131
  46.3 15.5 %collective-permute-start.9 = (bf16[384,384]{1,0:T(8,128)(2,1)}, bf16[384,384]{1,0:T(8,128)(2,1)S(1)}, u32[]{:S(2)}, u32[]{:S(2)}) collective-permute-start(bf16[384,384]{1,0:T(8,128)(2,1)} %get-tuple-element.146), channel_id=1, source_target_pairs={{0,16},{8,24},{16,0},{24,8},{1,17},{9,25},{17,1},{25,9},{2,18},{10... | collective-permute-start | bytes 884744 | tf_op jit(solution)/shard_map/ppermute | solution.py:131
  47.9 14.0 %collective-permute-start.10 = (bf16[384,384]{1,0:T(8,128)(2,1)}, bf16[384,384]{1,0:T(8,128)(2,1)S(1)}, u32[]{:S(2)}, u32[]{:S(2)}) collective-permute-start(bf16[384,384]{1,0:T(8,128)(2,1)} %get-tuple-element.145), channel_id=1, source_target_pairs={{0,24},{8,16},{16,8},{24,0},{1,25},{9,17},{17,9},{25,1},{2,26},{10... | collective-permute-start | bytes 884744 | tf_op jit(solution)/shard_map/ppermute | solution.py:131
  61.9 6.0 %collective-permute-start.12 = (bf16[768,384]{1,0:T(8,128)(2,1)S(1)}, bf16[768,384]{1,0:T(8,128)(2,1)}, u32[]{:S(2)}, u32[]{:S(2)}) collective-permute-start(bf16[768,384]{1,0:T(8,128)(2,1)S(1)} %get-tuple-element.113), channel_id=1, source_target_pairs={{0,1},{1,0},{2,3},{3,2},{4,5},{5,4},{6,7},{7,6},{8,9},{9,8},{10,11... | collective-permute-start | bytes 1769480 | tf_op jit(solution)/shard_map/ppermute | solution.py:117
  61.9 15.8 %collective-permute-start.11 = (bf16[528,384]{1,0:T(8,128)(2,1)}, bf16[528,384]{1,0:T(8,128)(2,1)S(1)}, u32[]{:S(2)}, u32[]{:S(2)}) collective-permute-start(bf16[528,384]{1,0:T(8,128)(2,1)} %get-tuple-element.111), channel_id=1, source_target_pairs={{0,1},{1,0},{2,3},{3,2},{4,5},{5,4},{6,7},{7,6},{8,9},{9,8},{10,11... | collective-permute-start | bytes 1216520 | tf_op jit(solution)/shard_map/ppermute | solution.py:117
  63.3 14.4 %all-to-all-start.1 = ((bf16[4,96,384]{2,1,0:T(8,128)(2,1)}), bf16[4,96,384]{2,1,0:T(8,128)(2,1)S(1)}, u32[]{:S(2)}, u32[]{:S(2)}) async-start(bf16[4,96,384]{2,1,0:T(8,128)(2,1)} %bitcast.13), calls=%async_computation.1 | async-start | bytes 589824 | tf_op jit(solution)/shard_map/all_to_all | solution.py:171
  69.3 10.4 %collective-permute-start.19 = (bf16[192,384]{1,0:T(8,128)(2,1)S(1)}, bf16[192,384]{1,0:T(8,128)(2,1)S(1)}, u32[]{:S(2)}, u32[]{:S(2)}) collective-permute-start(bf16[192,384]{1,0:T(8,128)(2,1)S(1)} %get-tuple-element.150), channel_id=1, source_target_pairs={{0,8},{8,0},{16,24},{24,16},{1,9},{9,1},{17,25},{25,17},{2,10},{10... | collective-permute-start | bytes 442376 | tf_op jit(solution)/shard_map/ppermute | solution.py:131
  70.6 11.5 %collective-permute-start.20 = (bf16[192,384]{1,0:T(8,128)(2,1)S(1)}, bf16[192,384]{1,0:T(8,128)(2,1)S(1)}, u32[]{:S(2)}, u32[]{:S(2)}) collective-permute-start(bf16[192,384]{1,0:T(8,128)(2,1)S(1)} %get-tuple-element.149), channel_id=1, source_target_pairs={{0,16},{8,24},{16,0},{24,8},{1,17},{9,25},{17,1},{25,9},{2,18},{10... | collective-permute-start | bytes 442376 | tf_op jit(solution)/shard_map/ppermute | solution.py:131
  71.5 10.7 %collective-permute-start.21 = (bf16[192,384]{1,0:T(8,128)(2,1)S(1)}, bf16[192,384]{1,0:T(8,128)(2,1)S(1)}, u32[]{:S(2)}, u32[]{:S(2)}) collective-permute-start(bf16[192,384]{1,0:T(8,128)(2,1)S(1)} %get-tuple-element.148), channel_id=1, source_target_pairs={{0,24},{8,16},{16,8},{24,0},{1,25},{9,17},{17,9},{25,1},{2,26},{10... | collective-permute-start | bytes 442376 | tf_op jit(solution)/shard_map/ppermute | solution.py:131
  77.7 6.6 %collective-permute-start.13 = (bf16[112,384]{1,0:T(8,128)(2,1)S(1)}, bf16[112,384]{1,0:T(8,128)(2,1)S(1)}, u32[]{:S(2)}, u32[]{:S(2)}) collective-permute-start(bf16[112,384]{1,0:T(8,128)(2,1)S(1)} %line_total.1.refs_0_), channel_id=1, source_target_pairs={{0,2},{1,3},{2,0},{3,1},{4,6},{5,7},{6,4},{7,5},{8,10},{9,11},{10,... | collective-permute-start | bytes 258056 | tf_op jit(solution)/shard_map/ppermute | solution.py:126
  77.8 9.6 %collective-permute-start.14 = (bf16[112,384]{1,0:T(8,128)(2,1)S(1)}, bf16[112,384]{1,0:T(8,128)(2,1)S(1)}, u32[]{:S(2)}, u32[]{:S(2)}) collective-permute-start(bf16[112,384]{1,0:T(8,128)(2,1)S(1)} %line_total.1.refs_0_), channel_id=1, source_target_pairs={{0,4},{1,5},{2,6},{3,7},{4,0},{5,1},{6,2},{7,3},{8,12},{9,13},{10,... | collective-permute-start | bytes 258056 | tf_op jit(solution)/shard_map/ppermute | solution.py:126
  79.7 7.7 %collective-permute-start.15 = (bf16[112,384]{1,0:T(8,128)(2,1)S(1)}, bf16[112,384]{1,0:T(8,128)(2,1)S(1)}, u32[]{:S(2)}, u32[]{:S(2)}) collective-permute-start(bf16[112,384]{1,0:T(8,128)(2,1)S(1)} %line_total.1.refs_0_), channel_id=1, source_target_pairs={{0,6},{1,7},{2,4},{3,5},{4,2},{5,3},{6,0},{7,1},{8,14},{9,15},{10,... | collective-permute-start | bytes 258056 | tf_op jit(solution)/shard_map/ppermute | solution.py:126
  82.3 7.3 %collective-permute-start.22 = (bf16[48,384]{1,0:T(8,128)(2,1)S(1)}, bf16[48,384]{1,0:T(8,128)(2,1)S(1)}, u32[]{:S(2)}, u32[]{:S(2)}) collective-permute-start(bf16[48,384]{1,0:T(8,128)(2,1)S(1)} %get-tuple-element.162), channel_id=1, source_target_pairs={{0,2},{1,3},{2,0},{3,1},{4,6},{5,7},{6,4},{7,5},{8,10},{9,11},{10,... | collective-permute-start | bytes 110600 | tf_op jit(solution)/shard_map/ppermute | solution.py:126
  82.3 8.7 %collective-permute-start.23 = (bf16[48,384]{1,0:T(8,128)(2,1)S(1)}, bf16[48,384]{1,0:T(8,128)(2,1)S(1)}, u32[]{:S(2)}, u32[]{:S(2)}) collective-permute-start(bf16[48,384]{1,0:T(8,128)(2,1)S(1)} %get-tuple-element.161), channel_id=1, source_target_pairs={{0,4},{1,5},{2,6},{3,7},{4,0},{5,1},{6,2},{7,3},{8,12},{9,13},{10,... | collective-permute-start | bytes 110600 | tf_op jit(solution)/shard_map/ppermute | solution.py:126
  84.3 25.1 %copy-start.1 = (bf16[384,2304]{1,0:T(8,128)(2,1)S(1)}, bf16[384,2304]{1,0:T(8,128)(2,1)}, u32[]{:S(2)}) copy-start(bf16[384,2304]{1,0:T(8,128)(2,1)} %refs_8_.1) | copy-start | bytes 5308420
  84.3 6.7 %collective-permute-start.24 = (bf16[48,384]{1,0:T(8,128)(2,1)S(1)}, bf16[48,384]{1,0:T(8,128)(2,1)S(1)}, u32[]{:S(2)}, u32[]{:S(2)}) collective-permute-start(bf16[48,384]{1,0:T(8,128)(2,1)S(1)} %get-tuple-element.160), channel_id=1, source_target_pairs={{0,6},{1,7},{2,4},{3,5},{4,2},{5,3},{6,0},{7,1},{8,14},{9,15},{10,... | collective-permute-start | bytes 110600 | tf_op jit(solution)/shard_map/ppermute | solution.py:126
  87.5 17.6 %collective-permute-start.16 = (bf16[400,384]{1,0:T(8,128)(2,1)S(1)}, bf16[400,384]{1,0:T(8,128)(2,1)S(1)}, u32[]{:S(2)}, u32[]{:S(2)}) collective-permute-start(bf16[400,384]{1,0:T(8,128)(2,1)S(1)} %line_join.1.refs_0_), channel_id=1, source_target_pairs={{0,8},{8,0},{16,24},{24,16},{1,9},{9,1},{17,25},{25,17},{2,10},{10... | collective-permute-start | bytes 921608 | tf_op jit(solution)/shard_map/ppermute | solution.py:131
  88.8 16.3 %collective-permute-start.17 = (bf16[400,384]{1,0:T(8,128)(2,1)S(1)}, bf16[400,384]{1,0:T(8,128)(2,1)S(1)}, u32[]{:S(2)}, u32[]{:S(2)}) collective-permute-start(bf16[400,384]{1,0:T(8,128)(2,1)S(1)} %line_join.1.refs_0_), channel_id=1, source_target_pairs={{0,16},{8,24},{16,0},{24,8},{1,17},{9,25},{17,1},{25,9},{2,18},{10... | collective-permute-start | bytes 921608 | tf_op jit(solution)/shard_map/ppermute | solution.py:131
  89.6 15.5 %collective-permute-start.18 = (bf16[400,384]{1,0:T(8,128)(2,1)S(1)}, bf16[400,384]{1,0:T(8,128)(2,1)S(1)}, u32[]{:S(2)}, u32[]{:S(2)}) collective-permute-start(bf16[400,384]{1,0:T(8,128)(2,1)S(1)} %line_join.1.refs_0_), channel_id=1, source_target_pairs={{0,24},{8,16},{16,8},{24,0},{1,25},{9,17},{17,9},{25,1},{2,26},{10... | collective-permute-start | bytes 921608 | tf_op jit(solution)/shard_map/ppermute | solution.py:131
  91.6 6.6 %collective-permute-start.25 = (bf16[176,384]{1,0:T(8,128)(2,1)S(1)}, bf16[176,384]{1,0:T(8,128)(2,1)S(1)}, u32[]{:S(2)}, u32[]{:S(2)}) collective-permute-start(bf16[176,384]{1,0:T(8,128)(2,1)S(1)} %get-tuple-element.121), channel_id=1, source_target_pairs={{0,2},{1,3},{2,0},{3,1},{4,6},{5,7},{6,4},{7,5},{8,10},{9,11},{10,... | collective-permute-start | bytes 405512 | tf_op jit(solution)/shard_map/ppermute | solution.py:83
  93.7 7.4 %collective-permute-start.26 = (bf16[176,384]{1,0:T(8,128)(2,1)S(1)}, bf16[176,384]{1,0:T(8,128)(2,1)S(1)}, u32[]{:S(2)}, u32[]{:S(2)}) collective-permute-start(bf16[176,384]{1,0:T(8,128)(2,1)S(1)} %get-tuple-element.122), channel_id=1, source_target_pairs={{0,4},{1,5},{2,6},{3,7},{4,0},{5,1},{6,2},{7,3},{8,12},{9,13},{10,... | collective-permute-start | bytes 405512 | tf_op jit(solution)/shard_map/ppermute | solution.py:83
  98.2 6.9 %collective-permute-start.27 = (bf16[176,384]{1,0:T(8,128)(2,1)S(1)}, bf16[176,384]{1,0:T(8,128)(2,1)S(1)}, u32[]{:S(2)}, u32[]{:S(2)}) collective-permute-start(bf16[176,384]{1,0:T(8,128)(2,1)S(1)} %get-tuple-element.123), channel_id=1, source_target_pairs={{0,6},{1,7},{2,4},{3,5},{4,2},{5,3},{6,0},{7,1},{8,14},{9,15},{10,... | collective-permute-start | bytes 405512 | tf_op jit(solution)/shard_map/ppermute | solution.py:83
  101.1 6.0 %collective-permute-start.28 = (bf16[400,384]{1,0:T(8,128)(2,1)S(1)}, bf16[400,384]{1,0:T(8,128)(2,1)S(1)}, u32[]{:S(2)}, u32[]{:S(2)}) collective-permute-start(bf16[400,384]{1,0:T(8,128)(2,1)S(1)} %line_join.1.refs_0_), channel_id=1, source_target_pairs={{0,1},{1,0},{2,3},{3,2},{4,5},{5,4},{6,7},{7,6},{8,9},{9,8},{10,11... | collective-permute-start | bytes 921608 | tf_op jit(solution)/shard_map/ppermute | solution.py:117
  105.1 2.9 %collective-permute-start.29 = (bf16[400,384]{1,0:T(8,128)(2,1)S(1)}, bf16[400,384]{1,0:T(8,128)(2,1)S(1)}, u32[]{:S(2)}, u32[]{:S(2)}) collective-permute-start(bf16[400,384]{1,0:T(8,128)(2,1)S(1)} %collective-permute-done.16.refs_1_), channel_id=1, source_target_pairs={{0,1},{1,0},{2,3},{3,2},{4,5},{5,4},{6,7},{7,6},{8,9},{9,8},{10,11... | collective-permute-start | bytes 921608 | tf_op jit(solution)/shard_map/ppermute | solution.py:117
  105.2 4.2 %collective-permute-start.30 = (bf16[400,384]{1,0:T(8,128)(2,1)S(1)}, bf16[400,384]{1,0:T(8,128)(2,1)S(1)}, u32[]{:S(2)}, u32[]{:S(2)}) collective-permute-start(bf16[400,384]{1,0:T(8,128)(2,1)S(1)} %collective-permute-done.17.refs_2_), channel_id=1, source_target_pairs={{0,1},{1,0},{2,3},{3,2},{4,5},{5,4},{6,7},{7,6},{8,9},{9,8},{10,11... | collective-permute-start | bytes 921608 | tf_op jit(solution)/shard_map/ppermute | solution.py:117
  105.7 3.7 %collective-permute-start.31 = (bf16[400,384]{1,0:T(8,128)(2,1)S(1)}, bf16[400,384]{1,0:T(8,128)(2,1)S(1)}, u32[]{:S(2)}, u32[]{:S(2)}) collective-permute-start(bf16[400,384]{1,0:T(8,128)(2,1)S(1)} %collective-permute-done.18.refs_3_), channel_id=1, source_target_pairs={{0,1},{1,0},{2,3},{3,2},{4,5},{5,4},{6,7},{7,6},{8,9},{9,8},{10,11... | collective-permute-start | bytes 921608 | tf_op jit(solution)/shard_map/ppermute | solution.py:117
  105.8 9.1 %collective-permute-start.32 = (bf16[192,384]{1,0:T(8,128)(2,1)S(1)}, bf16[192,384]{1,0:T(8,128)(2,1)S(1)}, u32[]{:S(2)}, u32[]{:S(2)}) collective-permute-start(bf16[192,384]{1,0:T(8,128)(2,1)S(1)} %pad_maximum_fusion.1.refs_0_), channel_id=1, source_target_pairs={{0,8},{8,0},{16,24},{24,16},{1,9},{9,1},{17,25},{25,17},{2,10},{10... | collective-permute-start | bytes 442376 | tf_op jit(solution)/shard_map/ppermute | solution.py:131
  107.1 7.8 %collective-permute-start.33 = (bf16[192,384]{1,0:T(8,128)(2,1)S(1)}, bf16[192,384]{1,0:T(8,128)(2,1)S(1)}, u32[]{:S(2)}, u32[]{:S(2)}) collective-permute-start(bf16[192,384]{1,0:T(8,128)(2,1)S(1)} %pad_maximum_fusion.1.refs_0_), channel_id=1, source_target_pairs={{0,16},{8,24},{16,0},{24,8},{1,17},{9,25},{17,1},{25,9},{2,18},{10... | collective-permute-start | bytes 442376 | tf_op jit(solution)/shard_map/ppermute | solution.py:131
  108.0 8.2 %collective-permute-start.34 = (bf16[192,384]{1,0:T(8,128)(2,1)S(1)}, bf16[192,384]{1,0:T(8,128)(2,1)S(1)}, u32[]{:S(2)}, u32[]{:S(2)}) collective-permute-start(bf16[192,384]{1,0:T(8,128)(2,1)S(1)} %pad_maximum_fusion.1.refs_0_), channel_id=1, source_target_pairs={{0,24},{8,16},{16,8},{24,0},{1,25},{9,17},{17,9},{25,1},{2,26},{10... | collective-permute-start | bytes 442376 | tf_op jit(solution)/shard_map/ppermute | solution.py:131
  109.4 7.3 %collective-permute-start.35 = (bf16[192,384]{1,0:T(8,128)(2,1)S(1)}, bf16[192,384]{1,0:T(8,128)(2,1)S(1)}, u32[]{:S(2)}, u32[]{:S(2)}) collective-permute-start(bf16[192,384]{1,0:T(8,128)(2,1)S(1)} %pad_maximum_fusion.1.refs_0_), channel_id=1, source_target_pairs={{0,1},{1,0},{2,3},{3,2},{4,5},{5,4},{6,7},{7,6},{8,9},{9,8},{10,11... | collective-permute-start | bytes 442376 | tf_op jit(solution)/shard_map/ppermute | solution.py:117
  116.2 1.4 %collective-permute-start.36 = (bf16[192,384]{1,0:T(8,128)(2,1)S(1)}, bf16[192,384]{1,0:T(8,128)(2,1)S(1)}, u32[]{:S(2)}, u32[]{:S(2)}) collective-permute-start(bf16[192,384]{1,0:T(8,128)(2,1)S(1)} %collective-permute-done.32.refs_1_), channel_id=1, source_target_pairs={{0,1},{1,0},{2,3},{3,2},{4,5},{5,4},{6,7},{7,6},{8,9},{9,8},{10,11... | collective-permute-start | bytes 442376 | tf_op jit(solution)/shard_map/ppermute | solution.py:117
  116.2 1.6 %collective-permute-start.37 = (bf16[192,384]{1,0:T(8,128)(2,1)S(1)}, bf16[192,384]{1,0:T(8,128)(2,1)S(1)}, u32[]{:S(2)}, u32[]{:S(2)}) collective-permute-start(bf16[192,384]{1,0:T(8,128)(2,1)S(1)} %collective-permute-done.33.refs_2_), channel_id=1, source_target_pairs={{0,1},{1,0},{2,3},{3,2},{4,5},{5,4},{6,7},{7,6},{8,9},{9,8},{10,11... | collective-permute-start | bytes 442376 | tf_op jit(solution)/shard_map/ppermute | solution.py:117
  116.7 1.4 %collective-permute-start.38 = (bf16[192,384]{1,0:T(8,128)(2,1)S(1)}, bf16[192,384]{1,0:T(8,128)(2,1)S(1)}, u32[]{:S(2)}, u32[]{:S(2)}) collective-permute-start(bf16[192,384]{1,0:T(8,128)(2,1)S(1)} %collective-permute-done.34.refs_3_), channel_id=1, source_target_pairs={{0,1},{1,0},{2,3},{3,2},{4,5},{5,4},{6,7},{7,6},{8,9},{9,8},{10,11... | collective-permute-start | bytes 442376 | tf_op jit(solution)/shard_map/ppermute | solution.py:117
  (1 other events, 1.5 us)
